TPU v7x, 32 devices: a whole 2x2x4 slice. The times are simulated.
32 devices in a mesh: patch: 2 (over x), wrow: 4 (over z), wcol: 4 (over y, core).
Axes of the slice: x: 2, y: 2, z: 4, core: 2. Of those that a mesh axis runs over, the one named last changes fastest.
Arguments:
- hidden_states: bfloat16 [4, 1024, 1536], P('wrow', ('patch', 'wcol')), may hold values from -6 to 6
- modulation: float32 [4, 3, 1536], P('wrow'), may hold values from -4 to 4
- w_qkv: bfloat16 [1536, 3, 1536], P('wrow', None, 'wcol'), may hold values from -1 to 1
- w_out: bfloat16 [1536, 1536], P('wcol', 'wrow'), may hold values from -0.15625 to 0.15625
- lengths: int32 [4], P('wrow'), may hold values from 1 to 1024, 2560 in all
Outputs:
- updated: bfloat16 [4, 1024, 1536], P('wrow', ('patch', 'wcol'))
Inputs may be any that keep to these rules, and one draw needn't show every extreme that they name: lengths[v] real tokens in video v, padding after them; the longest video fills all 1024 slots.
All inputs are finite; a program needn't handle non-finite values. No bound on the sum of `lengths` on one device may be relied on, other than what follows from the above.
Results may differ from a plain program's by a relative error of at most 0.015.
The roundings to bfloat16 on the way count: a program that leaves them out, or rounds other values in their place, can miss the bound.
Values may be sent and summed in bfloat16 or wider, within the bound.
No kernel may reach another device: no remote copies, remote signals or barrier semaphores. Data moves between devices by JAX's collectives and lax.ppermute only.
A program may use at most 64 MiB of HBM per device.

v0:
```python
import jax
import jax.numpy as jnp
from jax import lax
from jax.sharding import PartitionSpec as P

HD = 128


EPSILON = 1e-06
FLOOR = -1e30


def modulated_norm(states, shift, scale):
    values = states.astype(jnp.float32)
    center = jnp.mean(values, axis=-1, keepdims=True)
    spread = jnp.mean(jnp.square(values - center), axis=-1, keepdims=True)
    return ((values - center) * lax.rsqrt(spread + EPSILON) * (1.0 + scale) + shift).astype(
        jnp.bfloat16
    )


def absorb(carry, keys, values, first, queries, limits):
    peak, weight_sum, numer = carry
    videos_here = keys.shape[0]
    count = keys.shape[1]
    heads_here = queries.shape[2]
    head_size = queries.shape[3]
    key_heads = keys.reshape(videos_here, count, heads_here, head_size)
    value_heads = values.reshape(videos_here, count, heads_here, head_size)
    scores = jnp.einsum(
        "vqhd,vkhd->vhqk", queries, key_heads, preferred_element_type=jnp.float32
    ) * head_size ** (-0.5)
    position = first + jnp.arange(count, dtype=jnp.int32)
    valid = (position[None, :] < limits[:, None])[:, None, None, :]
    scores = jnp.where(valid, scores, FLOOR)
    new_peak = jnp.maximum(peak, jnp.max(scores, axis=-1))
    factor = jnp.exp(peak - new_peak)
    probs = jnp.exp(scores - new_peak[..., None]) * valid.astype(jnp.float32)
    weight_sum = weight_sum * factor + jnp.sum(probs, axis=-1)
    numer = numer * factor[..., None] + jnp.einsum(
        "vhqk,vkhd->vhqd",
        probs.astype(jnp.bfloat16),
        value_heads,
        preferred_element_type=jnp.float32,
    )
    return (new_peak, weight_sum, numer)


def body(hidden_states, modulation, w_qkv, w_out, lengths):
    videos_here = hidden_states.shape[0]
    width = hidden_states.shape[2]
    shift = modulation[:, 0][:, None, :]
    scale = modulation[:, 1][:, None, :]
    gate = modulation[:, 2][:, None, :]
    normed = modulated_norm(hidden_states, shift, scale)
    tile_rows = lax.all_gather(normed, "wcol", axis=1, tiled=True)
    tile_len = tile_rows.shape[1]
    local_cols = w_qkv.shape[2]
    flat_rows = tile_rows.reshape(videos_here * tile_len, width)
    piece = lax.all_gather(w_qkv, "wrow", axis=0, tiled=True)
    mixed = jnp.dot(
        flat_rows, piece.reshape(piece.shape[0], 3 * local_cols), preferred_element_type=jnp.float32
    )
    mixed = mixed.reshape(videos_here, tile_len, 3 * local_cols)
    mixed = mixed.astype(jnp.bfloat16).reshape(videos_here, tile_len, 3, local_cols)
    heads_here = local_cols // HD
    queries = mixed[:, :, 0].reshape(videos_here, tile_len, heads_here, HD)
    keys = mixed[:, :, 1]
    values = mixed[:, :, 2]
    start_peak = jnp.full((videos_here, heads_here, tile_len), FLOOR, jnp.float32)
    start_sum = jnp.zeros((videos_here, heads_here, tile_len), jnp.float32)
    start_numer = jnp.zeros((videos_here, heads_here, tile_len, HD), jnp.float32)
    key_piece = lax.all_gather(keys, "patch", axis=1, tiled=True)
    value_piece = lax.all_gather(values, "patch", axis=1, tiled=True)
    count = key_piece.shape[1]
    block_len = 512

    def one_block(index, inner):
        offset = index * block_len
        key_block = lax.dynamic_slice_in_dim(key_piece, offset, block_len, 1)
        value_block = lax.dynamic_slice_in_dim(value_piece, offset, block_len, 1)
        return absorb(inner, key_block, value_block, offset, queries, lengths)

    peak, weight_sum, numer = lax.fori_loop(
        0, count // block_len, one_block, (start_peak, start_sum, start_numer)
    )
    attended = (numer / weight_sum[..., None]).astype(jnp.bfloat16)
    attended = jnp.transpose(attended, (0, 2, 1, 3)).reshape(videos_here * tile_len, local_cols)
    partial_out = jnp.dot(
        attended,
        lax.all_gather(w_out, "wrow", axis=1, tiled=True),
        preferred_element_type=jnp.float32,
    )
    partial_out = partial_out.reshape(videos_here, tile_len, width)
    out_proj = lax.psum_scatter(
        partial_out.astype(jnp.bfloat16), "wcol", scatter_dimension=1, tiled=True
    ).astype(jnp.float32)
    return (hidden_states.astype(jnp.float32) + gate * out_proj).astype(jnp.bfloat16)


def solution(mesh):
    placed = (
        P("wrow", ("patch", "wcol"), None),
        P("wrow", None, None),
        P("wrow", None, "wcol"),
        P("wcol", "wrow"),
        P("wrow"),
    )
    return jax.shard_map(
        body,
        mesh=mesh,
        in_specs=placed,
        out_specs=P("wrow", ("patch", "wcol"), None),
        check_vma=False,
    )
```

profile of v0, /device:TPU:0, one launch (start us, length us, event | category | flops | bytes accessed | tf_op | source)
XLA Modules:
  0.0 193.7 jit_solution(153866179162445045)
XLA Ops:
  6.5 1.4 slice_reduce_fusion.1
  7.9 1.1 convert_reduce_fusion
  9.0 1.2 fusion.21
  10.3 2.1 %fusion.24 = bf16[1,128,1536]{2,1,0:T(8,128)(2,1)} fusion(bf16[1,128,1536]{2,1,0:T(8,128)(2,1)} %param.7, f32[1536]{0:T(1024)S(1)} %get-tuple-element.183, f32[1536]{0:T(1024)S(1)} %get-tuple-element.184, f32[128]{0:T(128)S(1)} %add_rsqrt_fusion, f32[128]{0:T(128)S(1)} %broadcast_multiply_fusion), kind=kLoop, calls=%fused_computation.35 | loop fusion | flops 1179648 | bytes 799744 | tf_op jit(solution)/shard_map/convert_element_type | solution.py:17
  12.4 2.3 %copy.12 = bf16[384,3,384]{0,2,1:T(8,128)(2,1)} copy(bf16[384,3,384]{2,0,1:T(8,128)(2,1)} %param.9) | data formatting | bytes 1769472 | tf_op args[2]
  15.6 19.3 %all-gather.6.cloned.1.call-done = bf16[1,512,1536]{2,1,0:T(8,128)(2,1)} async-done(((bf16[1,128,1536]{2,1,0:T(8,128)(2,1)}), bf16[1,512,1536]{2,1,0:T(8,128)(2,1)}) %all-gather.6.cloned.1.call-update) | async-done | bytes 1572880 | tf_op jit(solution)/shard_map/all_gather | solution.py:56
  34.9 71.5 %all-gather.8.cloned.1.call-done = bf16[1536,3,384]{0,2,1:T(8,128)(2,1)} async-done(((bf16[384,3,384]{0,2,1:T(8,128)(2,1)}), bf16[1536,3,384]{0,2,1:T(8,128)(2,1)}) %all-gather.8.cloned.1.call-update) | async-done | bytes 3538960 | tf_op jit(solution)/shard_map/all_gather | solution.py:60
  106.4 4.7 %convolution_convert_fusion = bf16[512,1152]{1,0:T(8,128)(2,1)S(1)} fusion(bf16[1536,1152]{0,1:T(8,128)(2,1)} %bitcast.89, bf16[1,512,1536]{2,1,0:T(8,128)(2,1)} %all-gather.6.cloned.1.call-done), kind=kOutput, calls=%fused_computation.23 | convolution fusion | flops 1812529152 | bytes 6291456 | tf_op jit(solution)/shard_map/dot_general | solution.py:61
  111.8 11.7 %all-gather = bf16[1,1024,1,384]{1,3,2,0:T(8,128)(2,1)} all-gather(bf16[1,512,1,384]{1,3,2,0:T(8,128)(2,1)S(1)} %get-tuple-element.211), channel_id=2, replica_groups=mesh['patch'=2,'wrow'=4,'wcol'=4] {'patch'}, dimensions={1}, use_global_device_ids=true | all-gather | bytes 1179648 | tf_op jit(solution)/shard_map/all_gather | solution.py:73
  123.5 10.8 %all-gather.1 = bf16[1,1024,1,384]{1,3,2,0:T(8,128)(2,1)} all-gather(bf16[1,512,1,384]{1,3,2,0:T(8,128)(2,1)S(1)} %get-tuple-element.209), channel_id=3, replica_groups=mesh['patch'=2,'wrow'=4,'wcol'=4] {'patch'}, dimensions={1}, use_global_device_ids=true | all-gather | bytes 1179648 | tf_op jit(solution)/shard_map/all_gather | solution.py:74
  134.5 17.7 %while.18 = (s32[]{:T(128)}, f32[1,3,512]{2,1,0:T(4,128)S(1)}, f32[1,3,512]{2,1,0:T(4,128)}, f32[1,3,512,128]{3,2,1,0:T(8,128)}, s32[1]{0:T(128)}, /*index=5*/bf...) while((s32[]{:T(128)}, f32[1,3,512]{2,1,0:T(4,128)S(1)}, ...), condition=%wide.region_5.6_spmd.clone, body=%wide.region_2.5_spmd.clone.sunk | while | flops 413477376 | bytes 13930823 | solution.py:84
  134.5 1.9 constant_dynamic-slice_fusion.3
  136.4 1.2 fusion.43
  138.5 3.2 %fusion.46 = f32[1,3,512,128]{3,2,1,0:T(8,128)} fusion(bf16[512,3,128]{0,2,1:T(8,128)(2,1)} %bitcast.82, f32[3,512,512]{2,1,0:T(8,128)S(1)} %get-tuple-element.273, f32[512]{0:T(512)} %get-tuple-element.274, f32[3,512]{1,0:T(4,128)S(1)} %bitcast.84, pred[512]{0:T(512)(128)(4,1)} %copy-done.4, f32[1,3,512,128]{3,2,1,0:T(8,128)} %get-tuple-element.292, ...), kind=kOutput, calls=%fused_computation.9.clone.1 | convolution fusion | flops 205848576 | bytes 5126657 | tf_op jit(solution)/shard_map/while/body/eval_jaxpr/vhqk,vkhd->vhqd/dot_general | solution.py:40
  141.7 0.9 fusion.45
  143.2 1.9 constant_dynamic-slice_fusion.3
  145.1 1.2 fusion.43
  147.2 3.4 %fusion.46 = f32[1,3,512,128]{3,2,1,0:T(8,128)} fusion(bf16[512,3,128]{0,2,1:T(8,128)(2,1)} %bitcast.82, f32[3,512,512]{2,1,0:T(8,128)S(1)} %get-tuple-element.273, f32[512]{0:T(512)} %get-tuple-element.274, f32[3,512]{1,0:T(4,128)S(1)} %bitcast.84, pred[512]{0:T(512)(128)(4,1)} %copy-done.4, f32[1,3,512,128]{3,2,1,0:T(8,128)} %get-tuple-element.292, ...), kind=kOutput, calls=%fused_computation.9.clone.1 | convolution fusion | flops 205848576 | bytes 5126657 | tf_op jit(solution)/shard_map/while/body/eval_jaxpr/vhqk,vkhd->vhqd/dot_general | solution.py:40
  150.7 0.9 fusion.45
  152.2 1.4 copy.15
  153.6 0.8 divide_convert_fusion
  154.5 3.4 %fusion.17 = bf16[1,512,1536]{2,1,0:T(8,128)(2,1)} fusion(bf16[512,384]{0,1:T(8,128)(2,1)S(1)} %bitcast.87, bf16[384,1536]{1,0:T(8,128)(2,1)} %all-gather.10.cloned.1.call-done), kind=kOutput, calls=%fused_computation.25 | convolution fusion | flops 604766208 | bytes 3145728 | tf_op jit(solution)/shard_map/dot_general | solution.py:89
  158.0 27.3 %reduce-scatter.2.cloned.1.call-done = bf16[1,128,1536]{2,1,0:T(8,128)(2,1)} async-done(((bf16[1,512,1536]{2,1,0:T(8,128)(2,1)}), bf16[1,128,1536]{2,1,0:T(8,128)(2,1)}) %reduce-scatter.2.cloned.1.call-update) | async-done | bytes 393232 | tf_op jit(solution)/shard_map/reduce_scatter | solution.py:95
  185.3 1.9 fusion.25
  (49 shorter events, 4.7 us)
Async XLA Ops:
  6.5 28.4 %all-gather.6.cloned.1.call-start = ((), (), s32[]{:S(2)}) async-start(), calls=%async_computation.1 | async-start | bytes 1966080 | tf_op jit(solution)/shard_map/all_gather | solution.py:56
  12.4 94.0 %all-gather.8.cloned.1.call-start = ((), (), s32[]{:S(2)}) async-start(), calls=%async_computation.2 | async-start | bytes 4423680 | tf_op jit(solution)/shard_map/all_gather | solution.py:60
  14.7 139.7 %all-gather.10.cloned.1.call-start = ((), (), s32[]{:S(2)}) async-start(), calls=%async_computation.3 | async-start | bytes 1474560 | tf_op jit(solution)/shard_map/all_gather | solution.py:91
  15.5 169.8 %reduce-scatter.2.cloned.1.call-start = ((), (), s32[]{:S(2)}) async-start(), calls=%async_computation.4 | async-start | bytes 1966080 | tf_op jit(solution)/shard_map/reduce_scatter | solution.py:95
  137.6 0.8 copy-start.4
  138.5 3.2 %copy-start.3 = (f32[512]{0:T(512)S(1)}, f32[512]{0:T(512)}, u32[]{:S(2)}) copy-start(f32[512]{0:T(512)} %get-tuple-element.274) | copy-start | bytes 6148 | tf_op jit(solution)/shard_map/while
  138.5 3.2 %copy-start.5 = (pred[512]{0:T(512)(128)(4,1)S(1)}, pred[512]{0:T(512)(128)(4,1)}, u32[]{:S(2)}) copy-start(pred[512]{0:T(512)(128)(4,1)} %copy-done.4) | copy-start | bytes 1540 | tf_op jit(solution)/shard_map/while
  141.7 0.9 copy-start.1
  142.6 0.6 copy-start.2
  146.4 0.8 copy-start.4
  147.2 3.5 %copy-start.3 = (f32[512]{0:T(512)S(1)}, f32[512]{0:T(512)}, u32[]{:S(2)}) copy-start(f32[512]{0:T(512)} %get-tuple-element.274) | copy-start | bytes 6148 | tf_op jit(solution)/shard_map/while
  147.2 3.5 %copy-start.5 = (pred[512]{0:T(512)(128)(4,1)S(1)}, pred[512]{0:T(512)(128)(4,1)}, u32[]{:S(2)}) copy-start(pred[512]{0:T(512)(128)(4,1)} %copy-done.4) | copy-start | bytes 1540 | tf_op jit(solution)/shard_map/while
  150.7 0.9 copy-start.1
  151.6 0.6 copy-start.2
  153.6 31.7 %copy-start = (bf16[1,128,1536]{2,1,0:T(8,128)(2,1)S(1)}, bf16[1,128,1536]{2,1,0:T(8,128)(2,1)}, u32[]{:S(2)}) copy-start(bf16[1,128,1536]{2,1,0:T(8,128)(2,1)} %param.7) | copy-start | bytes 1179652
  153.6 31.7 %copy-start.6 = (f32[1536]{0:T(1024)S(1)}, f32[1536]{0:T(1024)}, u32[]{:S(2)}) copy-start(f32[1536]{0:T(1024)} %get-tuple-element.182) | copy-start | bytes 18436
Sparse Core Ops, SparseCore 0:
  12.5 22.3 all-gather.5
  36.5 69.8 all-gather.7
  108.0 28.7 all-gather.9
  158.1 27.1 reduce-scatter.1
where the time goes:
time: 194 us
  waiting for transfers between devices  119 us (61%)
  blocking collectives  22.4 us (12%)
  matrix products  16.4 us (8%)
  between operations  13.2 us (7%)
  other arithmetic  12.8 us (7%)
  local copies, waits for them, and re-layouts  9.62 us (5%)
    all_gather x1, waiting for transfers between devices, body(): piece = lax.all_gather(w_qkv, 'wrow', axis=0, tiled=True)  71.5 us
    reduce_scatter x1, waiting for transfers between devices, body(): lax.psum_scatter(partial_out.astype(jnp.bfloat16), 'wcol', scatter_dimens...  27.3 us
    all_gather x1, waiting for transfers between devices, body(): tile_rows = lax.all_gather(normed, 'wcol', axis=1, tiled=True)  19.3 us
    all_gather x1, blocking collectives, body(): key_piece = lax.all_gather(keys, 'patch', axis=1, tiled=True)  11.7 us
    all_gather x1, blocking collectives, body(): value_piece = lax.all_gather(values, 'patch', axis=1, tiled=True)  10.8 us
    dot_general x2, matrix products, absorb(): jnp.einsum('vhqk,vkhd->vhqd', probs.astype(jnp.bfloat16), value_heads, pr...  6.61 us
    dot_general x1, matrix products, body(): jnp.dot(flat_rows, piece.reshape(piece.shape[0], 3 * local_cols), preferr...  4.7 us
  transfers between devices with their start and end apart: 4, of which 3 were waited for; matrix products, arithmetic and copies ran while one was open for 14% of the time, Pallas kernels for 0%

commit v1 on v0

--- a/solution.py
+++ b/solution.py
@@ -1,6 +1,11 @@
+import functools
+import math
+
 import jax
 import jax.numpy as jnp
 from jax import lax
+from jax.experimental import pallas as pl
+from jax.experimental.pallas import tpu as pltpu
 from jax.sharding import PartitionSpec as P
 
 HD = 128
@@ -46,7 +51,7 @@
     return (new_peak, weight_sum, numer)
 
 
-def body(hidden_states, modulation, w_qkv, w_out, lengths):
+def general_body(hidden_states, modulation, w_qkv, w_out, lengths):
     videos_here = hidden_states.shape[0]
     width = hidden_states.shape[2]
     shift = modulation[:, 0][:, None, :]
@@ -98,6 +103,276 @@
     return (hidden_states.astype(jnp.float32) + gate * out_proj).astype(jnp.bfloat16)
 
 
+SHIFTS = ((0, 0, 0), (0, 1, 0), (1, 0, 0), (1, 1, 0), (0, 0, 1), (0, 1, 1), (1, 0, 1), (1, 1, 1))
+VMEM_LIMIT = 40 * 1024 * 1024
+
+
+def norm_kernel(states_ref, mod_ref, out_ref):
+    values = states_ref[...].astype(jnp.float32)
+    center = jnp.mean(values, axis=-1, keepdims=True)
+    spread = jnp.mean(jnp.square(values - center), axis=-1, keepdims=True)
+    shift = mod_ref[0:1, :]
+    scale = mod_ref[1:2, :]
+    out_ref[...] = (
+        (values - center) * lax.rsqrt(spread + EPSILON) * (1.0 + scale) + shift
+    ).astype(jnp.bfloat16)
+
+
+def attend_kernel(spot_ref, len_ref, *refs):
+    tiles = refs[0:8]
+    first = refs[8:12]
+    second = refs[12:16]
+    own_ref, other_ref = refs[16:18]
+    rows_ref, weight_ref, mixed_ref, value_ref, tile_sem, weight_sem = refs[18:]
+    tile_len = tiles[0].shape[0]
+    count = 8 * tile_len
+    depth = first[0].shape[1]
+    x, y, z, core = spot_ref[0], spot_ref[1], spot_ref[2], spot_ref[3]
+    owner = x == core
+
+    def tile_copy(i):
+        return pltpu.make_async_copy(
+            tiles[i], rows_ref.at[pl.ds(i * tile_len, tile_len)], tile_sem.at[i]
+        )
+
+    def weight_copy(shards, d, kind, column):
+        start = pl.multiple_of((z ^ d) * depth, depth)
+        return pltpu.make_async_copy(
+            shards[d].at[kind],
+            weight_ref.at[pl.ds(start, depth), pl.ds(column, HD)],
+            weight_sem.at[column // HD, d],
+        )
+
+    copies = [tile_copy(i) for i in range(8)]
+    copies += [weight_copy(first, d, k, k * HD) for d in range(4) for k in range(3)]
+    extra = [weight_copy(second, d, k, (3 + k) * HD) for d in range(4) for k in range(3)]
+    for copy in copies:
+        copy.start()
+
+    @pl.when(owner)
+    def _():
+        for copy in extra:
+            copy.start()
+
+    limit = len_ref[0]
+    lane = lax.broadcasted_iota(jnp.int32, (1, tile_len), 1)
+    bias = []
+    for dx, dy, dc in SHIFTS:
+        base = ((x ^ dx) * 4 + (y ^ dy) * 2 + (core ^ dc)) * tile_len
+        bias.append(jnp.where(base + lane < limit, 0.0, FLOOR))
+    bias = jnp.concatenate(bias, axis=1)
+    value_ref[:, HD:] = jnp.ones((count, HD), jnp.bfloat16)
+    for copy in copies:
+        copy.wait()
+
+    step = 2 * tile_len
+    rate = HD ** (-0.5) * math.log2(math.e)
+
+    def one_head(column):
+        for r in range(count // step):
+            span = pl.ds(r * step, step)
+            mixed_ref[span, :] = jnp.dot(
+                rows_ref[span, :],
+                weight_ref[:, column : column + 3 * HD],
+                preferred_element_type=jnp.float32,
+            ).astype(jnp.bfloat16)
+        value_ref[:, :HD] = mixed_ref[:, 2 * HD :]
+        keys = mixed_ref[:, HD : 2 * HD]
+        for r in range(count // step):
+            scores = lax.dot_general(
+                mixed_ref[pl.ds(r * step, step), :HD],
+                keys,
+                (((1,), (1,)), ((), ())),
+                preferred_element_type=jnp.float32,
+            )
+            scores = scores + bias
+            peak = jnp.max(scores, axis=-1, keepdims=True)
+            probs = jnp.exp2((scores - peak) * rate).astype(jnp.bfloat16)
+            sums = jnp.dot(probs, value_ref[...], preferred_element_type=jnp.float32)
+            result = (sums[:, :HD] / sums[:, HD:]).astype(jnp.bfloat16)
+            half = count // step // 2
+            out = own_ref if r < half else other_ref
+            at = column // 3
+            out[pl.ds((r % half) * step, step), at : at + HD] = result
+
+    one_head(0)
+
+    @pl.when(owner)
+    def _():
+        for copy in extra:
+            copy.wait()
+        one_head(3 * HD)
+
+    @pl.when(jnp.logical_not(owner))
+    def _():
+        own_ref[:, HD:] = jnp.zeros((count // 2, HD), jnp.bfloat16)
+        other_ref[:, HD:] = jnp.zeros((count // 2, HD), jnp.bfloat16)
+
+
+def project_kernel(spot_ref, own_ref, recv_ref, *refs):
+    here = refs[0:4]
+    sent = refs[4:8]
+    outs = refs[8:12]
+    weight_ref, joined_ref, sem = refs[12:]
+    tile_len = outs[0].shape[0]
+    width = here[0].shape[1]
+    z = spot_ref[2]
+    owner = spot_ref[0] == spot_ref[3]
+
+    def weight_copy(shards, d):
+        start = pl.multiple_of((z ^ d) * width, width)
+        return pltpu.make_async_copy(shards[d], weight_ref.at[:, pl.ds(start, width)], sem.at[d])
+
+    @pl.when(owner)
+    def _():
+        for d in range(4):
+            weight_copy(here, d).start()
+        joined_ref[:, 0:HD] = own_ref[:, :HD]
+        joined_ref[:, HD : 2 * HD] = recv_ref[:, :HD]
+        joined_ref[:, 2 * HD :] = own_ref[:, HD:]
+
+    @pl.when(jnp.logical_not(owner))
+    def _():
+        for d in range(4):
+            weight_copy(sent, d).start()
+        joined_ref[:, 0:HD] = recv_ref[:, :HD]
+        joined_ref[:, HD : 2 * HD] = own_ref[:, :HD]
+        joined_ref[:, 2 * HD :] = recv_ref[:, HD:]
+
+    for d in range(4):
+        weight_copy(here, d).wait()
+    for i, out in enumerate(outs):
+        out[...] = jnp.dot(
+            joined_ref[pl.ds(i * tile_len, tile_len), :],
+            weight_ref[...],
+            preferred_element_type=jnp.float32,
+        ).astype(out.dtype)
+
+
+def tiled_body(hidden_states, modulation, w_qkv, w_out, lengths):
+    tile_len, width = hidden_states.shape[1:]
+    depth, _, local_cols = w_qkv.shape
+    states = hidden_states[0]
+    x = lax.axis_index("patch")
+    z = lax.axis_index("wrow")
+    w = lax.axis_index("wcol")
+    core = w % 2
+    owner = x == core
+    spot = jnp.stack([x, w // 2, z, core]).astype(jnp.int32)
+    everywhere = ("patch", "wrow", "wcol")
+
+    def index(a, b, c):
+        return (a * 4 + b) * 4 + c
+
+    def swap(array, axis, d, n):
+        return lax.ppermute(array, axis, [(i, i ^ d) for i in range(n)])
+
+    def owners_swap(array, d):
+        pairs = [
+            (index(a, b, c), index(a, b ^ d, c))
+            for a in range(2)
+            for b in range(4)
+            for c in range(4)
+            if c % 2 == a
+        ]
+        return lax.ppermute(array, everywhere, pairs)
+
+    def to_other_core(array):
+        pairs = [
+            (index(a, b, c), index(a, b, c ^ 1))
+            for a in range(2)
+            for b in range(4)
+            for c in range(4)
+            if c % 2 == a
+        ]
+        return lax.ppermute(array, everywhere, pairs)
+
+    kinds = jnp.transpose(w_qkv, (1, 0, 2))
+    head_a, head_b, head_c = (kinds[:, :, i * HD : (i + 1) * HD] for i in range(3))
+    second = [head_c, None, owners_swap(head_c, 2), None]
+    mine = jnp.where(owner, head_a, to_other_core(head_b))
+    first = [mine, None, swap(mine, "wrow", 2, 4), None]
+    second[1] = owners_swap(head_c, 1)
+    first[1] = swap(mine, "wrow", 1, 4)
+    second[3] = owners_swap(second[2], 1)
+    first[3] = swap(first[2], "wrow", 1, 4)
+
+    full = pl.BlockSpec(memory_space=pltpu.VMEM)
+    scalar = pl.BlockSpec(memory_space=pltpu.SMEM)
+    anywhere = pl.BlockSpec(memory_space=pl.ANY)
+    normed = pl.pallas_call(
+        norm_kernel,
+        out_shape=jax.ShapeDtypeStruct((tile_len, width), jnp.bfloat16),
+        in_specs=[full, full],
+        out_specs=full,
+        name="norm",
+    )(states, modulation[0])
+    along_x = swap(normed, "patch", 1, 2)
+    along_y = swap(normed, "wcol", 2, 4)
+    along_xy = swap(along_x, "wcol", 2, 4)
+    tiles = [normed, along_y, along_x, along_xy]
+    tiles = tiles + [swap(tile, "wcol", 1, 4) for tile in tiles]
+
+    count = 8 * tile_len
+    half = jax.ShapeDtypeStruct((count // 2, 2 * HD), jnp.bfloat16)
+    att_own, att_other = pl.pallas_call(
+        attend_kernel,
+        out_shape=(half, half),
+        in_specs=[scalar, scalar] + [anywhere] * 16,
+        out_specs=(full, full),
+        scratch_shapes=[
+            pltpu.VMEM((count, width), jnp.bfloat16),
+            pltpu.VMEM((width, 6 * HD), jnp.bfloat16),
+            pltpu.VMEM((count, 3 * HD), jnp.bfloat16),
+            pltpu.VMEM((count, 2 * HD), jnp.bfloat16),
+            pltpu.SemaphoreType.DMA((8,)),
+            pltpu.SemaphoreType.DMA((6, 4)),
+        ],
+        compiler_params=pltpu.CompilerParams(vmem_limit_bytes=VMEM_LIMIT),
+        name="attend",
+    )(spot, lengths, *tiles, *first, *second)
+
+    out_here = [w_out, owners_swap(w_out, 1), owners_swap(w_out, 2), None]
+    out_here[3] = owners_swap(out_here[2], 1)
+    out_sent = [to_other_core(shard) for shard in out_here]
+    att_recv = swap(att_other, "wcol", 1, 4)
+    sent = jax.ShapeDtypeStruct((tile_len, width), jnp.bfloat16)
+    part_own, part_y, part_x, part_xy = pl.pallas_call(
+        project_kernel,
+        out_shape=(jax.ShapeDtypeStruct((tile_len, width), jnp.float32), sent, sent, sent),
+        in_specs=[scalar, full, full] + [anywhere] * 8,
+        out_specs=(full,) * 4,
+        scratch_shapes=[
+            pltpu.VMEM((local_cols, width), jnp.bfloat16),
+            pltpu.VMEM((count // 2, local_cols), jnp.bfloat16),
+            pltpu.SemaphoreType.DMA((4,)),
+        ],
+        compiler_params=pltpu.CompilerParams(vmem_limit_bytes=VMEM_LIMIT),
+        name="project",
+    )(spot, att_own, att_recv, *out_here, *out_sent)
+    diagonal = [
+        (a * 4 + c, (a ^ 1) * 4 + (c ^ 2)) for a in range(2) for c in range(4)
+    ]
+    got_xy = lax.ppermute(part_xy, ("patch", "wcol"), diagonal)
+    got_x = swap(part_x, "patch", 1, 2)
+    got_y = swap(part_y, "wcol", 2, 4)
+    out_proj = (
+        part_own
+        + got_x.astype(jnp.float32)
+        + got_y.astype(jnp.float32)
+        + got_xy.astype(jnp.float32)
+    )
+    updated = states.astype(jnp.float32) + modulation[0, 2][None, :] * out_proj
+    return updated.astype(jnp.bfloat16)[None]
+
+
+def body(hidden_states, modulation, w_qkv, w_out, lengths, *, sizes):
+    fits = sizes == (2, 4, 4) and hidden_states.shape[0] == 1 and w_qkv.shape[2] == 3 * HD
+    if fits and hidden_states.shape[1] % HD == 0:
+        return tiled_body(hidden_states, modulation, w_qkv, w_out, lengths)
+    return general_body(hidden_states, modulation, w_qkv, w_out, lengths)
+
+
 def solution(mesh):
     placed = (
         P("wrow", ("patch", "wcol"), None),
@@ -106,8 +381,9 @@
         P("wcol", "wrow"),
         P("wrow"),
     )
+    sizes = tuple(mesh.shape[name] for name in ("patch", "wrow", "wcol"))
     return jax.shard_map(
-        body,
+        functools.partial(body, sizes=sizes),
         mesh=mesh,
         in_specs=placed,
         out_specs=P("wrow", ("patch", "wcol"), None),

time: 194 us -> 99.4 us (0.51)
  waiting for transfers between devices: 119 us -> 36.9 us
  starting transfers between devices: 0.12 us -> 36.4 us
  blocking collectives: 22.4 us -> 0 us
  matrix products: 16.4 us -> 0 us
  Pallas kernels: 0 us -> 14.9 us
  between operations: 13.2 us -> 0.98 us
  other arithmetic: 12.8 us -> 2.07 us
  local copies, waits for them, and re-layouts: 9.62 us -> 7.59 us
    all_gather x3 -> x0, waiting for transfers between devices: 90.9 us -> none  [the longest x1 71.5 us: body(): piece = lax.all_gather(w_qkv, 'wrow', axis=0, tiled=True)]
    ppermute x0 -> x25, waiting for transfers between devices: none -> 36.9 us  [the longest x13 20.2 us: swap(): return lax.ppermute(array, axis, [(i, i ^ d) for i in range(n)])]
    ppermute x0 -> x25, starting transfers between devices: none -> 36.4 us  [the longest x6 19 us: owners_swap(): return lax.ppermute(array, everywhere, pairs)]
    reduce_scatter x1 -> x0, waiting for transfers between devices: 27.3 us -> none  [body(): lax.psum_scatter(partial_out.astype(jnp.bfloat16), 'wcol', scatter_dimens...]
    all_gather x2 -> x0, blocking collectives: 22.4 us -> none  [the longest x1 11.7 us: body(): key_piece = lax.all_gather(keys, 'patch', axis=1, tiled=True)]
    dot_general x6 -> x0, matrix products: 16.4 us -> none  [the longest x2 6.61 us: absorb(): jnp.einsum('vhqk,vkhd->vhqd', probs.astype(jnp.bfloat16), value_heads, pr...]
    pallas_call x0 -> x3, Pallas kernels: none -> 14.9 us  [the longest x1 10.1 us: tiled_body(): pl.pallas_call(attend_kernel, out_shape=(half, half), in_specs=[scalar, s...]
    convert_element_type x5 -> x0, other arithmetic: 7.18 us -> none  [the longest x2 2.44 us: absorb(): probs = jnp.exp(scores - new_peak[..., None]) * valid.astype(jnp.float32)]
  transfers between devices with their start and end apart: 4 -> 25, of which waited for: 3 -> 10; matrix products, arithmetic and copies ran while one was open for 14% -> 2% of each run, Pallas kernels for 0% -> 12%
where the time goes in v1:
time: 99.4 us; the launch traced here: 98.9 us
  waiting for transfers between devices  36.9 us (37%)
  starting transfers between devices  36.4 us (37%)
  Pallas kernels  14.9 us (15%)
  local copies, waits for them, and re-layouts  7.59 us (8%)
  other arithmetic  2.07 us (2%)
    ppermute x13, waiting for transfers between devices, swap(): return lax.ppermute(array, axis, [(i, i ^ d) for i in range(n)])  20.2 us
    ppermute x6, starting transfers between devices, owners_swap(): return lax.ppermute(array, everywhere, pairs)  19 us
    ppermute x6, waiting for transfers between devices, owners_swap(): return lax.ppermute(array, everywhere, pairs)  15.1 us
    pallas_call x1, Pallas kernels, tiled_body(): pl.pallas_call(attend_kernel, out_shape=(half, half), in_specs=[scalar, s...  10.1 us
    ppermute x13, starting transfers between devices, swap(): return lax.ppermute(array, axis, [(i, i ^ d) for i in range(n)])  8.5 us
    ppermute x5, starting transfers between devices, to_other_core(): return lax.ppermute(array, everywhere, pairs)  7.6 us
    unnamed x31, local copies, waits for them, and re-layouts  6.47 us
    pallas_call x1, Pallas kernels, tiled_body(): pl.pallas_call(project_kernel, out_shape=(jax.ShapeDtypeStruct((tile_len,...  2.64 us
  transfers between devices with their start and end apart: 25, of which 10 were waited for; matrix products, arithmetic and copies ran while one was open for 2% of the time, Pallas kernels for 12%

profile of v1, /device:TPU:0, one launch (start us, length us, event | category | flops | bytes accessed | tf_op | source)
XLA Modules:
  0.0 98.9 jit_solution(7553684632610756717)
XLA Ops:
  1.1 2.4 %collective-permute-start.7 = (bf16[3,384,128]{2,1,0:T(8,128)(2,1)S(1)}, bf16[3,384,128]{2,1,0:T(8,128)(2,1)S(1)}, u32[]{:S(2)}, u32[]{:S(2)}) collective-permute-start(bf16[3,384,128]{2,1,0:T(8,128)(2,1)S(1)} %get-tuple-element.18), channel_id=1, source_target_pairs={{0,1},{2,3},{4,5},{6,7},{8,9},{10,11},{12,13},{14,15},{17,16},{19,... | collective-permute-start | bytes 884744 | tf_op jit(solution)/shard_map/ppermute | solution.py:288
  3.5 5.3 %collective-permute-start.12 = (bf16[3,384,128]{2,1,0:T(8,128)(2,1)S(1)}, bf16[3,384,128]{2,1,0:T(8,128)(2,1)}, u32[]{:S(2)}, u32[]{:S(2)}) collective-permute-start(bf16[3,384,128]{2,1,0:T(8,128)(2,1)S(1)} %get-tuple-element.17.refs_12_), channel_id=1, source_target_pairs={{0,8},{2,10},{4,12},{6,14},{8,0},{10,2},{12,4},{14,6},{17,25},{19,... | collective-permute-start | bytes 884744 | tf_op jit(solution)/shard_map/ppermute | solution.py:278
  8.8 3.5 %collective-permute-start.11 = (bf16[3,384,128]{2,1,0:T(8,128)(2,1)S(1)}, bf16[3,384,128]{2,1,0:T(8,128)(2,1)S(1)}, u32[]{:S(2)}, u32[]{:S(2)}) collective-permute-start(bf16[3,384,128]{2,1,0:T(8,128)(2,1)S(1)} %get-tuple-element.17.refs_12_), channel_id=1, source_target_pairs={{0,4},{2,6},{4,0},{6,2},{8,12},{10,14},{12,8},{14,10},{17,21},{19,... | collective-permute-start | bytes 884744 | tf_op jit(solution)/shard_map/ppermute | solution.py:278
  12.9 2.1 %norm.1.refs_0_ = bf16[128,1536]{1,0:T(8,128)(2,1)} custom-call(bf16[128,1536]{1,0:T(8,128)(2,1)} %bitcast.12, f32[3,1536]{1,0:T(4,128)} %bitcast.15), custom_call_target="tpu_custom_call" | custom-call | tf_op jit(solution)/shard_map/norm/pallas_call | solution.py:303
  15.1 2.2 %collective-permute-start.16 = (bf16[384,384]{1,0:T(8,128)(2,1)S(1)}, bf16[384,384]{1,0:T(8,128)(2,1)S(1)}, u32[]{:S(2)}, u32[]{:S(2)}) collective-permute-start(bf16[384,384]{1,0:T(8,128)(2,1)S(1)} %copy-done.1), channel_id=1, source_target_pairs={{0,8},{2,10},{4,12},{6,14},{8,0},{10,2},{12,4},{14,6},{17,25},{19,... | collective-permute-start | bytes 884744 | tf_op jit(solution)/shard_map/ppermute | solution.py:278
  17.3 1.6 %collective-permute-start = (bf16[128,1536]{1,0:T(8,128)(2,1)}, bf16[128,1536]{1,0:T(8,128)(2,1)S(1)}, u32[]{:S(2)}, u32[]{:S(2)}) collective-permute-start(bf16[128,1536]{1,0:T(8,128)(2,1)} %norm.1.refs_0_), channel_id=1, source_target_pairs={{0,2},{1,3},{2,0},{3,1},{4,6},{5,7},{6,4},{7,5},{8,10},{9,11},{10,... | collective-permute-start | bytes 1179656 | tf_op jit(solution)/shard_map/ppermute | solution.py:268
  19.9 2.1 %collective-permute-start.15 = (bf16[384,384]{1,0:T(8,128)(2,1)S(1)}, bf16[384,384]{1,0:T(8,128)(2,1)S(1)}, u32[]{:S(2)}, u32[]{:S(2)}) collective-permute-start(bf16[384,384]{1,0:T(8,128)(2,1)S(1)} %copy-done.1), channel_id=1, source_target_pairs={{0,4},{2,6},{4,0},{6,2},{8,12},{10,14},{12,8},{14,10},{17,21},{19,... | collective-permute-start | bytes 884744 | tf_op jit(solution)/shard_map/ppermute | solution.py:278
  23.0 10.1 %collective-permute-done.16.refs_2_ = bf16[384,384]{1,0:T(8,128)(2,1)S(1)} collective-permute-done((bf16[384,384]{1,0:T(8,128)(2,1)S(1)}, bf16[384,384]{1,0:T(8,128)(2,1)S(1)}, u32[]{:S(2)}, u32[]{:S(2)}) %collective-permute-start.16) | collective-permute-done | bytes 294944 | tf_op jit(solution)/shard_map/ppermute | solution.py:278
  33.8 2.8 %collective-permute-start.2 = (bf16[128,1536]{1,0:T(8,128)(2,1)S(1)}, bf16[128,1536]{1,0:T(8,128)(2,1)S(1)}, u32[]{:S(2)}, u32[]{:S(2)}) collective-permute-start(bf16[128,1536]{1,0:T(8,128)(2,1)S(1)} %collective-permute-done.1.refs_2_), channel_id=1, source_target_pairs={{0,2},{1,3},{2,0},{3,1},{4,6},{5,7},{6,4},{7,5},{8,10},{9,11},{10,... | collective-permute-start | bytes 1179656 | tf_op jit(solution)/shard_map/ppermute | solution.py:268
  36.6 3.9 %collective-permute-start.13 = (bf16[3,384,128]{2,1,0:T(8,128)(2,1)}, bf16[3,384,128]{2,1,0:T(8,128)(2,1)S(1)}, u32[]{:S(2)}, u32[]{:S(2)}) collective-permute-start(bf16[3,384,128]{2,1,0:T(8,128)(2,1)} %collective-permute-done.12.refs_14_), channel_id=1, source_target_pairs={{0,4},{2,6},{4,0},{6,2},{8,12},{10,14},{12,8},{14,10},{17,21},{19,... | collective-permute-start | bytes 884744 | tf_op jit(solution)/shard_map/ppermute | solution.py:278
  41.3 2.9 %collective-permute-done.8.refs_9_ = bf16[3,384,128]{2,1,0:T(8,128)(2,1)S(1)} collective-permute-done((bf16[3,384,128]{2,1,0:T(8,128)(2,1)S(1)}, bf16[3,384,128]{2,1,0:T(8,128)(2,1)S(1)}, u32[]{:S(2)}, u32[]{:S(2)}) %collective-permute-start.8) | collective-permute-done | bytes 294944 | tf_op jit(solution)/shard_map/ppermute | solution.py:268
  45.0 1.9 %collective-permute-start.17 = (bf16[384,384]{1,0:T(8,128)(2,1)}, bf16[384,384]{1,0:T(8,128)(2,1)}, u32[]{:S(2)}, u32[]{:S(2)}) collective-permute-start(bf16[384,384]{1,0:T(8,128)(2,1)} %copy-done.3), channel_id=1, source_target_pairs={{0,4},{2,6},{4,0},{6,2},{8,12},{10,14},{12,8},{14,10},{17,21},{19,... | collective-permute-start | bytes 884744 | tf_op jit(solution)/shard_map/ppermute | solution.py:278
  48.2 1.5 %collective-permute-start.10 = (bf16[3,384,128]{2,1,0:T(8,128)(2,1)}, bf16[3,384,128]{2,1,0:T(8,128)(2,1)}, u32[]{:S(2)}, u32[]{:S(2)}) collective-permute-start(bf16[3,384,128]{2,1,0:T(8,128)(2,1)} %collective-permute-done.9.refs_10_), channel_id=1, source_target_pairs={{0,4},{4,0},{8,12},{12,8},{1,5},{5,1},{9,13},{13,9},{2,6},{6,2},{1... | collective-permute-start | bytes 884744 | tf_op jit(solution)/shard_map/ppermute | solution.py:268
  49.7 4.2 %collective-permute-done.17.refs_3_ = bf16[384,384]{1,0:T(8,128)(2,1)} collective-permute-done((bf16[384,384]{1,0:T(8,128)(2,1)}, bf16[384,384]{1,0:T(8,128)(2,1)}, u32[]{:S(2)}, u32[]{:S(2)}) %collective-permute-start.17) | collective-permute-done | bytes 294944 | tf_op jit(solution)/shard_map/ppermute | solution.py:278
  55.2 1.3 %collective-permute-start.20 = (bf16[384,384]{1,0:T(8,128)(2,1)}, bf16[384,384]{1,0:T(8,128)(2,1)S(1)}, u32[]{:S(2)}, u32[]{:S(2)}) collective-permute-start(bf16[384,384]{1,0:T(8,128)(2,1)} %copy-done.3), channel_id=1, source_target_pairs={{0,1},{2,3},{4,5},{6,7},{8,9},{10,11},{12,13},{14,15},{17,16},{19,... | collective-permute-start | bytes 884744 | tf_op jit(solution)/shard_map/ppermute | solution.py:288
  56.6 1.3 %collective-permute-start.19 = (bf16[384,384]{1,0:T(8,128)(2,1)}, bf16[384,384]{1,0:T(8,128)(2,1)S(1)}, u32[]{:S(2)}, u32[]{:S(2)}) collective-permute-start(bf16[384,384]{1,0:T(8,128)(2,1)} %copy-done.7), channel_id=1, source_target_pairs={{0,1},{2,3},{4,5},{6,7},{8,9},{10,11},{12,13},{14,15},{17,16},{19,... | collective-permute-start | bytes 884744 | tf_op jit(solution)/shard_map/ppermute | solution.py:288
  62.9 10.1 %attend.1 = (bf16[512,256]{1,0:T(8,128)(2,1)S(1)}, bf16[512,256]{1,0:T(8,128)(2,1)S(1)}) custom-call(s32[4]{0:T(128)S(1)} %pad_add_fusion.spot_ref, s32[1]{0:T(128)S(6)} %copy.9.len_ref, bf16[128,1536]{1,0:T(8,128)(2,1)S(1)} %copy-done, bf16[128,1536]{1,0:T(8,128)(2,1)S(1)} %collective-permute-done.refs_1_, ...), custom_call_target="tpu_custom_call" | custom-call | tf_op jit(solution)/shard_map/attend/pallas_call | solution.py:318
  73.2 1.5 %collective-permute-done.14.recv_ref = bf16[512,256]{1,0:T(8,128)(2,1)S(1)} collective-permute-done((bf16[512,256]{1,0:T(8,128)(2,1)S(1)}, bf16[512,256]{1,0:T(8,128)(2,1)S(1)}, u32[]{:S(2)}, u32[]{:S(2)}) %collective-permute-start.14) | collective-permute-done | bytes 262176 | tf_op jit(solution)/shard_map/ppermute | solution.py:268
  74.7 2.6 %project.1 = (f32[128,1536]{1,0:T(8,128)S(1)}, bf16[128,1536]{1,0:T(8,128)(2,1)S(1)}, bf16[128,1536]{1,0:T(8,128)(2,1)S(1)}, bf16[128,1536]{1,0:T(8,128)(2,1)S(1)}) custom-call(s32[4]{0:T(128)S(1)} %pad_add_fusion.spot_ref, bf16[512,256]{1,0:T(8,128)(2,1)S(1)} %get-tuple-element.11.own_ref, bf16[512,256]{1,0:T(8,128)(2,1)S(1)} %collective-permute-done.14.recv_ref, ...), custom_call_target="tpu_custom_call" | custom-call | tf_op jit(solution)/shard_map/project/pallas_call | solution.py:340
  77.4 2.4 %collective-permute-start.23 = (bf16[128,1536]{1,0:T(8,128)(2,1)S(1)}, bf16[128,1536]{1,0:T(8,128)(2,1)S(1)}, u32[]{:S(2)}, u32[]{:S(2)}) collective-permute-start(bf16[128,1536]{1,0:T(8,128)(2,1)S(1)} %get-tuple-element.15), channel_id=1, source_target_pairs={{0,2},{1,3},{2,0},{3,1},{4,6},{5,7},{6,4},{7,5},{8,10},{9,11},{10,... | collective-permute-start | bytes 1179656 | tf_op jit(solution)/shard_map/ppermute | solution.py:268
  79.8 1.4 %collective-permute-start.24 = (bf16[128,1536]{1,0:T(8,128)(2,1)S(1)}, bf16[128,1536]{1,0:T(8,128)(2,1)S(1)}, u32[]{:S(2)}, u32[]{:S(2)}) collective-permute-start(bf16[128,1536]{1,0:T(8,128)(2,1)S(1)} %get-tuple-element.16), channel_id=1, source_target_pairs={{0,18},{1,19},{2,16},{3,17},{16,2},{17,3},{18,0},{19,1},{4,22},{5,... | collective-permute-start | bytes 1179656 | tf_op jit(solution)/shard_map/ppermute | solution.py:356
  81.2 8.2 %collective-permute-done.22 = bf16[128,1536]{1,0:T(8,128)(2,1)S(1)} collective-permute-done((bf16[128,1536]{1,0:T(8,128)(2,1)S(1)}, bf16[128,1536]{1,0:T(8,128)(2,1)S(1)}, u32[]{:S(2)}, u32[]{:S(2)}) %collective-permute-start.22) | collective-permute-done | bytes 393248 | tf_op jit(solution)/shard_map/ppermute | solution.py:268
  89.5 6.7 %collective-permute-done.23 = bf16[128,1536]{1,0:T(8,128)(2,1)S(1)} collective-permute-done((bf16[128,1536]{1,0:T(8,128)(2,1)S(1)}, bf16[128,1536]{1,0:T(8,128)(2,1)S(1)}, u32[]{:S(2)}, u32[]{:S(2)}) %collective-permute-start.23) | collective-permute-done | bytes 393248 | tf_op jit(solution)/shard_map/ppermute | solution.py:268
  96.2 1.7 %collective-permute-done.24 = bf16[128,1536]{1,0:T(8,128)(2,1)S(1)} collective-permute-done((bf16[128,1536]{1,0:T(8,128)(2,1)S(1)}, bf16[128,1536]{1,0:T(8,128)(2,1)S(1)}, u32[]{:S(2)}, u32[]{:S(2)}) %collective-permute-start.24) | collective-permute-done | bytes 393248 | tf_op jit(solution)/shard_map/ppermute | solution.py:356
  (65 shorter events, 14.0 us)
Async XLA Ops:
  1.1 16.2 %collective-permute-start.7 = (bf16[3,384,128]{2,1,0:T(8,128)(2,1)S(1)}, bf16[3,384,128]{2,1,0:T(8,128)(2,1)S(1)}, u32[]{:S(2)}, u32[]{:S(2)}) collective-permute-start(bf16[3,384,128]{2,1,0:T(8,128)(2,1)S(1)} %get-tuple-element.18), channel_id=1, source_target_pairs={{0,1},{2,3},{4,5},{6,7},{8,9},{10,11},{12,13},{14,15},{17,16},{19,... | collective-permute-start | bytes 884744 | tf_op jit(solution)/shard_map/ppermute | solution.py:288
  3.5 15.4 %collective-permute-start.12 = (bf16[3,384,128]{2,1,0:T(8,128)(2,1)S(1)}, bf16[3,384,128]{2,1,0:T(8,128)(2,1)}, u32[]{:S(2)}, u32[]{:S(2)}) collective-permute-start(bf16[3,384,128]{2,1,0:T(8,128)(2,1)S(1)} %get-tuple-element.17.refs_12_), channel_id=1, source_target_pairs={{0,8},{2,10},{4,12},{6,14},{8,0},{10,2},{12,4},{14,6},{17,25},{19,... | collective-permute-start | bytes 884744 | tf_op jit(solution)/shard_map/ppermute | solution.py:278
  8.8 10.3 %collective-permute-start.11 = (bf16[3,384,128]{2,1,0:T(8,128)(2,1)S(1)}, bf16[3,384,128]{2,1,0:T(8,128)(2,1)S(1)}, u32[]{:S(2)}, u32[]{:S(2)}) collective-permute-start(bf16[3,384,128]{2,1,0:T(8,128)(2,1)S(1)} %get-tuple-element.17.refs_12_), channel_id=1, source_target_pairs={{0,4},{2,6},{4,0},{6,2},{8,12},{10,14},{12,8},{14,10},{17,21},{19,... | collective-permute-start | bytes 884744 | tf_op jit(solution)/shard_map/ppermute | solution.py:278
  15.1 18.7 %collective-permute-start.1 = (bf16[128,1536]{1,0:T(8,128)(2,1)}, bf16[128,1536]{1,0:T(8,128)(2,1)S(1)}, u32[]{:S(2)}, u32[]{:S(2)}) collective-permute-start(bf16[128,1536]{1,0:T(8,128)(2,1)} %norm.1.refs_0_), channel_id=1, source_target_pairs={{0,16},{16,0},{1,17},{17,1},{2,18},{18,2},{3,19},{19,3},{4,20},{20... | collective-permute-start | bytes 1179656 | tf_op jit(solution)/shard_map/ppermute | solution.py:268
  15.1 18.0 %collective-permute-start.16 = (bf16[384,384]{1,0:T(8,128)(2,1)S(1)}, bf16[384,384]{1,0:T(8,128)(2,1)S(1)}, u32[]{:S(2)}, u32[]{:S(2)}) collective-permute-start(bf16[384,384]{1,0:T(8,128)(2,1)S(1)} %copy-done.1), channel_id=1, source_target_pairs={{0,8},{2,10},{4,12},{6,14},{8,0},{10,2},{12,4},{14,6},{17,25},{19,... | collective-permute-start | bytes 884744 | tf_op jit(solution)/shard_map/ppermute | solution.py:278
  17.3 19.3 %collective-permute-start = (bf16[128,1536]{1,0:T(8,128)(2,1)}, bf16[128,1536]{1,0:T(8,128)(2,1)S(1)}, u32[]{:S(2)}, u32[]{:S(2)}) collective-permute-start(bf16[128,1536]{1,0:T(8,128)(2,1)} %norm.1.refs_0_), channel_id=1, source_target_pairs={{0,2},{1,3},{2,0},{3,1},{4,6},{5,7},{6,4},{7,5},{8,10},{9,11},{10,... | collective-permute-start | bytes 1179656 | tf_op jit(solution)/shard_map/ppermute | solution.py:268
  18.9 21.6 %collective-permute-start.3 = (bf16[128,1536]{1,0:T(8,128)(2,1)}, bf16[128,1536]{1,0:T(8,128)(2,1)S(1)}, u32[]{:S(2)}, u32[]{:S(2)}) collective-permute-start(bf16[128,1536]{1,0:T(8,128)(2,1)} %norm.1.refs_0_), channel_id=1, source_target_pairs={{0,1},{1,0},{2,3},{3,2},{4,5},{5,4},{6,7},{7,6},{8,9},{9,8},{10,11... | collective-permute-start | bytes 1179656 | tf_op jit(solution)/shard_map/ppermute | solution.py:268
  19.9 16.7 %collective-permute-start.15 = (bf16[384,384]{1,0:T(8,128)(2,1)S(1)}, bf16[384,384]{1,0:T(8,128)(2,1)S(1)}, u32[]{:S(2)}, u32[]{:S(2)}) collective-permute-start(bf16[384,384]{1,0:T(8,128)(2,1)S(1)} %copy-done.1), channel_id=1, source_target_pairs={{0,4},{2,6},{4,0},{6,2},{8,12},{10,14},{12,8},{14,10},{17,21},{19,... | collective-permute-start | bytes 884744 | tf_op jit(solution)/shard_map/ppermute | solution.py:278
  33.0 8.3 %collective-permute-start.9 = (bf16[3,384,128]{2,1,0:T(8,128)(2,1)S(1)}, bf16[3,384,128]{2,1,0:T(8,128)(2,1)}, u32[]{:S(2)}, u32[]{:S(2)}) collective-permute-start(bf16[3,384,128]{2,1,0:T(8,128)(2,1)S(1)} %slice_select_fusion.refs_8_), channel_id=1, source_target_pairs={{0,8},{4,12},{8,0},{12,4},{1,9},{5,13},{9,1},{13,5},{2,10},{6,14},... | collective-permute-start | bytes 884744 | tf_op jit(solution)/shard_map/ppermute | solution.py:268
  33.8 15.9 %collective-permute-start.2 = (bf16[128,1536]{1,0:T(8,128)(2,1)S(1)}, bf16[128,1536]{1,0:T(8,128)(2,1)S(1)}, u32[]{:S(2)}, u32[]{:S(2)}) collective-permute-start(bf16[128,1536]{1,0:T(8,128)(2,1)S(1)} %collective-permute-done.1.refs_2_), channel_id=1, source_target_pairs={{0,2},{1,3},{2,0},{3,1},{4,6},{5,7},{6,4},{7,5},{8,10},{9,11},{10,... | collective-permute-start | bytes 1179656 | tf_op jit(solution)/shard_map/ppermute | solution.py:268
  36.5 7.7 %collective-permute-start.8 = (bf16[3,384,128]{2,1,0:T(8,128)(2,1)S(1)}, bf16[3,384,128]{2,1,0:T(8,128)(2,1)S(1)}, u32[]{:S(2)}, u32[]{:S(2)}) collective-permute-start(bf16[3,384,128]{2,1,0:T(8,128)(2,1)S(1)} %slice_select_fusion.refs_8_), channel_id=1, source_target_pairs={{0,4},{4,0},{8,12},{12,8},{1,5},{5,1},{9,13},{13,9},{2,6},{6,2},{1... | collective-permute-start | bytes 884744 | tf_op jit(solution)/shard_map/ppermute | solution.py:268
  36.6 10.9 %collective-permute-start.13 = (bf16[3,384,128]{2,1,0:T(8,128)(2,1)}, bf16[3,384,128]{2,1,0:T(8,128)(2,1)S(1)}, u32[]{:S(2)}, u32[]{:S(2)}) collective-permute-start(bf16[3,384,128]{2,1,0:T(8,128)(2,1)} %collective-permute-done.12.refs_14_), channel_id=1, source_target_pairs={{0,4},{2,6},{4,0},{6,2},{8,12},{10,14},{12,8},{14,10},{17,21},{19,... | collective-permute-start | bytes 884744 | tf_op jit(solution)/shard_map/ppermute | solution.py:278
  40.5 14.7 %collective-permute-start.5 = (bf16[128,1536]{1,0:T(8,128)(2,1)S(1)}, bf16[128,1536]{1,0:T(8,128)(2,1)S(1)}, u32[]{:S(2)}, u32[]{:S(2)}) collective-permute-start(bf16[128,1536]{1,0:T(8,128)(2,1)S(1)} %collective-permute-done.1.refs_2_), channel_id=1, source_target_pairs={{0,1},{1,0},{2,3},{3,2},{4,5},{5,4},{6,7},{7,6},{8,9},{9,8},{10,11... | collective-permute-start | bytes 1179656 | tf_op jit(solution)/shard_map/ppermute | solution.py:268
  41.3 15.2 %collective-permute-start.4 = (bf16[128,1536]{1,0:T(8,128)(2,1)S(1)}, bf16[128,1536]{1,0:T(8,128)(2,1)S(1)}, u32[]{:S(2)}, u32[]{:S(2)}) collective-permute-start(bf16[128,1536]{1,0:T(8,128)(2,1)S(1)} %collective-permute-done.refs_1_), channel_id=1, source_target_pairs={{0,1},{1,0},{2,3},{3,2},{4,5},{5,4},{6,7},{7,6},{8,9},{9,8},{10,11... | collective-permute-start | bytes 1179656 | tf_op jit(solution)/shard_map/ppermute | solution.py:268
  45.0 8.9 %collective-permute-start.17 = (bf16[384,384]{1,0:T(8,128)(2,1)}, bf16[384,384]{1,0:T(8,128)(2,1)}, u32[]{:S(2)}, u32[]{:S(2)}) collective-permute-start(bf16[384,384]{1,0:T(8,128)(2,1)} %copy-done.3), channel_id=1, source_target_pairs={{0,4},{2,6},{4,0},{6,2},{8,12},{10,14},{12,8},{14,10},{17,21},{19,... | collective-permute-start | bytes 884744 | tf_op jit(solution)/shard_map/ppermute | solution.py:278
  48.2 9.7 %collective-permute-start.10 = (bf16[3,384,128]{2,1,0:T(8,128)(2,1)}, bf16[3,384,128]{2,1,0:T(8,128)(2,1)}, u32[]{:S(2)}, u32[]{:S(2)}) collective-permute-start(bf16[3,384,128]{2,1,0:T(8,128)(2,1)} %collective-permute-done.9.refs_10_), channel_id=1, source_target_pairs={{0,4},{4,0},{8,12},{12,8},{1,5},{5,1},{9,13},{13,9},{2,6},{6,2},{1... | collective-permute-start | bytes 884744 | tf_op jit(solution)/shard_map/ppermute | solution.py:268
  49.7 10.3 %collective-permute-start.6 = (bf16[128,1536]{1,0:T(8,128)(2,1)S(1)}, bf16[128,1536]{1,0:T(8,128)(2,1)}, u32[]{:S(2)}, u32[]{:S(2)}) collective-permute-start(bf16[128,1536]{1,0:T(8,128)(2,1)S(1)} %collective-permute-done.2.refs_3_), channel_id=1, source_target_pairs={{0,1},{1,0},{2,3},{3,2},{4,5},{5,4},{6,7},{7,6},{8,9},{9,8},{10,11... | collective-permute-start | bytes 1179656 | tf_op jit(solution)/shard_map/ppermute | solution.py:268
  53.9 19.2 %collective-permute-start.18 = (bf16[384,384]{1,0:T(8,128)(2,1)}, bf16[384,384]{1,0:T(8,128)(2,1)S(1)}, u32[]{:S(2)}, u32[]{:S(2)}) collective-permute-start(bf16[384,384]{1,0:T(8,128)(2,1)} %refs_0_.1), channel_id=1, source_target_pairs={{0,1},{2,3},{4,5},{6,7},{8,9},{10,11},{12,13},{14,15},{17,16},{19,... | collective-permute-start | bytes 884744 | tf_op jit(solution)/shard_map/ppermute | solution.py:288
  55.2 17.9 %collective-permute-start.20 = (bf16[384,384]{1,0:T(8,128)(2,1)}, bf16[384,384]{1,0:T(8,128)(2,1)S(1)}, u32[]{:S(2)}, u32[]{:S(2)}) collective-permute-start(bf16[384,384]{1,0:T(8,128)(2,1)} %copy-done.3), channel_id=1, source_target_pairs={{0,1},{2,3},{4,5},{6,7},{8,9},{10,11},{12,13},{14,15},{17,16},{19,... | collective-permute-start | bytes 884744 | tf_op jit(solution)/shard_map/ppermute | solution.py:288
  56.6 16.6 %collective-permute-start.19 = (bf16[384,384]{1,0:T(8,128)(2,1)}, bf16[384,384]{1,0:T(8,128)(2,1)S(1)}, u32[]{:S(2)}, u32[]{:S(2)}) collective-permute-start(bf16[384,384]{1,0:T(8,128)(2,1)} %copy-done.7), channel_id=1, source_target_pairs={{0,1},{2,3},{4,5},{6,7},{8,9},{10,11},{12,13},{14,15},{17,16},{19,... | collective-permute-start | bytes 884744 | tf_op jit(solution)/shard_map/ppermute | solution.py:288
  57.9 15.3 %collective-permute-start.21 = (bf16[384,384]{1,0:T(8,128)(2,1)}, bf16[384,384]{1,0:T(8,128)(2,1)S(1)}, u32[]{:S(2)}, u32[]{:S(2)}) collective-permute-start(bf16[384,384]{1,0:T(8,128)(2,1)} %collective-permute-done.17.refs_3_), channel_id=1, source_target_pairs={{0,1},{2,3},{4,5},{6,7},{8,9},{10,11},{12,13},{14,15},{17,16},{19,... | collective-permute-start | bytes 884744 | tf_op jit(solution)/shard_map/ppermute | solution.py:288
  77.4 12.1 %collective-permute-start.22 = (bf16[128,1536]{1,0:T(8,128)(2,1)S(1)}, bf16[128,1536]{1,0:T(8,128)(2,1)S(1)}, u32[]{:S(2)}, u32[]{:S(2)}) collective-permute-start(bf16[128,1536]{1,0:T(8,128)(2,1)S(1)} %get-tuple-element.14), channel_id=1, source_target_pairs={{0,16},{16,0},{1,17},{17,1},{2,18},{18,2},{3,19},{19,3},{4,20},{20... | collective-permute-start | bytes 1179656 | tf_op jit(solution)/shard_map/ppermute | solution.py:268
  77.4 18.8 %collective-permute-start.23 = (bf16[128,1536]{1,0:T(8,128)(2,1)S(1)}, bf16[128,1536]{1,0:T(8,128)(2,1)S(1)}, u32[]{:S(2)}, u32[]{:S(2)}) collective-permute-start(bf16[128,1536]{1,0:T(8,128)(2,1)S(1)} %get-tuple-element.15), channel_id=1, source_target_pairs={{0,2},{1,3},{2,0},{3,1},{4,6},{5,7},{6,4},{7,5},{8,10},{9,11},{10,... | collective-permute-start | bytes 1179656 | tf_op jit(solution)/shard_map/ppermute | solution.py:268
  79.8 18.1 %collective-permute-start.24 = (bf16[128,1536]{1,0:T(8,128)(2,1)S(1)}, bf16[128,1536]{1,0:T(8,128)(2,1)S(1)}, u32[]{:S(2)}, u32[]{:S(2)}) collective-permute-start(bf16[128,1536]{1,0:T(8,128)(2,1)S(1)} %get-tuple-element.16), channel_id=1, source_target_pairs={{0,18},{1,19},{2,16},{3,17},{16,2},{17,3},{18,0},{19,1},{4,22},{5,... | collective-permute-start | bytes 1179656 | tf_op jit(solution)/shard_map/ppermute | solution.py:356
  (16 other events, 140.5 us)

commit v2 on v0

--- a/solution.py
+++ b/solution.py
@@ -1,6 +1,11 @@
+import functools
+import math
+
 import jax
 import jax.numpy as jnp
 from jax import lax
+from jax.experimental import pallas as pl
+from jax.experimental.pallas import tpu as pltpu
 from jax.sharding import PartitionSpec as P
 
 HD = 128
@@ -46,7 +51,7 @@
     return (new_peak, weight_sum, numer)
 
 
-def body(hidden_states, modulation, w_qkv, w_out, lengths):
+def general_body(hidden_states, modulation, w_qkv, w_out, lengths):
     videos_here = hidden_states.shape[0]
     width = hidden_states.shape[2]
     shift = modulation[:, 0][:, None, :]
@@ -98,6 +103,288 @@
     return (hidden_states.astype(jnp.float32) + gate * out_proj).astype(jnp.bfloat16)
 
 
+SHIFTS = ((0, 0, 0), (0, 1, 0), (1, 0, 0), (1, 1, 0), (0, 0, 1), (0, 1, 1), (1, 0, 1), (1, 1, 1))
+VMEM_LIMIT = 16 * 1024 * 1024
+
+
+def norm_kernel(states_ref, mod_ref, out_ref):
+    values = states_ref[...].astype(jnp.float32)
+    center = jnp.mean(values, axis=-1, keepdims=True)
+    spread = jnp.mean(jnp.square(values - center), axis=-1, keepdims=True)
+    shift = mod_ref[0]
+    scale = mod_ref[1]
+    out_ref[...] = (
+        (values - center) * lax.rsqrt(spread + EPSILON) * (1.0 + scale) + shift
+    ).astype(jnp.bfloat16)
+
+
+def start_shard(spot_ref, here, sent, start, weight_ref, sem):
+    depth, width = here.shape[1:]
+    owner = spot_ref[0] == spot_ref[3]
+    for role, shard in ((owner, here), (jnp.logical_not(owner), sent)):
+
+        @pl.when(role)
+        def _():
+            for k in range(3):
+                pltpu.make_async_copy(
+                    shard.at[k],
+                    weight_ref.at[pl.ds(start, depth), pl.ds(k * width, width)],
+                    sem.at[k],
+                ).start()
+
+
+def wait_shard(here, start, weight_ref, sem):
+    depth, width = here.shape[1:]
+    for k in range(3):
+        pltpu.make_async_copy(
+            here.at[k],
+            weight_ref.at[pl.ds(start, depth), pl.ds(k * width, width)],
+            sem.at[k],
+        ).wait()
+
+
+def early_kernel(spot_ref, *refs):
+    tiles = refs[0:4]
+    here = refs[4:7]
+    sent = refs[7:10]
+    total_ref, last_ref = refs[10:12]
+    rows_ref, weight_ref, tile_sem, weight_sem = refs[12:]
+    tile_len = tiles[0].shape[0]
+    depth = here[0].shape[1]
+    count = 4 * tile_len
+    z = spot_ref[2]
+    columns = [pl.multiple_of((z ^ d) * depth, HD) for d in range(4)]
+    sources = [tiles[i].at[:, pl.ds(columns[d], depth)] for d in range(4) for i in range(4)]
+    places = [
+        rows_ref.at[pl.ds(i * tile_len, tile_len), pl.ds(d * depth, depth)]
+        for d in range(3)
+        for i in range(4)
+    ]
+    places += [last_ref.at[pl.ds(i * tile_len, tile_len)] for i in range(4)]
+    copies = [
+        pltpu.make_async_copy(source, place, tile_sem.at[n])
+        for n, (source, place) in enumerate(zip(sources, places))
+    ]
+    for d in range(3):
+        start_shard(spot_ref, here[d], sent[d], d * depth, weight_ref, weight_sem.at[d])
+    for copy in copies:
+        copy.start()
+    for d in range(3):
+        wait_shard(here[d], d * depth, weight_ref, weight_sem.at[d])
+    for copy in copies:
+        copy.wait()
+    step = 2 * tile_len
+    skip = weight_ref.shape[1] - total_ref.shape[1]
+    for r in range(count // step):
+        span = pl.ds(r * step, step)
+        total_ref[span, :] = jnp.dot(
+            rows_ref[span, :], weight_ref[:, skip:], preferred_element_type=jnp.float32
+        )
+
+
+def attend_kernel(spot_ref, len_ref, *refs):
+    totals, lasts, here, sent = refs[0:2], refs[2:4], refs[4:8], refs[8:12]
+    out_refs = refs[12:16]
+    weight_ref, out_weight_ref, query_ref, key_ref, value_ref, weight_sem, out_sem = refs[16:]
+    count = key_ref.shape[0]
+    width = query_ref.shape[1]
+    tile_len = out_refs[0].shape[0]
+    x, y, z, core = (spot_ref[i] for i in range(4))
+    start_shard(spot_ref, here[3], sent[3], 0, weight_ref, weight_sem)
+    owner = x == core
+    places = [
+        out_weight_ref.at[:, pl.ds(pl.multiple_of((z ^ d) * width, HD), width)] for d in range(4)
+    ]
+    for role, shards in ((owner, here), (jnp.logical_not(owner), sent)):
+
+        @pl.when(role)
+        def _():
+            for d in range(4):
+                pltpu.make_async_copy(shards[d].at[3], places[d], out_sem.at[d]).start()
+
+    limit = len_ref[0]
+    lane = lax.broadcasted_iota(jnp.int32, (1, tile_len), 1)
+    bias = []
+    for dx, dy, dc in SHIFTS:
+        base = ((x ^ dx) * 4 + (y ^ dy) * 2 + (core ^ dc)) * tile_len
+        bias.append(jnp.where(base + lane < limit, 0.0, FLOOR))
+    bias = jnp.concatenate(bias, axis=1)
+    for h in range(width // HD):
+        value_ref[h, :, HD:] = jnp.ones((count, HD), jnp.bfloat16)
+    wait_shard(here[3], 0, weight_ref, weight_sem)
+    step = 2 * tile_len
+    rate = HD ** (-0.5) * math.log2(math.e)
+    half = count // step // 2
+    for r in range(count // step):
+        span = pl.ds((r % half) * step, step)
+        rows = pl.ds(r * step, step)
+        skip = 0 if r < half else width
+        mixed = (
+            totals[r // half][span, :]
+            + jnp.dot(
+                lasts[r // half][span, :],
+                weight_ref[:, skip:],
+                preferred_element_type=jnp.float32,
+            )
+        ).astype(jnp.bfloat16)
+        if r < half:
+            query_ref[rows, :] = mixed[:, :width]
+        key_ref[rows, :] = mixed[:, width - skip : 2 * width - skip]
+        for h in range(width // HD):
+            at = 2 * width - skip + h * HD
+            value_ref[h, rows, :HD] = mixed[:, at : at + HD]
+    for d in range(4):
+        pltpu.make_async_copy(here[d].at[3], places[d], out_sem.at[d]).wait()
+    for r in range(half):
+        heads = []
+        for h in range(width // HD):
+            column = slice(h * HD, (h + 1) * HD)
+            scores = lax.dot_general(
+                query_ref[pl.ds(r * step, step), column],
+                key_ref[:, column],
+                (((1,), (1,)), ((), ())),
+                preferred_element_type=jnp.float32,
+            )
+            scores = scores + bias
+            peak = jnp.max(scores, axis=-1, keepdims=True)
+            probs = jnp.exp2((scores - peak) * rate).astype(jnp.bfloat16)
+            sums = jnp.dot(probs, value_ref[h], preferred_element_type=jnp.float32)
+            heads.append((sums[:, :HD] / sums[:, HD:]).astype(jnp.bfloat16))
+        part = jnp.dot(
+            jnp.concatenate(heads, axis=1),
+            out_weight_ref[...],
+            preferred_element_type=jnp.float32,
+        )
+        for i in range(2):
+            out = out_refs[2 * r + i]
+            out[...] = part[i * tile_len : (i + 1) * tile_len].astype(out.dtype)
+
+
+def tiled_body(hidden_states, modulation, w_qkv, w_out, lengths):
+    tile_len, width = hidden_states.shape[1:]
+    depth, _, local_cols = w_qkv.shape
+    states = hidden_states[0]
+    x = lax.axis_index("patch")
+    z = lax.axis_index("wrow")
+    w = lax.axis_index("wcol")
+    core = w % 2
+    owner = x == core
+    spot = jnp.stack([x, w // 2, z, core]).astype(jnp.int32)
+    everywhere = ("patch", "wrow", "wcol")
+
+    def index(a, b, c):
+        return (a * 4 + b) * 4 + c
+
+    def swap(array, axis, d, n):
+        return lax.ppermute(array, axis, [(i, i ^ d) for i in range(n)])
+
+    def owners_swap(array, d):
+        pairs = [
+            (index(a, b, c), index(a, b ^ d, c))
+            for a in range(2)
+            for b in range(4)
+            for c in range(4)
+            if c % 2 == a
+        ]
+        return lax.ppermute(array, everywhere, pairs)
+
+    def core_swap(array):
+        return swap(array, "wcol", 1, 4)
+
+    full = pl.BlockSpec(memory_space=pltpu.VMEM)
+    scalar = pl.BlockSpec(memory_space=pltpu.SMEM)
+    anywhere = pl.BlockSpec(memory_space=pl.ANY)
+    params = pltpu.CompilerParams(vmem_limit_bytes=VMEM_LIMIT)
+    count = 8 * tile_len
+
+    mod = jnp.transpose(modulation, (1, 0, 2))
+    normed = pl.pallas_call(
+        norm_kernel,
+        out_shape=jax.ShapeDtypeStruct((tile_len, width), jnp.bfloat16),
+        in_specs=[full, full],
+        out_specs=full,
+        name="norm",
+    )(states, mod)
+    kinds = jnp.transpose(w_qkv, (1, 0, 2))
+
+    four = jnp.concatenate([kinds, w_out[None]], axis=0)
+    far = owners_swap(four, 2)
+    near = owners_swap(four, 1)
+    along_x = swap(normed, "patch", 1, 2)
+    along_y = swap(normed, "wcol", 2, 4)
+    along_xy = swap(along_y, "patch", 1, 2)
+    far, near, along_x, along_y, along_xy, normed, four = lax.optimization_barrier(
+        (far, near, along_x, along_y, along_xy, normed, four)
+    )
+    last = owners_swap(far, 1)
+    tiles = [normed, along_y, along_x, along_xy]
+    tiles_sent = [core_swap(tile) for tile in tiles]
+    early_here = [four, near, far]
+    early_sent = [core_swap(shard) for shard in early_here]
+
+    def early(rows, columns):
+        return pl.pallas_call(
+            early_kernel,
+            out_shape=(
+                jax.ShapeDtypeStruct((count // 2, columns), jnp.float32),
+                jax.ShapeDtypeStruct((count // 2, depth), jnp.bfloat16),
+            ),
+            in_specs=[scalar] + [anywhere] * 10,
+            out_specs=(full, full),
+            scratch_shapes=[
+                pltpu.VMEM((count // 2, 3 * depth), jnp.bfloat16),
+                pltpu.VMEM((3 * depth, 3 * local_cols), jnp.bfloat16),
+                pltpu.SemaphoreType.DMA((16,)),
+                pltpu.SemaphoreType.DMA((3, 3)),
+            ],
+            compiler_params=params,
+            name="early",
+        )(spot, *rows, *early_here, *early_sent)
+
+    total_a, rows_a = early(tiles, 3 * local_cols)
+    total_b, rows_b = early(tiles_sent, 2 * local_cols)
+    last, total_a, total_b = lax.optimization_barrier((last, total_a, total_b))
+    last_sent = core_swap(last)
+
+    sent = jax.ShapeDtypeStruct((tile_len, width), jnp.bfloat16)
+    part_own, part_y, part_x, part_xy = pl.pallas_call(
+        attend_kernel,
+        out_shape=(jax.ShapeDtypeStruct((tile_len, width), jnp.float32), sent, sent, sent),
+        in_specs=[scalar, scalar] + [full] * 4 + [anywhere] * 8,
+        out_specs=(full,) * 4,
+        scratch_shapes=[
+            pltpu.VMEM((depth, 3 * local_cols), jnp.bfloat16),
+            pltpu.VMEM((local_cols, width), jnp.bfloat16),
+            pltpu.VMEM((count // 2, local_cols), jnp.bfloat16),
+            pltpu.VMEM((count, local_cols), jnp.bfloat16),
+            pltpu.VMEM((local_cols // HD, count, 2 * HD), jnp.bfloat16),
+            pltpu.SemaphoreType.DMA((3,)),
+            pltpu.SemaphoreType.DMA((4,)),
+        ],
+        compiler_params=params,
+        name="attend",
+    )(spot, lengths, total_a, total_b, rows_a, rows_b, *early_here, last, *early_sent, last_sent)
+    diagonal = [(a * 4 + c, (a ^ 1) * 4 + (c ^ 2)) for a in range(2) for c in range(4)]
+    got_xy = lax.ppermute(part_xy, ("patch", "wcol"), diagonal)
+    got_x = swap(part_x, "patch", 1, 2)
+    got_y = swap(part_y, "wcol", 2, 4)
+    out_proj = (
+        part_own
+        + got_x.astype(jnp.float32)
+        + got_y.astype(jnp.float32)
+        + got_xy.astype(jnp.float32)
+    )
+    updated = states.astype(jnp.float32) + mod[2] * out_proj
+    return updated.astype(jnp.bfloat16)[None]
+
+
+def body(hidden_states, modulation, w_qkv, w_out, lengths, *, sizes):
+    fits = sizes == (2, 4, 4) and hidden_states.shape[0] == 1 and w_qkv.shape[2] == 3 * HD
+    if fits and hidden_states.shape[1] % HD == 0:
+        return tiled_body(hidden_states, modulation, w_qkv, w_out, lengths)
+    return general_body(hidden_states, modulation, w_qkv, w_out, lengths)
+
+
 def solution(mesh):
     placed = (
         P("wrow", ("patch", "wcol"), None),
@@ -106,8 +393,9 @@
         P("wcol", "wrow"),
         P("wrow"),
     )
+    sizes = tuple(mesh.shape[name] for name in ("patch", "wrow", "wcol"))
     return jax.shard_map(
-        body,
+        functools.partial(body, sizes=sizes),
         mesh=mesh,
         in_specs=placed,
         out_specs=P("wrow", ("patch", "wcol"), None),

time: 194 us -> 90.3 us (0.47)
  waiting for transfers between devices: 119 us -> 43.2 us
  blocking collectives: 22.4 us -> 0 us
  starting transfers between devices: 0.12 us -> 18.1 us
  Pallas kernels: 0 us -> 16.6 us
  matrix products: 16.4 us -> 0 us
  between operations: 13.2 us -> 0.78 us
  other arithmetic: 12.8 us -> 2.51 us
    all_gather x3 -> x0, waiting for transfers between devices: 90.9 us -> none  [the longest x1 71.5 us: body(): piece = lax.all_gather(w_qkv, 'wrow', axis=0, tiled=True)]
    ppermute x0 -> x17, waiting for transfers between devices: none -> 43.2 us  [the longest x13 37.7 us: swap(): return lax.ppermute(array, axis, [(i, i ^ d) for i in range(n)])]
    reduce_scatter x1 -> x0, waiting for transfers between devices: 27.3 us -> none  [body(): lax.psum_scatter(partial_out.astype(jnp.bfloat16), 'wcol', scatter_dimens...]
    all_gather x2 -> x0, blocking collectives: 22.4 us -> none  [the longest x1 11.7 us: body(): key_piece = lax.all_gather(keys, 'patch', axis=1, tiled=True)]
    ppermute x0 -> x17, starting transfers between devices: none -> 18.1 us  [the longest x3 11.3 us: owners_swap(): return lax.ppermute(array, everywhere, pairs)]
    pallas_call x0 -> x4, Pallas kernels: none -> 16.6 us  [the longest x2 7.94 us: early(): pl.pallas_call(early_kernel, out_shape=(jax.ShapeDtypeStruct((count // 2,...]
    dot_general x6 -> x0, matrix products: 16.4 us -> none  [the longest x2 6.61 us: absorb(): jnp.einsum('vhqk,vkhd->vhqd', probs.astype(jnp.bfloat16), value_heads, pr...]
    convert_element_type x5 -> x0, other arithmetic: 7.18 us -> none  [the longest x2 2.44 us: absorb(): probs = jnp.exp(scores - new_peak[..., None]) * valid.astype(jnp.float32)]
  transfers between devices with their start and end apart: 4 -> 17, of which waited for: 3 -> 12; matrix products, arithmetic and copies ran while one was open for 14% -> 1% of each run, Pallas kernels for 0% -> 11%
where the time goes in v2:
time: 90.3 us; the launch traced here: 89.8 us
  waiting for transfers between devices  43.2 us (48%)
  starting transfers between devices  18.1 us (20%)
  Pallas kernels  16.6 us (18%)
  local copies, waits for them, and re-layouts  8.6 us (10%)
  other arithmetic  2.51 us (3%)
    ppermute x13, waiting for transfers between devices, swap(): return lax.ppermute(array, axis, [(i, i ^ d) for i in range(n)])  37.7 us
    ppermute x3, starting transfers between devices, owners_swap(): return lax.ppermute(array, everywhere, pairs)  11.3 us
    pallas_call x2, Pallas kernels, early(): pl.pallas_call(early_kernel, out_shape=(jax.ShapeDtypeStruct((count // 2,...  7.94 us
    unnamed x18, local copies, waits for them, and re-layouts  7.89 us
    pallas_call x1, Pallas kernels, tiled_body(): pl.pallas_call(attend_kernel, out_shape=(jax.ShapeDtypeStruct((tile_len,...  6.59 us
    ppermute x13, starting transfers between devices, swap(): return lax.ppermute(array, axis, [(i, i ^ d) for i in range(n)])  5.19 us
    ppermute x3, waiting for transfers between devices, owners_swap(): return lax.ppermute(array, everywhere, pairs)  3.68 us
    pallas_call x1, Pallas kernels, tiled_body(): pl.pallas_call(norm_kernel, out_shape=jax.ShapeDtypeStruct((tile_len, wid...  2.07 us
  transfers between devices with their start and end apart: 17, of which 12 were waited for; matrix products, arithmetic and copies ran while one was open for 1% of the time, Pallas kernels for 11%

profile of v2, /device:TPU:0, one launch (start us, length us, event | category | flops | bytes accessed | tf_op | source)
XLA Modules:
  0.0 89.8 jit_solution(1430706716501418169)
XLA Ops:
  0.0 1.4 %pad_maximum_fusion.refs_4_ = bf16[4,384,384]{2,1,0:T(8,128)(2,1)S(1)} fusion(bf16[1,384,384]{2,1,0:T(8,128)(2,1)} %bitcast.13, bf16[3,384,384]{2,1,0:T(8,128)(2,1)} %bitcast.12), kind=kLoop, calls=%fused_computation | loop fusion | flops 589824 | bytes 2359296 | tf_op jit(solution)/shard_map/concatenate | solution.py:310
  1.4 5.9 %collective-permute-start = (bf16[4,384,384]{2,1,0:T(8,128)(2,1)S(1)}, bf16[4,384,384]{2,1,0:T(8,128)(2,1)S(1)}, u32[]{:S(2)}, u32[]{:S(2)}) collective-permute-start(bf16[4,384,384]{2,1,0:T(8,128)(2,1)S(1)} %pad_maximum_fusion.refs_4_), channel_id=1, source_target_pairs={{0,8},{2,10},{4,12},{6,14},{8,0},{10,2},{12,4},{14,6},{17,25},{19,... | collective-permute-start | bytes 3538952 | tf_op jit(solution)/shard_map/ppermute | solution.py:289
  7.4 3.5 %collective-permute-start.1 = (bf16[4,384,384]{2,1,0:T(8,128)(2,1)S(1)}, bf16[4,384,384]{2,1,0:T(8,128)(2,1)S(1)}, u32[]{:S(2)}, u32[]{:S(2)}) collective-permute-start(bf16[4,384,384]{2,1,0:T(8,128)(2,1)S(1)} %pad_maximum_fusion.refs_4_), channel_id=1, source_target_pairs={{0,4},{2,6},{4,0},{6,2},{8,12},{10,14},{12,8},{14,10},{17,21},{19,... | collective-permute-start | bytes 3538952 | tf_op jit(solution)/shard_map/ppermute | solution.py:289
  10.8 2.1 %norm.1.refs_0_ = bf16[128,1536]{1,0:T(8,128)(2,1)} custom-call(bf16[128,1536]{1,0:T(8,128)(2,1)} %bitcast.11, f32[3,1,1536]{2,1,0:T(1,128)} %bitcast.14), custom_call_target="tpu_custom_call" | custom-call | tf_op jit(solution)/shard_map/norm/pallas_call | solution.py:301
  12.9 1.5 %collective-permute-start.3 = (bf16[128,1536]{1,0:T(8,128)(2,1)}, bf16[128,1536]{1,0:T(8,128)(2,1)}, u32[]{:S(2)}, u32[]{:S(2)}) collective-permute-start(bf16[128,1536]{1,0:T(8,128)(2,1)} %norm.1.refs_0_), channel_id=1, source_target_pairs={{0,2},{1,3},{2,0},{3,1},{4,6},{5,7},{6,4},{7,5},{8,10},{9,11},{10,... | collective-permute-start | bytes 1179656 | tf_op jit(solution)/shard_map/ppermute | solution.py:279
  14.4 6.6 %collective-permute-done.3.refs_1_ = bf16[128,1536]{1,0:T(8,128)(2,1)} collective-permute-done((bf16[128,1536]{1,0:T(8,128)(2,1)}, bf16[128,1536]{1,0:T(8,128)(2,1)}, u32[]{:S(2)}, u32[]{:S(2)}) %collective-permute-start.3) | collective-permute-done | bytes 393248 | tf_op jit(solution)/shard_map/ppermute | solution.py:279
  21.0 5.8 %collective-permute-done.2.refs_2_ = bf16[128,1536]{1,0:T(8,128)(2,1)} collective-permute-done((bf16[128,1536]{1,0:T(8,128)(2,1)}, bf16[128,1536]{1,0:T(8,128)(2,1)}, u32[]{:S(2)}, u32[]{:S(2)}) %collective-permute-start.2) | collective-permute-done | bytes 393248 | tf_op jit(solution)/shard_map/ppermute | solution.py:279
  26.8 6.2 %collective-permute-done.4.refs_3_ = bf16[128,1536]{1,0:T(8,128)(2,1)} collective-permute-done((bf16[128,1536]{1,0:T(8,128)(2,1)}, bf16[128,1536]{1,0:T(8,128)(2,1)}, u32[]{:S(2)}, u32[]{:S(2)}) %collective-permute-start.4) | collective-permute-done | bytes 393248 | tf_op jit(solution)/shard_map/ppermute | solution.py:279
  33.0 1.3 %collective-permute-done.refs_6_ = bf16[4,384,384]{2,1,0:T(8,128)(2,1)S(1)} collective-permute-done((bf16[4,384,384]{2,1,0:T(8,128)(2,1)S(1)}, bf16[4,384,384]{2,1,0:T(8,128)(2,1)S(1)}, u32[]{:S(2)}, u32[]{:S(2)}) %collective-permute-start) | collective-permute-done | bytes 1179680 | tf_op jit(solution)/shard_map/ppermute | solution.py:289
  34.3 2.4 %collective-permute-done.1.refs_5_ = bf16[4,384,384]{2,1,0:T(8,128)(2,1)S(1)} collective-permute-done((bf16[4,384,384]{2,1,0:T(8,128)(2,1)S(1)}, bf16[4,384,384]{2,1,0:T(8,128)(2,1)S(1)}, u32[]{:S(2)}, u32[]{:S(2)}) %collective-permute-start.1) | collective-permute-done | bytes 1179680 | tf_op jit(solution)/shard_map/ppermute | solution.py:289
  37.2 1.9 %collective-permute-start.5 = (bf16[4,384,384]{2,1,0:T(8,128)(2,1)S(1)}, bf16[4,384,384]{2,1,0:T(8,128)(2,1)}, u32[]{:S(2)}, u32[]{:S(2)}) collective-permute-start(bf16[4,384,384]{2,1,0:T(8,128)(2,1)S(1)} %collective-permute-done.refs_6_), channel_id=1, source_target_pairs={{0,4},{2,6},{4,0},{6,2},{8,12},{10,14},{12,8},{14,10},{17,21},{19,... | collective-permute-start | bytes 3538952 | tf_op jit(solution)/shard_map/ppermute | solution.py:289
  42.3 2.2 %collective-permute-done.7.refs_8_.refs_9_ = bf16[4,384,384]{2,1,0:T(8,128)(2,1)S(1)} collective-permute-done((bf16[4,384,384]{2,1,0:T(8,128)(2,1)S(1)}, bf16[4,384,384]{2,1,0:T(8,128)(2,1)S(1)}, u32[]{:S(2)}, u32[]{:S(2)}) %collective-permute-start.7) | collective-permute-done | bytes 1179680 | tf_op jit(solution)/shard_map/ppermute | solution.py:279
  45.8 1.3 %copy-done.1 = bf16[4,384,384]{2,1,0:T(8,128)(2,1)S(1)} copy-done((bf16[4,384,384]{2,1,0:T(8,128)(2,1)S(1)}, bf16[4,384,384]{2,1,0:T(8,128)(2,1)}, u32[]{:S(2)}) %copy-start.1) | copy-done | bytes 1179672
  47.1 1.3 %copy-done.4 = bf16[4,384,384]{2,1,0:T(8,128)(2,1)S(1)} copy-done((bf16[4,384,384]{2,1,0:T(8,128)(2,1)S(1)}, bf16[4,384,384]{2,1,0:T(8,128)(2,1)}, u32[]{:S(2)}) %copy-start.4) | copy-done | bytes 1179672
  48.4 1.3 %copy-done.6 = bf16[4,384,384]{2,1,0:T(8,128)(2,1)S(1)} copy-done((bf16[4,384,384]{2,1,0:T(8,128)(2,1)S(1)}, bf16[4,384,384]{2,1,0:T(8,128)(2,1)}, u32[]{:S(2)}) %copy-start.6) | copy-done | bytes 1179672
  50.6 4.3 %early.2 = (f32[512,1152]{1,0:T(8,128)S(1)}, bf16[512,384]{1,0:T(8,128)(2,1)S(1)}) custom-call(s32[4]{0:T(128)S(1)} %pad_add_fusion.spot_ref, bf16[128,1536]{1,0:T(8,128)(2,1)S(1)} %copy-done.7, bf16[128,1536]{1,0:T(8,128)(2,1)} %collective-permute-done.3.refs_1_, bf16[128,1536]{1,0:T(8,128)(2,1)} %collective-permute-done.2.refs_2_, ...), custom_call_target="tpu_custom_call" | custom-call | tf_op jit(solution)/shard_map/early/pallas_call | solution.py:326
  55.0 3.7 %early.3 = (f32[512,768]{1,0:T(8,128)S(1)}, bf16[512,384]{1,0:T(8,128)(2,1)S(1)}) custom-call(s32[4]{0:T(128)S(1)} %pad_add_fusion.spot_ref, bf16[128,1536]{1,0:T(8,128)(2,1)} %collective-permute-done.9.refs_0_, bf16[128,1536]{1,0:T(8,128)(2,1)} %collective-permute-done.10.refs_1_, bf16[128,1536]{1,0:T(8,128)(2,1)} %collective-permute-done.11.refs_2_, ...), custom_call_target="tpu_custom_call" | custom-call | tf_op jit(solution)/shard_map/early/pallas_call | solution.py:326
  59.7 2.0 %collective-permute-done.13.refs_11_ = bf16[4,384,384]{2,1,0:T(8,128)(2,1)S(1)} collective-permute-done((bf16[4,384,384]{2,1,0:T(8,128)(2,1)}, bf16[4,384,384]{2,1,0:T(8,128)(2,1)S(1)}, u32[]{:S(2)}, u32[]{:S(2)}) %collective-permute-start.13) | collective-permute-done | bytes 1179680 | tf_op jit(solution)/shard_map/ppermute | solution.py:279
  61.8 6.6 %attend.1 = (f32[128,1536]{1,0:T(8,128)S(1)}, bf16[128,1536]{1,0:T(8,128)(2,1)S(1)}, bf16[128,1536]{1,0:T(8,128)(2,1)S(1)}, bf16[128,1536]{1,0:T(8,128)(2,1)S(1)}) custom-call(s32[4]{0:T(128)S(1)} %pad_add_fusion.spot_ref, s32[1]{0:T(128)S(6)} %copy.6.len_ref, f32[512,1152]{1,0:T(8,128)S(1)} %get-tuple-element.32.refs_0_, ...), custom_call_target="tpu_custom_call" | custom-call | tf_op jit(solution)/shard_map/attend/pallas_call | solution.py:350
  68.4 1.9 %collective-permute-start.15 = (bf16[128,1536]{1,0:T(8,128)(2,1)S(1)}, bf16[128,1536]{1,0:T(8,128)(2,1)S(1)}, u32[]{:S(2)}, u32[]{:S(2)}) collective-permute-start(bf16[128,1536]{1,0:T(8,128)(2,1)S(1)} %get-tuple-element.39), channel_id=1, source_target_pairs={{0,2},{1,3},{2,0},{3,1},{4,6},{5,7},{6,4},{7,5},{8,10},{9,11},{10,... | collective-permute-start | bytes 1179656 | tf_op jit(solution)/shard_map/ppermute | solution.py:279
  70.4 1.6 %collective-permute-start.16 = (bf16[128,1536]{1,0:T(8,128)(2,1)S(1)}, bf16[128,1536]{1,0:T(8,128)(2,1)S(1)}, u32[]{:S(2)}, u32[]{:S(2)}) collective-permute-start(bf16[128,1536]{1,0:T(8,128)(2,1)S(1)} %get-tuple-element.40), channel_id=1, source_target_pairs={{0,18},{1,19},{2,16},{3,17},{16,2},{17,3},{18,0},{19,1},{4,22},{5,... | collective-permute-start | bytes 1179656 | tf_op jit(solution)/shard_map/ppermute | solution.py:368
  72.6 7.8 %collective-permute-done.14 = bf16[128,1536]{1,0:T(8,128)(2,1)S(1)} collective-permute-done((bf16[128,1536]{1,0:T(8,128)(2,1)S(1)}, bf16[128,1536]{1,0:T(8,128)(2,1)S(1)}, u32[]{:S(2)}, u32[]{:S(2)}) %collective-permute-start.14) | collective-permute-done | bytes 393248 | tf_op jit(solution)/shard_map/ppermute | solution.py:279
  80.5 6.5 %collective-permute-done.15 = bf16[128,1536]{1,0:T(8,128)(2,1)S(1)} collective-permute-done((bf16[128,1536]{1,0:T(8,128)(2,1)S(1)}, bf16[128,1536]{1,0:T(8,128)(2,1)S(1)}, u32[]{:S(2)}, u32[]{:S(2)}) %collective-permute-start.15) | collective-permute-done | bytes 393248 | tf_op jit(solution)/shard_map/ppermute | solution.py:279
  86.9 1.8 %collective-permute-done.16 = bf16[128,1536]{1,0:T(8,128)(2,1)S(1)} collective-permute-done((bf16[128,1536]{1,0:T(8,128)(2,1)S(1)}, bf16[128,1536]{1,0:T(8,128)(2,1)S(1)}, u32[]{:S(2)}, u32[]{:S(2)}) %collective-permute-start.16) | collective-permute-done | bytes 393248 | tf_op jit(solution)/shard_map/ppermute | solution.py:368
  (36 shorter events, 8.3 us)
Async XLA Ops:
  1.4 32.9 %collective-permute-start = (bf16[4,384,384]{2,1,0:T(8,128)(2,1)S(1)}, bf16[4,384,384]{2,1,0:T(8,128)(2,1)S(1)}, u32[]{:S(2)}, u32[]{:S(2)}) collective-permute-start(bf16[4,384,384]{2,1,0:T(8,128)(2,1)S(1)} %pad_maximum_fusion.refs_4_), channel_id=1, source_target_pairs={{0,8},{2,10},{4,12},{6,14},{8,0},{10,2},{12,4},{14,6},{17,25},{19,... | collective-permute-start | bytes 3538952 | tf_op jit(solution)/shard_map/ppermute | solution.py:289
  7.4 29.3 %collective-permute-start.1 = (bf16[4,384,384]{2,1,0:T(8,128)(2,1)S(1)}, bf16[4,384,384]{2,1,0:T(8,128)(2,1)S(1)}, u32[]{:S(2)}, u32[]{:S(2)}) collective-permute-start(bf16[4,384,384]{2,1,0:T(8,128)(2,1)S(1)} %pad_maximum_fusion.refs_4_), channel_id=1, source_target_pairs={{0,4},{2,6},{4,0},{6,2},{8,12},{10,14},{12,8},{14,10},{17,21},{19,... | collective-permute-start | bytes 3538952 | tf_op jit(solution)/shard_map/ppermute | solution.py:289
  12.9 8.1 %collective-permute-start.3 = (bf16[128,1536]{1,0:T(8,128)(2,1)}, bf16[128,1536]{1,0:T(8,128)(2,1)}, u32[]{:S(2)}, u32[]{:S(2)}) collective-permute-start(bf16[128,1536]{1,0:T(8,128)(2,1)} %norm.1.refs_0_), channel_id=1, source_target_pairs={{0,2},{1,3},{2,0},{3,1},{4,6},{5,7},{6,4},{7,5},{8,10},{9,11},{10,... | collective-permute-start | bytes 1179656 | tf_op jit(solution)/shard_map/ppermute | solution.py:279
  14.4 12.4 %collective-permute-start.2 = (bf16[128,1536]{1,0:T(8,128)(2,1)}, bf16[128,1536]{1,0:T(8,128)(2,1)}, u32[]{:S(2)}, u32[]{:S(2)}) collective-permute-start(bf16[128,1536]{1,0:T(8,128)(2,1)} %norm.1.refs_0_), channel_id=1, source_target_pairs={{0,16},{16,0},{1,17},{17,1},{2,18},{18,2},{3,19},{19,3},{4,20},{20... | collective-permute-start | bytes 1179656 | tf_op jit(solution)/shard_map/ppermute | solution.py:279
  21.0 12.0 %collective-permute-start.4 = (bf16[128,1536]{1,0:T(8,128)(2,1)}, bf16[128,1536]{1,0:T(8,128)(2,1)}, u32[]{:S(2)}, u32[]{:S(2)}) collective-permute-start(bf16[128,1536]{1,0:T(8,128)(2,1)} %collective-permute-done.3.refs_1_), channel_id=1, source_target_pairs={{0,16},{16,0},{1,17},{17,1},{2,18},{18,2},{3,19},{19,3},{4,20},{20... | collective-permute-start | bytes 1179656 | tf_op jit(solution)/shard_map/ppermute | solution.py:279
  36.7 2.8 %collective-permute-start.8 = (bf16[4,384,384]{2,1,0:T(8,128)(2,1)S(1)}, bf16[4,384,384]{2,1,0:T(8,128)(2,1)S(1)}, u32[]{:S(2)}, u32[]{:S(2)}) collective-permute-start(bf16[4,384,384]{2,1,0:T(8,128)(2,1)S(1)} %collective-permute-done.refs_6_), channel_id=1, source_target_pairs={{0,1},{1,0},{2,3},{3,2},{4,5},{5,4},{6,7},{7,6},{8,9},{9,8},{10,11... | collective-permute-start | bytes 3538952 | tf_op jit(solution)/shard_map/ppermute | solution.py:279
  36.7 4.5 %collective-permute-start.6 = (bf16[4,384,384]{2,1,0:T(8,128)(2,1)S(1)}, bf16[4,384,384]{2,1,0:T(8,128)(2,1)S(1)}, u32[]{:S(2)}, u32[]{:S(2)}) collective-permute-start(bf16[4,384,384]{2,1,0:T(8,128)(2,1)S(1)} %pad_maximum_fusion.refs_4_), channel_id=1, source_target_pairs={{0,1},{1,0},{2,3},{3,2},{4,5},{5,4},{6,7},{7,6},{8,9},{9,8},{10,11... | collective-permute-start | bytes 3538952 | tf_op jit(solution)/shard_map/ppermute | solution.py:279
  37.2 7.4 %collective-permute-start.7 = (bf16[4,384,384]{2,1,0:T(8,128)(2,1)S(1)}, bf16[4,384,384]{2,1,0:T(8,128)(2,1)S(1)}, u32[]{:S(2)}, u32[]{:S(2)}) collective-permute-start(bf16[4,384,384]{2,1,0:T(8,128)(2,1)S(1)} %collective-permute-done.1.refs_5_), channel_id=1, source_target_pairs={{0,1},{1,0},{2,3},{3,2},{4,5},{5,4},{6,7},{7,6},{8,9},{9,8},{10,11... | collective-permute-start | bytes 3538952 | tf_op jit(solution)/shard_map/ppermute | solution.py:279
  37.2 21.5 %collective-permute-start.5 = (bf16[4,384,384]{2,1,0:T(8,128)(2,1)S(1)}, bf16[4,384,384]{2,1,0:T(8,128)(2,1)}, u32[]{:S(2)}, u32[]{:S(2)}) collective-permute-start(bf16[4,384,384]{2,1,0:T(8,128)(2,1)S(1)} %collective-permute-done.refs_6_), channel_id=1, source_target_pairs={{0,4},{2,6},{4,0},{6,2},{8,12},{10,14},{12,8},{14,10},{17,21},{19,... | collective-permute-start | bytes 3538952 | tf_op jit(solution)/shard_map/ppermute | solution.py:289
  39.1 15.8 %collective-permute-start.10 = (bf16[128,1536]{1,0:T(8,128)(2,1)}, bf16[128,1536]{1,0:T(8,128)(2,1)}, u32[]{:S(2)}, u32[]{:S(2)}) collective-permute-start(bf16[128,1536]{1,0:T(8,128)(2,1)} %collective-permute-done.3.refs_1_), channel_id=1, source_target_pairs={{0,1},{1,0},{2,3},{3,2},{4,5},{5,4},{6,7},{7,6},{8,9},{9,8},{10,11... | collective-permute-start | bytes 1179656 | tf_op jit(solution)/shard_map/ppermute | solution.py:279
  39.5 1.0 %copy-start = (bf16[4,384,384]{2,1,0:T(8,128)(2,1)}, bf16[4,384,384]{2,1,0:T(8,128)(2,1)S(1)}, u32[]{:S(2)}) copy-start(bf16[4,384,384]{2,1,0:T(8,128)(2,1)S(1)} %collective-permute-done.8.refs_9_.refs_10_) | copy-start | bytes 3538948
  40.5 14.4 %collective-permute-start.11 = (bf16[128,1536]{1,0:T(8,128)(2,1)}, bf16[128,1536]{1,0:T(8,128)(2,1)}, u32[]{:S(2)}, u32[]{:S(2)}) collective-permute-start(bf16[128,1536]{1,0:T(8,128)(2,1)} %collective-permute-done.2.refs_2_), channel_id=1, source_target_pairs={{0,1},{1,0},{2,3},{3,2},{4,5},{5,4},{6,7},{7,6},{8,9},{9,8},{10,11... | collective-permute-start | bytes 1179656 | tf_op jit(solution)/shard_map/ppermute | solution.py:279
  42.2 12.7 %collective-permute-start.12 = (bf16[128,1536]{1,0:T(8,128)(2,1)}, bf16[128,1536]{1,0:T(8,128)(2,1)}, u32[]{:S(2)}, u32[]{:S(2)}) collective-permute-start(bf16[128,1536]{1,0:T(8,128)(2,1)} %collective-permute-done.4.refs_3_), channel_id=1, source_target_pairs={{0,1},{1,0},{2,3},{3,2},{4,5},{5,4},{6,7},{7,6},{8,9},{9,8},{10,11... | collective-permute-start | bytes 1179656 | tf_op jit(solution)/shard_map/ppermute | solution.py:279
  44.6 1.0 %copy-start.5 = (bf16[4,384,384]{2,1,0:T(8,128)(2,1)}, bf16[4,384,384]{2,1,0:T(8,128)(2,1)S(1)}, u32[]{:S(2)}) copy-start(bf16[4,384,384]{2,1,0:T(8,128)(2,1)S(1)} %collective-permute-done.7.refs_8_.refs_9_) | copy-start | bytes 3538948
  45.6 9.3 %collective-permute-start.9 = (bf16[128,1536]{1,0:T(8,128)(2,1)}, bf16[128,1536]{1,0:T(8,128)(2,1)}, u32[]{:S(2)}, u32[]{:S(2)}) collective-permute-start(bf16[128,1536]{1,0:T(8,128)(2,1)} %norm.1.refs_0_), channel_id=1, source_target_pairs={{0,1},{1,0},{2,3},{3,2},{4,5},{5,4},{6,7},{7,6},{8,9},{9,8},{10,11... | collective-permute-start | bytes 1179656 | tf_op jit(solution)/shard_map/ppermute | solution.py:279
  45.8 1.3 %copy-start.1 = (bf16[4,384,384]{2,1,0:T(8,128)(2,1)S(1)}, bf16[4,384,384]{2,1,0:T(8,128)(2,1)}, u32[]{:S(2)}) copy-start(bf16[4,384,384]{2,1,0:T(8,128)(2,1)} %copy-done) | copy-start | bytes 3538948
  47.1 1.3 %copy-start.4 = (bf16[4,384,384]{2,1,0:T(8,128)(2,1)S(1)}, bf16[4,384,384]{2,1,0:T(8,128)(2,1)}, u32[]{:S(2)}) copy-start(bf16[4,384,384]{2,1,0:T(8,128)(2,1)} %copy-done.3) | copy-start | bytes 3538948
  48.4 1.3 %copy-start.6 = (bf16[4,384,384]{2,1,0:T(8,128)(2,1)S(1)}, bf16[4,384,384]{2,1,0:T(8,128)(2,1)}, u32[]{:S(2)}) copy-start(bf16[4,384,384]{2,1,0:T(8,128)(2,1)} %copy-done.5) | copy-start | bytes 3538948
  50.6 4.3 %copy-start.2 = (bf16[4,384,384]{2,1,0:T(8,128)(2,1)S(1)}, bf16[4,384,384]{2,1,0:T(8,128)(2,1)}, u32[]{:S(2)}) copy-start(bf16[4,384,384]{2,1,0:T(8,128)(2,1)} %copy-done) | copy-start | bytes 3538948
  58.6 3.1 %collective-permute-start.13 = (bf16[4,384,384]{2,1,0:T(8,128)(2,1)}, bf16[4,384,384]{2,1,0:T(8,128)(2,1)S(1)}, u32[]{:S(2)}, u32[]{:S(2)}) collective-permute-start(bf16[4,384,384]{2,1,0:T(8,128)(2,1)} %collective-permute-done.5.refs_7_), channel_id=1, source_target_pairs={{0,1},{1,0},{2,3},{3,2},{4,5},{5,4},{6,7},{7,6},{8,9},{9,8},{10,11... | collective-permute-start | bytes 3538952 | tf_op jit(solution)/shard_map/ppermute | solution.py:279
  61.8 27.0 %copy-start.8 = (bf16[1,128,1536]{2,1,0:T(8,128)(2,1)S(1)}, bf16[1,128,1536]{2,1,0:T(8,128)(2,1)}, u32[]{:S(2)}) copy-start(bf16[1,128,1536]{2,1,0:T(8,128)(2,1)} %param.5) | copy-start | bytes 1179652
  68.4 12.1 %collective-permute-start.14 = (bf16[128,1536]{1,0:T(8,128)(2,1)S(1)}, bf16[128,1536]{1,0:T(8,128)(2,1)S(1)}, u32[]{:S(2)}, u32[]{:S(2)}) collective-permute-start(bf16[128,1536]{1,0:T(8,128)(2,1)S(1)} %get-tuple-element.38), channel_id=1, source_target_pairs={{0,16},{16,0},{1,17},{17,1},{2,18},{18,2},{3,19},{19,3},{4,20},{20... | collective-permute-start | bytes 1179656 | tf_op jit(solution)/shard_map/ppermute | solution.py:279
  68.4 18.5 %collective-permute-start.15 = (bf16[128,1536]{1,0:T(8,128)(2,1)S(1)}, bf16[128,1536]{1,0:T(8,128)(2,1)S(1)}, u32[]{:S(2)}, u32[]{:S(2)}) collective-permute-start(bf16[128,1536]{1,0:T(8,128)(2,1)S(1)} %get-tuple-element.39), channel_id=1, source_target_pairs={{0,2},{1,3},{2,0},{3,1},{4,6},{5,7},{6,4},{7,5},{8,10},{9,11},{10,... | collective-permute-start | bytes 1179656 | tf_op jit(solution)/shard_map/ppermute | solution.py:279
  70.4 18.4 %collective-permute-start.16 = (bf16[128,1536]{1,0:T(8,128)(2,1)S(1)}, bf16[128,1536]{1,0:T(8,128)(2,1)S(1)}, u32[]{:S(2)}, u32[]{:S(2)}) collective-permute-start(bf16[128,1536]{1,0:T(8,128)(2,1)S(1)} %get-tuple-element.40), channel_id=1, source_target_pairs={{0,18},{1,19},{2,16},{3,17},{16,2},{17,3},{18,0},{19,1},{4,22},{5,... | collective-permute-start | bytes 1179656 | tf_op jit(solution)/shard_map/ppermute | solution.py:368
  (2 other events, 2.0 us)

commit v3 on v2

--- a/solution.py
+++ b/solution.py
@@ -104,18 +104,7 @@
 
 
 SHIFTS = ((0, 0, 0), (0, 1, 0), (1, 0, 0), (1, 1, 0), (0, 0, 1), (0, 1, 1), (1, 0, 1), (1, 1, 1))
-VMEM_LIMIT = 16 * 1024 * 1024
-
-
-def norm_kernel(states_ref, mod_ref, out_ref):
-    values = states_ref[...].astype(jnp.float32)
-    center = jnp.mean(values, axis=-1, keepdims=True)
-    spread = jnp.mean(jnp.square(values - center), axis=-1, keepdims=True)
-    shift = mod_ref[0]
-    scale = mod_ref[1]
-    out_ref[...] = (
-        (values - center) * lax.rsqrt(spread + EPSILON) * (1.0 + scale) + shift
-    ).astype(jnp.bfloat16)
+VMEM_LIMIT = 18 * 1024 * 1024
 
 
 def start_shard(spot_ref, here, sent, start, weight_ref, sem):
@@ -143,65 +132,80 @@
         ).wait()
 
 
-def early_kernel(spot_ref, *refs):
-    tiles = refs[0:4]
-    here = refs[4:7]
-    sent = refs[7:10]
-    total_ref, last_ref = refs[10:12]
-    rows_ref, weight_ref, tile_sem, weight_sem = refs[12:]
-    tile_len = tiles[0].shape[0]
+def norm_kernel(spot_ref, mod_ref, *refs):
+    tiles, out_ref, tile_ref = refs[0:4], refs[4], refs[5]
+    tile_len, width = tiles[0].shape
+    depth = width // 4
+    shift = mod_ref[0]
+    scale = 1.0 + mod_ref[1]
+    for i in range(4):
+        rows = pl.ds(i * tile_len, tile_len)
+        values = tiles[i][...].astype(jnp.float32)
+        center = jnp.mean(values, axis=-1, keepdims=True)
+        values = values - center
+        spread = jnp.mean(jnp.square(values), axis=-1, keepdims=True)
+        tile_ref[...] = (values * lax.rsqrt(spread + EPSILON) * scale + shift).astype(jnp.bfloat16)
+        for d in range(4):
+            start = pl.multiple_of((spot_ref[2] ^ d) * depth, HD)
+            out_ref[rows, d * depth : (d + 1) * depth] = tile_ref[:, pl.ds(start, depth)]
+
+
+def start_out_weights(spot_ref, here, sent, place, sem):
+    owner = spot_ref[0] == spot_ref[3]
+    for role, shard in ((owner, here), (jnp.logical_not(owner), sent)):
+
+        @pl.when(role)
+        def _():
+            pltpu.make_async_copy(shard.at[3], place, sem).start()
+
+
+def early_kernel(spot_ref, own_rows_ref, other_rows_ref, *refs):
+    here, sent = refs[0:3], refs[3:6]
+    own_ref, other_ref, out_weight_ref, weight_ref, weight_sem, out_sem = refs[6:]
     depth = here[0].shape[1]
-    count = 4 * tile_len
-    z = spot_ref[2]
-    columns = [pl.multiple_of((z ^ d) * depth, HD) for d in range(4)]
-    sources = [tiles[i].at[:, pl.ds(columns[d], depth)] for d in range(4) for i in range(4)]
-    places = [
-        rows_ref.at[pl.ds(i * tile_len, tile_len), pl.ds(d * depth, depth)]
-        for d in range(3)
-        for i in range(4)
-    ]
-    places += [last_ref.at[pl.ds(i * tile_len, tile_len)] for i in range(4)]
-    copies = [
-        pltpu.make_async_copy(source, place, tile_sem.at[n])
-        for n, (source, place) in enumerate(zip(sources, places))
-    ]
     for d in range(3):
         start_shard(spot_ref, here[d], sent[d], d * depth, weight_ref, weight_sem.at[d])
-    for copy in copies:
-        copy.start()
+    for d in range(3):
+        start_out_weights(spot_ref, here[d], sent[d], out_weight_ref.at[d], out_sem.at[d])
     for d in range(3):
         wait_shard(here[d], d * depth, weight_ref, weight_sem.at[d])
-    for copy in copies:
-        copy.wait()
-    step = 2 * tile_len
-    skip = weight_ref.shape[1] - total_ref.shape[1]
-    for r in range(count // step):
+    step = own_ref.shape[0] // 2
+    skip = weight_ref.shape[1] - other_ref.shape[1]
+    for r in range(2):
         span = pl.ds(r * step, step)
-        total_ref[span, :] = jnp.dot(
-            rows_ref[span, :], weight_ref[:, skip:], preferred_element_type=jnp.float32
+        own_ref[span, :] = jnp.dot(
+            own_rows_ref[span, : 3 * depth], weight_ref[...], preferred_element_type=jnp.float32
         )
+    for r in range(2):
+        span = pl.ds(r * step, step)
+        other_ref[span, :] = jnp.dot(
+            other_rows_ref[span, : 3 * depth],
+            weight_ref[:, skip:],
+            preferred_element_type=jnp.float32,
+        )
+    for d in range(3):
+        pltpu.make_async_copy(here[d].at[3], out_weight_ref.at[d], out_sem.at[d]).wait()
 
 
 def attend_kernel(spot_ref, len_ref, *refs):
-    totals, lasts, here, sent = refs[0:2], refs[2:4], refs[4:8], refs[8:12]
-    out_refs = refs[12:16]
-    weight_ref, out_weight_ref, query_ref, key_ref, value_ref, weight_sem, out_sem = refs[16:]
+    totals, rows_refs, (out_known_ref, here, sent) = refs[0:2], refs[2:4], refs[4:7]
+    out_refs = refs[7:11]
+    weight_ref, out_weight_ref, query_ref, key_ref, value_ref, weight_sem, out_sem = refs[11:]
     count = key_ref.shape[0]
     width = query_ref.shape[1]
+    depth = weight_ref.shape[0]
     tile_len = out_refs[0].shape[0]
     x, y, z, core = (spot_ref[i] for i in range(4))
-    start_shard(spot_ref, here[3], sent[3], 0, weight_ref, weight_sem)
-    owner = x == core
+    start_shard(spot_ref, here, sent, 0, weight_ref, weight_sem)
     places = [
         out_weight_ref.at[:, pl.ds(pl.multiple_of((z ^ d) * width, HD), width)] for d in range(4)
     ]
-    for role, shards in ((owner, here), (jnp.logical_not(owner), sent)):
-
-        @pl.when(role)
-        def _():
-            for d in range(4):
-                pltpu.make_async_copy(shards[d].at[3], places[d], out_sem.at[d]).start()
-
+    start_out_weights(spot_ref, here, sent, places[3], out_sem.at[3])
+    known = [
+        pltpu.make_async_copy(out_known_ref.at[d], places[d], out_sem.at[d]) for d in range(3)
+    ]
+    for copy in known:
+        copy.start()
     limit = len_ref[0]
     lane = lax.broadcasted_iota(jnp.int32, (1, tile_len), 1)
     bias = []
@@ -211,7 +215,7 @@
     bias = jnp.concatenate(bias, axis=1)
     for h in range(width // HD):
         value_ref[h, :, HD:] = jnp.ones((count, HD), jnp.bfloat16)
-    wait_shard(here[3], 0, weight_ref, weight_sem)
+    wait_shard(here, 0, weight_ref, weight_sem)
     step = 2 * tile_len
     rate = HD ** (-0.5) * math.log2(math.e)
     half = count // step // 2
@@ -222,7 +226,7 @@
         mixed = (
             totals[r // half][span, :]
             + jnp.dot(
-                lasts[r // half][span, :],
+                rows_refs[r // half][span, 3 * depth :],
                 weight_ref[:, skip:],
                 preferred_element_type=jnp.float32,
             )
@@ -233,8 +237,9 @@
         for h in range(width // HD):
             at = 2 * width - skip + h * HD
             value_ref[h, rows, :HD] = mixed[:, at : at + HD]
-    for d in range(4):
-        pltpu.make_async_copy(here[d].at[3], places[d], out_sem.at[d]).wait()
+    for copy in known:
+        copy.wait()
+    pltpu.make_async_copy(here.at[3], places[3], out_sem.at[3]).wait()
     for r in range(half):
         heads = []
         for h in range(width // HD):
@@ -298,59 +303,54 @@
     count = 8 * tile_len
 
     mod = jnp.transpose(modulation, (1, 0, 2))
-    normed = pl.pallas_call(
-        norm_kernel,
-        out_shape=jax.ShapeDtypeStruct((tile_len, width), jnp.bfloat16),
-        in_specs=[full, full],
-        out_specs=full,
-        name="norm",
-    )(states, mod)
     kinds = jnp.transpose(w_qkv, (1, 0, 2))
 
     four = jnp.concatenate([kinds, w_out[None]], axis=0)
     far = owners_swap(four, 2)
     near = owners_swap(four, 1)
-    along_x = swap(normed, "patch", 1, 2)
-    along_y = swap(normed, "wcol", 2, 4)
-    along_xy = swap(along_y, "patch", 1, 2)
-    far, near, along_x, along_y, along_xy, normed, four = lax.optimization_barrier(
-        (far, near, along_x, along_y, along_xy, normed, four)
-    )
+    along_x = swap(states, "patch", 1, 2)
+    along_y = swap(states, "wcol", 2, 4)
+    diagonal = [(a * 4 + c, (a ^ 1) * 4 + (c ^ 2)) for a in range(2) for c in range(4)]
+    along_xy = lax.ppermute(states, ("patch", "wcol"), diagonal)
+    tiles = [states, along_y, along_x, along_xy]
+    own_rows = pl.pallas_call(
+        norm_kernel,
+        out_shape=jax.ShapeDtypeStruct((count // 2, width), jnp.bfloat16),
+        in_specs=[scalar] + [full] * 5,
+        out_specs=full,
+        scratch_shapes=[pltpu.VMEM((tile_len, width), jnp.bfloat16)],
+        compiler_params=params,
+        name="norm",
+    )(spot, mod, *tiles)
+    other_rows = core_swap(own_rows)
+
     last = owners_swap(far, 1)
-    tiles = [normed, along_y, along_x, along_xy]
-    tiles_sent = [core_swap(tile) for tile in tiles]
-    early_here = [four, near, far]
-    early_sent = [core_swap(shard) for shard in early_here]
-
-    def early(rows, columns):
-        return pl.pallas_call(
-            early_kernel,
-            out_shape=(
-                jax.ShapeDtypeStruct((count // 2, columns), jnp.float32),
-                jax.ShapeDtypeStruct((count // 2, depth), jnp.bfloat16),
-            ),
-            in_specs=[scalar] + [anywhere] * 10,
-            out_specs=(full, full),
-            scratch_shapes=[
-                pltpu.VMEM((count // 2, 3 * depth), jnp.bfloat16),
-                pltpu.VMEM((3 * depth, 3 * local_cols), jnp.bfloat16),
-                pltpu.SemaphoreType.DMA((16,)),
-                pltpu.SemaphoreType.DMA((3, 3)),
-            ],
-            compiler_params=params,
-            name="early",
-        )(spot, *rows, *early_here, *early_sent)
-
-    total_a, rows_a = early(tiles, 3 * local_cols)
-    total_b, rows_b = early(tiles_sent, 2 * local_cols)
-    last, total_a, total_b = lax.optimization_barrier((last, total_a, total_b))
+    shards = [four, near, far]
+    total_own, total_other, out_known = pl.pallas_call(
+        early_kernel,
+        out_shape=(
+            jax.ShapeDtypeStruct((count // 2, 3 * local_cols), jnp.float32),
+            jax.ShapeDtypeStruct((count // 2, 2 * local_cols), jnp.float32),
+            jax.ShapeDtypeStruct((3,) + w_out.shape, jnp.bfloat16),
+        ),
+        in_specs=[scalar] + [full] * 2 + [anywhere] * 6,
+        out_specs=(full,) * 3,
+        scratch_shapes=[
+            pltpu.VMEM((3 * depth, 3 * local_cols), jnp.bfloat16),
+            pltpu.SemaphoreType.DMA((3, 3)),
+            pltpu.SemaphoreType.DMA((3,)),
+        ],
+        compiler_params=params,
+        name="early",
+    )(spot, own_rows, other_rows, *shards, *(core_swap(shard) for shard in shards))
+    last, total_own = lax.optimization_barrier((last, total_own))
     last_sent = core_swap(last)
 
     sent = jax.ShapeDtypeStruct((tile_len, width), jnp.bfloat16)
     part_own, part_y, part_x, part_xy = pl.pallas_call(
         attend_kernel,
         out_shape=(jax.ShapeDtypeStruct((tile_len, width), jnp.float32), sent, sent, sent),
-        in_specs=[scalar, scalar] + [full] * 4 + [anywhere] * 8,
+        in_specs=[scalar, scalar] + [full] * 5 + [anywhere] * 2,
         out_specs=(full,) * 4,
         scratch_shapes=[
             pltpu.VMEM((depth, 3 * local_cols), jnp.bfloat16),
@@ -363,8 +363,7 @@
         ],
         compiler_params=params,
         name="attend",
-    )(spot, lengths, total_a, total_b, rows_a, rows_b, *early_here, last, *early_sent, last_sent)
-    diagonal = [(a * 4 + c, (a ^ 1) * 4 + (c ^ 2)) for a in range(2) for c in range(4)]
+    )(spot, lengths, total_own, total_other, own_rows, other_rows, out_known, last, last_sent)
     got_xy = lax.ppermute(part_xy, ("patch", "wcol"), diagonal)
     got_x = swap(part_x, "patch", 1, 2)
     got_y = swap(part_y, "wcol", 2, 4)

time: 90.3 us -> 85.9 us (0.951)
  local copies, waits for them, and re-layouts: 8.6 us -> 1.44 us
  waiting for transfers between devices: 43.2 us -> 48.8 us
  Pallas kernels: 16.6 us -> 12.9 us
  starting transfers between devices: 18.1 us -> 19.1 us
    unnamed x18 -> x4, local copies, waits for them, and re-layouts: 7.89 us -> 0.73 us
    ppermute x13 -> x9, waiting for transfers between devices: 37.7 us -> 30.8 us  [swap(): return lax.ppermute(array, axis, [(i, i ^ d) for i in range(n)])]
    ppermute x3, waiting for transfers between devices: 3.68 us -> 10 us  [owners_swap(): return lax.ppermute(array, everywhere, pairs)]
    ppermute x0 -> x1, waiting for transfers between devices: none -> 6.18 us  [tiled_body(): along_xy = lax.ppermute(states, ('patch', 'wcol'), diagonal)]
    pallas_call x3 -> x2, Pallas kernels: 10 us -> 7.09 us  [the longest x1 4.81 us: tiled_body(): pl.pallas_call(early_kernel, out_shape=(jax.ShapeDtypeStruct((count // 2,...]
    ppermute x0 -> x1, starting transfers between devices: none -> 1.97 us  [tiled_body(): along_xy = lax.ppermute(states, ('patch', 'wcol'), diagonal)]
    ppermute x13 -> x9, starting transfers between devices: 5.19 us -> 4.22 us  [swap(): return lax.ppermute(array, axis, [(i, i ^ d) for i in range(n)])]
  transfers between devices with their start and end apart: 17 -> 14, of which waited for: 12 -> 12; matrix products, arithmetic and copies ran while one was open for 1% -> 1% of each run, Pallas kernels for 11% -> 8%
where the time goes in v3:
time: 85.9 us; the launch traced here: 85.5 us
  waiting for transfers between devices  48.8 us (57%)
  starting transfers between devices  19.1 us (22%)
  Pallas kernels  12.9 us (15%)
  other arithmetic  2.53 us (3%)
  local copies, waits for them, and re-layouts  1.44 us (2%)
    ppermute x9, waiting for transfers between devices, swap(): return lax.ppermute(array, axis, [(i, i ^ d) for i in range(n)])  30.8 us
    ppermute x3, starting transfers between devices, owners_swap(): return lax.ppermute(array, everywhere, pairs)  11.3 us
    ppermute x3, waiting for transfers between devices, owners_swap(): return lax.ppermute(array, everywhere, pairs)  10 us
    ppermute x1, waiting for transfers between devices, tiled_body(): along_xy = lax.ppermute(states, ('patch', 'wcol'), diagonal)  6.18 us
    pallas_call x1, Pallas kernels, tiled_body(): pl.pallas_call(attend_kernel, out_shape=(jax.ShapeDtypeStruct((tile_len,...  5.82 us
    pallas_call x1, Pallas kernels, tiled_body(): pl.pallas_call(early_kernel, out_shape=(jax.ShapeDtypeStruct((count // 2,...  4.81 us
    ppermute x9, starting transfers between devices, swap(): return lax.ppermute(array, axis, [(i, i ^ d) for i in range(n)])  4.22 us
    pallas_call x1, Pallas kernels, tiled_body(): pl.pallas_call(norm_kernel, out_shape=jax.ShapeDtypeStruct((count // 2, w...  2.28 us
  transfers between devices with their start and end apart: 14, of which 12 were waited for; matrix products, arithmetic and copies ran while one was open for 1% of the time, Pallas kernels for 8%

profile of v3, /device:TPU:0, one launch (start us, length us, event | category | flops | bytes accessed | tf_op | source)
XLA Modules:
  0.0 85.5 jit_solution(12979655032853464584)
XLA Ops:
  0.0 1.4 %pad_maximum_fusion.refs_0_ = bf16[4,384,384]{2,1,0:T(8,128)(2,1)S(1)} fusion(bf16[1,384,384]{2,1,0:T(8,128)(2,1)} %bitcast.17, bf16[3,384,384]{2,1,0:T(8,128)(2,1)} %bitcast.16), kind=kLoop, calls=%fused_computation | loop fusion | flops 589824 | bytes 2359296 | tf_op jit(solution)/shard_map/concatenate | solution.py:308
  1.4 5.9 %collective-permute-start = (bf16[4,384,384]{2,1,0:T(8,128)(2,1)S(1)}, bf16[4,384,384]{2,1,0:T(8,128)(2,1)S(1)}, u32[]{:S(2)}, u32[]{:S(2)}) collective-permute-start(bf16[4,384,384]{2,1,0:T(8,128)(2,1)S(1)} %pad_maximum_fusion.refs_0_), channel_id=1, source_target_pairs={{0,8},{2,10},{4,12},{6,14},{8,0},{10,2},{12,4},{14,6},{17,25},{19,... | collective-permute-start | bytes 3538952 | tf_op jit(solution)/shard_map/ppermute | solution.py:294
  7.4 3.5 %collective-permute-start.6 = (bf16[4,384,384]{2,1,0:T(8,128)(2,1)S(1)}, bf16[4,384,384]{2,1,0:T(8,128)(2,1)}, u32[]{:S(2)}, u32[]{:S(2)}) collective-permute-start(bf16[4,384,384]{2,1,0:T(8,128)(2,1)S(1)} %pad_maximum_fusion.refs_0_), channel_id=1, source_target_pairs={{0,4},{2,6},{4,0},{6,2},{8,12},{10,14},{12,8},{14,10},{17,21},{19,... | collective-permute-start | bytes 3538952 | tf_op jit(solution)/shard_map/ppermute | solution.py:294
  10.9 1.6 %collective-permute-start.2 = (bf16[128,1536]{1,0:T(8,128)(2,1)S(1)}, bf16[128,1536]{1,0:T(8,128)(2,1)S(1)}, u32[]{:S(2)}, u32[]{:S(2)}) collective-permute-start(bf16[128,1536]{1,0:T(8,128)(2,1)S(1)} %bitcast.11), channel_id=1, source_target_pairs={{0,2},{1,3},{2,0},{3,1},{4,6},{5,7},{6,4},{7,5},{8,10},{9,11},{10,... | collective-permute-start | bytes 1179656 | tf_op jit(solution)/shard_map/ppermute | solution.py:284
  12.5 2.0 %collective-permute-start.4 = (bf16[128,1536]{1,0:T(8,128)(2,1)S(1)}, bf16[128,1536]{1,0:T(8,128)(2,1)}, u32[]{:S(2)}, u32[]{:S(2)}) collective-permute-start(bf16[128,1536]{1,0:T(8,128)(2,1)S(1)} %bitcast.13), channel_id=1, source_target_pairs={{0,18},{1,19},{2,16},{3,17},{16,2},{17,3},{18,0},{19,1},{4,22},{5,... | collective-permute-start | bytes 1179656 | tf_op jit(solution)/shard_map/ppermute | solution.py:314
  14.5 4.2 %collective-permute-done.2.refs_1_ = bf16[128,1536]{1,0:T(8,128)(2,1)S(1)} collective-permute-done((bf16[128,1536]{1,0:T(8,128)(2,1)S(1)}, bf16[128,1536]{1,0:T(8,128)(2,1)S(1)}, u32[]{:S(2)}, u32[]{:S(2)}) %collective-permute-start.2) | collective-permute-done | bytes 393248 | tf_op jit(solution)/shard_map/ppermute | solution.py:284
  18.7 5.8 %collective-permute-done.3.refs_2_ = bf16[128,1536]{1,0:T(8,128)(2,1)S(1)} collective-permute-done((bf16[128,1536]{1,0:T(8,128)(2,1)S(1)}, bf16[128,1536]{1,0:T(8,128)(2,1)S(1)}, u32[]{:S(2)}, u32[]{:S(2)}) %collective-permute-start.3) | collective-permute-done | bytes 393248 | tf_op jit(solution)/shard_map/ppermute | solution.py:284
  24.5 6.2 %collective-permute-done.4.refs_3_ = bf16[128,1536]{1,0:T(8,128)(2,1)} collective-permute-done((bf16[128,1536]{1,0:T(8,128)(2,1)S(1)}, bf16[128,1536]{1,0:T(8,128)(2,1)}, u32[]{:S(2)}, u32[]{:S(2)}) %collective-permute-start.4) | collective-permute-done | bytes 393248 | tf_op jit(solution)/shard_map/ppermute | solution.py:314
  30.7 0.7 copy-done.1
  31.4 2.3 %norm.1.own_rows_ref.refs_2_ = bf16[512,1536]{1,0:T(8,128)(2,1)S(1)} custom-call(s32[4]{0:T(128)S(1)} %pad_add_fusion.spot_ref, f32[3,1,1536]{2,1,0:T(1,128)S(1)} %bitcast.15, bf16[128,1536]{1,0:T(8,128)(2,1)S(1)} %bitcast.14, bf16[128,1536]{1,0:T(8,128)(2,1)S(1)} %collective-permute-done.2.refs_1_, bf16[128,1536]{1,0:T(8,128)(2,1)S(1)} %collective-permute-done.3.refs_2_, ...), custom_call_target="tpu_custom_call" | custom-call | tf_op jit(solution)/shard_map/norm/pallas_call | solution.py:316
  34.4 2.4 %collective-permute-done.6.refs_1_ = bf16[4,384,384]{2,1,0:T(8,128)(2,1)} collective-permute-done((bf16[4,384,384]{2,1,0:T(8,128)(2,1)S(1)}, bf16[4,384,384]{2,1,0:T(8,128)(2,1)}, u32[]{:S(2)}, u32[]{:S(2)}) %collective-permute-start.6) | collective-permute-done | bytes 1179680 | tf_op jit(solution)/shard_map/ppermute | solution.py:294
  36.8 1.9 %collective-permute-start.1 = (bf16[4,384,384]{2,1,0:T(8,128)(2,1)S(1)}, bf16[4,384,384]{2,1,0:T(8,128)(2,1)S(1)}, u32[]{:S(2)}, u32[]{:S(2)}) collective-permute-start(bf16[4,384,384]{2,1,0:T(8,128)(2,1)S(1)} %collective-permute-done.refs_2_), channel_id=1, source_target_pairs={{0,4},{2,6},{4,0},{6,2},{8,12},{10,14},{12,8},{14,10},{17,21},{19,... | collective-permute-start | bytes 3538952 | tf_op jit(solution)/shard_map/ppermute | solution.py:294
  38.9 3.4 %collective-permute-done.9.refs_5_ = bf16[4,384,384]{2,1,0:T(8,128)(2,1)S(1)} collective-permute-done((bf16[4,384,384]{2,1,0:T(8,128)(2,1)S(1)}, bf16[4,384,384]{2,1,0:T(8,128)(2,1)S(1)}, u32[]{:S(2)}, u32[]{:S(2)}) %collective-permute-start.9) | collective-permute-done | bytes 1179680 | tf_op jit(solution)/shard_map/ppermute | solution.py:284
  42.5 4.8 %early.1 = (f32[512,1152]{1,0:T(8,128)S(1)}, f32[512,768]{1,0:T(8,128)S(1)}, bf16[3,384,384]{2,1,0:T(8,128)(2,1)S(1)}) custom-call(s32[4]{0:T(128)S(1)} %pad_add_fusion.spot_ref, bf16[512,1536]{1,0:T(8,128)(2,1)S(1)} %norm.1.own_rows_ref.refs_2_, bf16[512,1536]{1,0:T(8,128)(2,1)S(1)} %collective-permute-done.5.other_rows_ref.refs_3_, ...), custom_call_target="tpu_custom_call" | custom-call | tf_op jit(solution)/shard_map/early/pallas_call | solution.py:329
  47.3 7.6 %collective-permute-done.1.refs_5_ = bf16[4,384,384]{2,1,0:T(8,128)(2,1)S(1)} collective-permute-done((bf16[4,384,384]{2,1,0:T(8,128)(2,1)S(1)}, bf16[4,384,384]{2,1,0:T(8,128)(2,1)S(1)}, u32[]{:S(2)}, u32[]{:S(2)}) %collective-permute-start.1) | collective-permute-done | bytes 1179680 | tf_op jit(solution)/shard_map/ppermute | solution.py:294
  55.5 2.2 %collective-permute-done.10.refs_6_ = bf16[4,384,384]{2,1,0:T(8,128)(2,1)S(1)} collective-permute-done((bf16[4,384,384]{2,1,0:T(8,128)(2,1)S(1)}, bf16[4,384,384]{2,1,0:T(8,128)(2,1)S(1)}, u32[]{:S(2)}, u32[]{:S(2)}) %collective-permute-start.10) | collective-permute-done | bytes 1179680 | tf_op jit(solution)/shard_map/ppermute | solution.py:284
  57.7 5.8 %attend.1 = (f32[128,1536]{1,0:T(8,128)S(1)}, bf16[128,1536]{1,0:T(8,128)(2,1)S(1)}, bf16[128,1536]{1,0:T(8,128)(2,1)S(1)}, bf16[128,1536]{1,0:T(8,128)(2,1)S(1)}) custom-call(s32[4]{0:T(128)S(1)} %pad_add_fusion.spot_ref, s32[1]{0:T(128)S(6)} %copy.6.len_ref, f32[512,1152]{1,0:T(8,128)S(1)} %get-tuple-element.15.refs_0_, ...), custom_call_target="tpu_custom_call" | custom-call | tf_op jit(solution)/shard_map/attend/pallas_call | solution.py:350
  63.7 1.9 %collective-permute-start.12 = (bf16[128,1536]{1,0:T(8,128)(2,1)S(1)}, bf16[128,1536]{1,0:T(8,128)(2,1)S(1)}, u32[]{:S(2)}, u32[]{:S(2)}) collective-permute-start(bf16[128,1536]{1,0:T(8,128)(2,1)S(1)} %get-tuple-element.21), channel_id=1, source_target_pairs={{0,2},{1,3},{2,0},{3,1},{4,6},{5,7},{6,4},{7,5},{8,10},{9,11},{10,... | collective-permute-start | bytes 1179656 | tf_op jit(solution)/shard_map/ppermute | solution.py:284
  65.6 1.6 %collective-permute-start.13 = (bf16[128,1536]{1,0:T(8,128)(2,1)S(1)}, bf16[128,1536]{1,0:T(8,128)(2,1)S(1)}, u32[]{:S(2)}, u32[]{:S(2)}) collective-permute-start(bf16[128,1536]{1,0:T(8,128)(2,1)S(1)} %get-tuple-element.22), channel_id=1, source_target_pairs={{0,18},{1,19},{2,16},{3,17},{16,2},{17,3},{18,0},{19,1},{4,22},{5,... | collective-permute-start | bytes 1179656 | tf_op jit(solution)/shard_map/ppermute | solution.py:367
  67.1 0.7 slice_reduce_fusion
  67.8 7.8 %collective-permute-done.11 = bf16[128,1536]{1,0:T(8,128)(2,1)S(1)} collective-permute-done((bf16[128,1536]{1,0:T(8,128)(2,1)S(1)}, bf16[128,1536]{1,0:T(8,128)(2,1)S(1)}, u32[]{:S(2)}, u32[]{:S(2)}) %collective-permute-start.11) | collective-permute-done | bytes 393248 | tf_op jit(solution)/shard_map/ppermute | solution.py:284
  75.6 7.1 %collective-permute-done.12 = bf16[128,1536]{1,0:T(8,128)(2,1)S(1)} collective-permute-done((bf16[128,1536]{1,0:T(8,128)(2,1)S(1)}, bf16[128,1536]{1,0:T(8,128)(2,1)S(1)}, u32[]{:S(2)}, u32[]{:S(2)}) %collective-permute-start.12) | collective-permute-done | bytes 393248 | tf_op jit(solution)/shard_map/ppermute | solution.py:284
  82.7 1.8 %collective-permute-done.13 = bf16[128,1536]{1,0:T(8,128)(2,1)S(1)} collective-permute-done((bf16[128,1536]{1,0:T(8,128)(2,1)S(1)}, bf16[128,1536]{1,0:T(8,128)(2,1)S(1)}, u32[]{:S(2)}, u32[]{:S(2)}) %collective-permute-start.13) | collective-permute-done | bytes 393248 | tf_op jit(solution)/shard_map/ppermute | solution.py:367
  84.5 1.0 %fusion = bf16[1,128,1536]{2,1,0:T(8,128)(2,1)} fusion(bf16[128,1536]{1,0:T(8,128)(2,1)S(1)} %collective-permute-done.13, bf16[128,1536]{1,0:T(8,128)(2,1)S(1)} %collective-permute-done.12, f32[128,1536]{1,0:T(8,128)S(1)} %get-tuple-element.19, bf16[128,1536]{1,0:T(8,128)(2,1)S(1)} %collective-permute-done.11, f32[1536]{0:T(1024)S(1)} %slice_reduce_fusion, ...), kind=kLoop, calls=%fused_computation.2 | loop fusion | flops 1966080 | bytes 2758656 | tf_op jit(solution)/shard_map/broadcast_in_dim | solution.py:377
  (15 shorter events, 1.2 us)
Async XLA Ops:
  0.0 10.9 %copy-start = (bf16[1,128,1536]{2,1,0:T(8,128)(2,1)S(1)}, bf16[1,128,1536]{2,1,0:T(8,128)(2,1)}, u32[]{:S(2)}) copy-start(bf16[1,128,1536]{2,1,0:T(8,128)(2,1)} %param.5) | copy-start | bytes 1179652
  1.4 32.9 %collective-permute-start = (bf16[4,384,384]{2,1,0:T(8,128)(2,1)S(1)}, bf16[4,384,384]{2,1,0:T(8,128)(2,1)S(1)}, u32[]{:S(2)}, u32[]{:S(2)}) collective-permute-start(bf16[4,384,384]{2,1,0:T(8,128)(2,1)S(1)} %pad_maximum_fusion.refs_0_), channel_id=1, source_target_pairs={{0,8},{2,10},{4,12},{6,14},{8,0},{10,2},{12,4},{14,6},{17,25},{19,... | collective-permute-start | bytes 3538952 | tf_op jit(solution)/shard_map/ppermute | solution.py:294
  7.4 29.4 %collective-permute-start.6 = (bf16[4,384,384]{2,1,0:T(8,128)(2,1)S(1)}, bf16[4,384,384]{2,1,0:T(8,128)(2,1)}, u32[]{:S(2)}, u32[]{:S(2)}) collective-permute-start(bf16[4,384,384]{2,1,0:T(8,128)(2,1)S(1)} %pad_maximum_fusion.refs_0_), channel_id=1, source_target_pairs={{0,4},{2,6},{4,0},{6,2},{8,12},{10,14},{12,8},{14,10},{17,21},{19,... | collective-permute-start | bytes 3538952 | tf_op jit(solution)/shard_map/ppermute | solution.py:294
  10.9 7.8 %collective-permute-start.2 = (bf16[128,1536]{1,0:T(8,128)(2,1)S(1)}, bf16[128,1536]{1,0:T(8,128)(2,1)S(1)}, u32[]{:S(2)}, u32[]{:S(2)}) collective-permute-start(bf16[128,1536]{1,0:T(8,128)(2,1)S(1)} %bitcast.11), channel_id=1, source_target_pairs={{0,2},{1,3},{2,0},{3,1},{4,6},{5,7},{6,4},{7,5},{8,10},{9,11},{10,... | collective-permute-start | bytes 1179656 | tf_op jit(solution)/shard_map/ppermute | solution.py:284
  12.5 12.1 %collective-permute-start.3 = (bf16[128,1536]{1,0:T(8,128)(2,1)S(1)}, bf16[128,1536]{1,0:T(8,128)(2,1)S(1)}, u32[]{:S(2)}, u32[]{:S(2)}) collective-permute-start(bf16[128,1536]{1,0:T(8,128)(2,1)S(1)} %bitcast.12), channel_id=1, source_target_pairs={{0,16},{16,0},{1,17},{17,1},{2,18},{18,2},{3,19},{19,3},{4,20},{20... | collective-permute-start | bytes 1179656 | tf_op jit(solution)/shard_map/ppermute | solution.py:284
  12.5 18.2 %collective-permute-start.4 = (bf16[128,1536]{1,0:T(8,128)(2,1)S(1)}, bf16[128,1536]{1,0:T(8,128)(2,1)}, u32[]{:S(2)}, u32[]{:S(2)}) collective-permute-start(bf16[128,1536]{1,0:T(8,128)(2,1)S(1)} %bitcast.13), channel_id=1, source_target_pairs={{0,18},{1,19},{2,16},{3,17},{16,2},{17,3},{18,0},{19,1},{4,22},{5,... | collective-permute-start | bytes 1179656 | tf_op jit(solution)/shard_map/ppermute | solution.py:314
  30.7 0.7 copy-start.1
  33.7 5.2 %collective-permute-start.5 = (bf16[512,1536]{1,0:T(8,128)(2,1)S(1)}, bf16[512,1536]{1,0:T(8,128)(2,1)S(1)}, u32[]{:S(2)}, u32[]{:S(2)}) collective-permute-start(bf16[512,1536]{1,0:T(8,128)(2,1)S(1)} %norm.1.own_rows_ref.refs_2_), channel_id=1, source_target_pairs={{0,1},{1,0},{2,3},{3,2},{4,5},{5,4},{6,7},{7,6},{8,9},{9,8},{10,11... | collective-permute-start | bytes 4718600 | tf_op jit(solution)/shard_map/ppermute | solution.py:284
  33.8 5.1 %collective-permute-start.7 = (bf16[4,384,384]{2,1,0:T(8,128)(2,1)S(1)}, bf16[4,384,384]{2,1,0:T(8,128)(2,1)S(1)}, u32[]{:S(2)}, u32[]{:S(2)}) collective-permute-start(bf16[4,384,384]{2,1,0:T(8,128)(2,1)S(1)} %pad_maximum_fusion.refs_0_), channel_id=1, source_target_pairs={{0,1},{1,0},{2,3},{3,2},{4,5},{5,4},{6,7},{7,6},{8,9},{9,8},{10,11... | collective-permute-start | bytes 3538952 | tf_op jit(solution)/shard_map/ppermute | solution.py:284
  34.3 8.0 %collective-permute-start.9 = (bf16[4,384,384]{2,1,0:T(8,128)(2,1)S(1)}, bf16[4,384,384]{2,1,0:T(8,128)(2,1)S(1)}, u32[]{:S(2)}, u32[]{:S(2)}) collective-permute-start(bf16[4,384,384]{2,1,0:T(8,128)(2,1)S(1)} %collective-permute-done.refs_2_), channel_id=1, source_target_pairs={{0,1},{1,0},{2,3},{3,2},{4,5},{5,4},{6,7},{7,6},{8,9},{9,8},{10,11... | collective-permute-start | bytes 3538952 | tf_op jit(solution)/shard_map/ppermute | solution.py:284
  36.8 5.7 %collective-permute-start.8 = (bf16[4,384,384]{2,1,0:T(8,128)(2,1)}, bf16[4,384,384]{2,1,0:T(8,128)(2,1)S(1)}, u32[]{:S(2)}, u32[]{:S(2)}) collective-permute-start(bf16[4,384,384]{2,1,0:T(8,128)(2,1)} %collective-permute-done.6.refs_1_), channel_id=1, source_target_pairs={{0,1},{1,0},{2,3},{3,2},{4,5},{5,4},{6,7},{7,6},{8,9},{9,8},{10,11... | collective-permute-start | bytes 3538952 | tf_op jit(solution)/shard_map/ppermute | solution.py:284
  36.8 18.1 %collective-permute-start.1 = (bf16[4,384,384]{2,1,0:T(8,128)(2,1)S(1)}, bf16[4,384,384]{2,1,0:T(8,128)(2,1)S(1)}, u32[]{:S(2)}, u32[]{:S(2)}) collective-permute-start(bf16[4,384,384]{2,1,0:T(8,128)(2,1)S(1)} %collective-permute-done.refs_2_), channel_id=1, source_target_pairs={{0,4},{2,6},{4,0},{6,2},{8,12},{10,14},{12,8},{14,10},{17,21},{19,... | collective-permute-start | bytes 3538952 | tf_op jit(solution)/shard_map/ppermute | solution.py:294
  54.9 2.8 %collective-permute-start.10 = (bf16[4,384,384]{2,1,0:T(8,128)(2,1)S(1)}, bf16[4,384,384]{2,1,0:T(8,128)(2,1)S(1)}, u32[]{:S(2)}, u32[]{:S(2)}) collective-permute-start(bf16[4,384,384]{2,1,0:T(8,128)(2,1)S(1)} %collective-permute-done.1.refs_5_), channel_id=1, source_target_pairs={{0,1},{1,0},{2,3},{3,2},{4,5},{5,4},{6,7},{7,6},{8,9},{9,8},{10,11... | collective-permute-start | bytes 3538952 | tf_op jit(solution)/shard_map/ppermute | solution.py:284
  63.6 12.0 %collective-permute-start.11 = (bf16[128,1536]{1,0:T(8,128)(2,1)S(1)}, bf16[128,1536]{1,0:T(8,128)(2,1)S(1)}, u32[]{:S(2)}, u32[]{:S(2)}) collective-permute-start(bf16[128,1536]{1,0:T(8,128)(2,1)S(1)} %get-tuple-element.20), channel_id=1, source_target_pairs={{0,16},{16,0},{1,17},{17,1},{2,18},{18,2},{3,19},{19,3},{4,20},{20... | collective-permute-start | bytes 1179656 | tf_op jit(solution)/shard_map/ppermute | solution.py:284
  63.7 19.0 %collective-permute-start.12 = (bf16[128,1536]{1,0:T(8,128)(2,1)S(1)}, bf16[128,1536]{1,0:T(8,128)(2,1)S(1)}, u32[]{:S(2)}, u32[]{:S(2)}) collective-permute-start(bf16[128,1536]{1,0:T(8,128)(2,1)S(1)} %get-tuple-element.21), channel_id=1, source_target_pairs={{0,2},{1,3},{2,0},{3,1},{4,6},{5,7},{6,4},{7,5},{8,10},{9,11},{10,... | collective-permute-start | bytes 1179656 | tf_op jit(solution)/shard_map/ppermute | solution.py:284
  65.6 18.9 %collective-permute-start.13 = (bf16[128,1536]{1,0:T(8,128)(2,1)S(1)}, bf16[128,1536]{1,0:T(8,128)(2,1)S(1)}, u32[]{:S(2)}, u32[]{:S(2)}) collective-permute-start(bf16[128,1536]{1,0:T(8,128)(2,1)S(1)} %get-tuple-element.22), channel_id=1, source_target_pairs={{0,18},{1,19},{2,16},{3,17},{16,2},{17,3},{18,0},{19,1},{4,22},{5,... | collective-permute-start | bytes 1179656 | tf_op jit(solution)/shard_map/ppermute | solution.py:367

commit v4 on v3

--- a/solution.py
+++ b/solution.py
@@ -103,7 +103,7 @@
     return (hidden_states.astype(jnp.float32) + gate * out_proj).astype(jnp.bfloat16)
 
 
-SHIFTS = ((0, 0, 0), (0, 1, 0), (1, 0, 0), (1, 1, 0), (0, 0, 1), (0, 1, 1), (1, 0, 1), (1, 1, 1))
+SHIFTS = ((0, 1, 0), (1, 0, 0), (0, 0, 0), (1, 1, 0), (0, 1, 1), (1, 0, 1), (0, 0, 1), (1, 1, 1))
 VMEM_LIMIT = 18 * 1024 * 1024
 
 
@@ -187,15 +187,47 @@
         pltpu.make_async_copy(here[d].at[3], out_weight_ref.at[d], out_sem.at[d]).wait()
 
 
+def key_bias(spot_ref, len_ref, tile_len):
+    x, y, core = spot_ref[0], spot_ref[1], spot_ref[3]
+    lane = lax.broadcasted_iota(jnp.int32, (1, tile_len), 1)
+    bias = []
+    for dx, dy, dc in SHIFTS:
+        base = ((x ^ dx) * 4 + (y ^ dy) * 2 + (core ^ dc)) * tile_len
+        bias.append(jnp.where(base + lane < len_ref[0], 0.0, FLOOR))
+    return jnp.concatenate(bias, axis=1)
+
+
+def project(queries, key_ref, value_ref, out_weight_ref, bias, out_refs):
+    rate = HD ** (-0.5) * math.log2(math.e)
+    heads = []
+    for h in range(queries.shape[1] // HD):
+        column = slice(h * HD, (h + 1) * HD)
+        scores = lax.dot_general(
+            queries[:, column],
+            key_ref[:, column],
+            (((1,), (1,)), ((), ())),
+            preferred_element_type=jnp.float32,
+        )
+        scores = scores + bias
+        peak = jnp.max(scores, axis=-1, keepdims=True)
+        probs = jnp.exp2((scores - peak) * rate).astype(jnp.bfloat16)
+        sums = jnp.dot(probs, value_ref[h], preferred_element_type=jnp.float32)
+        heads.append((sums[:, :HD] / sums[:, HD:]).astype(jnp.bfloat16))
+    part = jnp.dot(
+        jnp.concatenate(heads, axis=1), out_weight_ref[...], preferred_element_type=jnp.float32
+    )
+    tile_len = out_refs[0].shape[0]
+    for i, out in enumerate(out_refs):
+        out[...] = part[i * tile_len : (i + 1) * tile_len].astype(out.dtype)
+
+
 def attend_kernel(spot_ref, len_ref, *refs):
     totals, rows_refs, (out_known_ref, here, sent) = refs[0:2], refs[2:4], refs[4:7]
-    out_refs = refs[7:11]
-    weight_ref, out_weight_ref, query_ref, key_ref, value_ref, weight_sem, out_sem = refs[11:]
-    count = key_ref.shape[0]
-    width = query_ref.shape[1]
+    out_refs, (query_ref, key_ref, value_ref, out_weight_ref) = refs[7:9], refs[9:13]
+    weight_ref, weight_sem, out_sem = refs[13:]
+    count, width = key_ref.shape
     depth = weight_ref.shape[0]
-    tile_len = out_refs[0].shape[0]
-    x, y, z, core = (spot_ref[i] for i in range(4))
+    z = spot_ref[2]
     start_shard(spot_ref, here, sent, 0, weight_ref, weight_sem)
     places = [
         out_weight_ref.at[:, pl.ds(pl.multiple_of((z ^ d) * width, HD), width)] for d in range(4)
@@ -206,33 +238,28 @@
     ]
     for copy in known:
         copy.start()
-    limit = len_ref[0]
-    lane = lax.broadcasted_iota(jnp.int32, (1, tile_len), 1)
-    bias = []
-    for dx, dy, dc in SHIFTS:
-        base = ((x ^ dx) * 4 + (y ^ dy) * 2 + (core ^ dc)) * tile_len
-        bias.append(jnp.where(base + lane < limit, 0.0, FLOOR))
-    bias = jnp.concatenate(bias, axis=1)
+    bias = key_bias(spot_ref, len_ref, count // 8)
     for h in range(width // HD):
         value_ref[h, :, HD:] = jnp.ones((count, HD), jnp.bfloat16)
     wait_shard(here, 0, weight_ref, weight_sem)
-    step = 2 * tile_len
-    rate = HD ** (-0.5) * math.log2(math.e)
-    half = count // step // 2
-    for r in range(count // step):
-        span = pl.ds((r % half) * step, step)
+    step = count // 4
+    queries = None
+    for r in range(4):
+        span = pl.ds((r % 2) * step, step)
         rows = pl.ds(r * step, step)
-        skip = 0 if r < half else width
+        skip = 0 if r < 2 else width
         mixed = (
-            totals[r // half][span, :]
+            totals[r // 2][span, :]
             + jnp.dot(
-                rows_refs[r // half][span, 3 * depth :],
+                rows_refs[r // 2][span, 3 * depth :],
                 weight_ref[:, skip:],
                 preferred_element_type=jnp.float32,
             )
         ).astype(jnp.bfloat16)
-        if r < half:
-            query_ref[rows, :] = mixed[:, :width]
+        if r == 0:
+            queries = mixed[:, :width]
+        elif r == 1:
+            query_ref[...] = mixed[:, :width]
         key_ref[rows, :] = mixed[:, width - skip : 2 * width - skip]
         for h in range(width // HD):
             at = 2 * width - skip + h * HD
@@ -240,29 +267,12 @@
     for copy in known:
         copy.wait()
     pltpu.make_async_copy(here.at[3], places[3], out_sem.at[3]).wait()
-    for r in range(half):
-        heads = []
-        for h in range(width // HD):
-            column = slice(h * HD, (h + 1) * HD)
-            scores = lax.dot_general(
-                query_ref[pl.ds(r * step, step), column],
-                key_ref[:, column],
-                (((1,), (1,)), ((), ())),
-                preferred_element_type=jnp.float32,
-            )
-            scores = scores + bias
-            peak = jnp.max(scores, axis=-1, keepdims=True)
-            probs = jnp.exp2((scores - peak) * rate).astype(jnp.bfloat16)
-            sums = jnp.dot(probs, value_ref[h], preferred_element_type=jnp.float32)
-            heads.append((sums[:, :HD] / sums[:, HD:]).astype(jnp.bfloat16))
-        part = jnp.dot(
-            jnp.concatenate(heads, axis=1),
-            out_weight_ref[...],
-            preferred_element_type=jnp.float32,
-        )
-        for i in range(2):
-            out = out_refs[2 * r + i]
-            out[...] = part[i * tile_len : (i + 1) * tile_len].astype(out.dtype)
+    project(queries, key_ref, value_ref, out_weight_ref, bias, out_refs)
+
+
+def attend_rest_kernel(spot_ref, len_ref, query_ref, key_ref, value_ref, out_weight_ref, *out_refs):
+    bias = key_bias(spot_ref, len_ref, key_ref.shape[0] // 8)
+    project(query_ref[...], key_ref, value_ref, out_weight_ref, bias, out_refs)
 
 
 def tiled_body(hidden_states, modulation, w_qkv, w_out, lengths):
@@ -312,7 +322,7 @@
     along_y = swap(states, "wcol", 2, 4)
     diagonal = [(a * 4 + c, (a ^ 1) * 4 + (c ^ 2)) for a in range(2) for c in range(4)]
     along_xy = lax.ppermute(states, ("patch", "wcol"), diagonal)
-    tiles = [states, along_y, along_x, along_xy]
+    tiles = [along_y, along_x, states, along_xy]
     own_rows = pl.pallas_call(
         norm_kernel,
         out_shape=jax.ShapeDtypeStruct((count // 2, width), jnp.bfloat16),
@@ -347,33 +357,40 @@
     last_sent = core_swap(last)
 
     sent = jax.ShapeDtypeStruct((tile_len, width), jnp.bfloat16)
-    part_own, part_y, part_x, part_xy = pl.pallas_call(
+    part_y, part_x, *kept = pl.pallas_call(
         attend_kernel,
-        out_shape=(jax.ShapeDtypeStruct((tile_len, width), jnp.float32), sent, sent, sent),
+        out_shape=(
+            sent,
+            sent,
+            jax.ShapeDtypeStruct((count // 4, local_cols), jnp.bfloat16),
+            jax.ShapeDtypeStruct((count, local_cols), jnp.bfloat16),
+            jax.ShapeDtypeStruct((local_cols // HD, count, 2 * HD), jnp.bfloat16),
+            jax.ShapeDtypeStruct((local_cols, width), jnp.bfloat16),
+        ),
         in_specs=[scalar, scalar] + [full] * 5 + [anywhere] * 2,
-        out_specs=(full,) * 4,
+        out_specs=(full,) * 6,
         scratch_shapes=[
             pltpu.VMEM((depth, 3 * local_cols), jnp.bfloat16),
-            pltpu.VMEM((local_cols, width), jnp.bfloat16),
-            pltpu.VMEM((count // 2, local_cols), jnp.bfloat16),
-            pltpu.VMEM((count, local_cols), jnp.bfloat16),
-            pltpu.VMEM((local_cols // HD, count, 2 * HD), jnp.bfloat16),
             pltpu.SemaphoreType.DMA((3,)),
             pltpu.SemaphoreType.DMA((4,)),
         ],
         compiler_params=params,
         name="attend",
     )(spot, lengths, total_own, total_other, own_rows, other_rows, out_known, last, last_sent)
-    got_xy = lax.ppermute(part_xy, ("patch", "wcol"), diagonal)
     got_x = swap(part_x, "patch", 1, 2)
     got_y = swap(part_y, "wcol", 2, 4)
-    out_proj = (
-        part_own
-        + got_x.astype(jnp.float32)
-        + got_y.astype(jnp.float32)
-        + got_xy.astype(jnp.float32)
-    )
-    updated = states.astype(jnp.float32) + mod[2] * out_proj
+    part_own, part_xy = pl.pallas_call(
+        attend_rest_kernel,
+        out_shape=(jax.ShapeDtypeStruct((tile_len, width), jnp.float32), sent),
+        in_specs=[scalar, scalar] + [full] * 4,
+        out_specs=(full,) * 2,
+        compiler_params=params,
+        name="attend_rest",
+    )(spot, lengths, *kept)
+    got_xy = lax.ppermute(part_xy, ("patch", "wcol"), diagonal)
+    near_sum = part_own + got_x.astype(jnp.float32) + got_y.astype(jnp.float32)
+    near_sum, got_xy = lax.optimization_barrier((near_sum, got_xy))
+    updated = states.astype(jnp.float32) + mod[2] * (near_sum + got_xy.astype(jnp.float32))
     return updated.astype(jnp.bfloat16)[None]
 
 

time: 85.9 us -> 84.1 us (0.979)
  waiting for transfers between devices: 48.8 us -> 46.1 us
  Pallas kernels: 12.9 us -> 13.8 us
    ppermute x9, waiting for transfers between devices: 30.8 us -> 28.2 us  [swap(): return lax.ppermute(array, axis, [(i, i ^ d) for i in range(n)])]
    pallas_call x1 -> x2, Pallas kernels: 5.82 us -> 6.66 us  [the longest x1 4.17 us: tiled_body(): pl.pallas_call(attend_kernel, out_shape=(sent, sent, jax.ShapeDtypeStruct...]
  transfers between devices with their start and end apart: 14 -> 14, of which waited for: 12 -> 12; matrix products, arithmetic and copies ran while one was open for 1% -> 1% of each run, Pallas kernels for 8% -> 11%
where the time goes in v4:
time: 84.1 us; the launch traced here: 83.8 us
  waiting for transfers between devices  46.1 us (55%)
  starting transfers between devices  19.2 us (23%)
  Pallas kernels  13.8 us (16%)
  other arithmetic  2.53 us (3%)
  local copies, waits for them, and re-layouts  1.44 us (2%)
    ppermute x9, waiting for transfers between devices, swap(): return lax.ppermute(array, axis, [(i, i ^ d) for i in range(n)])  28.2 us
    ppermute x3, starting transfers between devices, owners_swap(): return lax.ppermute(array, everywhere, pairs)  11.3 us
    ppermute x3, waiting for transfers between devices, owners_swap(): return lax.ppermute(array, everywhere, pairs)  10 us
    ppermute x1, waiting for transfers between devices, tiled_body(): along_xy = lax.ppermute(states, ('patch', 'wcol'), diagonal)  6.18 us
    pallas_call x1, Pallas kernels, tiled_body(): pl.pallas_call(early_kernel, out_shape=(jax.ShapeDtypeStruct((count // 2,...  4.81 us
    ppermute x9, starting transfers between devices, swap(): return lax.ppermute(array, axis, [(i, i ^ d) for i in range(n)])  4.22 us
    pallas_call x1, Pallas kernels, tiled_body(): pl.pallas_call(attend_kernel, out_shape=(sent, sent, jax.ShapeDtypeStruct...  4.17 us
    pallas_call x1, Pallas kernels, tiled_body(): pl.pallas_call(attend_rest_kernel, out_shape=(jax.ShapeDtypeStruct((tile_...  2.49 us
  transfers between devices with their start and end apart: 14, of which 12 were waited for; matrix products, arithmetic and copies ran while one was open for 1% of the time, Pallas kernels for 11%

profile of v4, /device:TPU:0, one launch (start us, length us, event | category | flops | bytes accessed | tf_op | source)
XLA Modules:
  0.0 83.8 jit_solution(17664130487875316283)
XLA Ops:
  0.0 1.4 %pad_maximum_fusion.refs_0_ = bf16[4,384,384]{2,1,0:T(8,128)(2,1)S(1)} fusion(bf16[1,384,384]{2,1,0:T(8,128)(2,1)} %bitcast.17, bf16[3,384,384]{2,1,0:T(8,128)(2,1)} %bitcast.16), kind=kLoop, calls=%fused_computation | loop fusion | flops 589824 | bytes 2359296 | tf_op jit(solution)/shard_map/concatenate | solution.py:318
  1.4 5.9 %collective-permute-start = (bf16[4,384,384]{2,1,0:T(8,128)(2,1)S(1)}, bf16[4,384,384]{2,1,0:T(8,128)(2,1)S(1)}, u32[]{:S(2)}, u32[]{:S(2)}) collective-permute-start(bf16[4,384,384]{2,1,0:T(8,128)(2,1)S(1)} %pad_maximum_fusion.refs_0_), channel_id=1, source_target_pairs={{0,8},{2,10},{4,12},{6,14},{8,0},{10,2},{12,4},{14,6},{17,25},{19,... | collective-permute-start | bytes 3538952 | tf_op jit(solution)/shard_map/ppermute | solution.py:304
  7.4 3.5 %collective-permute-start.6 = (bf16[4,384,384]{2,1,0:T(8,128)(2,1)S(1)}, bf16[4,384,384]{2,1,0:T(8,128)(2,1)}, u32[]{:S(2)}, u32[]{:S(2)}) collective-permute-start(bf16[4,384,384]{2,1,0:T(8,128)(2,1)S(1)} %pad_maximum_fusion.refs_0_), channel_id=1, source_target_pairs={{0,4},{2,6},{4,0},{6,2},{8,12},{10,14},{12,8},{14,10},{17,21},{19,... | collective-permute-start | bytes 3538952 | tf_op jit(solution)/shard_map/ppermute | solution.py:304
  10.9 1.6 %collective-permute-start.2 = (bf16[128,1536]{1,0:T(8,128)(2,1)S(1)}, bf16[128,1536]{1,0:T(8,128)(2,1)S(1)}, u32[]{:S(2)}, u32[]{:S(2)}) collective-permute-start(bf16[128,1536]{1,0:T(8,128)(2,1)S(1)} %bitcast.11), channel_id=1, source_target_pairs={{0,2},{1,3},{2,0},{3,1},{4,6},{5,7},{6,4},{7,5},{8,10},{9,11},{10,... | collective-permute-start | bytes 1179656 | tf_op jit(solution)/shard_map/ppermute | solution.py:294
  12.5 2.0 %collective-permute-start.4 = (bf16[128,1536]{1,0:T(8,128)(2,1)S(1)}, bf16[128,1536]{1,0:T(8,128)(2,1)}, u32[]{:S(2)}, u32[]{:S(2)}) collective-permute-start(bf16[128,1536]{1,0:T(8,128)(2,1)S(1)} %bitcast.13), channel_id=1, source_target_pairs={{0,18},{1,19},{2,16},{3,17},{16,2},{17,3},{18,0},{19,1},{4,22},{5,... | collective-permute-start | bytes 1179656 | tf_op jit(solution)/shard_map/ppermute | solution.py:324
  14.5 4.2 %collective-permute-done.2.refs_0_ = bf16[128,1536]{1,0:T(8,128)(2,1)S(1)} collective-permute-done((bf16[128,1536]{1,0:T(8,128)(2,1)S(1)}, bf16[128,1536]{1,0:T(8,128)(2,1)S(1)}, u32[]{:S(2)}, u32[]{:S(2)}) %collective-permute-start.2) | collective-permute-done | bytes 393248 | tf_op jit(solution)/shard_map/ppermute | solution.py:294
  18.7 5.8 %collective-permute-done.3.refs_1_ = bf16[128,1536]{1,0:T(8,128)(2,1)S(1)} collective-permute-done((bf16[128,1536]{1,0:T(8,128)(2,1)S(1)}, bf16[128,1536]{1,0:T(8,128)(2,1)S(1)}, u32[]{:S(2)}, u32[]{:S(2)}) %collective-permute-start.3) | collective-permute-done | bytes 393248 | tf_op jit(solution)/shard_map/ppermute | solution.py:294
  24.5 6.2 %collective-permute-done.4.refs_3_ = bf16[128,1536]{1,0:T(8,128)(2,1)} collective-permute-done((bf16[128,1536]{1,0:T(8,128)(2,1)S(1)}, bf16[128,1536]{1,0:T(8,128)(2,1)}, u32[]{:S(2)}, u32[]{:S(2)}) %collective-permute-start.4) | collective-permute-done | bytes 393248 | tf_op jit(solution)/shard_map/ppermute | solution.py:324
  30.7 0.7 copy-done.1
  31.4 2.3 %norm.1.own_rows_ref.refs_2_ = bf16[512,1536]{1,0:T(8,128)(2,1)S(1)} custom-call(s32[4]{0:T(128)S(1)} %pad_add_fusion.spot_ref, f32[3,1,1536]{2,1,0:T(1,128)S(1)} %bitcast.15, bf16[128,1536]{1,0:T(8,128)(2,1)S(1)} %collective-permute-done.2.refs_0_, bf16[128,1536]{1,0:T(8,128)(2,1)S(1)} %collective-permute-done.3.refs_1_, bf16[128,1536]{1,0:T(8,128)(2,1)S(1)} %bitcast.14, ...), custom_call_target="tpu_custom_call" | custom-call | tf_op jit(solution)/shard_map/norm/pallas_call | solution.py:326
  34.4 2.4 %collective-permute-done.6.refs_1_ = bf16[4,384,384]{2,1,0:T(8,128)(2,1)} collective-permute-done((bf16[4,384,384]{2,1,0:T(8,128)(2,1)S(1)}, bf16[4,384,384]{2,1,0:T(8,128)(2,1)}, u32[]{:S(2)}, u32[]{:S(2)}) %collective-permute-start.6) | collective-permute-done | bytes 1179680 | tf_op jit(solution)/shard_map/ppermute | solution.py:304
  36.8 1.9 %collective-permute-start.1 = (bf16[4,384,384]{2,1,0:T(8,128)(2,1)S(1)}, bf16[4,384,384]{2,1,0:T(8,128)(2,1)S(1)}, u32[]{:S(2)}, u32[]{:S(2)}) collective-permute-start(bf16[4,384,384]{2,1,0:T(8,128)(2,1)S(1)} %collective-permute-done.refs_2_), channel_id=1, source_target_pairs={{0,4},{2,6},{4,0},{6,2},{8,12},{10,14},{12,8},{14,10},{17,21},{19,... | collective-permute-start | bytes 3538952 | tf_op jit(solution)/shard_map/ppermute | solution.py:304
  38.9 3.4 %collective-permute-done.9.refs_5_ = bf16[4,384,384]{2,1,0:T(8,128)(2,1)S(1)} collective-permute-done((bf16[4,384,384]{2,1,0:T(8,128)(2,1)S(1)}, bf16[4,384,384]{2,1,0:T(8,128)(2,1)S(1)}, u32[]{:S(2)}, u32[]{:S(2)}) %collective-permute-start.9) | collective-permute-done | bytes 1179680 | tf_op jit(solution)/shard_map/ppermute | solution.py:294
  42.5 4.8 %early.1 = (f32[512,1152]{1,0:T(8,128)S(1)}, f32[512,768]{1,0:T(8,128)S(1)}, bf16[3,384,384]{2,1,0:T(8,128)(2,1)S(1)}) custom-call(s32[4]{0:T(128)S(1)} %pad_add_fusion.spot_ref, bf16[512,1536]{1,0:T(8,128)(2,1)S(1)} %norm.1.own_rows_ref.refs_2_, bf16[512,1536]{1,0:T(8,128)(2,1)S(1)} %collective-permute-done.5.other_rows_ref.refs_3_, ...), custom_call_target="tpu_custom_call" | custom-call | tf_op jit(solution)/shard_map/early/pallas_call | solution.py:339
  47.3 7.6 %collective-permute-done.1.refs_5_ = bf16[4,384,384]{2,1,0:T(8,128)(2,1)S(1)} collective-permute-done((bf16[4,384,384]{2,1,0:T(8,128)(2,1)S(1)}, bf16[4,384,384]{2,1,0:T(8,128)(2,1)S(1)}, u32[]{:S(2)}, u32[]{:S(2)}) %collective-permute-start.1) | collective-permute-done | bytes 1179680 | tf_op jit(solution)/shard_map/ppermute | solution.py:304
  55.5 2.2 %collective-permute-done.10.refs_6_ = bf16[4,384,384]{2,1,0:T(8,128)(2,1)S(1)} collective-permute-done((bf16[4,384,384]{2,1,0:T(8,128)(2,1)S(1)}, bf16[4,384,384]{2,1,0:T(8,128)(2,1)S(1)}, u32[]{:S(2)}, u32[]{:S(2)}) %collective-permute-start.10) | collective-permute-done | bytes 1179680 | tf_op jit(solution)/shard_map/ppermute | solution.py:294
  57.7 4.2 %attend.1 = (bf16[128,1536]{1,0:T(8,128)(2,1)S(1)}, bf16[128,1536]{1,0:T(8,128)(2,1)S(1)}, bf16[256,384]{1,0:T(8,128)(2,1)S(1)}, bf16[1024,384]{1,0:T(8,128)(2,1...) custom-call(s32[4]{0:T(128)S(1)} %pad_add_fusion.spot_ref, s32[1]{0:T(128)S(6)} %copy.6.len_ref, ...), custom_call_target="tpu_custom_call" | custom-call | tf_op jit(solution)/shard_map/attend/pallas_call | solution.py:360
  62.0 1.9 %collective-permute-start.12 = (bf16[128,1536]{1,0:T(8,128)(2,1)S(1)}, bf16[128,1536]{1,0:T(8,128)(2,1)S(1)}, u32[]{:S(2)}, u32[]{:S(2)}) collective-permute-start(bf16[128,1536]{1,0:T(8,128)(2,1)S(1)} %get-tuple-element.31), channel_id=1, source_target_pairs={{0,2},{1,3},{2,0},{3,1},{4,6},{5,7},{6,4},{7,5},{8,10},{9,11},{10,... | collective-permute-start | bytes 1179656 | tf_op jit(solution)/shard_map/ppermute | solution.py:294
  64.6 2.5 %attend_rest.1 = (f32[128,1536]{1,0:T(8,128)S(1)}, bf16[128,1536]{1,0:T(8,128)(2,1)S(1)}) custom-call(s32[4]{0:T(128)S(1)} %pad_add_fusion.spot_ref, s32[1]{0:T(128)S(6)} %copy.6.len_ref, bf16[256,384]{1,0:T(8,128)(2,1)S(1)} %get-tuple-element.25.query_ref, bf16[1024,384]{1,0:T(8,128)(2,1)S(1)} %get-tuple-element.26.key_ref, ...), custom_call_target="tpu_custom_call" | custom-call | tf_op jit(solution)/shard_map/attend_rest/pallas_call | solution.py:382
  67.1 1.6 %collective-permute-start.13 = (bf16[128,1536]{1,0:T(8,128)(2,1)S(1)}, bf16[128,1536]{1,0:T(8,128)(2,1)S(1)}, u32[]{:S(2)}, u32[]{:S(2)}) collective-permute-start(bf16[128,1536]{1,0:T(8,128)(2,1)S(1)} %get-tuple-element.32), channel_id=1, source_target_pairs={{0,18},{1,19},{2,16},{3,17},{16,2},{17,3},{18,0},{19,1},{4,22},{5,... | collective-permute-start | bytes 1179656 | tf_op jit(solution)/shard_map/ppermute | solution.py:390
  68.8 5.2 %collective-permute-done.11 = bf16[128,1536]{1,0:T(8,128)(2,1)S(1)} collective-permute-done((bf16[128,1536]{1,0:T(8,128)(2,1)S(1)}, bf16[128,1536]{1,0:T(8,128)(2,1)S(1)}, u32[]{:S(2)}, u32[]{:S(2)}) %collective-permute-start.11) | collective-permute-done | bytes 393248 | tf_op jit(solution)/shard_map/ppermute | solution.py:294
  74.0 7.1 %collective-permute-done.12 = bf16[128,1536]{1,0:T(8,128)(2,1)S(1)} collective-permute-done((bf16[128,1536]{1,0:T(8,128)(2,1)S(1)}, bf16[128,1536]{1,0:T(8,128)(2,1)S(1)}, u32[]{:S(2)}, u32[]{:S(2)}) %collective-permute-start.12) | collective-permute-done | bytes 393248 | tf_op jit(solution)/shard_map/ppermute | solution.py:294
  81.2 1.7 %collective-permute-done.13 = bf16[128,1536]{1,0:T(8,128)(2,1)S(1)} collective-permute-done((bf16[128,1536]{1,0:T(8,128)(2,1)S(1)}, bf16[128,1536]{1,0:T(8,128)(2,1)S(1)}, u32[]{:S(2)}, u32[]{:S(2)}) %collective-permute-start.13) | collective-permute-done | bytes 393248 | tf_op jit(solution)/shard_map/ppermute | solution.py:390
  82.8 0.9 %fusion = bf16[1,128,1536]{2,1,0:T(8,128)(2,1)} fusion(f32[128,1536]{1,0:T(8,128)S(1)} %convert_add_fusion, bf16[128,1536]{1,0:T(8,128)(2,1)S(1)} %collective-permute-done.13, f32[1536]{0:T(1024)S(1)} %slice_reduce_fusion, bf16[1,128,1536]{2,1,0:T(8,128)(2,1)S(1)} %copy-done), kind=kLoop, calls=%fused_computation.3 | loop fusion | flops 1179648 | bytes 1972224 | tf_op jit(solution)/shard_map/broadcast_in_dim | solution.py:394
  (17 shorter events, 2.0 us)
Async XLA Ops:
  0.0 10.9 %copy-start = (bf16[1,128,1536]{2,1,0:T(8,128)(2,1)S(1)}, bf16[1,128,1536]{2,1,0:T(8,128)(2,1)}, u32[]{:S(2)}) copy-start(bf16[1,128,1536]{2,1,0:T(8,128)(2,1)} %param.5) | copy-start | bytes 1179652
  1.4 32.9 %collective-permute-start = (bf16[4,384,384]{2,1,0:T(8,128)(2,1)S(1)}, bf16[4,384,384]{2,1,0:T(8,128)(2,1)S(1)}, u32[]{:S(2)}, u32[]{:S(2)}) collective-permute-start(bf16[4,384,384]{2,1,0:T(8,128)(2,1)S(1)} %pad_maximum_fusion.refs_0_), channel_id=1, source_target_pairs={{0,8},{2,10},{4,12},{6,14},{8,0},{10,2},{12,4},{14,6},{17,25},{19,... | collective-permute-start | bytes 3538952 | tf_op jit(solution)/shard_map/ppermute | solution.py:304
  7.4 29.4 %collective-permute-start.6 = (bf16[4,384,384]{2,1,0:T(8,128)(2,1)S(1)}, bf16[4,384,384]{2,1,0:T(8,128)(2,1)}, u32[]{:S(2)}, u32[]{:S(2)}) collective-permute-start(bf16[4,384,384]{2,1,0:T(8,128)(2,1)S(1)} %pad_maximum_fusion.refs_0_), channel_id=1, source_target_pairs={{0,4},{2,6},{4,0},{6,2},{8,12},{10,14},{12,8},{14,10},{17,21},{19,... | collective-permute-start | bytes 3538952 | tf_op jit(solution)/shard_map/ppermute | solution.py:304
  10.9 7.8 %collective-permute-start.2 = (bf16[128,1536]{1,0:T(8,128)(2,1)S(1)}, bf16[128,1536]{1,0:T(8,128)(2,1)S(1)}, u32[]{:S(2)}, u32[]{:S(2)}) collective-permute-start(bf16[128,1536]{1,0:T(8,128)(2,1)S(1)} %bitcast.11), channel_id=1, source_target_pairs={{0,2},{1,3},{2,0},{3,1},{4,6},{5,7},{6,4},{7,5},{8,10},{9,11},{10,... | collective-permute-start | bytes 1179656 | tf_op jit(solution)/shard_map/ppermute | solution.py:294
  12.5 12.1 %collective-permute-start.3 = (bf16[128,1536]{1,0:T(8,128)(2,1)S(1)}, bf16[128,1536]{1,0:T(8,128)(2,1)S(1)}, u32[]{:S(2)}, u32[]{:S(2)}) collective-permute-start(bf16[128,1536]{1,0:T(8,128)(2,1)S(1)} %bitcast.12), channel_id=1, source_target_pairs={{0,16},{16,0},{1,17},{17,1},{2,18},{18,2},{3,19},{19,3},{4,20},{20... | collective-permute-start | bytes 1179656 | tf_op jit(solution)/shard_map/ppermute | solution.py:294
  12.5 18.2 %collective-permute-start.4 = (bf16[128,1536]{1,0:T(8,128)(2,1)S(1)}, bf16[128,1536]{1,0:T(8,128)(2,1)}, u32[]{:S(2)}, u32[]{:S(2)}) collective-permute-start(bf16[128,1536]{1,0:T(8,128)(2,1)S(1)} %bitcast.13), channel_id=1, source_target_pairs={{0,18},{1,19},{2,16},{3,17},{16,2},{17,3},{18,0},{19,1},{4,22},{5,... | collective-permute-start | bytes 1179656 | tf_op jit(solution)/shard_map/ppermute | solution.py:324
  30.7 0.7 copy-start.1
  33.7 5.2 %collective-permute-start.5 = (bf16[512,1536]{1,0:T(8,128)(2,1)S(1)}, bf16[512,1536]{1,0:T(8,128)(2,1)S(1)}, u32[]{:S(2)}, u32[]{:S(2)}) collective-permute-start(bf16[512,1536]{1,0:T(8,128)(2,1)S(1)} %norm.1.own_rows_ref.refs_2_), channel_id=1, source_target_pairs={{0,1},{1,0},{2,3},{3,2},{4,5},{5,4},{6,7},{7,6},{8,9},{9,8},{10,11... | collective-permute-start | bytes 4718600 | tf_op jit(solution)/shard_map/ppermute | solution.py:294
  33.8 5.1 %collective-permute-start.7 = (bf16[4,384,384]{2,1,0:T(8,128)(2,1)S(1)}, bf16[4,384,384]{2,1,0:T(8,128)(2,1)S(1)}, u32[]{:S(2)}, u32[]{:S(2)}) collective-permute-start(bf16[4,384,384]{2,1,0:T(8,128)(2,1)S(1)} %pad_maximum_fusion.refs_0_), channel_id=1, source_target_pairs={{0,1},{1,0},{2,3},{3,2},{4,5},{5,4},{6,7},{7,6},{8,9},{9,8},{10,11... | collective-permute-start | bytes 3538952 | tf_op jit(solution)/shard_map/ppermute | solution.py:294
  34.3 8.0 %collective-permute-start.9 = (bf16[4,384,384]{2,1,0:T(8,128)(2,1)S(1)}, bf16[4,384,384]{2,1,0:T(8,128)(2,1)S(1)}, u32[]{:S(2)}, u32[]{:S(2)}) collective-permute-start(bf16[4,384,384]{2,1,0:T(8,128)(2,1)S(1)} %collective-permute-done.refs_2_), channel_id=1, source_target_pairs={{0,1},{1,0},{2,3},{3,2},{4,5},{5,4},{6,7},{7,6},{8,9},{9,8},{10,11... | collective-permute-start | bytes 3538952 | tf_op jit(solution)/shard_map/ppermute | solution.py:294
  36.8 5.7 %collective-permute-start.8 = (bf16[4,384,384]{2,1,0:T(8,128)(2,1)}, bf16[4,384,384]{2,1,0:T(8,128)(2,1)S(1)}, u32[]{:S(2)}, u32[]{:S(2)}) collective-permute-start(bf16[4,384,384]{2,1,0:T(8,128)(2,1)} %collective-permute-done.6.refs_1_), channel_id=1, source_target_pairs={{0,1},{1,0},{2,3},{3,2},{4,5},{5,4},{6,7},{7,6},{8,9},{9,8},{10,11... | collective-permute-start | bytes 3538952 | tf_op jit(solution)/shard_map/ppermute | solution.py:294
  36.8 18.1 %collective-permute-start.1 = (bf16[4,384,384]{2,1,0:T(8,128)(2,1)S(1)}, bf16[4,384,384]{2,1,0:T(8,128)(2,1)S(1)}, u32[]{:S(2)}, u32[]{:S(2)}) collective-permute-start(bf16[4,384,384]{2,1,0:T(8,128)(2,1)S(1)} %collective-permute-done.refs_2_), channel_id=1, source_target_pairs={{0,4},{2,6},{4,0},{6,2},{8,12},{10,14},{12,8},{14,10},{17,21},{19,... | collective-permute-start | bytes 3538952 | tf_op jit(solution)/shard_map/ppermute | solution.py:304
  54.9 2.8 %collective-permute-start.10 = (bf16[4,384,384]{2,1,0:T(8,128)(2,1)S(1)}, bf16[4,384,384]{2,1,0:T(8,128)(2,1)S(1)}, u32[]{:S(2)}, u32[]{:S(2)}) collective-permute-start(bf16[4,384,384]{2,1,0:T(8,128)(2,1)S(1)} %collective-permute-done.1.refs_5_), channel_id=1, source_target_pairs={{0,1},{1,0},{2,3},{3,2},{4,5},{5,4},{6,7},{7,6},{8,9},{9,8},{10,11... | collective-permute-start | bytes 3538952 | tf_op jit(solution)/shard_map/ppermute | solution.py:294
  61.9 12.0 %collective-permute-start.11 = (bf16[128,1536]{1,0:T(8,128)(2,1)S(1)}, bf16[128,1536]{1,0:T(8,128)(2,1)S(1)}, u32[]{:S(2)}, u32[]{:S(2)}) collective-permute-start(bf16[128,1536]{1,0:T(8,128)(2,1)S(1)} %get-tuple-element.30), channel_id=1, source_target_pairs={{0,16},{16,0},{1,17},{17,1},{2,18},{18,2},{3,19},{19,3},{4,20},{20... | collective-permute-start | bytes 1179656 | tf_op jit(solution)/shard_map/ppermute | solution.py:294
  62.0 19.0 %collective-permute-start.12 = (bf16[128,1536]{1,0:T(8,128)(2,1)S(1)}, bf16[128,1536]{1,0:T(8,128)(2,1)S(1)}, u32[]{:S(2)}, u32[]{:S(2)}) collective-permute-start(bf16[128,1536]{1,0:T(8,128)(2,1)S(1)} %get-tuple-element.31), channel_id=1, source_target_pairs={{0,2},{1,3},{2,0},{3,1},{4,6},{5,7},{6,4},{7,5},{8,10},{9,11},{10,... | collective-permute-start | bytes 1179656 | tf_op jit(solution)/shard_map/ppermute | solution.py:294
  67.1 15.7 %collective-permute-start.13 = (bf16[128,1536]{1,0:T(8,128)(2,1)S(1)}, bf16[128,1536]{1,0:T(8,128)(2,1)S(1)}, u32[]{:S(2)}, u32[]{:S(2)}) collective-permute-start(bf16[128,1536]{1,0:T(8,128)(2,1)S(1)} %get-tuple-element.32), channel_id=1, source_target_pairs={{0,18},{1,19},{2,16},{3,17},{16,2},{17,3},{18,0},{19,1},{4,22},{5,... | collective-permute-start | bytes 1179656 | tf_op jit(solution)/shard_map/ppermute | solution.py:390

commit v5 on v4

--- a/solution.py
+++ b/solution.py
@@ -103,7 +103,7 @@
     return (hidden_states.astype(jnp.float32) + gate * out_proj).astype(jnp.bfloat16)
 
 
-SHIFTS = ((0, 1, 0), (1, 0, 0), (0, 0, 0), (1, 1, 0), (0, 1, 1), (1, 0, 1), (0, 0, 1), (1, 1, 1))
+SHIFTS = ((0, 0, 0), (1, 1, 0), (0, 1, 0), (1, 0, 0), (0, 0, 1), (1, 1, 1), (0, 1, 1), (1, 0, 1))
 VMEM_LIMIT = 18 * 1024 * 1024
 
 
@@ -197,7 +197,7 @@
     return jnp.concatenate(bias, axis=1)
 
 
-def project(queries, key_ref, value_ref, out_weight_ref, bias, out_refs):
+def project(queries, key_ref, value_ref, out_weight_ref, bias):
     rate = HD ** (-0.5) * math.log2(math.e)
     heads = []
     for h in range(queries.shape[1] // HD):
@@ -216,15 +216,13 @@
     part = jnp.dot(
         jnp.concatenate(heads, axis=1), out_weight_ref[...], preferred_element_type=jnp.float32
     )
-    tile_len = out_refs[0].shape[0]
-    for i, out in enumerate(out_refs):
-        out[...] = part[i * tile_len : (i + 1) * tile_len].astype(out.dtype)
+    return part[: part.shape[0] // 2], part[part.shape[0] // 2 :]
 
 
 def attend_kernel(spot_ref, len_ref, *refs):
     totals, rows_refs, (out_known_ref, here, sent) = refs[0:2], refs[2:4], refs[4:7]
-    out_refs, (query_ref, key_ref, value_ref, out_weight_ref) = refs[7:9], refs[9:13]
-    weight_ref, weight_sem, out_sem = refs[13:]
+    own_ref, left_ref, right_ref, query_ref, key_ref, value_ref, out_weight_ref = refs[7:14]
+    weight_ref, weight_sem, out_sem = refs[14:]
     count, width = key_ref.shape
     depth = weight_ref.shape[0]
     z = spot_ref[2]
@@ -267,12 +265,24 @@
     for copy in known:
         copy.wait()
     pltpu.make_async_copy(here.at[3], places[3], out_sem.at[3]).wait()
-    project(queries, key_ref, value_ref, out_weight_ref, bias, out_refs)
-
-
-def attend_rest_kernel(spot_ref, len_ref, query_ref, key_ref, value_ref, out_weight_ref, *out_refs):
+    own, diagonal = project(queries, key_ref, value_ref, out_weight_ref, bias)
+    own_ref[...] = own
+    middle = left_ref.shape[1]
+    left_ref[...] = diagonal[:, :middle].astype(jnp.bfloat16)
+    right_ref[...] = diagonal[:, middle:].astype(jnp.bfloat16)
+
+
+def attend_rest_kernel(
+    spot_ref, len_ref, query_ref, key_ref, value_ref, out_weight_ref, *out_refs
+):
+    y_left_ref, y_right_ref, x_left_ref, x_right_ref = out_refs
     bias = key_bias(spot_ref, len_ref, key_ref.shape[0] // 8)
-    project(query_ref[...], key_ref, value_ref, out_weight_ref, bias, out_refs)
+    along_y, along_x = project(query_ref[...], key_ref, value_ref, out_weight_ref, bias)
+    middle = y_left_ref.shape[1]
+    y_left_ref[...] = along_y[:, :middle]
+    y_right_ref[...] = along_y[:, middle:].astype(jnp.bfloat16)
+    x_left_ref[...] = along_x[:, :middle].astype(jnp.bfloat16)
+    x_right_ref[...] = along_x[:, middle:]
 
 
 def tiled_body(hidden_states, modulation, w_qkv, w_out, lengths):
@@ -322,7 +332,7 @@
     along_y = swap(states, "wcol", 2, 4)
     diagonal = [(a * 4 + c, (a ^ 1) * 4 + (c ^ 2)) for a in range(2) for c in range(4)]
     along_xy = lax.ppermute(states, ("patch", "wcol"), diagonal)
-    tiles = [along_y, along_x, states, along_xy]
+    tiles = [states, along_xy, along_y, along_x]
     own_rows = pl.pallas_call(
         norm_kernel,
         out_shape=jax.ShapeDtypeStruct((count // 2, width), jnp.bfloat16),
@@ -356,19 +366,21 @@
     last, total_own = lax.optimization_barrier((last, total_own))
     last_sent = core_swap(last)
 
-    sent = jax.ShapeDtypeStruct((tile_len, width), jnp.bfloat16)
-    part_y, part_x, *kept = pl.pallas_call(
+    half = jax.ShapeDtypeStruct((tile_len, width // 2), jnp.bfloat16)
+    half_f32 = jax.ShapeDtypeStruct((tile_len, width // 2), jnp.float32)
+    part_own, xy_left, xy_right, *kept = pl.pallas_call(
         attend_kernel,
         out_shape=(
-            sent,
-            sent,
+            jax.ShapeDtypeStruct((tile_len, width), jnp.float32),
+            half,
+            half,
             jax.ShapeDtypeStruct((count // 4, local_cols), jnp.bfloat16),
             jax.ShapeDtypeStruct((count, local_cols), jnp.bfloat16),
             jax.ShapeDtypeStruct((local_cols // HD, count, 2 * HD), jnp.bfloat16),
             jax.ShapeDtypeStruct((local_cols, width), jnp.bfloat16),
         ),
         in_specs=[scalar, scalar] + [full] * 5 + [anywhere] * 2,
-        out_specs=(full,) * 6,
+        out_specs=(full,) * 7,
         scratch_shapes=[
             pltpu.VMEM((depth, 3 * local_cols), jnp.bfloat16),
             pltpu.SemaphoreType.DMA((3,)),
@@ -377,21 +389,36 @@
         compiler_params=params,
         name="attend",
     )(spot, lengths, total_own, total_other, own_rows, other_rows, out_known, last, last_sent)
-    got_x = swap(part_x, "patch", 1, 2)
-    got_y = swap(part_y, "wcol", 2, 4)
-    part_own, part_xy = pl.pallas_call(
+    from_x = swap(xy_left, "patch", 1, 2)
+    from_y = swap(xy_right, "wcol", 2, 4)
+    y_left, y_right, x_left, x_right = pl.pallas_call(
         attend_rest_kernel,
-        out_shape=(jax.ShapeDtypeStruct((tile_len, width), jnp.float32), sent),
+        out_shape=(half_f32, half, half, half_f32),
         in_specs=[scalar, scalar] + [full] * 4,
-        out_specs=(full,) * 2,
+        out_specs=(full,) * 4,
         compiler_params=params,
         name="attend_rest",
     )(spot, lengths, *kept)
-    got_xy = lax.ppermute(part_xy, ("patch", "wcol"), diagonal)
-    near_sum = part_own + got_x.astype(jnp.float32) + got_y.astype(jnp.float32)
-    near_sum, got_xy = lax.optimization_barrier((near_sum, got_xy))
-    updated = states.astype(jnp.float32) + mod[2] * (near_sum + got_xy.astype(jnp.float32))
-    return updated.astype(jnp.bfloat16)[None]
+    got_x_left = swap(x_left, "patch", 1, 2)
+    got_y_right = swap(y_right, "wcol", 2, 4)
+    y_left = (y_left + from_x.astype(jnp.float32)).astype(jnp.bfloat16)
+    x_right = (x_right + from_y.astype(jnp.float32)).astype(jnp.bfloat16)
+    got_x_right = swap(x_right, "patch", 1, 2)
+    got_y_left = swap(y_left, "wcol", 2, 4)
+    middle = width // 2
+    updated = []
+    for columns, parts in (
+        (slice(0, middle), (got_x_left, got_y_left)),
+        (slice(middle, width), (got_x_right, got_y_right)),
+    ):
+        out_proj = part_own[:, columns] + parts[0].astype(jnp.float32) + parts[1].astype(jnp.float32)
+        updated.append(
+            (states[:, columns].astype(jnp.float32) + mod[2, :, columns] * out_proj).astype(
+                jnp.bfloat16
+            )
+        )
+    updated = jnp.concatenate(updated, axis=1)
+    return updated[None]
 
 
 def body(hidden_states, modulation, w_qkv, w_out, lengths, *, sizes):

time: 84.1 us -> 80.3 us (0.955)
  waiting for transfers between devices: 46.1 us -> 41.4 us
    ppermute x9 -> x13, waiting for transfers between devices: 28.2 us -> 21.2 us  [swap(): return lax.ppermute(array, axis, [(i, i ^ d) for i in range(n)])]
    ppermute x9 -> x13, starting transfers between devices: 4.22 us -> 8.53 us  [swap(): return lax.ppermute(array, axis, [(i, i ^ d) for i in range(n)])]
    ppermute x1, waiting for transfers between devices: 6.18 us -> 9.43 us  [tiled_body(): along_xy = lax.ppermute(states, ('patch', 'wcol'), diagonal)]
    ppermute x1, starting transfers between devices: 1.97 us -> 0.07 us  [tiled_body(): along_xy = lax.ppermute(states, ('patch', 'wcol'), diagonal)]
    ppermute x1 -> x0, waiting for transfers between devices: 1.69 us -> none  [tiled_body(): got_xy = lax.ppermute(part_xy, ('patch', 'wcol'), diagonal)]
    ppermute x1 -> x0, starting transfers between devices: 1.63 us -> none  [tiled_body(): got_xy = lax.ppermute(part_xy, ('patch', 'wcol'), diagonal)]
  transfers between devices with their start and end apart: 14 -> 17, of which waited for: 12 -> 13; matrix products, arithmetic and copies ran while one was open for 1% -> 1% of each run, Pallas kernels for 11% -> 12%
where the time goes in v5:
time: 80.3 us; the launch traced here: 79.9 us
  waiting for transfers between devices  41.4 us (52%)
  starting transfers between devices  19.9 us (25%)
  Pallas kernels  13.7 us (17%)
  other arithmetic  2.57 us (3%)
  local copies, waits for them, and re-layouts  1.45 us (2%)
    ppermute x13, waiting for transfers between devices, swap(): return lax.ppermute(array, axis, [(i, i ^ d) for i in range(n)])  21.2 us
    ppermute x3, starting transfers between devices, owners_swap(): return lax.ppermute(array, everywhere, pairs)  11.3 us
    ppermute x3, waiting for transfers between devices, owners_swap(): return lax.ppermute(array, everywhere, pairs)  10.8 us
    ppermute x1, waiting for transfers between devices, tiled_body(): along_xy = lax.ppermute(states, ('patch', 'wcol'), diagonal)  9.43 us
    ppermute x13, starting transfers between devices, swap(): return lax.ppermute(array, axis, [(i, i ^ d) for i in range(n)])  8.53 us
    pallas_call x1, Pallas kernels, tiled_body(): pl.pallas_call(early_kernel, out_shape=(jax.ShapeDtypeStruct((count // 2,...  4.81 us
    pallas_call x1, Pallas kernels, tiled_body(): pl.pallas_call(attend_kernel, out_shape=(jax.ShapeDtypeStruct((tile_len,...  4.17 us
    pallas_call x1, Pallas kernels, tiled_body(): pl.pallas_call(attend_rest_kernel, out_shape=(half_f32, half, half, half_...  2.48 us
  transfers between devices with their start and end apart: 17, of which 13 were waited for; matrix products, arithmetic and copies ran while one was open for 1% of the time, Pallas kernels for 12%

profile of v5, /device:TPU:0, one launch (start us, length us, event | category | flops | bytes accessed | tf_op | source)
XLA Modules:
  0.0 79.9 jit_solution(14222249628401869168)
XLA Ops:
  0.0 1.4 %pad_maximum_fusion.refs_0_ = bf16[4,384,384]{2,1,0:T(8,128)(2,1)S(1)} fusion(bf16[1,384,384]{2,1,0:T(8,128)(2,1)} %bitcast.18, bf16[3,384,384]{2,1,0:T(8,128)(2,1)} %bitcast.17), kind=kLoop, calls=%fused_computation | loop fusion | flops 589824 | bytes 2359296 | tf_op jit(solution)/shard_map/concatenate | solution.py:328
  1.4 5.9 %collective-permute-start = (bf16[4,384,384]{2,1,0:T(8,128)(2,1)S(1)}, bf16[4,384,384]{2,1,0:T(8,128)(2,1)S(1)}, u32[]{:S(2)}, u32[]{:S(2)}) collective-permute-start(bf16[4,384,384]{2,1,0:T(8,128)(2,1)S(1)} %pad_maximum_fusion.refs_0_), channel_id=1, source_target_pairs={{0,8},{2,10},{4,12},{6,14},{8,0},{10,2},{12,4},{14,6},{17,25},{19,... | collective-permute-start | bytes 3538952 | tf_op jit(solution)/shard_map/ppermute | solution.py:314
  7.4 3.5 %collective-permute-start.6 = (bf16[4,384,384]{2,1,0:T(8,128)(2,1)S(1)}, bf16[4,384,384]{2,1,0:T(8,128)(2,1)}, u32[]{:S(2)}, u32[]{:S(2)}) collective-permute-start(bf16[4,384,384]{2,1,0:T(8,128)(2,1)S(1)} %pad_maximum_fusion.refs_0_), channel_id=1, source_target_pairs={{0,4},{2,6},{4,0},{6,2},{8,12},{10,14},{12,8},{14,10},{17,21},{19,... | collective-permute-start | bytes 3538952 | tf_op jit(solution)/shard_map/ppermute | solution.py:314
  11.0 1.6 %collective-permute-start.3 = (bf16[128,1536]{1,0:T(8,128)(2,1)S(1)}, bf16[128,1536]{1,0:T(8,128)(2,1)S(1)}, u32[]{:S(2)}, u32[]{:S(2)}) collective-permute-start(bf16[128,1536]{1,0:T(8,128)(2,1)S(1)} %bitcast.11), channel_id=1, source_target_pairs={{0,2},{1,3},{2,0},{3,1},{4,6},{5,7},{6,4},{7,5},{8,10},{9,11},{10,... | collective-permute-start | bytes 1179656 | tf_op jit(solution)/shard_map/ppermute | solution.py:304
  12.6 1.9 %collective-permute-start.4 = (bf16[128,1536]{1,0:T(8,128)(2,1)S(1)}, bf16[128,1536]{1,0:T(8,128)(2,1)}, u32[]{:S(2)}, u32[]{:S(2)}) collective-permute-start(bf16[128,1536]{1,0:T(8,128)(2,1)S(1)} %bitcast.12), channel_id=1, source_target_pairs={{0,16},{16,0},{1,17},{17,1},{2,18},{18,2},{3,19},{19,3},{4,20},{20... | collective-permute-start | bytes 1179656 | tf_op jit(solution)/shard_map/ppermute | solution.py:304
  14.5 9.4 %collective-permute-done.2.refs_1_ = bf16[128,1536]{1,0:T(8,128)(2,1)S(1)} collective-permute-done((bf16[128,1536]{1,0:T(8,128)(2,1)S(1)}, bf16[128,1536]{1,0:T(8,128)(2,1)S(1)}, u32[]{:S(2)}, u32[]{:S(2)}) %collective-permute-start.2) | collective-permute-done | bytes 393248 | tf_op jit(solution)/shard_map/ppermute | solution.py:334
  24.0 6.4 %collective-permute-done.3.refs_2_ = bf16[128,1536]{1,0:T(8,128)(2,1)S(1)} collective-permute-done((bf16[128,1536]{1,0:T(8,128)(2,1)S(1)}, bf16[128,1536]{1,0:T(8,128)(2,1)S(1)}, u32[]{:S(2)}, u32[]{:S(2)}) %collective-permute-start.3) | collective-permute-done | bytes 393248 | tf_op jit(solution)/shard_map/ppermute | solution.py:304
  30.4 0.7 copy-done.1
  31.1 2.3 %norm.1.own_rows_ref.refs_2_ = bf16[512,1536]{1,0:T(8,128)(2,1)S(1)} custom-call(s32[4]{0:T(128)S(1)} %pad_add_fusion.spot_ref, f32[3,1,1536]{2,1,0:T(1,128)S(1)} %bitcast.16, bf16[128,1536]{1,0:T(8,128)(2,1)S(1)} %bitcast.13, bf16[128,1536]{1,0:T(8,128)(2,1)S(1)} %collective-permute-done.2.refs_1_, bf16[128,1536]{1,0:T(8,128)(2,1)S(1)} %collective-permute-done.3.refs_2_, ...), custom_call_target="tpu_custom_call" | custom-call | tf_op jit(solution)/shard_map/norm/pallas_call | solution.py:336
  34.3 2.5 %collective-permute-done.6.refs_1_ = bf16[4,384,384]{2,1,0:T(8,128)(2,1)} collective-permute-done((bf16[4,384,384]{2,1,0:T(8,128)(2,1)S(1)}, bf16[4,384,384]{2,1,0:T(8,128)(2,1)}, u32[]{:S(2)}, u32[]{:S(2)}) %collective-permute-start.6) | collective-permute-done | bytes 1179680 | tf_op jit(solution)/shard_map/ppermute | solution.py:314
  36.8 1.9 %collective-permute-start.1 = (bf16[4,384,384]{2,1,0:T(8,128)(2,1)S(1)}, bf16[4,384,384]{2,1,0:T(8,128)(2,1)S(1)}, u32[]{:S(2)}, u32[]{:S(2)}) collective-permute-start(bf16[4,384,384]{2,1,0:T(8,128)(2,1)S(1)} %collective-permute-done.refs_2_), channel_id=1, source_target_pairs={{0,4},{2,6},{4,0},{6,2},{8,12},{10,14},{12,8},{14,10},{17,21},{19,... | collective-permute-start | bytes 3538952 | tf_op jit(solution)/shard_map/ppermute | solution.py:314
  38.7 3.2 %collective-permute-done.9.refs_5_ = bf16[4,384,384]{2,1,0:T(8,128)(2,1)S(1)} collective-permute-done((bf16[4,384,384]{2,1,0:T(8,128)(2,1)S(1)}, bf16[4,384,384]{2,1,0:T(8,128)(2,1)S(1)}, u32[]{:S(2)}, u32[]{:S(2)}) %collective-permute-start.9) | collective-permute-done | bytes 1179680 | tf_op jit(solution)/shard_map/ppermute | solution.py:304
  42.1 4.8 %early.1 = (f32[512,1152]{1,0:T(8,128)S(1)}, f32[512,768]{1,0:T(8,128)S(1)}, bf16[3,384,384]{2,1,0:T(8,128)(2,1)S(1)}) custom-call(s32[4]{0:T(128)S(1)} %pad_add_fusion.spot_ref, bf16[512,1536]{1,0:T(8,128)(2,1)S(1)} %norm.1.own_rows_ref.refs_2_, bf16[512,1536]{1,0:T(8,128)(2,1)S(1)} %collective-permute-done.5.other_rows_ref.refs_3_, ...), custom_call_target="tpu_custom_call" | custom-call | tf_op jit(solution)/shard_map/early/pallas_call | solution.py:349
  46.9 8.0 %collective-permute-done.1.refs_5_ = bf16[4,384,384]{2,1,0:T(8,128)(2,1)S(1)} collective-permute-done((bf16[4,384,384]{2,1,0:T(8,128)(2,1)S(1)}, bf16[4,384,384]{2,1,0:T(8,128)(2,1)S(1)}, u32[]{:S(2)}, u32[]{:S(2)}) %collective-permute-start.1) | collective-permute-done | bytes 1179680 | tf_op jit(solution)/shard_map/ppermute | solution.py:314
  55.5 2.2 %collective-permute-done.10.refs_6_ = bf16[4,384,384]{2,1,0:T(8,128)(2,1)S(1)} collective-permute-done((bf16[4,384,384]{2,1,0:T(8,128)(2,1)S(1)}, bf16[4,384,384]{2,1,0:T(8,128)(2,1)S(1)}, u32[]{:S(2)}, u32[]{:S(2)}) %collective-permute-start.10) | collective-permute-done | bytes 1179680 | tf_op jit(solution)/shard_map/ppermute | solution.py:304
  57.7 4.2 %attend.1 = (f32[128,1536]{1,0:T(8,128)S(1)}, bf16[128,768]{1,0:T(8,128)(2,1)S(1)}, bf16[128,768]{1,0:T(8,128)(2,1)S(1)}, bf16[256,384]{1,0:T(8,128)(2,1)S(1)}, ...) custom-call(s32[4]{0:T(128)S(1)} %pad_add_fusion.spot_ref, ...), custom_call_target="tpu_custom_call" | custom-call | tf_op jit(solution)/shard_map/attend/pallas_call | solution.py:371
  61.9 1.9 %collective-permute-start.14 = (bf16[128,768]{1,0:T(8,128)(2,1)S(1)}, bf16[128,768]{1,0:T(8,128)(2,1)S(1)}, u32[]{:S(2)}, u32[]{:S(2)}) collective-permute-start(bf16[128,768]{1,0:T(8,128)(2,1)S(1)} %get-tuple-element.35), channel_id=1, source_target_pairs={{0,2},{1,3},{2,0},{3,1},{4,6},{5,7},{6,4},{7,5},{8,10},{9,11},{10,... | collective-permute-start | bytes 589832 | tf_op jit(solution)/shard_map/ppermute | solution.py:304
  63.8 2.5 %attend_rest.1 = (f32[128,768]{1,0:T(8,128)S(1)}, bf16[128,768]{1,0:T(8,128)(2,1)S(1)}, bf16[128,768]{1,0:T(8,128)(2,1)S(1)}, f32[128,768]{1,0:T(8,128)S(1)}) custom-call(s32[4]{0:T(128)S(1)} %pad_add_fusion.spot_ref, s32[1]{0:T(128)S(6)} %copy.6.len_ref, bf16[256,384]{1,0:T(8,128)(2,1)S(1)} %get-tuple-element.27.query_ref, ...), custom_call_target="tpu_custom_call" | custom-call | tf_op jit(solution)/shard_map/attend_rest/pallas_call | solution.py:394
  66.3 2.1 %collective-permute-start.11 = (bf16[128,768]{1,0:T(8,128)(2,1)S(1)}, bf16[128,768]{1,0:T(8,128)(2,1)S(1)}, u32[]{:S(2)}, u32[]{:S(2)}) collective-permute-start(bf16[128,768]{1,0:T(8,128)(2,1)S(1)} %get-tuple-element.31), channel_id=1, source_target_pairs={{0,16},{16,0},{1,17},{17,1},{2,18},{18,2},{3,19},{19,3},{4,20},{20... | collective-permute-start | bytes 589832 | tf_op jit(solution)/shard_map/ppermute | solution.py:304
  69.2 2.5 %collective-permute-done.12 = bf16[128,768]{1,0:T(8,128)(2,1)S(1)} collective-permute-done((bf16[128,768]{1,0:T(8,128)(2,1)S(1)}, bf16[128,768]{1,0:T(8,128)(2,1)S(1)}, u32[]{:S(2)}, u32[]{:S(2)}) %collective-permute-start.12) | collective-permute-done | bytes 196640 | tf_op jit(solution)/shard_map/ppermute | solution.py:304
  71.9 0.7 slice_reduce_fusion.1
  72.6 3.2 %collective-permute-done.11 = bf16[128,768]{1,0:T(8,128)(2,1)S(1)} collective-permute-done((bf16[128,768]{1,0:T(8,128)(2,1)S(1)}, bf16[128,768]{1,0:T(8,128)(2,1)S(1)}, u32[]{:S(2)}, u32[]{:S(2)}) %collective-permute-start.11) | collective-permute-done | bytes 196640 | tf_op jit(solution)/shard_map/ppermute | solution.py:304
  76.3 2.7 %collective-permute-done.15 = bf16[128,768]{1,0:T(8,128)(2,1)S(1)} collective-permute-done((bf16[128,768]{1,0:T(8,128)(2,1)S(1)}, bf16[128,768]{1,0:T(8,128)(2,1)S(1)}, u32[]{:S(2)}, u32[]{:S(2)}) %collective-permute-start.15) | collective-permute-done | bytes 196640 | tf_op jit(solution)/shard_map/ppermute | solution.py:304
  79.1 0.8 maximum_bitcast_fusion
  (25 shorter events, 2.9 us)
Async XLA Ops:
  0.0 10.9 %copy-start = (bf16[1,128,1536]{2,1,0:T(8,128)(2,1)S(1)}, bf16[1,128,1536]{2,1,0:T(8,128)(2,1)}, u32[]{:S(2)}) copy-start(bf16[1,128,1536]{2,1,0:T(8,128)(2,1)} %param.5) | copy-start | bytes 1179652
  1.4 32.9 %collective-permute-start = (bf16[4,384,384]{2,1,0:T(8,128)(2,1)S(1)}, bf16[4,384,384]{2,1,0:T(8,128)(2,1)S(1)}, u32[]{:S(2)}, u32[]{:S(2)}) collective-permute-start(bf16[4,384,384]{2,1,0:T(8,128)(2,1)S(1)} %pad_maximum_fusion.refs_0_), channel_id=1, source_target_pairs={{0,8},{2,10},{4,12},{6,14},{8,0},{10,2},{12,4},{14,6},{17,25},{19,... | collective-permute-start | bytes 3538952 | tf_op jit(solution)/shard_map/ppermute | solution.py:314
  7.4 29.4 %collective-permute-start.6 = (bf16[4,384,384]{2,1,0:T(8,128)(2,1)S(1)}, bf16[4,384,384]{2,1,0:T(8,128)(2,1)}, u32[]{:S(2)}, u32[]{:S(2)}) collective-permute-start(bf16[4,384,384]{2,1,0:T(8,128)(2,1)S(1)} %pad_maximum_fusion.refs_0_), channel_id=1, source_target_pairs={{0,4},{2,6},{4,0},{6,2},{8,12},{10,14},{12,8},{14,10},{17,21},{19,... | collective-permute-start | bytes 3538952 | tf_op jit(solution)/shard_map/ppermute | solution.py:314
  10.9 13.1 %collective-permute-start.2 = (bf16[128,1536]{1,0:T(8,128)(2,1)S(1)}, bf16[128,1536]{1,0:T(8,128)(2,1)S(1)}, u32[]{:S(2)}, u32[]{:S(2)}) collective-permute-start(bf16[128,1536]{1,0:T(8,128)(2,1)S(1)} %bitcast.10), channel_id=1, source_target_pairs={{0,18},{1,19},{2,16},{3,17},{16,2},{17,3},{18,0},{19,1},{4,22},{5,... | collective-permute-start | bytes 1179656 | tf_op jit(solution)/shard_map/ppermute | solution.py:334
  11.0 19.4 %collective-permute-start.3 = (bf16[128,1536]{1,0:T(8,128)(2,1)S(1)}, bf16[128,1536]{1,0:T(8,128)(2,1)S(1)}, u32[]{:S(2)}, u32[]{:S(2)}) collective-permute-start(bf16[128,1536]{1,0:T(8,128)(2,1)S(1)} %bitcast.11), channel_id=1, source_target_pairs={{0,2},{1,3},{2,0},{3,1},{4,6},{5,7},{6,4},{7,5},{8,10},{9,11},{10,... | collective-permute-start | bytes 1179656 | tf_op jit(solution)/shard_map/ppermute | solution.py:304
  12.6 17.8 %collective-permute-start.4 = (bf16[128,1536]{1,0:T(8,128)(2,1)S(1)}, bf16[128,1536]{1,0:T(8,128)(2,1)}, u32[]{:S(2)}, u32[]{:S(2)}) collective-permute-start(bf16[128,1536]{1,0:T(8,128)(2,1)S(1)} %bitcast.12), channel_id=1, source_target_pairs={{0,16},{16,0},{1,17},{17,1},{2,18},{18,2},{3,19},{19,3},{4,20},{20... | collective-permute-start | bytes 1179656 | tf_op jit(solution)/shard_map/ppermute | solution.py:304
  30.4 0.7 copy-start.1
  33.4 5.4 %collective-permute-start.5 = (bf16[512,1536]{1,0:T(8,128)(2,1)S(1)}, bf16[512,1536]{1,0:T(8,128)(2,1)S(1)}, u32[]{:S(2)}, u32[]{:S(2)}) collective-permute-start(bf16[512,1536]{1,0:T(8,128)(2,1)S(1)} %norm.1.own_rows_ref.refs_2_), channel_id=1, source_target_pairs={{0,1},{1,0},{2,3},{3,2},{4,5},{5,4},{6,7},{7,6},{8,9},{9,8},{10,11... | collective-permute-start | bytes 4718600 | tf_op jit(solution)/shard_map/ppermute | solution.py:304
  33.7 5.0 %collective-permute-start.7 = (bf16[4,384,384]{2,1,0:T(8,128)(2,1)S(1)}, bf16[4,384,384]{2,1,0:T(8,128)(2,1)S(1)}, u32[]{:S(2)}, u32[]{:S(2)}) collective-permute-start(bf16[4,384,384]{2,1,0:T(8,128)(2,1)S(1)} %pad_maximum_fusion.refs_0_), channel_id=1, source_target_pairs={{0,1},{1,0},{2,3},{3,2},{4,5},{5,4},{6,7},{7,6},{8,9},{9,8},{10,11... | collective-permute-start | bytes 3538952 | tf_op jit(solution)/shard_map/ppermute | solution.py:304
  34.3 7.6 %collective-permute-start.9 = (bf16[4,384,384]{2,1,0:T(8,128)(2,1)S(1)}, bf16[4,384,384]{2,1,0:T(8,128)(2,1)S(1)}, u32[]{:S(2)}, u32[]{:S(2)}) collective-permute-start(bf16[4,384,384]{2,1,0:T(8,128)(2,1)S(1)} %collective-permute-done.refs_2_), channel_id=1, source_target_pairs={{0,1},{1,0},{2,3},{3,2},{4,5},{5,4},{6,7},{7,6},{8,9},{9,8},{10,11... | collective-permute-start | bytes 3538952 | tf_op jit(solution)/shard_map/ppermute | solution.py:304
  36.8 5.3 %collective-permute-start.8 = (bf16[4,384,384]{2,1,0:T(8,128)(2,1)}, bf16[4,384,384]{2,1,0:T(8,128)(2,1)S(1)}, u32[]{:S(2)}, u32[]{:S(2)}) collective-permute-start(bf16[4,384,384]{2,1,0:T(8,128)(2,1)} %collective-permute-done.6.refs_1_), channel_id=1, source_target_pairs={{0,1},{1,0},{2,3},{3,2},{4,5},{5,4},{6,7},{7,6},{8,9},{9,8},{10,11... | collective-permute-start | bytes 3538952 | tf_op jit(solution)/shard_map/ppermute | solution.py:304
  36.8 18.1 %collective-permute-start.1 = (bf16[4,384,384]{2,1,0:T(8,128)(2,1)S(1)}, bf16[4,384,384]{2,1,0:T(8,128)(2,1)S(1)}, u32[]{:S(2)}, u32[]{:S(2)}) collective-permute-start(bf16[4,384,384]{2,1,0:T(8,128)(2,1)S(1)} %collective-permute-done.refs_2_), channel_id=1, source_target_pairs={{0,4},{2,6},{4,0},{6,2},{8,12},{10,14},{12,8},{14,10},{17,21},{19,... | collective-permute-start | bytes 3538952 | tf_op jit(solution)/shard_map/ppermute | solution.py:314
  54.9 2.8 %collective-permute-start.10 = (bf16[4,384,384]{2,1,0:T(8,128)(2,1)S(1)}, bf16[4,384,384]{2,1,0:T(8,128)(2,1)S(1)}, u32[]{:S(2)}, u32[]{:S(2)}) collective-permute-start(bf16[4,384,384]{2,1,0:T(8,128)(2,1)S(1)} %collective-permute-done.1.refs_5_), channel_id=1, source_target_pairs={{0,1},{1,0},{2,3},{3,2},{4,5},{5,4},{6,7},{7,6},{8,9},{9,8},{10,11... | collective-permute-start | bytes 3538952 | tf_op jit(solution)/shard_map/ppermute | solution.py:304
  61.9 7.1 %collective-permute-start.14 = (bf16[128,768]{1,0:T(8,128)(2,1)S(1)}, bf16[128,768]{1,0:T(8,128)(2,1)S(1)}, u32[]{:S(2)}, u32[]{:S(2)}) collective-permute-start(bf16[128,768]{1,0:T(8,128)(2,1)S(1)} %get-tuple-element.35), channel_id=1, source_target_pairs={{0,2},{1,3},{2,0},{3,1},{4,6},{5,7},{6,4},{7,5},{8,10},{9,11},{10,... | collective-permute-start | bytes 589832 | tf_op jit(solution)/shard_map/ppermute | solution.py:304
  63.8 7.8 %collective-permute-start.12 = (bf16[128,768]{1,0:T(8,128)(2,1)S(1)}, bf16[128,768]{1,0:T(8,128)(2,1)S(1)}, u32[]{:S(2)}, u32[]{:S(2)}) collective-permute-start(bf16[128,768]{1,0:T(8,128)(2,1)S(1)} %get-tuple-element.33), channel_id=1, source_target_pairs={{0,16},{16,0},{1,17},{17,1},{2,18},{18,2},{3,19},{19,3},{4,20},{20... | collective-permute-start | bytes 589832 | tf_op jit(solution)/shard_map/ppermute | solution.py:304
  66.3 9.5 %collective-permute-start.11 = (bf16[128,768]{1,0:T(8,128)(2,1)S(1)}, bf16[128,768]{1,0:T(8,128)(2,1)S(1)}, u32[]{:S(2)}, u32[]{:S(2)}) collective-permute-start(bf16[128,768]{1,0:T(8,128)(2,1)S(1)} %get-tuple-element.31), channel_id=1, source_target_pairs={{0,16},{16,0},{1,17},{17,1},{2,18},{18,2},{3,19},{19,3},{4,20},{20... | collective-permute-start | bytes 589832 | tf_op jit(solution)/shard_map/ppermute | solution.py:304
  68.4 7.8 %collective-permute-start.16 = (bf16[128,768]{1,0:T(8,128)(2,1)S(1)}, bf16[128,768]{1,0:T(8,128)(2,1)S(1)}, u32[]{:S(2)}, u32[]{:S(2)}) collective-permute-start(bf16[128,768]{1,0:T(8,128)(2,1)S(1)} %get-tuple-element.36), channel_id=1, source_target_pairs={{0,2},{1,3},{2,0},{3,1},{4,6},{5,7},{6,4},{7,5},{8,10},{9,11},{10,... | collective-permute-start | bytes 589832 | tf_op jit(solution)/shard_map/ppermute | solution.py:304
  69.1 9.8 %collective-permute-start.15 = (bf16[128,768]{1,0:T(8,128)(2,1)S(1)}, bf16[128,768]{1,0:T(8,128)(2,1)S(1)}, u32[]{:S(2)}, u32[]{:S(2)}) collective-permute-start(bf16[128,768]{1,0:T(8,128)(2,1)S(1)} %add_convert_fusion.1), channel_id=1, source_target_pairs={{0,16},{16,0},{1,17},{17,1},{2,18},{18,2},{3,19},{19,3},{4,20},{20... | collective-permute-start | bytes 589832 | tf_op jit(solution)/shard_map/ppermute | solution.py:304
  71.7 7.3 %collective-permute-start.13 = (bf16[128,768]{1,0:T(8,128)(2,1)S(1)}, bf16[128,768]{1,0:T(8,128)(2,1)S(1)}, u32[]{:S(2)}, u32[]{:S(2)}) collective-permute-start(bf16[128,768]{1,0:T(8,128)(2,1)S(1)} %add_convert_fusion.3), channel_id=1, source_target_pairs={{0,2},{1,3},{2,0},{3,1},{4,6},{5,7},{6,4},{7,5},{8,10},{9,11},{10,... | collective-permute-start | bytes 589832 | tf_op jit(solution)/shard_map/ppermute | solution.py:304

commit v6 on v5

--- a/solution.py
+++ b/solution.py
@@ -150,13 +150,13 @@
             out_ref[rows, d * depth : (d + 1) * depth] = tile_ref[:, pl.ds(start, depth)]
 
 
-def start_out_weights(spot_ref, here, sent, place, sem):
+def start_by_role(spot_ref, here, sent, place, sem):
     owner = spot_ref[0] == spot_ref[3]
-    for role, shard in ((owner, here), (jnp.logical_not(owner), sent)):
+    for role, source in ((owner, here), (jnp.logical_not(owner), sent)):
 
         @pl.when(role)
         def _():
-            pltpu.make_async_copy(shard.at[3], place, sem).start()
+            pltpu.make_async_copy(source, place, sem).start()
 
 
 def early_kernel(spot_ref, own_rows_ref, other_rows_ref, *refs):
@@ -166,7 +166,7 @@
     for d in range(3):
         start_shard(spot_ref, here[d], sent[d], d * depth, weight_ref, weight_sem.at[d])
     for d in range(3):
-        start_out_weights(spot_ref, here[d], sent[d], out_weight_ref.at[d], out_sem.at[d])
+        pltpu.make_async_copy(here[d].at[3], out_weight_ref.at[d], out_sem.at[d]).start()
     for d in range(3):
         wait_shard(here[d], d * depth, weight_ref, weight_sem.at[d])
     step = own_ref.shape[0] // 2
@@ -220,9 +220,9 @@
 
 
 def attend_kernel(spot_ref, len_ref, *refs):
-    totals, rows_refs, (out_known_ref, here, sent) = refs[0:2], refs[2:4], refs[4:7]
-    own_ref, left_ref, right_ref, query_ref, key_ref, value_ref, out_weight_ref = refs[7:14]
-    weight_ref, weight_sem, out_sem = refs[14:]
+    totals, rows_refs, out_here, out_sent, (here, sent) = refs[0:2], refs[2:4], refs[4], refs[5:8], refs[8:10]
+    own_ref, left_ref, right_ref, query_ref, key_ref, value_ref, out_weight_ref = refs[10:17]
+    weight_ref, weight_sem, out_sem = refs[17:]
     count, width = key_ref.shape
     depth = weight_ref.shape[0]
     z = spot_ref[2]
@@ -230,12 +230,9 @@
     places = [
         out_weight_ref.at[:, pl.ds(pl.multiple_of((z ^ d) * width, HD), width)] for d in range(4)
     ]
-    start_out_weights(spot_ref, here, sent, places[3], out_sem.at[3])
-    known = [
-        pltpu.make_async_copy(out_known_ref.at[d], places[d], out_sem.at[d]) for d in range(3)
-    ]
-    for copy in known:
-        copy.start()
+    for d in range(3):
+        start_by_role(spot_ref, out_here.at[d], out_sent[d].at[0], places[d], out_sem.at[d])
+    start_by_role(spot_ref, here.at[3], sent.at[3], places[3], out_sem.at[3])
     bias = key_bias(spot_ref, len_ref, count // 8)
     for h in range(width // HD):
         value_ref[h, :, HD:] = jnp.ones((count, HD), jnp.bfloat16)
@@ -262,9 +259,9 @@
         for h in range(width // HD):
             at = 2 * width - skip + h * HD
             value_ref[h, rows, :HD] = mixed[:, at : at + HD]
-    for copy in known:
-        copy.wait()
-    pltpu.make_async_copy(here.at[3], places[3], out_sem.at[3]).wait()
+    for d in range(4):
+        source = out_here.at[d] if d < 3 else here.at[3]
+        pltpu.make_async_copy(source, places[d], out_sem.at[d]).wait()
     own, diagonal = project(queries, key_ref, value_ref, out_weight_ref, bias)
     own_ref[...] = own
     middle = left_ref.shape[1]
@@ -272,10 +269,10 @@
     right_ref[...] = diagonal[:, middle:].astype(jnp.bfloat16)
 
 
-def attend_rest_kernel(
-    spot_ref, len_ref, query_ref, key_ref, value_ref, out_weight_ref, *out_refs
-):
-    y_left_ref, y_right_ref, x_left_ref, x_right_ref = out_refs
+def attend_rest_kernel(spot_ref, len_ref, states_ref, mod_ref, *refs):
+    part_ref, query_ref, key_ref, value_ref, out_weight_ref, base_ref = refs[:6]
+    y_left_ref, y_right_ref, x_left_ref, x_right_ref = refs[6:]
+    base_ref[...] = states_ref[...].astype(jnp.float32) + mod_ref[2] * part_ref[...]
     bias = key_bias(spot_ref, len_ref, key_ref.shape[0] // 8)
     along_y, along_x = project(query_ref[...], key_ref, value_ref, out_weight_ref, bias)
     middle = y_left_ref.shape[1]
@@ -362,8 +359,9 @@
         ],
         compiler_params=params,
         name="early",
-    )(spot, own_rows, other_rows, *shards, *(core_swap(shard) for shard in shards))
-    last, total_own = lax.optimization_barrier((last, total_own))
+    )(spot, own_rows, other_rows, *shards, *(core_swap(shard[:3]) for shard in shards))
+    out_sent = [core_swap(shard[3:]) for shard in shards]
+    last, total_own, *out_sent = lax.optimization_barrier((last, total_own, *out_sent))
     last_sent = core_swap(last)
 
     half = jax.ShapeDtypeStruct((tile_len, width // 2), jnp.bfloat16)
@@ -379,7 +377,7 @@
             jax.ShapeDtypeStruct((local_cols // HD, count, 2 * HD), jnp.bfloat16),
             jax.ShapeDtypeStruct((local_cols, width), jnp.bfloat16),
         ),
-        in_specs=[scalar, scalar] + [full] * 5 + [anywhere] * 2,
+        in_specs=[scalar, scalar] + [full] * 4 + [anywhere] * 6,
         out_specs=(full,) * 7,
         scratch_shapes=[
             pltpu.VMEM((depth, 3 * local_cols), jnp.bfloat16),
@@ -388,17 +386,23 @@
         ],
         compiler_params=params,
         name="attend",
-    )(spot, lengths, total_own, total_other, own_rows, other_rows, out_known, last, last_sent)
+    )(spot, lengths, total_own, total_other, own_rows, other_rows, out_known, *out_sent, last, last_sent)
     from_x = swap(xy_left, "patch", 1, 2)
     from_y = swap(xy_right, "wcol", 2, 4)
-    y_left, y_right, x_left, x_right = pl.pallas_call(
+    base, y_left, y_right, x_left, x_right = pl.pallas_call(
         attend_rest_kernel,
-        out_shape=(half_f32, half, half, half_f32),
-        in_specs=[scalar, scalar] + [full] * 4,
-        out_specs=(full,) * 4,
+        out_shape=(
+            jax.ShapeDtypeStruct((tile_len, width), jnp.float32),
+            half_f32,
+            half,
+            half,
+            half_f32,
+        ),
+        in_specs=[scalar, scalar] + [full] * 7,
+        out_specs=(full,) * 5,
         compiler_params=params,
         name="attend_rest",
-    )(spot, lengths, *kept)
+    )(spot, lengths, states, mod, part_own, *kept)
     got_x_left = swap(x_left, "patch", 1, 2)
     got_y_right = swap(y_right, "wcol", 2, 4)
     y_left = (y_left + from_x.astype(jnp.float32)).astype(jnp.bfloat16)
@@ -411,12 +415,8 @@
         (slice(0, middle), (got_x_left, got_y_left)),
         (slice(middle, width), (got_x_right, got_y_right)),
     ):
-        out_proj = part_own[:, columns] + parts[0].astype(jnp.float32) + parts[1].astype(jnp.float32)
-        updated.append(
-            (states[:, columns].astype(jnp.float32) + mod[2, :, columns] * out_proj).astype(
-                jnp.bfloat16
-            )
-        )
+        out_proj = parts[0].astype(jnp.float32) + parts[1].astype(jnp.float32)
+        updated.append((base[:, columns] + mod[2, :, columns] * out_proj).astype(jnp.bfloat16))
     updated = jnp.concatenate(updated, axis=1)
     return updated[None]
 

time: 80.3 us -> 78.6 us (0.979)
  waiting for transfers between devices: 41.4 us -> 37.6 us
  starting transfers between devices: 19.9 us -> 22.2 us
    ppermute x1, waiting for transfers between devices: 9.43 us -> 6.24 us  [tiled_body(): along_xy = lax.ppermute(states, ('patch', 'wcol'), diagonal)]
    ppermute x13 -> x16, waiting for transfers between devices: 21.2 us -> 19.6 us  [swap(): return lax.ppermute(array, axis, [(i, i ^ d) for i in range(n)])]
    ppermute x13 -> x16, starting transfers between devices: 8.53 us -> 9.92 us  [swap(): return lax.ppermute(array, axis, [(i, i ^ d) for i in range(n)])]
    ppermute x3, starting transfers between devices: 11.3 us -> 12.3 us  [owners_swap(): return lax.ppermute(array, everywhere, pairs)]
    ppermute x3, waiting for transfers between devices: 10.8 us -> 11.7 us  [owners_swap(): return lax.ppermute(array, everywhere, pairs)]
  transfers between devices with their start and end apart: 17 -> 20, of which waited for: 13 -> 12; matrix products, arithmetic and copies ran while one was open for 1% -> 1% of each run, Pallas kernels for 12% -> 13%
where the time goes in v6:
time: 78.6 us; the launch traced here: 78.2 us
  waiting for transfers between devices  37.6 us (48%)
  starting transfers between devices  22.2 us (28%)
  Pallas kernels  14 us (18%)
  other arithmetic  2.49 us (3%)
  local copies, waits for them, and re-layouts  1 us (1%)
  between operations  0.85 us (1%)
    ppermute x16, waiting for transfers between devices, swap(): return lax.ppermute(array, axis, [(i, i ^ d) for i in range(n)])  19.6 us
    ppermute x3, starting transfers between devices, owners_swap(): return lax.ppermute(array, everywhere, pairs)  12.3 us
    ppermute x3, waiting for transfers between devices, owners_swap(): return lax.ppermute(array, everywhere, pairs)  11.7 us
    ppermute x16, starting transfers between devices, swap(): return lax.ppermute(array, axis, [(i, i ^ d) for i in range(n)])  9.92 us
    ppermute x1, waiting for transfers between devices, tiled_body(): along_xy = lax.ppermute(states, ('patch', 'wcol'), diagonal)  6.24 us
    pallas_call x1, Pallas kernels, tiled_body(): pl.pallas_call(attend_kernel, out_shape=(jax.ShapeDtypeStruct((tile_len,...  4.21 us
    pallas_call x1, Pallas kernels, tiled_body(): pl.pallas_call(early_kernel, out_shape=(jax.ShapeDtypeStruct((count // 2,...  4.06 us
    pallas_call x1, Pallas kernels, tiled_body(): pl.pallas_call(attend_rest_kernel, out_shape=(jax.ShapeDtypeStruct((tile_...  3.04 us
  transfers between devices with their start and end apart: 20, of which 12 were waited for; matrix products, arithmetic and copies ran while one was open for 1% of the time, Pallas kernels for 13%

profile of v6, /device:TPU:0, one launch (start us, length us, event | category | flops | bytes accessed | tf_op | source)
XLA Modules:
  0.0 78.2 jit_solution(17509554497137050489)
XLA Ops:
  0.0 1.4 %pad_maximum_fusion.refs_0_ = bf16[4,384,384]{2,1,0:T(8,128)(2,1)S(1)} fusion(bf16[1,384,384]{2,1,0:T(8,128)(2,1)} %bitcast.15, bf16[3,384,384]{2,1,0:T(8,128)(2,1)} %bitcast.13), kind=kLoop, calls=%fused_computation | loop fusion | flops 589824 | bytes 2359296 | tf_op jit(solution)/shard_map/concatenate | solution.py:325
  1.4 5.9 %collective-permute-start = (bf16[4,384,384]{2,1,0:T(8,128)(2,1)S(1)}, bf16[4,384,384]{2,1,0:T(8,128)(2,1)S(1)}, u32[]{:S(2)}, u32[]{:S(2)}) collective-permute-start(bf16[4,384,384]{2,1,0:T(8,128)(2,1)S(1)} %pad_maximum_fusion.refs_0_), channel_id=1, source_target_pairs={{0,8},{2,10},{4,12},{6,14},{8,0},{10,2},{12,4},{14,6},{17,25},{19,... | collective-permute-start | bytes 3538952 | tf_op jit(solution)/shard_map/ppermute | solution.py:311
  7.4 1.6 %collective-permute-start.3 = (bf16[128,1536]{1,0:T(8,128)(2,1)}, bf16[128,1536]{1,0:T(8,128)(2,1)}, u32[]{:S(2)}, u32[]{:S(2)}) collective-permute-start(bf16[128,1536]{1,0:T(8,128)(2,1)} %bitcast.4.refs_0_.states_ref), channel_id=1, source_target_pairs={{0,2},{1,3},{2,0},{3,1},{4,6},{5,7},{6,4},{7,5},{8,10},{9,11},{10,... | collective-permute-start | bytes 1179656 | tf_op jit(solution)/shard_map/ppermute | solution.py:301
  9.0 1.9 %collective-permute-start.4 = (bf16[128,1536]{1,0:T(8,128)(2,1)}, bf16[128,1536]{1,0:T(8,128)(2,1)}, u32[]{:S(2)}, u32[]{:S(2)}) collective-permute-start(bf16[128,1536]{1,0:T(8,128)(2,1)} %bitcast.4.refs_0_.states_ref), channel_id=1, source_target_pairs={{0,16},{16,0},{1,17},{17,1},{2,18},{18,2},{3,19},{19,3},{4,20},{20... | collective-permute-start | bytes 1179656 | tf_op jit(solution)/shard_map/ppermute | solution.py:301
  10.9 3.5 %collective-permute-start.6 = (bf16[4,384,384]{2,1,0:T(8,128)(2,1)S(1)}, bf16[4,384,384]{2,1,0:T(8,128)(2,1)S(1)}, u32[]{:S(2)}, u32[]{:S(2)}) collective-permute-start(bf16[4,384,384]{2,1,0:T(8,128)(2,1)S(1)} %pad_maximum_fusion.refs_0_), channel_id=1, source_target_pairs={{0,4},{2,6},{4,0},{6,2},{8,12},{10,14},{12,8},{14,10},{17,21},{19,... | collective-permute-start | bytes 3538952 | tf_op jit(solution)/shard_map/ppermute | solution.py:311
  14.5 6.2 %collective-permute-done.2.refs_1_ = bf16[128,1536]{1,0:T(8,128)(2,1)} collective-permute-done((bf16[128,1536]{1,0:T(8,128)(2,1)}, bf16[128,1536]{1,0:T(8,128)(2,1)}, u32[]{:S(2)}, u32[]{:S(2)}) %collective-permute-start.2) | collective-permute-done | bytes 393248 | tf_op jit(solution)/shard_map/ppermute | solution.py:331
  20.7 6.6 %collective-permute-done.3.refs_2_ = bf16[128,1536]{1,0:T(8,128)(2,1)} collective-permute-done((bf16[128,1536]{1,0:T(8,128)(2,1)}, bf16[128,1536]{1,0:T(8,128)(2,1)}, u32[]{:S(2)}, u32[]{:S(2)}) %collective-permute-start.3) | collective-permute-done | bytes 393248 | tf_op jit(solution)/shard_map/ppermute | solution.py:301
  28.1 2.7 %norm.1.own_rows_ref.refs_2_ = bf16[512,1536]{1,0:T(8,128)(2,1)S(1)} custom-call(s32[4]{0:T(128)S(1)} %pad_add_fusion.spot_ref, f32[3,1,1536]{2,1,0:T(1,128)S(1)} %bitcast.10, bf16[128,1536]{1,0:T(8,128)(2,1)} %bitcast.4.refs_0_.states_ref, bf16[128,1536]{1,0:T(8,128)(2,1)} %collective-permute-done.2.refs_1_, ...), custom_call_target="tpu_custom_call" | custom-call | tf_op jit(solution)/shard_map/norm/pallas_call | solution.py:333
  31.4 2.9 %collective-permute-done.refs_2_ = bf16[4,384,384]{2,1,0:T(8,128)(2,1)S(1)} collective-permute-done((bf16[4,384,384]{2,1,0:T(8,128)(2,1)S(1)}, bf16[4,384,384]{2,1,0:T(8,128)(2,1)S(1)}, u32[]{:S(2)}, u32[]{:S(2)}) %collective-permute-start) | collective-permute-done | bytes 1179680 | tf_op jit(solution)/shard_map/ppermute | solution.py:311
  34.4 2.8 %collective-permute-start.1 = (bf16[4,384,384]{2,1,0:T(8,128)(2,1)S(1)}, bf16[4,384,384]{2,1,0:T(8,128)(2,1)S(1)}, u32[]{:S(2)}, u32[]{:S(2)}) collective-permute-start(bf16[4,384,384]{2,1,0:T(8,128)(2,1)S(1)} %collective-permute-done.refs_2_), channel_id=1, source_target_pairs={{0,4},{2,6},{4,0},{6,2},{8,12},{10,14},{12,8},{14,10},{17,21},{19,... | collective-permute-start | bytes 3538952 | tf_op jit(solution)/shard_map/ppermute | solution.py:311
  37.3 2.9 %collective-permute-done.6.refs_1_ = bf16[4,384,384]{2,1,0:T(8,128)(2,1)S(1)} collective-permute-done((bf16[4,384,384]{2,1,0:T(8,128)(2,1)S(1)}, bf16[4,384,384]{2,1,0:T(8,128)(2,1)S(1)}, u32[]{:S(2)}, u32[]{:S(2)}) %collective-permute-start.6) | collective-permute-done | bytes 1179680 | tf_op jit(solution)/shard_map/ppermute | solution.py:311
  41.5 1.2 %collective-permute-done.8.refs_4_ = bf16[3,384,384]{2,1,0:T(8,128)(2,1)S(1)} collective-permute-done((bf16[3,384,384]{2,1,0:T(8,128)(2,1)S(1)}, bf16[3,384,384]{2,1,0:T(8,128)(2,1)S(1)}, u32[]{:S(2)}, u32[]{:S(2)}) %collective-permute-start.8) | collective-permute-done | bytes 884768 | tf_op jit(solution)/shard_map/ppermute | solution.py:301
  42.8 4.1 %early.1 = (f32[512,1152]{1,0:T(8,128)S(1)}, f32[512,768]{1,0:T(8,128)S(1)}, bf16[3,384,384]{2,1,0:T(8,128)(2,1)S(1)}) custom-call(s32[4]{0:T(128)S(1)} %pad_add_fusion.spot_ref, bf16[512,1536]{1,0:T(8,128)(2,1)S(1)} %norm.1.own_rows_ref.refs_2_, bf16[512,1536]{1,0:T(8,128)(2,1)S(1)} %collective-permute-done.5.other_rows_ref.refs_3_, ...), custom_call_target="tpu_custom_call" | custom-call | tf_op jit(solution)/shard_map/early/pallas_call | solution.py:346
  46.9 5.9 %collective-permute-done.1.refs_8_ = bf16[4,384,384]{2,1,0:T(8,128)(2,1)S(1)} collective-permute-done((bf16[4,384,384]{2,1,0:T(8,128)(2,1)S(1)}, bf16[4,384,384]{2,1,0:T(8,128)(2,1)S(1)}, u32[]{:S(2)}, u32[]{:S(2)}) %collective-permute-start.1) | collective-permute-done | bytes 1179680 | tf_op jit(solution)/shard_map/ppermute | solution.py:311
  53.5 2.2 %collective-permute-done.13.refs_9_ = bf16[4,384,384]{2,1,0:T(8,128)(2,1)S(1)} collective-permute-done((bf16[4,384,384]{2,1,0:T(8,128)(2,1)S(1)}, bf16[4,384,384]{2,1,0:T(8,128)(2,1)S(1)}, u32[]{:S(2)}, u32[]{:S(2)}) %collective-permute-start.13) | collective-permute-done | bytes 1179680 | tf_op jit(solution)/shard_map/ppermute | solution.py:301
  55.7 4.2 %attend.1 = (f32[128,1536]{1,0:T(8,128)S(1)}, bf16[128,768]{1,0:T(8,128)(2,1)S(1)}, bf16[128,768]{1,0:T(8,128)(2,1)S(1)}, bf16[256,384]{1,0:T(8,128)(2,1)S(1)}, ...) custom-call(s32[4]{0:T(128)S(1)} %pad_add_fusion.spot_ref, ...), custom_call_target="tpu_custom_call" | custom-call | tf_op jit(solution)/shard_map/attend/pallas_call | solution.py:369
  59.9 1.9 %collective-permute-start.17 = (bf16[128,768]{1,0:T(8,128)(2,1)S(1)}, bf16[128,768]{1,0:T(8,128)(2,1)S(1)}, u32[]{:S(2)}, u32[]{:S(2)}) collective-permute-start(bf16[128,768]{1,0:T(8,128)(2,1)S(1)} %get-tuple-element.43), channel_id=1, source_target_pairs={{0,2},{1,3},{2,0},{3,1},{4,6},{5,7},{6,4},{7,5},{8,10},{9,11},{10,... | collective-permute-start | bytes 589832 | tf_op jit(solution)/shard_map/ppermute | solution.py:301
  61.8 3.0 %attend_rest.1 = (f32[128,1536]{1,0:T(8,128)S(1)}, f32[128,768]{1,0:T(8,128)S(1)}, bf16[128,768]{1,0:T(8,128)(2,1)S(1)}, bf16[128,768]{1,0:T(8,128)(2,1)S(1)}, f32[128,768]{1,0:T(8,128)S(1)}) custom-call(s32[4]{0:T(128)S(1)} %pad_add_fusion.spot_ref, s32[1]{0:T(128)S(6)} %copy.6.len_ref, bf16[128,1536]{1,0:T(8,128)(2,1)} %bitcast.4.refs_0_.states_ref, ...), custom_call_target="tpu_custom_call" | custom-call | tf_op jit(solution)/shard_map/attend_rest/pallas_call | solution.py:392
  64.8 2.1 %collective-permute-start.14 = (bf16[128,768]{1,0:T(8,128)(2,1)S(1)}, bf16[128,768]{1,0:T(8,128)(2,1)S(1)}, u32[]{:S(2)}, u32[]{:S(2)}) collective-permute-start(bf16[128,768]{1,0:T(8,128)(2,1)S(1)} %get-tuple-element.39), channel_id=1, source_target_pairs={{0,16},{16,0},{1,17},{17,1},{2,18},{18,2},{3,19},{19,3},{4,20},{20... | collective-permute-start | bytes 589832 | tf_op jit(solution)/shard_map/ppermute | solution.py:301
  67.3 2.2 %collective-permute-done.15 = bf16[128,768]{1,0:T(8,128)(2,1)S(1)} collective-permute-done((bf16[128,768]{1,0:T(8,128)(2,1)S(1)}, bf16[128,768]{1,0:T(8,128)(2,1)S(1)}, u32[]{:S(2)}, u32[]{:S(2)}) %collective-permute-start.15) | collective-permute-done | bytes 196640 | tf_op jit(solution)/shard_map/ppermute | solution.py:301
  69.9 3.8 %collective-permute-done.14 = bf16[128,768]{1,0:T(8,128)(2,1)S(1)} collective-permute-done((bf16[128,768]{1,0:T(8,128)(2,1)S(1)}, bf16[128,768]{1,0:T(8,128)(2,1)S(1)}, u32[]{:S(2)}, u32[]{:S(2)}) %collective-permute-start.14) | collective-permute-done | bytes 196640 | tf_op jit(solution)/shard_map/ppermute | solution.py:301
  73.7 1.1 %collective-permute-done.19 = bf16[128,768]{1,0:T(8,128)(2,1)S(1)} collective-permute-done((bf16[128,768]{1,0:T(8,128)(2,1)S(1)}, bf16[128,768]{1,0:T(8,128)(2,1)S(1)}, u32[]{:S(2)}, u32[]{:S(2)}) %collective-permute-start.19) | collective-permute-done | bytes 196640 | tf_op jit(solution)/shard_map/ppermute | solution.py:301
  74.8 2.1 %collective-permute-done.18 = bf16[128,768]{1,0:T(8,128)(2,1)S(1)} collective-permute-done((bf16[128,768]{1,0:T(8,128)(2,1)S(1)}, bf16[128,768]{1,0:T(8,128)(2,1)S(1)}, u32[]{:S(2)}, u32[]{:S(2)}) %collective-permute-start.18) | collective-permute-done | bytes 196640 | tf_op jit(solution)/shard_map/ppermute | solution.py:301
  77.4 0.8 maximum_bitcast_fusion
  (39 shorter events, 4.2 us)
Async XLA Ops:
  1.4 32.9 %collective-permute-start = (bf16[4,384,384]{2,1,0:T(8,128)(2,1)S(1)}, bf16[4,384,384]{2,1,0:T(8,128)(2,1)S(1)}, u32[]{:S(2)}, u32[]{:S(2)}) collective-permute-start(bf16[4,384,384]{2,1,0:T(8,128)(2,1)S(1)} %pad_maximum_fusion.refs_0_), channel_id=1, source_target_pairs={{0,8},{2,10},{4,12},{6,14},{8,0},{10,2},{12,4},{14,6},{17,25},{19,... | collective-permute-start | bytes 3538952 | tf_op jit(solution)/shard_map/ppermute | solution.py:311
  7.4 13.4 %collective-permute-start.2 = (bf16[128,1536]{1,0:T(8,128)(2,1)}, bf16[128,1536]{1,0:T(8,128)(2,1)}, u32[]{:S(2)}, u32[]{:S(2)}) collective-permute-start(bf16[128,1536]{1,0:T(8,128)(2,1)} %bitcast.4.refs_0_.states_ref), channel_id=1, source_target_pairs={{0,18},{1,19},{2,16},{3,17},{16,2},{17,3},{18,0},{19,1},{4,22},{5,... | collective-permute-start | bytes 1179656 | tf_op jit(solution)/shard_map/ppermute | solution.py:331
  7.4 19.9 %collective-permute-start.3 = (bf16[128,1536]{1,0:T(8,128)(2,1)}, bf16[128,1536]{1,0:T(8,128)(2,1)}, u32[]{:S(2)}, u32[]{:S(2)}) collective-permute-start(bf16[128,1536]{1,0:T(8,128)(2,1)} %bitcast.4.refs_0_.states_ref), channel_id=1, source_target_pairs={{0,2},{1,3},{2,0},{3,1},{4,6},{5,7},{6,4},{7,5},{8,10},{9,11},{10,... | collective-permute-start | bytes 1179656 | tf_op jit(solution)/shard_map/ppermute | solution.py:301
  9.0 18.4 %collective-permute-start.4 = (bf16[128,1536]{1,0:T(8,128)(2,1)}, bf16[128,1536]{1,0:T(8,128)(2,1)}, u32[]{:S(2)}, u32[]{:S(2)}) collective-permute-start(bf16[128,1536]{1,0:T(8,128)(2,1)} %bitcast.4.refs_0_.states_ref), channel_id=1, source_target_pairs={{0,16},{16,0},{1,17},{17,1},{2,18},{18,2},{3,19},{19,3},{4,20},{20... | collective-permute-start | bytes 1179656 | tf_op jit(solution)/shard_map/ppermute | solution.py:301
  10.9 29.3 %collective-permute-start.6 = (bf16[4,384,384]{2,1,0:T(8,128)(2,1)S(1)}, bf16[4,384,384]{2,1,0:T(8,128)(2,1)S(1)}, u32[]{:S(2)}, u32[]{:S(2)}) collective-permute-start(bf16[4,384,384]{2,1,0:T(8,128)(2,1)S(1)} %pad_maximum_fusion.refs_0_), channel_id=1, source_target_pairs={{0,4},{2,6},{4,0},{6,2},{8,12},{10,14},{12,8},{14,10},{17,21},{19,... | collective-permute-start | bytes 3538952 | tf_op jit(solution)/shard_map/ppermute | solution.py:311
  27.4 0.7 copy-start
  28.1 2.9 %copy-start.2 = (bf16[384,3,384]{2,0,1:T(8,128)(2,1)S(1)}, bf16[384,3,384]{2,0,1:T(8,128)(2,1)}, u32[]{:S(2)}) copy-start(bf16[384,3,384]{2,0,1:T(8,128)(2,1)} %param.7) | copy-start | bytes 2654212
  30.8 10.2 %collective-permute-start.5 = (bf16[512,1536]{1,0:T(8,128)(2,1)S(1)}, bf16[512,1536]{1,0:T(8,128)(2,1)S(1)}, u32[]{:S(2)}, u32[]{:S(2)}) collective-permute-start(bf16[512,1536]{1,0:T(8,128)(2,1)S(1)} %norm.1.own_rows_ref.refs_2_), channel_id=1, source_target_pairs={{0,1},{1,0},{2,3},{3,2},{4,5},{5,4},{6,7},{7,6},{8,9},{9,8},{10,11... | collective-permute-start | bytes 4718600 | tf_op jit(solution)/shard_map/ppermute | solution.py:301
  31.0 9.4 %collective-permute-start.7 = (bf16[3,384,384]{2,1,0:T(8,128)(2,1)S(1)}, bf16[3,384,384]{2,1,0:T(8,128)(2,1)S(1)}, u32[]{:S(2)}, u32[]{:S(2)}) collective-permute-start(bf16[3,384,384]{2,1,0:T(8,128)(2,1)S(1)} %bitcast.14), channel_id=1, source_target_pairs={{0,1},{1,0},{2,3},{3,2},{4,5},{5,4},{6,7},{7,6},{8,9},{9,8},{10,11... | collective-permute-start | bytes 2654216 | tf_op jit(solution)/shard_map/ppermute | solution.py:301
  34.4 6.1 %copy-start.3 = (bf16[384,384]{1,0:T(8,128)(2,1)S(1)}, bf16[384,384]{1,0:T(8,128)(2,1)}, u32[]{:S(2)}) copy-start(bf16[384,384]{1,0:T(8,128)(2,1)} %param.8) | copy-start | bytes 884740
  34.4 6.7 %collective-permute-start.9 = (bf16[3,384,384]{2,1,0:T(8,128)(2,1)S(1)}, bf16[3,384,384]{2,1,0:T(8,128)(2,1)S(1)}, u32[]{:S(2)}, u32[]{:S(2)}) collective-permute-start(bf16[3,384,384]{2,1,0:T(8,128)(2,1)S(1)} %slice.33), channel_id=1, source_target_pairs={{0,1},{1,0},{2,3},{3,2},{4,5},{5,4},{6,7},{7,6},{8,9},{9,8},{10,11... | collective-permute-start | bytes 2654216 | tf_op jit(solution)/shard_map/ppermute | solution.py:301
  34.4 18.4 %collective-permute-start.1 = (bf16[4,384,384]{2,1,0:T(8,128)(2,1)S(1)}, bf16[4,384,384]{2,1,0:T(8,128)(2,1)S(1)}, u32[]{:S(2)}, u32[]{:S(2)}) collective-permute-start(bf16[4,384,384]{2,1,0:T(8,128)(2,1)S(1)} %collective-permute-done.refs_2_), channel_id=1, source_target_pairs={{0,4},{2,6},{4,0},{6,2},{8,12},{10,14},{12,8},{14,10},{17,21},{19,... | collective-permute-start | bytes 3538952 | tf_op jit(solution)/shard_map/ppermute | solution.py:311
  40.3 2.5 %collective-permute-start.8 = (bf16[3,384,384]{2,1,0:T(8,128)(2,1)S(1)}, bf16[3,384,384]{2,1,0:T(8,128)(2,1)S(1)}, u32[]{:S(2)}, u32[]{:S(2)}) collective-permute-start(bf16[3,384,384]{2,1,0:T(8,128)(2,1)S(1)} %slice.32), channel_id=1, source_target_pairs={{0,1},{1,0},{2,3},{3,2},{4,5},{5,4},{6,7},{7,6},{8,9},{9,8},{10,11... | collective-permute-start | bytes 2654216 | tf_op jit(solution)/shard_map/ppermute | solution.py:301
  40.5 6.4 %collective-permute-start.10 = (bf16[1,384,384]{2,1,0:T(8,128)(2,1)S(1)}, bf16[1,384,384]{2,1,0:T(8,128)(2,1)S(1)}, u32[]{:S(2)}, u32[]{:S(2)}) collective-permute-start(bf16[1,384,384]{2,1,0:T(8,128)(2,1)S(1)} %bitcast.16), channel_id=1, source_target_pairs={{0,1},{1,0},{2,3},{3,2},{4,5},{5,4},{6,7},{7,6},{8,9},{9,8},{10,11... | collective-permute-start | bytes 884744 | tf_op jit(solution)/shard_map/ppermute | solution.py:301
  41.0 5.8 %collective-permute-start.12 = (bf16[1,384,384]{2,1,0:T(8,128)(2,1)S(1)}, bf16[1,384,384]{2,1,0:T(8,128)(2,1)S(1)}, u32[]{:S(2)}, u32[]{:S(2)}) collective-permute-start(bf16[1,384,384]{2,1,0:T(8,128)(2,1)S(1)} %slice.35), channel_id=1, source_target_pairs={{0,1},{1,0},{2,3},{3,2},{4,5},{5,4},{6,7},{7,6},{8,9},{9,8},{10,11... | collective-permute-start | bytes 884744 | tf_op jit(solution)/shard_map/ppermute | solution.py:301
  41.1 5.8 %collective-permute-start.11 = (bf16[1,384,384]{2,1,0:T(8,128)(2,1)S(1)}, bf16[1,384,384]{2,1,0:T(8,128)(2,1)S(1)}, u32[]{:S(2)}, u32[]{:S(2)}) collective-permute-start(bf16[1,384,384]{2,1,0:T(8,128)(2,1)S(1)} %slice.34), channel_id=1, source_target_pairs={{0,1},{1,0},{2,3},{3,2},{4,5},{5,4},{6,7},{7,6},{8,9},{9,8},{10,11... | collective-permute-start | bytes 884744 | tf_op jit(solution)/shard_map/ppermute | solution.py:301
  52.8 2.8 %collective-permute-start.13 = (bf16[4,384,384]{2,1,0:T(8,128)(2,1)S(1)}, bf16[4,384,384]{2,1,0:T(8,128)(2,1)S(1)}, u32[]{:S(2)}, u32[]{:S(2)}) collective-permute-start(bf16[4,384,384]{2,1,0:T(8,128)(2,1)S(1)} %collective-permute-done.1.refs_8_), channel_id=1, source_target_pairs={{0,1},{1,0},{2,3},{3,2},{4,5},{5,4},{6,7},{7,6},{8,9},{9,8},{10,11... | collective-permute-start | bytes 3538952 | tf_op jit(solution)/shard_map/ppermute | solution.py:301
  55.7 6.1 %copy-start.1 = (f32[1,3,1536]{2,0,1:T(1,128)S(1)}, f32[1,3,1536]{2,0,1:T(1,128)}, u32[]{:S(2)}) copy-start(f32[1,3,1536]{2,0,1:T(1,128)} %param.6) | copy-start | bytes 55300
  59.9 7.2 %collective-permute-start.17 = (bf16[128,768]{1,0:T(8,128)(2,1)S(1)}, bf16[128,768]{1,0:T(8,128)(2,1)S(1)}, u32[]{:S(2)}, u32[]{:S(2)}) collective-permute-start(bf16[128,768]{1,0:T(8,128)(2,1)S(1)} %get-tuple-element.43), channel_id=1, source_target_pairs={{0,2},{1,3},{2,0},{3,1},{4,6},{5,7},{6,4},{7,5},{8,10},{9,11},{10,... | collective-permute-start | bytes 589832 | tf_op jit(solution)/shard_map/ppermute | solution.py:301
  61.8 7.7 %collective-permute-start.15 = (bf16[128,768]{1,0:T(8,128)(2,1)S(1)}, bf16[128,768]{1,0:T(8,128)(2,1)S(1)}, u32[]{:S(2)}, u32[]{:S(2)}) collective-permute-start(bf16[128,768]{1,0:T(8,128)(2,1)S(1)} %get-tuple-element.41), channel_id=1, source_target_pairs={{0,16},{16,0},{1,17},{17,1},{2,18},{18,2},{3,19},{19,3},{4,20},{20... | collective-permute-start | bytes 589832 | tf_op jit(solution)/shard_map/ppermute | solution.py:301
  64.8 8.9 %collective-permute-start.14 = (bf16[128,768]{1,0:T(8,128)(2,1)S(1)}, bf16[128,768]{1,0:T(8,128)(2,1)S(1)}, u32[]{:S(2)}, u32[]{:S(2)}) collective-permute-start(bf16[128,768]{1,0:T(8,128)(2,1)S(1)} %get-tuple-element.39), channel_id=1, source_target_pairs={{0,16},{16,0},{1,17},{17,1},{2,18},{18,2},{3,19},{19,3},{4,20},{20... | collective-permute-start | bytes 589832 | tf_op jit(solution)/shard_map/ppermute | solution.py:301
  66.9 7.8 %collective-permute-start.19 = (bf16[128,768]{1,0:T(8,128)(2,1)S(1)}, bf16[128,768]{1,0:T(8,128)(2,1)S(1)}, u32[]{:S(2)}, u32[]{:S(2)}) collective-permute-start(bf16[128,768]{1,0:T(8,128)(2,1)S(1)} %get-tuple-element.44), channel_id=1, source_target_pairs={{0,2},{1,3},{2,0},{3,1},{4,6},{5,7},{6,4},{7,5},{8,10},{9,11},{10,... | collective-permute-start | bytes 589832 | tf_op jit(solution)/shard_map/ppermute | solution.py:301
  67.2 9.7 %collective-permute-start.18 = (bf16[128,768]{1,0:T(8,128)(2,1)S(1)}, bf16[128,768]{1,0:T(8,128)(2,1)S(1)}, u32[]{:S(2)}, u32[]{:S(2)}) collective-permute-start(bf16[128,768]{1,0:T(8,128)(2,1)S(1)} %add_convert_fusion.1), channel_id=1, source_target_pairs={{0,16},{16,0},{1,17},{17,1},{2,18},{18,2},{3,19},{19,3},{4,20},{20... | collective-permute-start | bytes 589832 | tf_op jit(solution)/shard_map/ppermute | solution.py:301
  69.5 7.7 %collective-permute-start.16 = (bf16[128,768]{1,0:T(8,128)(2,1)S(1)}, bf16[128,768]{1,0:T(8,128)(2,1)S(1)}, u32[]{:S(2)}, u32[]{:S(2)}) collective-permute-start(bf16[128,768]{1,0:T(8,128)(2,1)S(1)} %add_convert_fusion.3), channel_id=1, source_target_pairs={{0,2},{1,3},{2,0},{3,1},{4,6},{5,7},{6,4},{7,5},{8,10},{9,11},{10,... | collective-permute-start | bytes 589832 | tf_op jit(solution)/shard_map/ppermute | solution.py:301

commit v7 on v6

--- a/solution.py
+++ b/solution.py
@@ -103,7 +103,7 @@
     return (hidden_states.astype(jnp.float32) + gate * out_proj).astype(jnp.bfloat16)
 
 
-SHIFTS = ((0, 0, 0), (1, 1, 0), (0, 1, 0), (1, 0, 0), (0, 0, 1), (1, 1, 1), (0, 1, 1), (1, 0, 1))
+SHIFTS = ((1, 1, 0), (0, 0, 0), (0, 1, 0), (1, 0, 0), (1, 1, 1), (0, 0, 1), (0, 1, 1), (1, 0, 1))
 VMEM_LIMIT = 18 * 1024 * 1024
 
 
@@ -160,9 +160,11 @@
 
 
 def early_kernel(spot_ref, own_rows_ref, other_rows_ref, *refs):
-    here, sent = refs[0:3], refs[3:6]
-    own_ref, other_ref, out_weight_ref, weight_ref, weight_sem, out_sem = refs[6:]
+    here, sent, states_ref = refs[0:3], refs[3:6], refs[6]
+    own_ref, other_ref, out_weight_ref, kept_ref, weight_ref, weight_sem, out_sem = refs[7:]
     depth = here[0].shape[1]
+    keep = pltpu.make_async_copy(states_ref, kept_ref, out_sem.at[3])
+    keep.start()
     for d in range(3):
         start_shard(spot_ref, here[d], sent[d], d * depth, weight_ref, weight_sem.at[d])
     for d in range(3):
@@ -185,6 +187,7 @@
         )
     for d in range(3):
         pltpu.make_async_copy(here[d].at[3], out_weight_ref.at[d], out_sem.at[d]).wait()
+    keep.wait()
 
 
 def key_bias(spot_ref, len_ref, tile_len):
@@ -216,70 +219,80 @@
     part = jnp.dot(
         jnp.concatenate(heads, axis=1), out_weight_ref[...], preferred_element_type=jnp.float32
     )
-    return part[: part.shape[0] // 2], part[part.shape[0] // 2 :]
+    return part
 
 
 def attend_kernel(spot_ref, len_ref, *refs):
     totals, rows_refs, out_here, out_sent, (here, sent) = refs[0:2], refs[2:4], refs[4], refs[5:8], refs[8:10]
-    own_ref, left_ref, right_ref, query_ref, key_ref, value_ref, out_weight_ref = refs[10:17]
-    weight_ref, weight_sem, out_sem = refs[17:]
+    left_ref, right_ref, bias_ref, query_ref, key_ref, value_ref, out_weight_ref = refs[10:17]
+    out_sem = refs[17]
     count, width = key_ref.shape
-    depth = weight_ref.shape[0]
+    depth = here.shape[1]
     z = spot_ref[2]
-    start_shard(spot_ref, here, sent, 0, weight_ref, weight_sem)
     places = [
         out_weight_ref.at[:, pl.ds(pl.multiple_of((z ^ d) * width, HD), width)] for d in range(4)
     ]
     for d in range(3):
         start_by_role(spot_ref, out_here.at[d], out_sent[d].at[0], places[d], out_sem.at[d])
     start_by_role(spot_ref, here.at[3], sent.at[3], places[3], out_sem.at[3])
-    bias = key_bias(spot_ref, len_ref, count // 8)
+    bias_ref[...] = key_bias(spot_ref, len_ref, count // 8)
     for h in range(width // HD):
         value_ref[h, :, HD:] = jnp.ones((count, HD), jnp.bfloat16)
-    wait_shard(here, 0, weight_ref, weight_sem)
     step = count // 4
-    queries = None
-    for r in range(4):
-        span = pl.ds((r % 2) * step, step)
-        rows = pl.ds(r * step, step)
-        skip = 0 if r < 2 else width
-        mixed = (
-            totals[r // 2][span, :]
-            + jnp.dot(
-                rows_refs[r // 2][span, 3 * depth :],
-                weight_ref[:, skip:],
-                preferred_element_type=jnp.float32,
-            )
-        ).astype(jnp.bfloat16)
-        if r == 0:
-            queries = mixed[:, :width]
-        elif r == 1:
-            query_ref[...] = mixed[:, :width]
-        key_ref[rows, :] = mixed[:, width - skip : 2 * width - skip]
-        for h in range(width // HD):
-            at = 2 * width - skip + h * HD
-            value_ref[h, rows, :HD] = mixed[:, at : at + HD]
+
+    def finish(shard):
+        weights = jnp.concatenate([shard[k] for k in range(3)], axis=1)
+        for r in range(4):
+            span = pl.ds((r % 2) * step, step)
+            rows = pl.ds(r * step, step)
+            skip = 0 if r < 2 else width
+            mixed = (
+                totals[r // 2][span, :]
+                + jnp.dot(
+                    rows_refs[r // 2][span, 3 * depth :],
+                    weights[:, skip:],
+                    preferred_element_type=jnp.float32,
+                )
+            ).astype(jnp.bfloat16)
+            if r < 2:
+                query_ref[rows, :] = mixed[:, :width]
+            key_ref[rows, :] = mixed[:, width - skip : 2 * width - skip]
+            for h in range(width // HD):
+                at = 2 * width - skip + h * HD
+                value_ref[h, rows, :HD] = mixed[:, at : at + HD]
+
+    owner = spot_ref[0] == spot_ref[3]
+    for role, shard in ((owner, here), (jnp.logical_not(owner), sent)):
+
+        @pl.when(role)
+        def _():
+            finish(shard)
+
     for d in range(4):
         source = out_here.at[d] if d < 3 else here.at[3]
         pltpu.make_async_copy(source, places[d], out_sem.at[d]).wait()
-    own, diagonal = project(queries, key_ref, value_ref, out_weight_ref, bias)
-    own_ref[...] = own
+    diagonal = project(query_ref[: step // 2, :], key_ref, value_ref, out_weight_ref, bias_ref[...])
     middle = left_ref.shape[1]
     left_ref[...] = diagonal[:, :middle].astype(jnp.bfloat16)
     right_ref[...] = diagonal[:, middle:].astype(jnp.bfloat16)
 
 
-def attend_rest_kernel(spot_ref, len_ref, states_ref, mod_ref, *refs):
-    part_ref, query_ref, key_ref, value_ref, out_weight_ref, base_ref = refs[:6]
+def attend_rest_kernel(states_ref, mod_ref, *refs):
+    bias_ref, query_ref, key_ref, value_ref, out_weight_ref, base_ref = refs[:6]
     y_left_ref, y_right_ref, x_left_ref, x_right_ref = refs[6:]
-    base_ref[...] = states_ref[...].astype(jnp.float32) + mod_ref[2] * part_ref[...]
-    bias = key_bias(spot_ref, len_ref, key_ref.shape[0] // 8)
-    along_y, along_x = project(query_ref[...], key_ref, value_ref, out_weight_ref, bias)
-    middle = y_left_ref.shape[1]
-    y_left_ref[...] = along_y[:, :middle]
-    y_right_ref[...] = along_y[:, middle:].astype(jnp.bfloat16)
-    x_left_ref[...] = along_x[:, :middle].astype(jnp.bfloat16)
-    x_right_ref[...] = along_x[:, middle:]
+    tile_len, middle = y_left_ref.shape
+    held = (key_ref, value_ref, out_weight_ref, bias_ref[...])
+    part = project(query_ref[2 * tile_len :, :], *held)
+    y_left_ref[...] = part[:tile_len, :middle]
+    y_right_ref[...] = part[:tile_len, middle:].astype(jnp.bfloat16)
+    x_left_ref[...] = part[tile_len:, :middle].astype(jnp.bfloat16)
+    x_right_ref[...] = part[tile_len:, middle:]
+    own = project(query_ref[tile_len : 2 * tile_len, :], *held)
+    base_ref[...] = states_ref[...].astype(jnp.float32) + mod_ref[2] * own
+
+
+def backwards(kernel, count):
+    return lambda *refs: kernel(*refs[:count][::-1], *refs[count:])
 
 
 def tiled_body(hidden_states, modulation, w_qkv, w_out, lengths):
@@ -329,68 +342,65 @@
     along_y = swap(states, "wcol", 2, 4)
     diagonal = [(a * 4 + c, (a ^ 1) * 4 + (c ^ 2)) for a in range(2) for c in range(4)]
     along_xy = lax.ppermute(states, ("patch", "wcol"), diagonal)
-    tiles = [states, along_xy, along_y, along_x]
+    tiles = [along_xy, states, along_y, along_x]
     own_rows = pl.pallas_call(
-        norm_kernel,
+        backwards(norm_kernel, 6),
         out_shape=jax.ShapeDtypeStruct((count // 2, width), jnp.bfloat16),
-        in_specs=[scalar] + [full] * 5,
+        in_specs=[full] * 5 + [scalar],
         out_specs=full,
         scratch_shapes=[pltpu.VMEM((tile_len, width), jnp.bfloat16)],
         compiler_params=params,
         name="norm",
-    )(spot, mod, *tiles)
+    )(*tiles[::-1], mod, spot)
     other_rows = core_swap(own_rows)
 
     last = owners_swap(far, 1)
     shards = [four, near, far]
-    total_own, total_other, out_known = pl.pallas_call(
-        early_kernel,
+    total_own, total_other, out_known, states_kept = pl.pallas_call(
+        backwards(early_kernel, 10),
         out_shape=(
             jax.ShapeDtypeStruct((count // 2, 3 * local_cols), jnp.float32),
             jax.ShapeDtypeStruct((count // 2, 2 * local_cols), jnp.float32),
             jax.ShapeDtypeStruct((3,) + w_out.shape, jnp.bfloat16),
+            jax.ShapeDtypeStruct((tile_len, width), jnp.bfloat16),
         ),
-        in_specs=[scalar] + [full] * 2 + [anywhere] * 6,
-        out_specs=(full,) * 3,
+        in_specs=[anywhere] * 7 + [full] * 2 + [scalar],
+        out_specs=(full,) * 4,
         scratch_shapes=[
             pltpu.VMEM((3 * depth, 3 * local_cols), jnp.bfloat16),
             pltpu.SemaphoreType.DMA((3, 3)),
-            pltpu.SemaphoreType.DMA((3,)),
+            pltpu.SemaphoreType.DMA((4,)),
         ],
         compiler_params=params,
         name="early",
-    )(spot, own_rows, other_rows, *shards, *(core_swap(shard[:3]) for shard in shards))
+    )(states, *(core_swap(shard[:3]) for shard in shards[::-1]), *shards[::-1], other_rows, own_rows, spot)
     out_sent = [core_swap(shard[3:]) for shard in shards]
     last, total_own, *out_sent = lax.optimization_barrier((last, total_own, *out_sent))
     last_sent = core_swap(last)
 
     half = jax.ShapeDtypeStruct((tile_len, width // 2), jnp.bfloat16)
     half_f32 = jax.ShapeDtypeStruct((tile_len, width // 2), jnp.float32)
-    part_own, xy_left, xy_right, *kept = pl.pallas_call(
-        attend_kernel,
+    xy_left, xy_right, *kept = pl.pallas_call(
+        backwards(attend_kernel, 12),
         out_shape=(
-            jax.ShapeDtypeStruct((tile_len, width), jnp.float32),
             half,
             half,
-            jax.ShapeDtypeStruct((count // 4, local_cols), jnp.bfloat16),
+            jax.ShapeDtypeStruct((1, count), jnp.float32),
+            jax.ShapeDtypeStruct((count // 2, local_cols), jnp.bfloat16),
             jax.ShapeDtypeStruct((count, local_cols), jnp.bfloat16),
             jax.ShapeDtypeStruct((local_cols // HD, count, 2 * HD), jnp.bfloat16),
             jax.ShapeDtypeStruct((local_cols, width), jnp.bfloat16),
         ),
-        in_specs=[scalar, scalar] + [full] * 4 + [anywhere] * 6,
+        in_specs=[full] * 2 + [anywhere] * 4 + [full] * 4 + [scalar, scalar],
         out_specs=(full,) * 7,
-        scratch_shapes=[
-            pltpu.VMEM((depth, 3 * local_cols), jnp.bfloat16),
-            pltpu.SemaphoreType.DMA((3,)),
-            pltpu.SemaphoreType.DMA((4,)),
-        ],
+        scratch_shapes=[pltpu.SemaphoreType.DMA((4,))],
         compiler_params=params,
         name="attend",
-    )(spot, lengths, total_own, total_other, own_rows, other_rows, out_known, *out_sent, last, last_sent)
+    )(last_sent, last, *out_sent[::-1], out_known, other_rows, own_rows, total_other, total_own, lengths, spot)
     from_x = swap(xy_left, "patch", 1, 2)
     from_y = swap(xy_right, "wcol", 2, 4)
     base, y_left, y_right, x_left, x_right = pl.pallas_call(
-        attend_rest_kernel,
+        backwards(attend_rest_kernel, 7),
         out_shape=(
             jax.ShapeDtypeStruct((tile_len, width), jnp.float32),
             half_f32,
@@ -398,11 +408,11 @@
             half,
             half_f32,
         ),
-        in_specs=[scalar, scalar] + [full] * 7,
+        in_specs=[full] * 7,
         out_specs=(full,) * 5,
         compiler_params=params,
         name="attend_rest",
-    )(spot, lengths, states, mod, part_own, *kept)
+    )(*kept[::-1], mod, states_kept)
     got_x_left = swap(x_left, "patch", 1, 2)
     got_y_right = swap(y_right, "wcol", 2, 4)
     y_left = (y_left + from_x.astype(jnp.float32)).astype(jnp.bfloat16)

time: 78.6 us -> 77.9 us (level)
    ppermute x16, waiting for transfers between devices: 19.6 us -> 26.5 us  [swap(): return lax.ppermute(array, axis, [(i, i ^ d) for i in range(n)])]
    ppermute x1, waiting for transfers between devices: 6.24 us -> 0.01 us  [tiled_body(): along_xy = lax.ppermute(states, ('patch', 'wcol'), diagonal)]
    ppermute x16, starting transfers between devices: 9.92 us -> 8.06 us  [swap(): return lax.ppermute(array, axis, [(i, i ^ d) for i in range(n)])]
    ppermute x1, starting transfers between devices: 0.07 us -> 1.89 us  [tiled_body(): along_xy = lax.ppermute(states, ('patch', 'wcol'), diagonal)]
where the time goes in v7:
time: 77.9 us; the launch traced here: 77.6 us
  waiting for transfers between devices  37.7 us (48%)
  starting transfers between devices  22.2 us (28%)
  Pallas kernels  13.3 us (17%)
  other arithmetic  2.49 us (3%)
  local copies, waits for them, and re-layouts  1 us (1%)
  between operations  0.87 us (1%)
    ppermute x16, waiting for transfers between devices, swap(): return lax.ppermute(array, axis, [(i, i ^ d) for i in range(n)])  26.5 us
    ppermute x3, starting transfers between devices, owners_swap(): return lax.ppermute(array, everywhere, pairs)  12.3 us
    ppermute x3, waiting for transfers between devices, owners_swap(): return lax.ppermute(array, everywhere, pairs)  11.2 us
    ppermute x16, starting transfers between devices, swap(): return lax.ppermute(array, axis, [(i, i ^ d) for i in range(n)])  8.06 us
    pallas_call x1, Pallas kernels, tiled_body(): pl.pallas_call(backwards(early_kernel, 10), out_shape=(jax.ShapeDtypeStru...  4.01 us
    pallas_call x1, Pallas kernels, tiled_body(): pl.pallas_call(backwards(attend_kernel, 12), out_shape=(half, half, jax.S...  3.57 us
    pallas_call x1, Pallas kernels, tiled_body(): pl.pallas_call(backwards(attend_rest_kernel, 7), out_shape=(jax.ShapeDtyp...  3.05 us
    pallas_call x1, Pallas kernels, tiled_body(): pl.pallas_call(backwards(norm_kernel, 6), out_shape=jax.ShapeDtypeStruct(...  2.71 us
  transfers between devices with their start and end apart: 20, of which 12 were waited for; matrix products, arithmetic and copies ran while one was open for 1% of the time, Pallas kernels for 13%

profile of v7, /device:TPU:0, one launch (start us, length us, event | category | flops | bytes accessed | tf_op | source)
XLA Modules:
  0.0 77.6 jit_solution(12718579478624914852)
XLA Ops:
  0.0 1.4 %pad_maximum_fusion.refs_6_ = bf16[4,384,384]{2,1,0:T(8,128)(2,1)S(1)} fusion(bf16[1,384,384]{2,1,0:T(8,128)(2,1)} %bitcast.15, bf16[3,384,384]{2,1,0:T(8,128)(2,1)} %bitcast.13), kind=kLoop, calls=%fused_computation | loop fusion | flops 589824 | bytes 2359296 | tf_op jit(solution)/shard_map/concatenate | solution.py:338
  1.4 5.9 %collective-permute-start = (bf16[4,384,384]{2,1,0:T(8,128)(2,1)S(1)}, bf16[4,384,384]{2,1,0:T(8,128)(2,1)S(1)}, u32[]{:S(2)}, u32[]{:S(2)}) collective-permute-start(bf16[4,384,384]{2,1,0:T(8,128)(2,1)S(1)} %pad_maximum_fusion.refs_6_), channel_id=1, source_target_pairs={{0,8},{2,10},{4,12},{6,14},{8,0},{10,2},{12,4},{14,6},{17,25},{19,... | collective-permute-start | bytes 3538952 | tf_op jit(solution)/shard_map/ppermute | solution.py:324
  7.4 1.6 %collective-permute-start.7 = (bf16[128,1536]{1,0:T(8,128)(2,1)}, bf16[128,1536]{1,0:T(8,128)(2,1)}, u32[]{:S(2)}, u32[]{:S(2)}) collective-permute-start(bf16[128,1536]{1,0:T(8,128)(2,1)} %bitcast.2.refs_2_.refs_0_), channel_id=1, source_target_pairs={{0,2},{1,3},{2,0},{3,1},{4,6},{5,7},{6,4},{7,5},{8,10},{9,11},{10,... | collective-permute-start | bytes 1179656 | tf_op jit(solution)/shard_map/ppermute | solution.py:314
  9.0 1.9 %collective-permute-start.8 = (bf16[128,1536]{1,0:T(8,128)(2,1)}, bf16[128,1536]{1,0:T(8,128)(2,1)}, u32[]{:S(2)}, u32[]{:S(2)}) collective-permute-start(bf16[128,1536]{1,0:T(8,128)(2,1)} %bitcast.2.refs_2_.refs_0_), channel_id=1, source_target_pairs={{0,18},{1,19},{2,16},{3,17},{16,2},{17,3},{18,0},{19,1},{4,22},{5,... | collective-permute-start | bytes 1179656 | tf_op jit(solution)/shard_map/ppermute | solution.py:344
  10.9 3.5 %collective-permute-start.3 = (bf16[4,384,384]{2,1,0:T(8,128)(2,1)S(1)}, bf16[4,384,384]{2,1,0:T(8,128)(2,1)S(1)}, u32[]{:S(2)}, u32[]{:S(2)}) collective-permute-start(bf16[4,384,384]{2,1,0:T(8,128)(2,1)S(1)} %pad_maximum_fusion.refs_6_), channel_id=1, source_target_pairs={{0,4},{2,6},{4,0},{6,2},{8,12},{10,14},{12,8},{14,10},{17,21},{19,... | collective-permute-start | bytes 3538952 | tf_op jit(solution)/shard_map/ppermute | solution.py:324
  14.5 5.3 %collective-permute-done.6.refs_0_ = bf16[128,1536]{1,0:T(8,128)(2,1)} collective-permute-done((bf16[128,1536]{1,0:T(8,128)(2,1)}, bf16[128,1536]{1,0:T(8,128)(2,1)}, u32[]{:S(2)}, u32[]{:S(2)}) %collective-permute-start.6) | collective-permute-done | bytes 393248 | tf_op jit(solution)/shard_map/ppermute | solution.py:314
  19.8 8.2 %collective-permute-done.7.refs_1_ = bf16[128,1536]{1,0:T(8,128)(2,1)} collective-permute-done((bf16[128,1536]{1,0:T(8,128)(2,1)}, bf16[128,1536]{1,0:T(8,128)(2,1)}, u32[]{:S(2)}, u32[]{:S(2)}) %collective-permute-start.7) | collective-permute-done | bytes 393248 | tf_op jit(solution)/shard_map/ppermute | solution.py:314
  28.7 2.7 %norm.1.refs_8_.refs_7_ = bf16[512,1536]{1,0:T(8,128)(2,1)S(1)} custom-call(bf16[128,1536]{1,0:T(8,128)(2,1)} %collective-permute-done.6.refs_0_, bf16[128,1536]{1,0:T(8,128)(2,1)} %collective-permute-done.7.refs_1_, bf16[128,1536]{1,0:T(8,128)(2,1)} %bitcast.2.refs_2_.refs_0_, bf16[128,1536]{1,0:T(8,128)(2,1)} %collective-permute-done.8.refs_3_, ...), custom_call_target="tpu_custom_call" | custom-call | tf_op jit(solution)/shard_map/norm/pallas_call | solution.py:346
  32.0 2.3 %collective-permute-done.refs_4_ = bf16[4,384,384]{2,1,0:T(8,128)(2,1)S(1)} collective-permute-done((bf16[4,384,384]{2,1,0:T(8,128)(2,1)S(1)}, bf16[4,384,384]{2,1,0:T(8,128)(2,1)S(1)}, u32[]{:S(2)}, u32[]{:S(2)}) %collective-permute-start) | collective-permute-done | bytes 1179680 | tf_op jit(solution)/shard_map/ppermute | solution.py:324
  34.4 2.8 %collective-permute-start.1 = (bf16[4,384,384]{2,1,0:T(8,128)(2,1)S(1)}, bf16[4,384,384]{2,1,0:T(8,128)(2,1)S(1)}, u32[]{:S(2)}, u32[]{:S(2)}) collective-permute-start(bf16[4,384,384]{2,1,0:T(8,128)(2,1)S(1)} %collective-permute-done.refs_4_), channel_id=1, source_target_pairs={{0,4},{2,6},{4,0},{6,2},{8,12},{10,14},{12,8},{14,10},{17,21},{19,... | collective-permute-start | bytes 3538952 | tf_op jit(solution)/shard_map/ppermute | solution.py:324
  37.3 2.9 %collective-permute-done.3.refs_5_ = bf16[4,384,384]{2,1,0:T(8,128)(2,1)S(1)} collective-permute-done((bf16[4,384,384]{2,1,0:T(8,128)(2,1)S(1)}, bf16[4,384,384]{2,1,0:T(8,128)(2,1)S(1)}, u32[]{:S(2)}, u32[]{:S(2)}) %collective-permute-start.3) | collective-permute-done | bytes 1179680 | tf_op jit(solution)/shard_map/ppermute | solution.py:324
  41.5 1.2 %collective-permute-done.4.refs_2_ = bf16[3,384,384]{2,1,0:T(8,128)(2,1)S(1)} collective-permute-done((bf16[3,384,384]{2,1,0:T(8,128)(2,1)S(1)}, bf16[3,384,384]{2,1,0:T(8,128)(2,1)S(1)}, u32[]{:S(2)}, u32[]{:S(2)}) %collective-permute-start.4) | collective-permute-done | bytes 884768 | tf_op jit(solution)/shard_map/ppermute | solution.py:314
  42.8 4.0 %early.1 = (f32[512,1152]{1,0:T(8,128)S(1)}, f32[512,768]{1,0:T(8,128)S(1)}, bf16[3,384,384]{2,1,0:T(8,128)(2,1)S(1)}, bf16[128,1536]{1,0:T(8,128)(2,1)S(1)}) custom-call(bf16[128,1536]{1,0:T(8,128)(2,1)} %bitcast.2.refs_2_.refs_0_, bf16[3,384,384]{2,1,0:T(8,128)(2,1)S(1)} %collective-permute-done.2.refs_1_, ...), custom_call_target="tpu_custom_call" | custom-call | tf_op jit(solution)/shard_map/early/pallas_call | solution.py:359
  46.8 6.0 %collective-permute-done.1.refs_1_ = bf16[4,384,384]{2,1,0:T(8,128)(2,1)S(1)} collective-permute-done((bf16[4,384,384]{2,1,0:T(8,128)(2,1)S(1)}, bf16[4,384,384]{2,1,0:T(8,128)(2,1)S(1)}, u32[]{:S(2)}, u32[]{:S(2)}) %collective-permute-start.1) | collective-permute-done | bytes 1179680 | tf_op jit(solution)/shard_map/ppermute | solution.py:324
  53.5 2.2 %collective-permute-done.13.refs_0_ = bf16[4,384,384]{2,1,0:T(8,128)(2,1)S(1)} collective-permute-done((bf16[4,384,384]{2,1,0:T(8,128)(2,1)S(1)}, bf16[4,384,384]{2,1,0:T(8,128)(2,1)S(1)}, u32[]{:S(2)}, u32[]{:S(2)}) %collective-permute-start.13) | collective-permute-done | bytes 1179680 | tf_op jit(solution)/shard_map/ppermute | solution.py:314
  55.7 3.6 %attend.1 = (bf16[128,768]{1,0:T(8,128)(2,1)S(1)}, bf16[128,768]{1,0:T(8,128)(2,1)S(1)}, f32[1,1024]{1,0:T(1,128)S(1)}, bf16[512,384]{1,0:T(8,128)(2,1)S(1)}, bf...) custom-call(bf16[4,384,384]{2,1,0:T(8,128)(2,1)S(1)} %collective-permute-done.13.refs_0, ...), custom_call_target="tpu_custom_call" | custom-call | tf_op jit(solution)/shard_map/attend/pallas_call | solution.py:383
  59.3 1.9 %collective-permute-start.17 = (bf16[128,768]{1,0:T(8,128)(2,1)S(1)}, bf16[128,768]{1,0:T(8,128)(2,1)S(1)}, u32[]{:S(2)}, u32[]{:S(2)}) collective-permute-start(bf16[128,768]{1,0:T(8,128)(2,1)S(1)} %get-tuple-element.45), channel_id=1, source_target_pairs={{0,2},{1,3},{2,0},{3,1},{4,6},{5,7},{6,4},{7,5},{8,10},{9,11},{10,... | collective-permute-start | bytes 589832 | tf_op jit(solution)/shard_map/ppermute | solution.py:314
  61.2 3.0 %attend_rest.1 = (f32[128,1536]{1,0:T(8,128)S(1)}, f32[128,768]{1,0:T(8,128)S(1)}, bf16[128,768]{1,0:T(8,128)(2,1)S(1)}, bf16[128,768]{1,0:T(8,128)(2,1)S(1)}, f32[128,768]{1,0:T(8,128)S(1)}) custom-call(bf16[384,1536]{1,0:T(8,128)(2,1)S(1)} %get-tuple-element.34.refs_0_, bf16[3,1024,256]{2,1,0:T(8,128)(2,1)S(1)} %get-tuple-element.35.refs_1_, ...), custom_call_target="tpu_custom_call" | custom-call | tf_op jit(solution)/shard_map/attend_rest/pallas_call | solution.py:402
  64.2 2.1 %collective-permute-start.14 = (bf16[128,768]{1,0:T(8,128)(2,1)S(1)}, bf16[128,768]{1,0:T(8,128)(2,1)S(1)}, u32[]{:S(2)}, u32[]{:S(2)}) collective-permute-start(bf16[128,768]{1,0:T(8,128)(2,1)S(1)} %get-tuple-element.41), channel_id=1, source_target_pairs={{0,16},{16,0},{1,17},{17,1},{2,18},{18,2},{3,19},{19,3},{4,20},{20... | collective-permute-start | bytes 589832 | tf_op jit(solution)/shard_map/ppermute | solution.py:314
  66.7 2.2 %collective-permute-done.15 = bf16[128,768]{1,0:T(8,128)(2,1)S(1)} collective-permute-done((bf16[128,768]{1,0:T(8,128)(2,1)S(1)}, bf16[128,768]{1,0:T(8,128)(2,1)S(1)}, u32[]{:S(2)}, u32[]{:S(2)}) %collective-permute-start.15) | collective-permute-done | bytes 196640 | tf_op jit(solution)/shard_map/ppermute | solution.py:314
  69.3 3.8 %collective-permute-done.14 = bf16[128,768]{1,0:T(8,128)(2,1)S(1)} collective-permute-done((bf16[128,768]{1,0:T(8,128)(2,1)S(1)}, bf16[128,768]{1,0:T(8,128)(2,1)S(1)}, u32[]{:S(2)}, u32[]{:S(2)}) %collective-permute-start.14) | collective-permute-done | bytes 196640 | tf_op jit(solution)/shard_map/ppermute | solution.py:314
  73.1 1.1 %collective-permute-done.19 = bf16[128,768]{1,0:T(8,128)(2,1)S(1)} collective-permute-done((bf16[128,768]{1,0:T(8,128)(2,1)S(1)}, bf16[128,768]{1,0:T(8,128)(2,1)S(1)}, u32[]{:S(2)}, u32[]{:S(2)}) %collective-permute-start.19) | collective-permute-done | bytes 196640 | tf_op jit(solution)/shard_map/ppermute | solution.py:314
  74.2 2.1 %collective-permute-done.18 = bf16[128,768]{1,0:T(8,128)(2,1)S(1)} collective-permute-done((bf16[128,768]{1,0:T(8,128)(2,1)S(1)}, bf16[128,768]{1,0:T(8,128)(2,1)S(1)}, u32[]{:S(2)}, u32[]{:S(2)}) %collective-permute-start.18) | collective-permute-done | bytes 196640 | tf_op jit(solution)/shard_map/ppermute | solution.py:314
  76.8 0.8 maximum_bitcast_fusion
  (39 shorter events, 4.2 us)
Async XLA Ops:
  1.4 32.9 %collective-permute-start = (bf16[4,384,384]{2,1,0:T(8,128)(2,1)S(1)}, bf16[4,384,384]{2,1,0:T(8,128)(2,1)S(1)}, u32[]{:S(2)}, u32[]{:S(2)}) collective-permute-start(bf16[4,384,384]{2,1,0:T(8,128)(2,1)S(1)} %pad_maximum_fusion.refs_6_), channel_id=1, source_target_pairs={{0,8},{2,10},{4,12},{6,14},{8,0},{10,2},{12,4},{14,6},{17,25},{19,... | collective-permute-start | bytes 3538952 | tf_op jit(solution)/shard_map/ppermute | solution.py:324
  7.4 12.4 %collective-permute-start.6 = (bf16[128,1536]{1,0:T(8,128)(2,1)}, bf16[128,1536]{1,0:T(8,128)(2,1)}, u32[]{:S(2)}, u32[]{:S(2)}) collective-permute-start(bf16[128,1536]{1,0:T(8,128)(2,1)} %bitcast.2.refs_2_.refs_0_), channel_id=1, source_target_pairs={{0,16},{16,0},{1,17},{17,1},{2,18},{18,2},{3,19},{19,3},{4,20},{20... | collective-permute-start | bytes 1179656 | tf_op jit(solution)/shard_map/ppermute | solution.py:314
  7.4 20.5 %collective-permute-start.7 = (bf16[128,1536]{1,0:T(8,128)(2,1)}, bf16[128,1536]{1,0:T(8,128)(2,1)}, u32[]{:S(2)}, u32[]{:S(2)}) collective-permute-start(bf16[128,1536]{1,0:T(8,128)(2,1)} %bitcast.2.refs_2_.refs_0_), channel_id=1, source_target_pairs={{0,2},{1,3},{2,0},{3,1},{4,6},{5,7},{6,4},{7,5},{8,10},{9,11},{10,... | collective-permute-start | bytes 1179656 | tf_op jit(solution)/shard_map/ppermute | solution.py:314
  9.0 18.9 %collective-permute-start.8 = (bf16[128,1536]{1,0:T(8,128)(2,1)}, bf16[128,1536]{1,0:T(8,128)(2,1)}, u32[]{:S(2)}, u32[]{:S(2)}) collective-permute-start(bf16[128,1536]{1,0:T(8,128)(2,1)} %bitcast.2.refs_2_.refs_0_), channel_id=1, source_target_pairs={{0,18},{1,19},{2,16},{3,17},{16,2},{17,3},{18,0},{19,1},{4,22},{5,... | collective-permute-start | bytes 1179656 | tf_op jit(solution)/shard_map/ppermute | solution.py:344
  10.9 29.3 %collective-permute-start.3 = (bf16[4,384,384]{2,1,0:T(8,128)(2,1)S(1)}, bf16[4,384,384]{2,1,0:T(8,128)(2,1)S(1)}, u32[]{:S(2)}, u32[]{:S(2)}) collective-permute-start(bf16[4,384,384]{2,1,0:T(8,128)(2,1)S(1)} %pad_maximum_fusion.refs_6_), channel_id=1, source_target_pairs={{0,4},{2,6},{4,0},{6,2},{8,12},{10,14},{12,8},{14,10},{17,21},{19,... | collective-permute-start | bytes 3538952 | tf_op jit(solution)/shard_map/ppermute | solution.py:324
  27.9 0.7 copy-start
  28.7 2.8 %copy-start.2 = (bf16[384,3,384]{2,0,1:T(8,128)(2,1)S(1)}, bf16[384,3,384]{2,0,1:T(8,128)(2,1)}, u32[]{:S(2)}) copy-start(bf16[384,3,384]{2,0,1:T(8,128)(2,1)} %param.7) | copy-start | bytes 2654212
  31.4 9.6 %collective-permute-start.9 = (bf16[512,1536]{1,0:T(8,128)(2,1)S(1)}, bf16[512,1536]{1,0:T(8,128)(2,1)S(1)}, u32[]{:S(2)}, u32[]{:S(2)}) collective-permute-start(bf16[512,1536]{1,0:T(8,128)(2,1)S(1)} %norm.1.refs_8_.refs_7_), channel_id=1, source_target_pairs={{0,1},{1,0},{2,3},{3,2},{4,5},{5,4},{6,7},{7,6},{8,9},{9,8},{10,11... | collective-permute-start | bytes 4718600 | tf_op jit(solution)/shard_map/ppermute | solution.py:314
  31.5 9.0 %collective-permute-start.5 = (bf16[3,384,384]{2,1,0:T(8,128)(2,1)S(1)}, bf16[3,384,384]{2,1,0:T(8,128)(2,1)S(1)}, u32[]{:S(2)}, u32[]{:S(2)}) collective-permute-start(bf16[3,384,384]{2,1,0:T(8,128)(2,1)S(1)} %bitcast.14), channel_id=1, source_target_pairs={{0,1},{1,0},{2,3},{3,2},{4,5},{5,4},{6,7},{7,6},{8,9},{9,8},{10,11... | collective-permute-start | bytes 2654216 | tf_op jit(solution)/shard_map/ppermute | solution.py:314
  34.4 6.1 %copy-start.3 = (bf16[384,384]{1,0:T(8,128)(2,1)S(1)}, bf16[384,384]{1,0:T(8,128)(2,1)}, u32[]{:S(2)}) copy-start(bf16[384,384]{1,0:T(8,128)(2,1)} %param.8) | copy-start | bytes 884740
  34.4 6.7 %collective-permute-start.2 = (bf16[3,384,384]{2,1,0:T(8,128)(2,1)S(1)}, bf16[3,384,384]{2,1,0:T(8,128)(2,1)S(1)}, u32[]{:S(2)}, u32[]{:S(2)}) collective-permute-start(bf16[3,384,384]{2,1,0:T(8,128)(2,1)S(1)} %slice.32), channel_id=1, source_target_pairs={{0,1},{1,0},{2,3},{3,2},{4,5},{5,4},{6,7},{7,6},{8,9},{9,8},{10,11... | collective-permute-start | bytes 2654216 | tf_op jit(solution)/shard_map/ppermute | solution.py:314
  34.4 18.4 %collective-permute-start.1 = (bf16[4,384,384]{2,1,0:T(8,128)(2,1)S(1)}, bf16[4,384,384]{2,1,0:T(8,128)(2,1)S(1)}, u32[]{:S(2)}, u32[]{:S(2)}) collective-permute-start(bf16[4,384,384]{2,1,0:T(8,128)(2,1)S(1)} %collective-permute-done.refs_4_), channel_id=1, source_target_pairs={{0,4},{2,6},{4,0},{6,2},{8,12},{10,14},{12,8},{14,10},{17,21},{19,... | collective-permute-start | bytes 3538952 | tf_op jit(solution)/shard_map/ppermute | solution.py:324
  40.3 2.5 %collective-permute-start.4 = (bf16[3,384,384]{2,1,0:T(8,128)(2,1)S(1)}, bf16[3,384,384]{2,1,0:T(8,128)(2,1)S(1)}, u32[]{:S(2)}, u32[]{:S(2)}) collective-permute-start(bf16[3,384,384]{2,1,0:T(8,128)(2,1)S(1)} %slice.33), channel_id=1, source_target_pairs={{0,1},{1,0},{2,3},{3,2},{4,5},{5,4},{6,7},{7,6},{8,9},{9,8},{10,11... | collective-permute-start | bytes 2654216 | tf_op jit(solution)/shard_map/ppermute | solution.py:314
  40.5 6.3 %collective-permute-start.10 = (bf16[1,384,384]{2,1,0:T(8,128)(2,1)S(1)}, bf16[1,384,384]{2,1,0:T(8,128)(2,1)S(1)}, u32[]{:S(2)}, u32[]{:S(2)}) collective-permute-start(bf16[1,384,384]{2,1,0:T(8,128)(2,1)S(1)} %bitcast.16), channel_id=1, source_target_pairs={{0,1},{1,0},{2,3},{3,2},{4,5},{5,4},{6,7},{7,6},{8,9},{9,8},{10,11... | collective-permute-start | bytes 884744 | tf_op jit(solution)/shard_map/ppermute | solution.py:314
  41.0 5.8 %collective-permute-start.12 = (bf16[1,384,384]{2,1,0:T(8,128)(2,1)S(1)}, bf16[1,384,384]{2,1,0:T(8,128)(2,1)S(1)}, u32[]{:S(2)}, u32[]{:S(2)}) collective-permute-start(bf16[1,384,384]{2,1,0:T(8,128)(2,1)S(1)} %slice.35), channel_id=1, source_target_pairs={{0,1},{1,0},{2,3},{3,2},{4,5},{5,4},{6,7},{7,6},{8,9},{9,8},{10,11... | collective-permute-start | bytes 884744 | tf_op jit(solution)/shard_map/ppermute | solution.py:314
  41.1 5.7 %collective-permute-start.11 = (bf16[1,384,384]{2,1,0:T(8,128)(2,1)S(1)}, bf16[1,384,384]{2,1,0:T(8,128)(2,1)S(1)}, u32[]{:S(2)}, u32[]{:S(2)}) collective-permute-start(bf16[1,384,384]{2,1,0:T(8,128)(2,1)S(1)} %slice.34), channel_id=1, source_target_pairs={{0,1},{1,0},{2,3},{3,2},{4,5},{5,4},{6,7},{7,6},{8,9},{9,8},{10,11... | collective-permute-start | bytes 884744 | tf_op jit(solution)/shard_map/ppermute | solution.py:314
  52.8 2.8 %collective-permute-start.13 = (bf16[4,384,384]{2,1,0:T(8,128)(2,1)S(1)}, bf16[4,384,384]{2,1,0:T(8,128)(2,1)S(1)}, u32[]{:S(2)}, u32[]{:S(2)}) collective-permute-start(bf16[4,384,384]{2,1,0:T(8,128)(2,1)S(1)} %collective-permute-done.1.refs_1_), channel_id=1, source_target_pairs={{0,1},{1,0},{2,3},{3,2},{4,5},{5,4},{6,7},{7,6},{8,9},{9,8},{10,11... | collective-permute-start | bytes 3538952 | tf_op jit(solution)/shard_map/ppermute | solution.py:314
  55.7 5.5 %copy-start.1 = (f32[1,3,1536]{2,0,1:T(1,128)S(1)}, f32[1,3,1536]{2,0,1:T(1,128)}, u32[]{:S(2)}) copy-start(f32[1,3,1536]{2,0,1:T(1,128)} %param.6) | copy-start | bytes 55300
  59.3 7.2 %collective-permute-start.17 = (bf16[128,768]{1,0:T(8,128)(2,1)S(1)}, bf16[128,768]{1,0:T(8,128)(2,1)S(1)}, u32[]{:S(2)}, u32[]{:S(2)}) collective-permute-start(bf16[128,768]{1,0:T(8,128)(2,1)S(1)} %get-tuple-element.45), channel_id=1, source_target_pairs={{0,2},{1,3},{2,0},{3,1},{4,6},{5,7},{6,4},{7,5},{8,10},{9,11},{10,... | collective-permute-start | bytes 589832 | tf_op jit(solution)/shard_map/ppermute | solution.py:314
  61.2 7.7 %collective-permute-start.15 = (bf16[128,768]{1,0:T(8,128)(2,1)S(1)}, bf16[128,768]{1,0:T(8,128)(2,1)S(1)}, u32[]{:S(2)}, u32[]{:S(2)}) collective-permute-start(bf16[128,768]{1,0:T(8,128)(2,1)S(1)} %get-tuple-element.43), channel_id=1, source_target_pairs={{0,16},{16,0},{1,17},{17,1},{2,18},{18,2},{3,19},{19,3},{4,20},{20... | collective-permute-start | bytes 589832 | tf_op jit(solution)/shard_map/ppermute | solution.py:314
  64.2 8.9 %collective-permute-start.14 = (bf16[128,768]{1,0:T(8,128)(2,1)S(1)}, bf16[128,768]{1,0:T(8,128)(2,1)S(1)}, u32[]{:S(2)}, u32[]{:S(2)}) collective-permute-start(bf16[128,768]{1,0:T(8,128)(2,1)S(1)} %get-tuple-element.41), channel_id=1, source_target_pairs={{0,16},{16,0},{1,17},{17,1},{2,18},{18,2},{3,19},{19,3},{4,20},{20... | collective-permute-start | bytes 589832 | tf_op jit(solution)/shard_map/ppermute | solution.py:314
  66.3 7.8 %collective-permute-start.19 = (bf16[128,768]{1,0:T(8,128)(2,1)S(1)}, bf16[128,768]{1,0:T(8,128)(2,1)S(1)}, u32[]{:S(2)}, u32[]{:S(2)}) collective-permute-start(bf16[128,768]{1,0:T(8,128)(2,1)S(1)} %get-tuple-element.46), channel_id=1, source_target_pairs={{0,2},{1,3},{2,0},{3,1},{4,6},{5,7},{6,4},{7,5},{8,10},{9,11},{10,... | collective-permute-start | bytes 589832 | tf_op jit(solution)/shard_map/ppermute | solution.py:314
  66.5 9.7 %collective-permute-start.18 = (bf16[128,768]{1,0:T(8,128)(2,1)S(1)}, bf16[128,768]{1,0:T(8,128)(2,1)S(1)}, u32[]{:S(2)}, u32[]{:S(2)}) collective-permute-start(bf16[128,768]{1,0:T(8,128)(2,1)S(1)} %add_convert_fusion.1), channel_id=1, source_target_pairs={{0,16},{16,0},{1,17},{17,1},{2,18},{18,2},{3,19},{19,3},{4,20},{20... | collective-permute-start | bytes 589832 | tf_op jit(solution)/shard_map/ppermute | solution.py:314
  68.9 7.7 %collective-permute-start.16 = (bf16[128,768]{1,0:T(8,128)(2,1)S(1)}, bf16[128,768]{1,0:T(8,128)(2,1)S(1)}, u32[]{:S(2)}, u32[]{:S(2)}) collective-permute-start(bf16[128,768]{1,0:T(8,128)(2,1)S(1)} %add_convert_fusion.3), channel_id=1, source_target_pairs={{0,2},{1,3},{2,0},{3,1},{4,6},{5,7},{6,4},{7,5},{8,10},{9,11},{10,... | collective-permute-start | bytes 589832 | tf_op jit(solution)/shard_map/ppermute | solution.py:314

commit v8 on v7

--- a/solution.py
+++ b/solution.py
@@ -277,22 +277,24 @@
     right_ref[...] = diagonal[:, middle:].astype(jnp.bfloat16)
 
 
-def attend_rest_kernel(states_ref, mod_ref, *refs):
-    bias_ref, query_ref, key_ref, value_ref, out_weight_ref, base_ref = refs[:6]
-    y_left_ref, y_right_ref, x_left_ref, x_right_ref = refs[6:]
+def attend_rest_kernel(bias_ref, query_ref, key_ref, value_ref, out_weight_ref, *out_refs):
+    y_left_ref, y_right_ref, x_left_ref, x_right_ref = out_refs
     tile_len, middle = y_left_ref.shape
-    held = (key_ref, value_ref, out_weight_ref, bias_ref[...])
-    part = project(query_ref[2 * tile_len :, :], *held)
+    queries = query_ref[2 * tile_len :, :]
+    part = project(queries, key_ref, value_ref, out_weight_ref, bias_ref[...])
     y_left_ref[...] = part[:tile_len, :middle]
     y_right_ref[...] = part[:tile_len, middle:].astype(jnp.bfloat16)
     x_left_ref[...] = part[tile_len:, :middle].astype(jnp.bfloat16)
     x_right_ref[...] = part[tile_len:, middle:]
-    own = project(query_ref[tile_len : 2 * tile_len, :], *held)
+
+
+def attend_own_kernel(
+    out_weight_ref, value_ref, key_ref, query_ref, bias_ref, mod_ref, states_ref, base_ref
+):
+    tile_len = base_ref.shape[0]
+    queries = query_ref[tile_len : 2 * tile_len, :]
+    own = project(queries, key_ref, value_ref, out_weight_ref, bias_ref[...])
     base_ref[...] = states_ref[...].astype(jnp.float32) + mod_ref[2] * own
-
-
-def backwards(kernel, count):
-    return lambda *refs: kernel(*refs[:count][::-1], *refs[count:])
 
 
 def tiled_body(hidden_states, modulation, w_qkv, w_out, lengths):
@@ -344,27 +346,27 @@
     along_xy = lax.ppermute(states, ("patch", "wcol"), diagonal)
     tiles = [along_xy, states, along_y, along_x]
     own_rows = pl.pallas_call(
-        backwards(norm_kernel, 6),
+        norm_kernel,
         out_shape=jax.ShapeDtypeStruct((count // 2, width), jnp.bfloat16),
-        in_specs=[full] * 5 + [scalar],
+        in_specs=[scalar] + [full] * 5,
         out_specs=full,
         scratch_shapes=[pltpu.VMEM((tile_len, width), jnp.bfloat16)],
         compiler_params=params,
         name="norm",
-    )(*tiles[::-1], mod, spot)
+    )(spot, mod, *tiles)
     other_rows = core_swap(own_rows)
 
     last = owners_swap(far, 1)
     shards = [four, near, far]
     total_own, total_other, out_known, states_kept = pl.pallas_call(
-        backwards(early_kernel, 10),
+        early_kernel,
         out_shape=(
             jax.ShapeDtypeStruct((count // 2, 3 * local_cols), jnp.float32),
             jax.ShapeDtypeStruct((count // 2, 2 * local_cols), jnp.float32),
             jax.ShapeDtypeStruct((3,) + w_out.shape, jnp.bfloat16),
             jax.ShapeDtypeStruct((tile_len, width), jnp.bfloat16),
         ),
-        in_specs=[anywhere] * 7 + [full] * 2 + [scalar],
+        in_specs=[scalar] + [full] * 2 + [anywhere] * 7,
         out_specs=(full,) * 4,
         scratch_shapes=[
             pltpu.VMEM((3 * depth, 3 * local_cols), jnp.bfloat16),
@@ -373,7 +375,7 @@
         ],
         compiler_params=params,
         name="early",
-    )(states, *(core_swap(shard[:3]) for shard in shards[::-1]), *shards[::-1], other_rows, own_rows, spot)
+    )(spot, own_rows, other_rows, *shards, *(core_swap(shard[:3]) for shard in shards), states)
     out_sent = [core_swap(shard[3:]) for shard in shards]
     last, total_own, *out_sent = lax.optimization_barrier((last, total_own, *out_sent))
     last_sent = core_swap(last)
@@ -381,7 +383,7 @@
     half = jax.ShapeDtypeStruct((tile_len, width // 2), jnp.bfloat16)
     half_f32 = jax.ShapeDtypeStruct((tile_len, width // 2), jnp.float32)
     xy_left, xy_right, *kept = pl.pallas_call(
-        backwards(attend_kernel, 12),
+        attend_kernel,
         out_shape=(
             half,
             half,
@@ -391,27 +393,29 @@
             jax.ShapeDtypeStruct((local_cols // HD, count, 2 * HD), jnp.bfloat16),
             jax.ShapeDtypeStruct((local_cols, width), jnp.bfloat16),
         ),
-        in_specs=[full] * 2 + [anywhere] * 4 + [full] * 4 + [scalar, scalar],
+        in_specs=[scalar, scalar] + [full] * 4 + [anywhere] * 4 + [full] * 2,
         out_specs=(full,) * 7,
         scratch_shapes=[pltpu.SemaphoreType.DMA((4,))],
         compiler_params=params,
         name="attend",
-    )(last_sent, last, *out_sent[::-1], out_known, other_rows, own_rows, total_other, total_own, lengths, spot)
+    )(spot, lengths, total_own, total_other, own_rows, other_rows, out_known, *out_sent, last, last_sent)
     from_x = swap(xy_left, "patch", 1, 2)
     from_y = swap(xy_right, "wcol", 2, 4)
-    base, y_left, y_right, x_left, x_right = pl.pallas_call(
-        backwards(attend_rest_kernel, 7),
-        out_shape=(
-            jax.ShapeDtypeStruct((tile_len, width), jnp.float32),
-            half_f32,
-            half,
-            half,
-            half_f32,
-        ),
-        in_specs=[full] * 7,
-        out_specs=(full,) * 5,
+    y_left, y_right, x_left, x_right = pl.pallas_call(
+        attend_rest_kernel,
+        out_shape=(half_f32, half, half, half_f32),
+        in_specs=[full] * 5,
+        out_specs=(full,) * 4,
         compiler_params=params,
         name="attend_rest",
+    )(*kept)
+    base = pl.pallas_call(
+        attend_own_kernel,
+        out_shape=jax.ShapeDtypeStruct((tile_len, width), jnp.float32),
+        in_specs=[full] * 7,
+        out_specs=full,
+        compiler_params=params,
+        name="attend_own",
     )(*kept[::-1], mod, states_kept)
     got_x_left = swap(x_left, "patch", 1, 2)
     got_y_right = swap(y_right, "wcol", 2, 4)
@@ -425,8 +429,8 @@
         (slice(0, middle), (got_x_left, got_y_left)),
         (slice(middle, width), (got_x_right, got_y_right)),
     ):
-        out_proj = parts[0].astype(jnp.float32) + parts[1].astype(jnp.float32)
-        updated.append((base[:, columns] + mod[2, :, columns] * out_proj).astype(jnp.bfloat16))
+        out_proj = parts[1].astype(jnp.float32) + parts[0].astype(jnp.float32)
+        updated.append((mod[2, :, columns] * out_proj + base[:, columns]).astype(jnp.bfloat16))
     updated = jnp.concatenate(updated, axis=1)
     return updated[None]
 

time: 77.9 us -> 77.5 us (level)
    ppermute x16, waiting for transfers between devices: 26.5 us -> 19.3 us  [swap(): return lax.ppermute(array, axis, [(i, i ^ d) for i in range(n)])]
    ppermute x1, waiting for transfers between devices: 0.01 us -> 6.24 us  [tiled_body(): along_xy = lax.ppermute(states, ('patch', 'wcol'), diagonal)]
    ppermute x1, starting transfers between devices: 1.89 us -> 0.07 us  [tiled_body(): along_xy = lax.ppermute(states, ('patch', 'wcol'), diagonal)]
    ppermute x16, starting transfers between devices: 8.06 us -> 9.74 us  [swap(): return lax.ppermute(array, axis, [(i, i ^ d) for i in range(n)])]
    pallas_call x4 -> x5, Pallas kernels: 13.3 us -> 13.5 us  [the longest x1 4.01 us: tiled_body(): pl.pallas_call(early_kernel, out_shape=(jax.ShapeDtypeStruct((count // 2,...]
  transfers between devices with their start and end apart: 20 -> 20, of which waited for: 12 -> 11; matrix products, arithmetic and copies ran while one was open for 1% -> 1% of each run, Pallas kernels for 13% -> 13%
where the time goes in v8:
time: 77.5 us; the launch traced here: 77.2 us
  waiting for transfers between devices  37.3 us (48%)
  starting transfers between devices  22.1 us (29%)
  Pallas kernels  13.5 us (17%)
  other arithmetic  2.47 us (3%)
  local copies, waits for them, and re-layouts  1 us (1%)
  between operations  0.88 us (1%)
    ppermute x16, waiting for transfers between devices, swap(): return lax.ppermute(array, axis, [(i, i ^ d) for i in range(n)])  19.3 us
    ppermute x3, starting transfers between devices, owners_swap(): return lax.ppermute(array, everywhere, pairs)  12.3 us
    ppermute x3, waiting for transfers between devices, owners_swap(): return lax.ppermute(array, everywhere, pairs)  11.8 us
    ppermute x16, starting transfers between devices, swap(): return lax.ppermute(array, axis, [(i, i ^ d) for i in range(n)])  9.74 us
    ppermute x1, waiting for transfers between devices, tiled_body(): along_xy = lax.ppermute(states, ('patch', 'wcol'), diagonal)  6.24 us
    pallas_call x1, Pallas kernels, tiled_body(): pl.pallas_call(early_kernel, out_shape=(jax.ShapeDtypeStruct((count // 2,...  4.01 us
    pallas_call x1, Pallas kernels, tiled_body(): pl.pallas_call(attend_kernel, out_shape=(half, half, jax.ShapeDtypeStruct...  3.56 us
    pallas_call x1, Pallas kernels, tiled_body(): pl.pallas_call(norm_kernel, out_shape=jax.ShapeDtypeStruct((count // 2, w...  2.71 us
  transfers between devices with their start and end apart: 20, of which 11 were waited for; matrix products, arithmetic and copies ran while one was open for 1% of the time, Pallas kernels for 13%

profile of v8, /device:TPU:0, one launch (start us, length us, event | category | flops | bytes accessed | tf_op | source)
XLA Modules:
  0.0 77.2 jit_solution(13277544607042103093)
XLA Ops:
  0.0 1.4 %pad_maximum_fusion.refs_0_ = bf16[4,384,384]{2,1,0:T(8,128)(2,1)S(1)} fusion(bf16[1,384,384]{2,1,0:T(8,128)(2,1)} %bitcast.15, bf16[3,384,384]{2,1,0:T(8,128)(2,1)} %bitcast.13), kind=kLoop, calls=%fused_computation | loop fusion | flops 589824 | bytes 2359296 | tf_op jit(solution)/shard_map/concatenate | solution.py:340
  1.4 5.9 %collective-permute-start = (bf16[4,384,384]{2,1,0:T(8,128)(2,1)S(1)}, bf16[4,384,384]{2,1,0:T(8,128)(2,1)S(1)}, u32[]{:S(2)}, u32[]{:S(2)}) collective-permute-start(bf16[4,384,384]{2,1,0:T(8,128)(2,1)S(1)} %pad_maximum_fusion.refs_0_), channel_id=1, source_target_pairs={{0,8},{2,10},{4,12},{6,14},{8,0},{10,2},{12,4},{14,6},{17,25},{19,... | collective-permute-start | bytes 3538952 | tf_op jit(solution)/shard_map/ppermute | solution.py:326
  7.4 1.6 %collective-permute-start.3 = (bf16[128,1536]{1,0:T(8,128)(2,1)}, bf16[128,1536]{1,0:T(8,128)(2,1)}, u32[]{:S(2)}, u32[]{:S(2)}) collective-permute-start(bf16[128,1536]{1,0:T(8,128)(2,1)} %bitcast.7.refs_1_.refs_6_), channel_id=1, source_target_pairs={{0,2},{1,3},{2,0},{3,1},{4,6},{5,7},{6,4},{7,5},{8,10},{9,11},{10,... | collective-permute-start | bytes 1179656 | tf_op jit(solution)/shard_map/ppermute | solution.py:316
  9.0 1.9 %collective-permute-start.4 = (bf16[128,1536]{1,0:T(8,128)(2,1)}, bf16[128,1536]{1,0:T(8,128)(2,1)}, u32[]{:S(2)}, u32[]{:S(2)}) collective-permute-start(bf16[128,1536]{1,0:T(8,128)(2,1)} %bitcast.7.refs_1_.refs_6_), channel_id=1, source_target_pairs={{0,16},{16,0},{1,17},{17,1},{2,18},{18,2},{3,19},{19,3},{4,20},{20... | collective-permute-start | bytes 1179656 | tf_op jit(solution)/shard_map/ppermute | solution.py:316
  10.9 3.5 %collective-permute-start.6 = (bf16[4,384,384]{2,1,0:T(8,128)(2,1)S(1)}, bf16[4,384,384]{2,1,0:T(8,128)(2,1)S(1)}, u32[]{:S(2)}, u32[]{:S(2)}) collective-permute-start(bf16[4,384,384]{2,1,0:T(8,128)(2,1)S(1)} %pad_maximum_fusion.refs_0_), channel_id=1, source_target_pairs={{0,4},{2,6},{4,0},{6,2},{8,12},{10,14},{12,8},{14,10},{17,21},{19,... | collective-permute-start | bytes 3538952 | tf_op jit(solution)/shard_map/ppermute | solution.py:326
  14.5 6.2 %collective-permute-done.2.refs_0_ = bf16[128,1536]{1,0:T(8,128)(2,1)} collective-permute-done((bf16[128,1536]{1,0:T(8,128)(2,1)}, bf16[128,1536]{1,0:T(8,128)(2,1)}, u32[]{:S(2)}, u32[]{:S(2)}) %collective-permute-start.2) | collective-permute-done | bytes 393248 | tf_op jit(solution)/shard_map/ppermute | solution.py:346
  20.7 6.6 %collective-permute-done.3.refs_2_ = bf16[128,1536]{1,0:T(8,128)(2,1)} collective-permute-done((bf16[128,1536]{1,0:T(8,128)(2,1)}, bf16[128,1536]{1,0:T(8,128)(2,1)}, u32[]{:S(2)}, u32[]{:S(2)}) %collective-permute-start.3) | collective-permute-done | bytes 393248 | tf_op jit(solution)/shard_map/ppermute | solution.py:316
  28.1 2.7 %norm.1.own_rows_ref.refs_2_ = bf16[512,1536]{1,0:T(8,128)(2,1)S(1)} custom-call(s32[4]{0:T(128)S(1)} %pad_add_fusion.spot_ref, f32[3,1,1536]{2,1,0:T(1,128)S(1)} %bitcast.10, bf16[128,1536]{1,0:T(8,128)(2,1)} %collective-permute-done.2.refs_0_, bf16[128,1536]{1,0:T(8,128)(2,1)} %bitcast.7.refs_1_.refs_6_, bf16[128,1536]{1,0:T(8,128)(2,1)} %collective-permute-done.3.refs_2_, ...), custom_call_target="tpu_custom_call" | custom-call | tf_op jit(solution)/shard_map/norm/pallas_call | solution.py:348
  31.4 2.9 %collective-permute-done.refs_2_ = bf16[4,384,384]{2,1,0:T(8,128)(2,1)S(1)} collective-permute-done((bf16[4,384,384]{2,1,0:T(8,128)(2,1)S(1)}, bf16[4,384,384]{2,1,0:T(8,128)(2,1)S(1)}, u32[]{:S(2)}, u32[]{:S(2)}) %collective-permute-start) | collective-permute-done | bytes 1179680 | tf_op jit(solution)/shard_map/ppermute | solution.py:326
  34.4 2.8 %collective-permute-start.1 = (bf16[4,384,384]{2,1,0:T(8,128)(2,1)S(1)}, bf16[4,384,384]{2,1,0:T(8,128)(2,1)S(1)}, u32[]{:S(2)}, u32[]{:S(2)}) collective-permute-start(bf16[4,384,384]{2,1,0:T(8,128)(2,1)S(1)} %collective-permute-done.refs_2_), channel_id=1, source_target_pairs={{0,4},{2,6},{4,0},{6,2},{8,12},{10,14},{12,8},{14,10},{17,21},{19,... | collective-permute-start | bytes 3538952 | tf_op jit(solution)/shard_map/ppermute | solution.py:326
  37.3 2.9 %collective-permute-done.6.refs_1_ = bf16[4,384,384]{2,1,0:T(8,128)(2,1)S(1)} collective-permute-done((bf16[4,384,384]{2,1,0:T(8,128)(2,1)S(1)}, bf16[4,384,384]{2,1,0:T(8,128)(2,1)S(1)}, u32[]{:S(2)}, u32[]{:S(2)}) %collective-permute-start.6) | collective-permute-done | bytes 1179680 | tf_op jit(solution)/shard_map/ppermute | solution.py:326
  41.5 1.2 %collective-permute-done.8.refs_4_ = bf16[3,384,384]{2,1,0:T(8,128)(2,1)S(1)} collective-permute-done((bf16[3,384,384]{2,1,0:T(8,128)(2,1)S(1)}, bf16[3,384,384]{2,1,0:T(8,128)(2,1)S(1)}, u32[]{:S(2)}, u32[]{:S(2)}) %collective-permute-start.8) | collective-permute-done | bytes 884768 | tf_op jit(solution)/shard_map/ppermute | solution.py:316
  42.8 4.0 %early.1 = (f32[512,1152]{1,0:T(8,128)S(1)}, f32[512,768]{1,0:T(8,128)S(1)}, bf16[3,384,384]{2,1,0:T(8,128)(2,1)S(1)}, bf16[128,1536]{1,0:T(8,128)(2,1)S(1)}) custom-call(s32[4]{0:T(128)S(1)} %pad_add_fusion.spot_ref, bf16[512,1536]{1,0:T(8,128)(2,1)S(1)} %norm.1.own_rows_ref.refs_2_, bf16[512,1536]{1,0:T(8,128)(2,1)S(1)} %collective-permute-done.5.other_rows_ref.refs_3_, ...), custom_call_target="tpu_custom_call" | custom-call | tf_op jit(solution)/shard_map/early/pallas_call | solution.py:361
  46.8 6.0 %collective-permute-done.1.refs_8_ = bf16[4,384,384]{2,1,0:T(8,128)(2,1)S(1)} collective-permute-done((bf16[4,384,384]{2,1,0:T(8,128)(2,1)S(1)}, bf16[4,384,384]{2,1,0:T(8,128)(2,1)S(1)}, u32[]{:S(2)}, u32[]{:S(2)}) %collective-permute-start.1) | collective-permute-done | bytes 1179680 | tf_op jit(solution)/shard_map/ppermute | solution.py:326
  53.5 2.2 %collective-permute-done.13.refs_9_ = bf16[4,384,384]{2,1,0:T(8,128)(2,1)S(1)} collective-permute-done((bf16[4,384,384]{2,1,0:T(8,128)(2,1)S(1)}, bf16[4,384,384]{2,1,0:T(8,128)(2,1)S(1)}, u32[]{:S(2)}, u32[]{:S(2)}) %collective-permute-start.13) | collective-permute-done | bytes 1179680 | tf_op jit(solution)/shard_map/ppermute | solution.py:316
  55.7 3.6 %attend.1 = (bf16[128,768]{1,0:T(8,128)(2,1)S(1)}, bf16[128,768]{1,0:T(8,128)(2,1)S(1)}, f32[1,1024]{1,0:T(1,128)S(1)}, bf16[512,384]{1,0:T(8,128)(2,1)S(1)}, bf...) custom-call(s32[4]{0:T(128)S(1)} %pad_add_fusion.spot_ref, ...), custom_call_target="tpu_custom_call" | custom-call | tf_op jit(solution)/shard_map/attend/pallas_call | solution.py:385
  59.3 1.9 %collective-permute-start.18 = (bf16[128,768]{1,0:T(8,128)(2,1)S(1)}, bf16[128,768]{1,0:T(8,128)(2,1)S(1)}, u32[]{:S(2)}, u32[]{:S(2)}) collective-permute-start(bf16[128,768]{1,0:T(8,128)(2,1)S(1)} %get-tuple-element.44), channel_id=1, source_target_pairs={{0,2},{1,3},{2,0},{3,1},{4,6},{5,7},{6,4},{7,5},{8,10},{9,11},{10,... | collective-permute-start | bytes 589832 | tf_op jit(solution)/shard_map/ppermute | solution.py:316
  61.2 2.0 %attend_rest.1 = (f32[128,768]{1,0:T(8,128)S(1)}, bf16[128,768]{1,0:T(8,128)(2,1)S(1)}, bf16[128,768]{1,0:T(8,128)(2,1)S(1)}, f32[128,768]{1,0:T(8,128)S(1)}) custom-call(f32[1,1024]{1,0:T(1,128)S(1)} %get-tuple-element.33.bias_ref, bf16[512,384]{1,0:T(8,128)(2,1)S(1)} %get-tuple-element.34.query_ref, bf16[1024,384]{1,0:T(8,128)(2,1)S(1)} %get-tuple-element.35.key_ref, ...), custom_call_target="tpu_custom_call" | custom-call | tf_op jit(solution)/shard_map/attend_rest/pallas_call | solution.py:404
  63.1 2.1 %collective-permute-start.16 = (bf16[128,768]{1,0:T(8,128)(2,1)S(1)}, bf16[128,768]{1,0:T(8,128)(2,1)S(1)}, u32[]{:S(2)}, u32[]{:S(2)}) collective-permute-start(bf16[128,768]{1,0:T(8,128)(2,1)S(1)} %get-tuple-element.40), channel_id=1, source_target_pairs={{0,16},{16,0},{1,17},{17,1},{2,18},{18,2},{3,19},{19,3},{4,20},{20... | collective-permute-start | bytes 589832 | tf_op jit(solution)/shard_map/ppermute | solution.py:316
  65.4 1.0 %collective-permute-done.18 = bf16[128,768]{1,0:T(8,128)(2,1)S(1)} collective-permute-done((bf16[128,768]{1,0:T(8,128)(2,1)S(1)}, bf16[128,768]{1,0:T(8,128)(2,1)S(1)}, u32[]{:S(2)}, u32[]{:S(2)}) %collective-permute-start.18) | collective-permute-done | bytes 196640 | tf_op jit(solution)/shard_map/ppermute | solution.py:316
  66.5 2.5 %collective-permute-done.14 = bf16[128,768]{1,0:T(8,128)(2,1)S(1)} collective-permute-done((bf16[128,768]{1,0:T(8,128)(2,1)S(1)}, bf16[128,768]{1,0:T(8,128)(2,1)S(1)}, u32[]{:S(2)}, u32[]{:S(2)}) %collective-permute-start.14) | collective-permute-done | bytes 196640 | tf_op jit(solution)/shard_map/ppermute | solution.py:316
  69.2 1.3 %attend_own.1 = f32[128,1536]{1,0:T(8,128)S(1)} custom-call(bf16[384,1536]{1,0:T(8,128)(2,1)S(1)} %get-tuple-element.37.out_weight_ref, bf16[3,1024,256]{2,1,0:T(8,128)(2,1)S(1)} %get-tuple-element.36.value_ref, bf16[1024,384]{1,0:T(8,128)(2,1)S(1)} %get-tuple-element.35.key_ref, bf16[512,384]{1,0:T(8,128)(2,1)S(1)} %get-tuple-element.34.query_ref, ...), custom_call_target="tpu_custom_call" | custom-call | tf_op jit(solution)/shard_map/attend_own/pallas_call | solution.py:412
  70.5 2.7 %collective-permute-done.16 = bf16[128,768]{1,0:T(8,128)(2,1)S(1)} collective-permute-done((bf16[128,768]{1,0:T(8,128)(2,1)S(1)}, bf16[128,768]{1,0:T(8,128)(2,1)S(1)}, u32[]{:S(2)}, u32[]{:S(2)}) %collective-permute-start.16) | collective-permute-done | bytes 196640 | tf_op jit(solution)/shard_map/ppermute | solution.py:316
  73.2 3.1 %collective-permute-done.19 = bf16[128,768]{1,0:T(8,128)(2,1)S(1)} collective-permute-done((bf16[128,768]{1,0:T(8,128)(2,1)S(1)}, bf16[128,768]{1,0:T(8,128)(2,1)S(1)}, u32[]{:S(2)}, u32[]{:S(2)}) %collective-permute-start.19) | collective-permute-done | bytes 196640 | tf_op jit(solution)/shard_map/ppermute | solution.py:316
  (40 shorter events, 4.4 us)
Async XLA Ops:
  1.4 32.9 %collective-permute-start = (bf16[4,384,384]{2,1,0:T(8,128)(2,1)S(1)}, bf16[4,384,384]{2,1,0:T(8,128)(2,1)S(1)}, u32[]{:S(2)}, u32[]{:S(2)}) collective-permute-start(bf16[4,384,384]{2,1,0:T(8,128)(2,1)S(1)} %pad_maximum_fusion.refs_0_), channel_id=1, source_target_pairs={{0,8},{2,10},{4,12},{6,14},{8,0},{10,2},{12,4},{14,6},{17,25},{19,... | collective-permute-start | bytes 3538952 | tf_op jit(solution)/shard_map/ppermute | solution.py:326
  7.4 13.4 %collective-permute-start.2 = (bf16[128,1536]{1,0:T(8,128)(2,1)}, bf16[128,1536]{1,0:T(8,128)(2,1)}, u32[]{:S(2)}, u32[]{:S(2)}) collective-permute-start(bf16[128,1536]{1,0:T(8,128)(2,1)} %bitcast.7.refs_1_.refs_6_), channel_id=1, source_target_pairs={{0,18},{1,19},{2,16},{3,17},{16,2},{17,3},{18,0},{19,1},{4,22},{5,... | collective-permute-start | bytes 1179656 | tf_op jit(solution)/shard_map/ppermute | solution.py:346
  7.4 19.9 %collective-permute-start.3 = (bf16[128,1536]{1,0:T(8,128)(2,1)}, bf16[128,1536]{1,0:T(8,128)(2,1)}, u32[]{:S(2)}, u32[]{:S(2)}) collective-permute-start(bf16[128,1536]{1,0:T(8,128)(2,1)} %bitcast.7.refs_1_.refs_6_), channel_id=1, source_target_pairs={{0,2},{1,3},{2,0},{3,1},{4,6},{5,7},{6,4},{7,5},{8,10},{9,11},{10,... | collective-permute-start | bytes 1179656 | tf_op jit(solution)/shard_map/ppermute | solution.py:316
  9.0 18.4 %collective-permute-start.4 = (bf16[128,1536]{1,0:T(8,128)(2,1)}, bf16[128,1536]{1,0:T(8,128)(2,1)}, u32[]{:S(2)}, u32[]{:S(2)}) collective-permute-start(bf16[128,1536]{1,0:T(8,128)(2,1)} %bitcast.7.refs_1_.refs_6_), channel_id=1, source_target_pairs={{0,16},{16,0},{1,17},{17,1},{2,18},{18,2},{3,19},{19,3},{4,20},{20... | collective-permute-start | bytes 1179656 | tf_op jit(solution)/shard_map/ppermute | solution.py:316
  10.9 29.3 %collective-permute-start.6 = (bf16[4,384,384]{2,1,0:T(8,128)(2,1)S(1)}, bf16[4,384,384]{2,1,0:T(8,128)(2,1)S(1)}, u32[]{:S(2)}, u32[]{:S(2)}) collective-permute-start(bf16[4,384,384]{2,1,0:T(8,128)(2,1)S(1)} %pad_maximum_fusion.refs_0_), channel_id=1, source_target_pairs={{0,4},{2,6},{4,0},{6,2},{8,12},{10,14},{12,8},{14,10},{17,21},{19,... | collective-permute-start | bytes 3538952 | tf_op jit(solution)/shard_map/ppermute | solution.py:326
  27.4 0.7 copy-start
  28.1 2.9 %copy-start.2 = (bf16[384,3,384]{2,0,1:T(8,128)(2,1)S(1)}, bf16[384,3,384]{2,0,1:T(8,128)(2,1)}, u32[]{:S(2)}) copy-start(bf16[384,3,384]{2,0,1:T(8,128)(2,1)} %param.7) | copy-start | bytes 2654212
  30.8 10.2 %collective-permute-start.5 = (bf16[512,1536]{1,0:T(8,128)(2,1)S(1)}, bf16[512,1536]{1,0:T(8,128)(2,1)S(1)}, u32[]{:S(2)}, u32[]{:S(2)}) collective-permute-start(bf16[512,1536]{1,0:T(8,128)(2,1)S(1)} %norm.1.own_rows_ref.refs_2_), channel_id=1, source_target_pairs={{0,1},{1,0},{2,3},{3,2},{4,5},{5,4},{6,7},{7,6},{8,9},{9,8},{10,11... | collective-permute-start | bytes 4718600 | tf_op jit(solution)/shard_map/ppermute | solution.py:316
  31.0 9.4 %collective-permute-start.7 = (bf16[3,384,384]{2,1,0:T(8,128)(2,1)S(1)}, bf16[3,384,384]{2,1,0:T(8,128)(2,1)S(1)}, u32[]{:S(2)}, u32[]{:S(2)}) collective-permute-start(bf16[3,384,384]{2,1,0:T(8,128)(2,1)S(1)} %bitcast.14), channel_id=1, source_target_pairs={{0,1},{1,0},{2,3},{3,2},{4,5},{5,4},{6,7},{7,6},{8,9},{9,8},{10,11... | collective-permute-start | bytes 2654216 | tf_op jit(solution)/shard_map/ppermute | solution.py:316
  34.4 6.1 %copy-start.3 = (bf16[384,384]{1,0:T(8,128)(2,1)S(1)}, bf16[384,384]{1,0:T(8,128)(2,1)}, u32[]{:S(2)}) copy-start(bf16[384,384]{1,0:T(8,128)(2,1)} %param.8) | copy-start | bytes 884740
  34.4 6.7 %collective-permute-start.9 = (bf16[3,384,384]{2,1,0:T(8,128)(2,1)S(1)}, bf16[3,384,384]{2,1,0:T(8,128)(2,1)S(1)}, u32[]{:S(2)}, u32[]{:S(2)}) collective-permute-start(bf16[3,384,384]{2,1,0:T(8,128)(2,1)S(1)} %slice.34), channel_id=1, source_target_pairs={{0,1},{1,0},{2,3},{3,2},{4,5},{5,4},{6,7},{7,6},{8,9},{9,8},{10,11... | collective-permute-start | bytes 2654216 | tf_op jit(solution)/shard_map/ppermute | solution.py:316
  34.4 18.4 %collective-permute-start.1 = (bf16[4,384,384]{2,1,0:T(8,128)(2,1)S(1)}, bf16[4,384,384]{2,1,0:T(8,128)(2,1)S(1)}, u32[]{:S(2)}, u32[]{:S(2)}) collective-permute-start(bf16[4,384,384]{2,1,0:T(8,128)(2,1)S(1)} %collective-permute-done.refs_2_), channel_id=1, source_target_pairs={{0,4},{2,6},{4,0},{6,2},{8,12},{10,14},{12,8},{14,10},{17,21},{19,... | collective-permute-start | bytes 3538952 | tf_op jit(solution)/shard_map/ppermute | solution.py:326
  40.3 2.5 %collective-permute-start.8 = (bf16[3,384,384]{2,1,0:T(8,128)(2,1)S(1)}, bf16[3,384,384]{2,1,0:T(8,128)(2,1)S(1)}, u32[]{:S(2)}, u32[]{:S(2)}) collective-permute-start(bf16[3,384,384]{2,1,0:T(8,128)(2,1)S(1)} %slice.33), channel_id=1, source_target_pairs={{0,1},{1,0},{2,3},{3,2},{4,5},{5,4},{6,7},{7,6},{8,9},{9,8},{10,11... | collective-permute-start | bytes 2654216 | tf_op jit(solution)/shard_map/ppermute | solution.py:316
  40.5 6.3 %collective-permute-start.10 = (bf16[1,384,384]{2,1,0:T(8,128)(2,1)S(1)}, bf16[1,384,384]{2,1,0:T(8,128)(2,1)S(1)}, u32[]{:S(2)}, u32[]{:S(2)}) collective-permute-start(bf16[1,384,384]{2,1,0:T(8,128)(2,1)S(1)} %bitcast.16), channel_id=1, source_target_pairs={{0,1},{1,0},{2,3},{3,2},{4,5},{5,4},{6,7},{7,6},{8,9},{9,8},{10,11... | collective-permute-start | bytes 884744 | tf_op jit(solution)/shard_map/ppermute | solution.py:316
  41.0 5.8 %collective-permute-start.12 = (bf16[1,384,384]{2,1,0:T(8,128)(2,1)S(1)}, bf16[1,384,384]{2,1,0:T(8,128)(2,1)S(1)}, u32[]{:S(2)}, u32[]{:S(2)}) collective-permute-start(bf16[1,384,384]{2,1,0:T(8,128)(2,1)S(1)} %slice.36), channel_id=1, source_target_pairs={{0,1},{1,0},{2,3},{3,2},{4,5},{5,4},{6,7},{7,6},{8,9},{9,8},{10,11... | collective-permute-start | bytes 884744 | tf_op jit(solution)/shard_map/ppermute | solution.py:316
  41.1 5.7 %collective-permute-start.11 = (bf16[1,384,384]{2,1,0:T(8,128)(2,1)S(1)}, bf16[1,384,384]{2,1,0:T(8,128)(2,1)S(1)}, u32[]{:S(2)}, u32[]{:S(2)}) collective-permute-start(bf16[1,384,384]{2,1,0:T(8,128)(2,1)S(1)} %slice.35), channel_id=1, source_target_pairs={{0,1},{1,0},{2,3},{3,2},{4,5},{5,4},{6,7},{7,6},{8,9},{9,8},{10,11... | collective-permute-start | bytes 884744 | tf_op jit(solution)/shard_map/ppermute | solution.py:316
  52.8 2.8 %collective-permute-start.13 = (bf16[4,384,384]{2,1,0:T(8,128)(2,1)S(1)}, bf16[4,384,384]{2,1,0:T(8,128)(2,1)S(1)}, u32[]{:S(2)}, u32[]{:S(2)}) collective-permute-start(bf16[4,384,384]{2,1,0:T(8,128)(2,1)S(1)} %collective-permute-done.1.refs_8_), channel_id=1, source_target_pairs={{0,1},{1,0},{2,3},{3,2},{4,5},{5,4},{6,7},{7,6},{8,9},{9,8},{10,11... | collective-permute-start | bytes 3538952 | tf_op jit(solution)/shard_map/ppermute | solution.py:316
  59.3 7.1 %collective-permute-start.18 = (bf16[128,768]{1,0:T(8,128)(2,1)S(1)}, bf16[128,768]{1,0:T(8,128)(2,1)S(1)}, u32[]{:S(2)}, u32[]{:S(2)}) collective-permute-start(bf16[128,768]{1,0:T(8,128)(2,1)S(1)} %get-tuple-element.44), channel_id=1, source_target_pairs={{0,2},{1,3},{2,0},{3,1},{4,6},{5,7},{6,4},{7,5},{8,10},{9,11},{10,... | collective-permute-start | bytes 589832 | tf_op jit(solution)/shard_map/ppermute | solution.py:316
  61.2 7.8 %collective-permute-start.14 = (bf16[128,768]{1,0:T(8,128)(2,1)S(1)}, bf16[128,768]{1,0:T(8,128)(2,1)S(1)}, u32[]{:S(2)}, u32[]{:S(2)}) collective-permute-start(bf16[128,768]{1,0:T(8,128)(2,1)S(1)} %get-tuple-element.39), channel_id=1, source_target_pairs={{0,16},{16,0},{1,17},{17,1},{2,18},{18,2},{3,19},{19,3},{4,20},{20... | collective-permute-start | bytes 589832 | tf_op jit(solution)/shard_map/ppermute | solution.py:316
  63.1 6.1 %copy-start.1 = (f32[1,3,1536]{2,0,1:T(1,128)S(1)}, f32[1,3,1536]{2,0,1:T(1,128)}, u32[]{:S(2)}) copy-start(f32[1,3,1536]{2,0,1:T(1,128)} %param.6) | copy-start | bytes 55300
  63.1 10.0 %collective-permute-start.16 = (bf16[128,768]{1,0:T(8,128)(2,1)S(1)}, bf16[128,768]{1,0:T(8,128)(2,1)S(1)}, u32[]{:S(2)}, u32[]{:S(2)}) collective-permute-start(bf16[128,768]{1,0:T(8,128)(2,1)S(1)} %get-tuple-element.40), channel_id=1, source_target_pairs={{0,16},{16,0},{1,17},{17,1},{2,18},{18,2},{3,19},{19,3},{4,20},{20... | collective-permute-start | bytes 589832 | tf_op jit(solution)/shard_map/ppermute | solution.py:316
  65.2 7.9 %collective-permute-start.17 = (bf16[128,768]{1,0:T(8,128)(2,1)S(1)}, bf16[128,768]{1,0:T(8,128)(2,1)S(1)}, u32[]{:S(2)}, u32[]{:S(2)}) collective-permute-start(bf16[128,768]{1,0:T(8,128)(2,1)S(1)} %get-tuple-element.42), channel_id=1, source_target_pairs={{0,2},{1,3},{2,0},{3,1},{4,6},{5,7},{6,4},{7,5},{8,10},{9,11},{10,... | collective-permute-start | bytes 589832 | tf_op jit(solution)/shard_map/ppermute | solution.py:316
  66.4 9.8 %collective-permute-start.19 = (bf16[128,768]{1,0:T(8,128)(2,1)S(1)}, bf16[128,768]{1,0:T(8,128)(2,1)S(1)}, u32[]{:S(2)}, u32[]{:S(2)}) collective-permute-start(bf16[128,768]{1,0:T(8,128)(2,1)S(1)} %add_convert_fusion), channel_id=1, source_target_pairs={{0,16},{16,0},{1,17},{17,1},{2,18},{18,2},{3,19},{19,3},{4,20},{20... | collective-permute-start | bytes 589832 | tf_op jit(solution)/shard_map/ppermute | solution.py:316
  69.0 7.3 %collective-permute-start.15 = (bf16[128,768]{1,0:T(8,128)(2,1)S(1)}, bf16[128,768]{1,0:T(8,128)(2,1)S(1)}, u32[]{:S(2)}, u32[]{:S(2)}) collective-permute-start(bf16[128,768]{1,0:T(8,128)(2,1)S(1)} %add_convert_fusion.1), channel_id=1, source_target_pairs={{0,2},{1,3},{2,0},{3,1},{4,6},{5,7},{6,4},{7,5},{8,10},{9,11},{10,... | collective-permute-start | bytes 589832 | tf_op jit(solution)/shard_map/ppermute | solution.py:316

commit v9 on v8

--- a/solution.py
+++ b/solution.py
@@ -225,16 +225,9 @@
 def attend_kernel(spot_ref, len_ref, *refs):
     totals, rows_refs, out_here, out_sent, (here, sent) = refs[0:2], refs[2:4], refs[4], refs[5:8], refs[8:10]
     left_ref, right_ref, bias_ref, query_ref, key_ref, value_ref, out_weight_ref = refs[10:17]
-    out_sem = refs[17]
     count, width = key_ref.shape
     depth = here.shape[1]
     z = spot_ref[2]
-    places = [
-        out_weight_ref.at[:, pl.ds(pl.multiple_of((z ^ d) * width, HD), width)] for d in range(4)
-    ]
-    for d in range(3):
-        start_by_role(spot_ref, out_here.at[d], out_sent[d].at[0], places[d], out_sem.at[d])
-    start_by_role(spot_ref, here.at[3], sent.at[3], places[3], out_sem.at[3])
     bias_ref[...] = key_bias(spot_ref, len_ref, count // 8)
     for h in range(width // HD):
         value_ref[h, :, HD:] = jnp.ones((count, HD), jnp.bfloat16)
@@ -262,15 +255,16 @@
                 value_ref[h, rows, :HD] = mixed[:, at : at + HD]
 
     owner = spot_ref[0] == spot_ref[3]
-    for role, shard in ((owner, here), (jnp.logical_not(owner), sent)):
+    held = [out_here.at[d] for d in range(3)], [part.at[0] for part in out_sent]
+    for role, shard, parts in ((owner, here, held[0]), (jnp.logical_not(owner), sent, held[1])):
 
         @pl.when(role)
         def _():
             finish(shard)
-
-    for d in range(4):
-        source = out_here.at[d] if d < 3 else here.at[3]
-        pltpu.make_async_copy(source, places[d], out_sem.at[d]).wait()
+            for d, part in enumerate(parts + [shard.at[3]]):
+                start = pl.multiple_of((z ^ d) * width, HD)
+                out_weight_ref[:, pl.ds(start, width)] = part[...]
+
     diagonal = project(query_ref[: step // 2, :], key_ref, value_ref, out_weight_ref, bias_ref[...])
     middle = left_ref.shape[1]
     left_ref[...] = diagonal[:, :middle].astype(jnp.bfloat16)
@@ -393,9 +387,8 @@
             jax.ShapeDtypeStruct((local_cols // HD, count, 2 * HD), jnp.bfloat16),
             jax.ShapeDtypeStruct((local_cols, width), jnp.bfloat16),
         ),
-        in_specs=[scalar, scalar] + [full] * 4 + [anywhere] * 4 + [full] * 2,
+        in_specs=[scalar, scalar] + [full] * 10,
         out_specs=(full,) * 7,
-        scratch_shapes=[pltpu.SemaphoreType.DMA((4,))],
         compiler_params=params,
         name="attend",
     )(spot, lengths, total_own, total_other, own_rows, other_rows, out_known, *out_sent, last, last_sent)

time: 77.5 us -> 77.4 us (level)
  no operation moved by 1% of the time
where the time goes in v9:
time: 77.4 us; the launch traced here: 77 us
  waiting for transfers between devices  37.3 us (48%)
  starting transfers between devices  22.1 us (29%)
  Pallas kernels  13.3 us (17%)
  other arithmetic  2.47 us (3%)
  local copies, waits for them, and re-layouts  1 us (1%)
  between operations  0.88 us (1%)
    ppermute x16, waiting for transfers between devices, swap(): return lax.ppermute(array, axis, [(i, i ^ d) for i in range(n)])  19.3 us
    ppermute x3, starting transfers between devices, owners_swap(): return lax.ppermute(array, everywhere, pairs)  12.3 us
    ppermute x3, waiting for transfers between devices, owners_swap(): return lax.ppermute(array, everywhere, pairs)  11.8 us
    ppermute x16, starting transfers between devices, swap(): return lax.ppermute(array, axis, [(i, i ^ d) for i in range(n)])  9.74 us
    ppermute x1, waiting for transfers between devices, tiled_body(): along_xy = lax.ppermute(states, ('patch', 'wcol'), diagonal)  6.24 us
    pallas_call x1, Pallas kernels, tiled_body(): pl.pallas_call(early_kernel, out_shape=(jax.ShapeDtypeStruct((count // 2,...  4.01 us
    pallas_call x1, Pallas kernels, tiled_body(): pl.pallas_call(attend_kernel, out_shape=(half, half, jax.ShapeDtypeStruct...  3.4 us
    pallas_call x1, Pallas kernels, tiled_body(): pl.pallas_call(norm_kernel, out_shape=jax.ShapeDtypeStruct((count // 2, w...  2.71 us
  transfers between devices with their start and end apart: 20, of which 11 were waited for; matrix products, arithmetic and copies ran while one was open for 1% of the time, Pallas kernels for 13%

profile of v9, /device:TPU:0, one launch (start us, length us, event | category | flops | bytes accessed | tf_op | source)
XLA Modules:
  0.0 77.0 jit_solution(8681896141821244092)
XLA Ops:
  0.0 1.4 %pad_maximum_fusion.refs_0_ = bf16[4,384,384]{2,1,0:T(8,128)(2,1)S(1)} fusion(bf16[1,384,384]{2,1,0:T(8,128)(2,1)} %bitcast.15, bf16[3,384,384]{2,1,0:T(8,128)(2,1)} %bitcast.13), kind=kLoop, calls=%fused_computation | loop fusion | flops 589824 | bytes 2359296 | tf_op jit(solution)/shard_map/concatenate | solution.py:334
  1.4 5.9 %collective-permute-start = (bf16[4,384,384]{2,1,0:T(8,128)(2,1)S(1)}, bf16[4,384,384]{2,1,0:T(8,128)(2,1)S(1)}, u32[]{:S(2)}, u32[]{:S(2)}) collective-permute-start(bf16[4,384,384]{2,1,0:T(8,128)(2,1)S(1)} %pad_maximum_fusion.refs_0_), channel_id=1, source_target_pairs={{0,8},{2,10},{4,12},{6,14},{8,0},{10,2},{12,4},{14,6},{17,25},{19,... | collective-permute-start | bytes 3538952 | tf_op jit(solution)/shard_map/ppermute | solution.py:320
  7.4 1.6 %collective-permute-start.3 = (bf16[128,1536]{1,0:T(8,128)(2,1)}, bf16[128,1536]{1,0:T(8,128)(2,1)}, u32[]{:S(2)}, u32[]{:S(2)}) collective-permute-start(bf16[128,1536]{1,0:T(8,128)(2,1)} %bitcast.7.refs_1_.refs_6_), channel_id=1, source_target_pairs={{0,2},{1,3},{2,0},{3,1},{4,6},{5,7},{6,4},{7,5},{8,10},{9,11},{10,... | collective-permute-start | bytes 1179656 | tf_op jit(solution)/shard_map/ppermute | solution.py:310
  9.0 1.9 %collective-permute-start.4 = (bf16[128,1536]{1,0:T(8,128)(2,1)}, bf16[128,1536]{1,0:T(8,128)(2,1)}, u32[]{:S(2)}, u32[]{:S(2)}) collective-permute-start(bf16[128,1536]{1,0:T(8,128)(2,1)} %bitcast.7.refs_1_.refs_6_), channel_id=1, source_target_pairs={{0,16},{16,0},{1,17},{17,1},{2,18},{18,2},{3,19},{19,3},{4,20},{20... | collective-permute-start | bytes 1179656 | tf_op jit(solution)/shard_map/ppermute | solution.py:310
  10.9 3.5 %collective-permute-start.6 = (bf16[4,384,384]{2,1,0:T(8,128)(2,1)S(1)}, bf16[4,384,384]{2,1,0:T(8,128)(2,1)S(1)}, u32[]{:S(2)}, u32[]{:S(2)}) collective-permute-start(bf16[4,384,384]{2,1,0:T(8,128)(2,1)S(1)} %pad_maximum_fusion.refs_0_), channel_id=1, source_target_pairs={{0,4},{2,6},{4,0},{6,2},{8,12},{10,14},{12,8},{14,10},{17,21},{19,... | collective-permute-start | bytes 3538952 | tf_op jit(solution)/shard_map/ppermute | solution.py:320
  14.5 6.2 %collective-permute-done.2.refs_0_ = bf16[128,1536]{1,0:T(8,128)(2,1)} collective-permute-done((bf16[128,1536]{1,0:T(8,128)(2,1)}, bf16[128,1536]{1,0:T(8,128)(2,1)}, u32[]{:S(2)}, u32[]{:S(2)}) %collective-permute-start.2) | collective-permute-done | bytes 393248 | tf_op jit(solution)/shard_map/ppermute | solution.py:340
  20.7 6.6 %collective-permute-done.3.refs_2_ = bf16[128,1536]{1,0:T(8,128)(2,1)} collective-permute-done((bf16[128,1536]{1,0:T(8,128)(2,1)}, bf16[128,1536]{1,0:T(8,128)(2,1)}, u32[]{:S(2)}, u32[]{:S(2)}) %collective-permute-start.3) | collective-permute-done | bytes 393248 | tf_op jit(solution)/shard_map/ppermute | solution.py:310
  28.1 2.7 %norm.1.own_rows_ref.refs_2_ = bf16[512,1536]{1,0:T(8,128)(2,1)S(1)} custom-call(s32[4]{0:T(128)S(1)} %pad_add_fusion.spot_ref, f32[3,1,1536]{2,1,0:T(1,128)S(1)} %bitcast.10, bf16[128,1536]{1,0:T(8,128)(2,1)} %collective-permute-done.2.refs_0_, bf16[128,1536]{1,0:T(8,128)(2,1)} %bitcast.7.refs_1_.refs_6_, bf16[128,1536]{1,0:T(8,128)(2,1)} %collective-permute-done.3.refs_2_, ...), custom_call_target="tpu_custom_call" | custom-call | tf_op jit(solution)/shard_map/norm/pallas_call | solution.py:342
  31.4 2.9 %collective-permute-done.refs_2_ = bf16[4,384,384]{2,1,0:T(8,128)(2,1)S(1)} collective-permute-done((bf16[4,384,384]{2,1,0:T(8,128)(2,1)S(1)}, bf16[4,384,384]{2,1,0:T(8,128)(2,1)S(1)}, u32[]{:S(2)}, u32[]{:S(2)}) %collective-permute-start) | collective-permute-done | bytes 1179680 | tf_op jit(solution)/shard_map/ppermute | solution.py:320
  34.4 2.8 %collective-permute-start.1 = (bf16[4,384,384]{2,1,0:T(8,128)(2,1)S(1)}, bf16[4,384,384]{2,1,0:T(8,128)(2,1)S(1)}, u32[]{:S(2)}, u32[]{:S(2)}) collective-permute-start(bf16[4,384,384]{2,1,0:T(8,128)(2,1)S(1)} %collective-permute-done.refs_2_), channel_id=1, source_target_pairs={{0,4},{2,6},{4,0},{6,2},{8,12},{10,14},{12,8},{14,10},{17,21},{19,... | collective-permute-start | bytes 3538952 | tf_op jit(solution)/shard_map/ppermute | solution.py:320
  37.3 2.9 %collective-permute-done.6.refs_1_ = bf16[4,384,384]{2,1,0:T(8,128)(2,1)S(1)} collective-permute-done((bf16[4,384,384]{2,1,0:T(8,128)(2,1)S(1)}, bf16[4,384,384]{2,1,0:T(8,128)(2,1)S(1)}, u32[]{:S(2)}, u32[]{:S(2)}) %collective-permute-start.6) | collective-permute-done | bytes 1179680 | tf_op jit(solution)/shard_map/ppermute | solution.py:320
  41.5 1.2 %collective-permute-done.8.refs_4_ = bf16[3,384,384]{2,1,0:T(8,128)(2,1)S(1)} collective-permute-done((bf16[3,384,384]{2,1,0:T(8,128)(2,1)S(1)}, bf16[3,384,384]{2,1,0:T(8,128)(2,1)S(1)}, u32[]{:S(2)}, u32[]{:S(2)}) %collective-permute-start.8) | collective-permute-done | bytes 884768 | tf_op jit(solution)/shard_map/ppermute | solution.py:310
  42.8 4.0 %early.1 = (f32[512,1152]{1,0:T(8,128)S(1)}, f32[512,768]{1,0:T(8,128)S(1)}, bf16[3,384,384]{2,1,0:T(8,128)(2,1)S(1)}, bf16[128,1536]{1,0:T(8,128)(2,1)S(1)}) custom-call(s32[4]{0:T(128)S(1)} %pad_add_fusion.spot_ref, bf16[512,1536]{1,0:T(8,128)(2,1)S(1)} %norm.1.own_rows_ref.refs_2_, bf16[512,1536]{1,0:T(8,128)(2,1)S(1)} %collective-permute-done.5.other_rows_ref.refs_3_, ...), custom_call_target="tpu_custom_call" | custom-call | tf_op jit(solution)/shard_map/early/pallas_call | solution.py:355
  46.8 6.0 %collective-permute-done.1.refs_8_ = bf16[4,384,384]{2,1,0:T(8,128)(2,1)S(1)} collective-permute-done((bf16[4,384,384]{2,1,0:T(8,128)(2,1)S(1)}, bf16[4,384,384]{2,1,0:T(8,128)(2,1)S(1)}, u32[]{:S(2)}, u32[]{:S(2)}) %collective-permute-start.1) | collective-permute-done | bytes 1179680 | tf_op jit(solution)/shard_map/ppermute | solution.py:320
  53.5 2.2 %collective-permute-done.13.refs_9_ = bf16[4,384,384]{2,1,0:T(8,128)(2,1)S(1)} collective-permute-done((bf16[4,384,384]{2,1,0:T(8,128)(2,1)S(1)}, bf16[4,384,384]{2,1,0:T(8,128)(2,1)S(1)}, u32[]{:S(2)}, u32[]{:S(2)}) %collective-permute-start.13) | collective-permute-done | bytes 1179680 | tf_op jit(solution)/shard_map/ppermute | solution.py:310
  55.7 3.4 %attend.1 = (bf16[128,768]{1,0:T(8,128)(2,1)S(1)}, bf16[128,768]{1,0:T(8,128)(2,1)S(1)}, f32[1,1024]{1,0:T(1,128)S(1)}, bf16[512,384]{1,0:T(8,128)(2,1)S(1)}, bf...) custom-call(s32[4]{0:T(128)S(1)} %pad_add_fusion.spot_ref, ...), custom_call_target="tpu_custom_call" | custom-call | tf_op jit(solution)/shard_map/attend/pallas_call | solution.py:379
  59.1 1.9 %collective-permute-start.18 = (bf16[128,768]{1,0:T(8,128)(2,1)S(1)}, bf16[128,768]{1,0:T(8,128)(2,1)S(1)}, u32[]{:S(2)}, u32[]{:S(2)}) collective-permute-start(bf16[128,768]{1,0:T(8,128)(2,1)S(1)} %get-tuple-element.44), channel_id=1, source_target_pairs={{0,2},{1,3},{2,0},{3,1},{4,6},{5,7},{6,4},{7,5},{8,10},{9,11},{10,... | collective-permute-start | bytes 589832 | tf_op jit(solution)/shard_map/ppermute | solution.py:310
  61.0 2.0 %attend_rest.1 = (f32[128,768]{1,0:T(8,128)S(1)}, bf16[128,768]{1,0:T(8,128)(2,1)S(1)}, bf16[128,768]{1,0:T(8,128)(2,1)S(1)}, f32[128,768]{1,0:T(8,128)S(1)}) custom-call(f32[1,1024]{1,0:T(1,128)S(1)} %get-tuple-element.33.bias_ref, bf16[512,384]{1,0:T(8,128)(2,1)S(1)} %get-tuple-element.34.query_ref, bf16[1024,384]{1,0:T(8,128)(2,1)S(1)} %get-tuple-element.35.key_ref, ...), custom_call_target="tpu_custom_call" | custom-call | tf_op jit(solution)/shard_map/attend_rest/pallas_call | solution.py:397
  63.0 2.1 %collective-permute-start.16 = (bf16[128,768]{1,0:T(8,128)(2,1)S(1)}, bf16[128,768]{1,0:T(8,128)(2,1)S(1)}, u32[]{:S(2)}, u32[]{:S(2)}) collective-permute-start(bf16[128,768]{1,0:T(8,128)(2,1)S(1)} %get-tuple-element.40), channel_id=1, source_target_pairs={{0,16},{16,0},{1,17},{17,1},{2,18},{18,2},{3,19},{19,3},{4,20},{20... | collective-permute-start | bytes 589832 | tf_op jit(solution)/shard_map/ppermute | solution.py:310
  65.3 1.0 %collective-permute-done.18 = bf16[128,768]{1,0:T(8,128)(2,1)S(1)} collective-permute-done((bf16[128,768]{1,0:T(8,128)(2,1)S(1)}, bf16[128,768]{1,0:T(8,128)(2,1)S(1)}, u32[]{:S(2)}, u32[]{:S(2)}) %collective-permute-start.18) | collective-permute-done | bytes 196640 | tf_op jit(solution)/shard_map/ppermute | solution.py:310
  66.3 2.4 %collective-permute-done.14 = bf16[128,768]{1,0:T(8,128)(2,1)S(1)} collective-permute-done((bf16[128,768]{1,0:T(8,128)(2,1)S(1)}, bf16[128,768]{1,0:T(8,128)(2,1)S(1)}, u32[]{:S(2)}, u32[]{:S(2)}) %collective-permute-start.14) | collective-permute-done | bytes 196640 | tf_op jit(solution)/shard_map/ppermute | solution.py:310
  69.1 1.3 %attend_own.1 = f32[128,1536]{1,0:T(8,128)S(1)} custom-call(bf16[384,1536]{1,0:T(8,128)(2,1)S(1)} %get-tuple-element.37.out_weight_ref, bf16[3,1024,256]{2,1,0:T(8,128)(2,1)S(1)} %get-tuple-element.36.value_ref, bf16[1024,384]{1,0:T(8,128)(2,1)S(1)} %get-tuple-element.35.key_ref, bf16[512,384]{1,0:T(8,128)(2,1)S(1)} %get-tuple-element.34.query_ref, ...), custom_call_target="tpu_custom_call" | custom-call | tf_op jit(solution)/shard_map/attend_own/pallas_call | solution.py:405
  70.3 2.6 %collective-permute-done.16 = bf16[128,768]{1,0:T(8,128)(2,1)S(1)} collective-permute-done((bf16[128,768]{1,0:T(8,128)(2,1)S(1)}, bf16[128,768]{1,0:T(8,128)(2,1)S(1)}, u32[]{:S(2)}, u32[]{:S(2)}) %collective-permute-start.16) | collective-permute-done | bytes 196640 | tf_op jit(solution)/shard_map/ppermute | solution.py:310
  73.0 3.1 %collective-permute-done.19 = bf16[128,768]{1,0:T(8,128)(2,1)S(1)} collective-permute-done((bf16[128,768]{1,0:T(8,128)(2,1)S(1)}, bf16[128,768]{1,0:T(8,128)(2,1)S(1)}, u32[]{:S(2)}, u32[]{:S(2)}) %collective-permute-start.19) | collective-permute-done | bytes 196640 | tf_op jit(solution)/shard_map/ppermute | solution.py:310
  (40 shorter events, 4.5 us)
Async XLA Ops:
  1.4 32.9 %collective-permute-start = (bf16[4,384,384]{2,1,0:T(8,128)(2,1)S(1)}, bf16[4,384,384]{2,1,0:T(8,128)(2,1)S(1)}, u32[]{:S(2)}, u32[]{:S(2)}) collective-permute-start(bf16[4,384,384]{2,1,0:T(8,128)(2,1)S(1)} %pad_maximum_fusion.refs_0_), channel_id=1, source_target_pairs={{0,8},{2,10},{4,12},{6,14},{8,0},{10,2},{12,4},{14,6},{17,25},{19,... | collective-permute-start | bytes 3538952 | tf_op jit(solution)/shard_map/ppermute | solution.py:320
  7.4 13.4 %collective-permute-start.2 = (bf16[128,1536]{1,0:T(8,128)(2,1)}, bf16[128,1536]{1,0:T(8,128)(2,1)}, u32[]{:S(2)}, u32[]{:S(2)}) collective-permute-start(bf16[128,1536]{1,0:T(8,128)(2,1)} %bitcast.7.refs_1_.refs_6_), channel_id=1, source_target_pairs={{0,18},{1,19},{2,16},{3,17},{16,2},{17,3},{18,0},{19,1},{4,22},{5,... | collective-permute-start | bytes 1179656 | tf_op jit(solution)/shard_map/ppermute | solution.py:340
  7.4 19.9 %collective-permute-start.3 = (bf16[128,1536]{1,0:T(8,128)(2,1)}, bf16[128,1536]{1,0:T(8,128)(2,1)}, u32[]{:S(2)}, u32[]{:S(2)}) collective-permute-start(bf16[128,1536]{1,0:T(8,128)(2,1)} %bitcast.7.refs_1_.refs_6_), channel_id=1, source_target_pairs={{0,2},{1,3},{2,0},{3,1},{4,6},{5,7},{6,4},{7,5},{8,10},{9,11},{10,... | collective-permute-start | bytes 1179656 | tf_op jit(solution)/shard_map/ppermute | solution.py:310
  9.0 18.4 %collective-permute-start.4 = (bf16[128,1536]{1,0:T(8,128)(2,1)}, bf16[128,1536]{1,0:T(8,128)(2,1)}, u32[]{:S(2)}, u32[]{:S(2)}) collective-permute-start(bf16[128,1536]{1,0:T(8,128)(2,1)} %bitcast.7.refs_1_.refs_6_), channel_id=1, source_target_pairs={{0,16},{16,0},{1,17},{17,1},{2,18},{18,2},{3,19},{19,3},{4,20},{20... | collective-permute-start | bytes 1179656 | tf_op jit(solution)/shard_map/ppermute | solution.py:310
  10.9 29.3 %collective-permute-start.6 = (bf16[4,384,384]{2,1,0:T(8,128)(2,1)S(1)}, bf16[4,384,384]{2,1,0:T(8,128)(2,1)S(1)}, u32[]{:S(2)}, u32[]{:S(2)}) collective-permute-start(bf16[4,384,384]{2,1,0:T(8,128)(2,1)S(1)} %pad_maximum_fusion.refs_0_), channel_id=1, source_target_pairs={{0,4},{2,6},{4,0},{6,2},{8,12},{10,14},{12,8},{14,10},{17,21},{19,... | collective-permute-start | bytes 3538952 | tf_op jit(solution)/shard_map/ppermute | solution.py:320
  27.4 0.7 copy-start
  28.1 2.9 %copy-start.2 = (bf16[384,3,384]{2,0,1:T(8,128)(2,1)S(1)}, bf16[384,3,384]{2,0,1:T(8,128)(2,1)}, u32[]{:S(2)}) copy-start(bf16[384,3,384]{2,0,1:T(8,128)(2,1)} %param.7) | copy-start | bytes 2654212
  30.8 10.2 %collective-permute-start.5 = (bf16[512,1536]{1,0:T(8,128)(2,1)S(1)}, bf16[512,1536]{1,0:T(8,128)(2,1)S(1)}, u32[]{:S(2)}, u32[]{:S(2)}) collective-permute-start(bf16[512,1536]{1,0:T(8,128)(2,1)S(1)} %norm.1.own_rows_ref.refs_2_), channel_id=1, source_target_pairs={{0,1},{1,0},{2,3},{3,2},{4,5},{5,4},{6,7},{7,6},{8,9},{9,8},{10,11... | collective-permute-start | bytes 4718600 | tf_op jit(solution)/shard_map/ppermute | solution.py:310
  31.0 9.4 %collective-permute-start.7 = (bf16[3,384,384]{2,1,0:T(8,128)(2,1)S(1)}, bf16[3,384,384]{2,1,0:T(8,128)(2,1)S(1)}, u32[]{:S(2)}, u32[]{:S(2)}) collective-permute-start(bf16[3,384,384]{2,1,0:T(8,128)(2,1)S(1)} %bitcast.14), channel_id=1, source_target_pairs={{0,1},{1,0},{2,3},{3,2},{4,5},{5,4},{6,7},{7,6},{8,9},{9,8},{10,11... | collective-permute-start | bytes 2654216 | tf_op jit(solution)/shard_map/ppermute | solution.py:310
  34.4 6.1 %copy-start.3 = (bf16[384,384]{1,0:T(8,128)(2,1)S(1)}, bf16[384,384]{1,0:T(8,128)(2,1)}, u32[]{:S(2)}) copy-start(bf16[384,384]{1,0:T(8,128)(2,1)} %param.8) | copy-start | bytes 884740
  34.4 6.7 %collective-permute-start.9 = (bf16[3,384,384]{2,1,0:T(8,128)(2,1)S(1)}, bf16[3,384,384]{2,1,0:T(8,128)(2,1)S(1)}, u32[]{:S(2)}, u32[]{:S(2)}) collective-permute-start(bf16[3,384,384]{2,1,0:T(8,128)(2,1)S(1)} %slice.34), channel_id=1, source_target_pairs={{0,1},{1,0},{2,3},{3,2},{4,5},{5,4},{6,7},{7,6},{8,9},{9,8},{10,11... | collective-permute-start | bytes 2654216 | tf_op jit(solution)/shard_map/ppermute | solution.py:310
  34.4 18.4 %collective-permute-start.1 = (bf16[4,384,384]{2,1,0:T(8,128)(2,1)S(1)}, bf16[4,384,384]{2,1,0:T(8,128)(2,1)S(1)}, u32[]{:S(2)}, u32[]{:S(2)}) collective-permute-start(bf16[4,384,384]{2,1,0:T(8,128)(2,1)S(1)} %collective-permute-done.refs_2_), channel_id=1, source_target_pairs={{0,4},{2,6},{4,0},{6,2},{8,12},{10,14},{12,8},{14,10},{17,21},{19,... | collective-permute-start | bytes 3538952 | tf_op jit(solution)/shard_map/ppermute | solution.py:320
  40.3 2.5 %collective-permute-start.8 = (bf16[3,384,384]{2,1,0:T(8,128)(2,1)S(1)}, bf16[3,384,384]{2,1,0:T(8,128)(2,1)S(1)}, u32[]{:S(2)}, u32[]{:S(2)}) collective-permute-start(bf16[3,384,384]{2,1,0:T(8,128)(2,1)S(1)} %slice.33), channel_id=1, source_target_pairs={{0,1},{1,0},{2,3},{3,2},{4,5},{5,4},{6,7},{7,6},{8,9},{9,8},{10,11... | collective-permute-start | bytes 2654216 | tf_op jit(solution)/shard_map/ppermute | solution.py:310
  40.5 6.3 %collective-permute-start.10 = (bf16[1,384,384]{2,1,0:T(8,128)(2,1)S(1)}, bf16[1,384,384]{2,1,0:T(8,128)(2,1)S(1)}, u32[]{:S(2)}, u32[]{:S(2)}) collective-permute-start(bf16[1,384,384]{2,1,0:T(8,128)(2,1)S(1)} %bitcast.16), channel_id=1, source_target_pairs={{0,1},{1,0},{2,3},{3,2},{4,5},{5,4},{6,7},{7,6},{8,9},{9,8},{10,11... | collective-permute-start | bytes 884744 | tf_op jit(solution)/shard_map/ppermute | solution.py:310
  41.0 5.8 %collective-permute-start.12 = (bf16[1,384,384]{2,1,0:T(8,128)(2,1)S(1)}, bf16[1,384,384]{2,1,0:T(8,128)(2,1)S(1)}, u32[]{:S(2)}, u32[]{:S(2)}) collective-permute-start(bf16[1,384,384]{2,1,0:T(8,128)(2,1)S(1)} %slice.36), channel_id=1, source_target_pairs={{0,1},{1,0},{2,3},{3,2},{4,5},{5,4},{6,7},{7,6},{8,9},{9,8},{10,11... | collective-permute-start | bytes 884744 | tf_op jit(solution)/shard_map/ppermute | solution.py:310
  41.1 5.7 %collective-permute-start.11 = (bf16[1,384,384]{2,1,0:T(8,128)(2,1)S(1)}, bf16[1,384,384]{2,1,0:T(8,128)(2,1)S(1)}, u32[]{:S(2)}, u32[]{:S(2)}) collective-permute-start(bf16[1,384,384]{2,1,0:T(8,128)(2,1)S(1)} %slice.35), channel_id=1, source_target_pairs={{0,1},{1,0},{2,3},{3,2},{4,5},{5,4},{6,7},{7,6},{8,9},{9,8},{10,11... | collective-permute-start | bytes 884744 | tf_op jit(solution)/shard_map/ppermute | solution.py:310
  52.8 2.8 %collective-permute-start.13 = (bf16[4,384,384]{2,1,0:T(8,128)(2,1)S(1)}, bf16[4,384,384]{2,1,0:T(8,128)(2,1)S(1)}, u32[]{:S(2)}, u32[]{:S(2)}) collective-permute-start(bf16[4,384,384]{2,1,0:T(8,128)(2,1)S(1)} %collective-permute-done.1.refs_8_), channel_id=1, source_target_pairs={{0,1},{1,0},{2,3},{3,2},{4,5},{5,4},{6,7},{7,6},{8,9},{9,8},{10,11... | collective-permute-start | bytes 3538952 | tf_op jit(solution)/shard_map/ppermute | solution.py:310
  59.1 7.1 %collective-permute-start.18 = (bf16[128,768]{1,0:T(8,128)(2,1)S(1)}, bf16[128,768]{1,0:T(8,128)(2,1)S(1)}, u32[]{:S(2)}, u32[]{:S(2)}) collective-permute-start(bf16[128,768]{1,0:T(8,128)(2,1)S(1)} %get-tuple-element.44), channel_id=1, source_target_pairs={{0,2},{1,3},{2,0},{3,1},{4,6},{5,7},{6,4},{7,5},{8,10},{9,11},{10,... | collective-permute-start | bytes 589832 | tf_op jit(solution)/shard_map/ppermute | solution.py:310
  61.0 7.8 %collective-permute-start.14 = (bf16[128,768]{1,0:T(8,128)(2,1)S(1)}, bf16[128,768]{1,0:T(8,128)(2,1)S(1)}, u32[]{:S(2)}, u32[]{:S(2)}) collective-permute-start(bf16[128,768]{1,0:T(8,128)(2,1)S(1)} %get-tuple-element.39), channel_id=1, source_target_pairs={{0,16},{16,0},{1,17},{17,1},{2,18},{18,2},{3,19},{19,3},{4,20},{20... | collective-permute-start | bytes 589832 | tf_op jit(solution)/shard_map/ppermute | solution.py:310
  63.0 6.1 %copy-start.1 = (f32[1,3,1536]{2,0,1:T(1,128)S(1)}, f32[1,3,1536]{2,0,1:T(1,128)}, u32[]{:S(2)}) copy-start(f32[1,3,1536]{2,0,1:T(1,128)} %param.6) | copy-start | bytes 55300
  63.0 10.0 %collective-permute-start.16 = (bf16[128,768]{1,0:T(8,128)(2,1)S(1)}, bf16[128,768]{1,0:T(8,128)(2,1)S(1)}, u32[]{:S(2)}, u32[]{:S(2)}) collective-permute-start(bf16[128,768]{1,0:T(8,128)(2,1)S(1)} %get-tuple-element.40), channel_id=1, source_target_pairs={{0,16},{16,0},{1,17},{17,1},{2,18},{18,2},{3,19},{19,3},{4,20},{20... | collective-permute-start | bytes 589832 | tf_op jit(solution)/shard_map/ppermute | solution.py:310
  65.1 7.9 %collective-permute-start.17 = (bf16[128,768]{1,0:T(8,128)(2,1)S(1)}, bf16[128,768]{1,0:T(8,128)(2,1)S(1)}, u32[]{:S(2)}, u32[]{:S(2)}) collective-permute-start(bf16[128,768]{1,0:T(8,128)(2,1)S(1)} %get-tuple-element.42), channel_id=1, source_target_pairs={{0,2},{1,3},{2,0},{3,1},{4,6},{5,7},{6,4},{7,5},{8,10},{9,11},{10,... | collective-permute-start | bytes 589832 | tf_op jit(solution)/shard_map/ppermute | solution.py:310
  66.3 9.8 %collective-permute-start.19 = (bf16[128,768]{1,0:T(8,128)(2,1)S(1)}, bf16[128,768]{1,0:T(8,128)(2,1)S(1)}, u32[]{:S(2)}, u32[]{:S(2)}) collective-permute-start(bf16[128,768]{1,0:T(8,128)(2,1)S(1)} %add_convert_fusion), channel_id=1, source_target_pairs={{0,16},{16,0},{1,17},{17,1},{2,18},{18,2},{3,19},{19,3},{4,20},{20... | collective-permute-start | bytes 589832 | tf_op jit(solution)/shard_map/ppermute | solution.py:310
  68.8 7.3 %collective-permute-start.15 = (bf16[128,768]{1,0:T(8,128)(2,1)S(1)}, bf16[128,768]{1,0:T(8,128)(2,1)S(1)}, u32[]{:S(2)}, u32[]{:S(2)}) collective-permute-start(bf16[128,768]{1,0:T(8,128)(2,1)S(1)} %add_convert_fusion.1), channel_id=1, source_target_pairs={{0,2},{1,3},{2,0},{3,1},{4,6},{5,7},{6,4},{7,5},{8,10},{9,11},{10,... | collective-permute-start | bytes 589832 | tf_op jit(solution)/shard_map/ppermute | solution.py:310

commit v10 on v9

--- a/solution.py
+++ b/solution.py
@@ -224,7 +224,7 @@
 
 def attend_kernel(spot_ref, len_ref, *refs):
     totals, rows_refs, out_here, out_sent, (here, sent) = refs[0:2], refs[2:4], refs[4], refs[5:8], refs[8:10]
-    left_ref, right_ref, bias_ref, query_ref, key_ref, value_ref, out_weight_ref = refs[10:17]
+    top_ref, bottom_ref, bias_ref, query_ref, key_ref, value_ref, out_weight_ref = refs[10:17]
     count, width = key_ref.shape
     depth = here.shape[1]
     z = spot_ref[2]
@@ -266,20 +266,21 @@
                 out_weight_ref[:, pl.ds(start, width)] = part[...]
 
     diagonal = project(query_ref[: step // 2, :], key_ref, value_ref, out_weight_ref, bias_ref[...])
-    middle = left_ref.shape[1]
-    left_ref[...] = diagonal[:, :middle].astype(jnp.bfloat16)
-    right_ref[...] = diagonal[:, middle:].astype(jnp.bfloat16)
+    middle = top_ref.shape[0]
+    top_ref[...] = diagonal[:middle].astype(jnp.bfloat16)
+    bottom_ref[...] = diagonal[middle:].astype(jnp.bfloat16)
 
 
 def attend_rest_kernel(bias_ref, query_ref, key_ref, value_ref, out_weight_ref, *out_refs):
-    y_left_ref, y_right_ref, x_left_ref, x_right_ref = out_refs
-    tile_len, middle = y_left_ref.shape
+    y_top_ref, y_bottom_ref, x_top_ref, x_bottom_ref = out_refs
+    middle = y_top_ref.shape[0]
+    tile_len = 2 * middle
     queries = query_ref[2 * tile_len :, :]
     part = project(queries, key_ref, value_ref, out_weight_ref, bias_ref[...])
-    y_left_ref[...] = part[:tile_len, :middle]
-    y_right_ref[...] = part[:tile_len, middle:].astype(jnp.bfloat16)
-    x_left_ref[...] = part[tile_len:, :middle].astype(jnp.bfloat16)
-    x_right_ref[...] = part[tile_len:, middle:]
+    y_top_ref[...] = part[:middle]
+    y_bottom_ref[...] = part[middle:tile_len].astype(jnp.bfloat16)
+    x_top_ref[...] = part[tile_len : tile_len + middle].astype(jnp.bfloat16)
+    x_bottom_ref[...] = part[tile_len + middle :]
 
 
 def attend_own_kernel(
@@ -374,9 +375,9 @@
     last, total_own, *out_sent = lax.optimization_barrier((last, total_own, *out_sent))
     last_sent = core_swap(last)
 
-    half = jax.ShapeDtypeStruct((tile_len, width // 2), jnp.bfloat16)
-    half_f32 = jax.ShapeDtypeStruct((tile_len, width // 2), jnp.float32)
-    xy_left, xy_right, *kept = pl.pallas_call(
+    half = jax.ShapeDtypeStruct((tile_len // 2, width), jnp.bfloat16)
+    half_f32 = jax.ShapeDtypeStruct((tile_len // 2, width), jnp.float32)
+    xy_top, xy_bottom, *kept = pl.pallas_call(
         attend_kernel,
         out_shape=(
             half,
@@ -392,9 +393,9 @@
         compiler_params=params,
         name="attend",
     )(spot, lengths, total_own, total_other, own_rows, other_rows, out_known, *out_sent, last, last_sent)
-    from_x = swap(xy_left, "patch", 1, 2)
-    from_y = swap(xy_right, "wcol", 2, 4)
-    y_left, y_right, x_left, x_right = pl.pallas_call(
+    from_x = swap(xy_top, "patch", 1, 2)
+    from_y = swap(xy_bottom, "wcol", 2, 4)
+    y_top, y_bottom, x_top, x_bottom = pl.pallas_call(
         attend_rest_kernel,
         out_shape=(half_f32, half, half, half_f32),
         in_specs=[full] * 5,
@@ -410,21 +411,16 @@
         compiler_params=params,
         name="attend_own",
     )(*kept[::-1], mod, states_kept)
-    got_x_left = swap(x_left, "patch", 1, 2)
-    got_y_right = swap(y_right, "wcol", 2, 4)
-    y_left = (y_left + from_x.astype(jnp.float32)).astype(jnp.bfloat16)
-    x_right = (x_right + from_y.astype(jnp.float32)).astype(jnp.bfloat16)
-    got_x_right = swap(x_right, "patch", 1, 2)
-    got_y_left = swap(y_left, "wcol", 2, 4)
-    middle = width // 2
-    updated = []
-    for columns, parts in (
-        (slice(0, middle), (got_x_left, got_y_left)),
-        (slice(middle, width), (got_x_right, got_y_right)),
-    ):
-        out_proj = parts[1].astype(jnp.float32) + parts[0].astype(jnp.float32)
-        updated.append((mod[2, :, columns] * out_proj + base[:, columns]).astype(jnp.bfloat16))
-    updated = jnp.concatenate(updated, axis=1)
+    got_x_top = swap(x_top, "patch", 1, 2)
+    got_y_bottom = swap(y_bottom, "wcol", 2, 4)
+    y_top = (y_top + from_x.astype(jnp.float32)).astype(jnp.bfloat16)
+    x_bottom = (x_bottom + from_y.astype(jnp.float32)).astype(jnp.bfloat16)
+    got_x_bottom = swap(x_bottom, "patch", 1, 2)
+    got_y_top = swap(y_top, "wcol", 2, 4)
+    from_x = jnp.concatenate([got_x_top, got_x_bottom], axis=0)
+    from_y = jnp.concatenate([got_y_top, got_y_bottom], axis=0)
+    out_proj = from_y.astype(jnp.float32) + from_x.astype(jnp.float32)
+    updated = (mod[2] * out_proj + base).astype(jnp.bfloat16)
     return updated[None]
 
 

time: 77.4 us -> 77.3 us (level)
  transfers between devices with their start and end apart: 20 -> 20, of which waited for: 11 -> 12; matrix products, arithmetic and copies ran while one was open for 1% -> 1% of each run, Pallas kernels for 13% -> 13%
where the time goes in v10:
time: 77.3 us; the launch traced here: 77 us
  waiting for transfers between devices  37.3 us (48%)
  starting transfers between devices  22 us (28%)
  Pallas kernels  13.3 us (17%)
  other arithmetic  2.44 us (3%)
  local copies, waits for them, and re-layouts  1 us (1%)
  between operations  0.87 us (1%)
    ppermute x16, waiting for transfers between devices, swap(): return lax.ppermute(array, axis, [(i, i ^ d) for i in range(n)])  19.3 us
    ppermute x3, starting transfers between devices, owners_swap(): return lax.ppermute(array, everywhere, pairs)  12.3 us
    ppermute x3, waiting for transfers between devices, owners_swap(): return lax.ppermute(array, everywhere, pairs)  11.8 us
    ppermute x16, starting transfers between devices, swap(): return lax.ppermute(array, axis, [(i, i ^ d) for i in range(n)])  9.67 us
    ppermute x1, waiting for transfers between devices, tiled_body(): along_xy = lax.ppermute(states, ('patch', 'wcol'), diagonal)  6.24 us
    pallas_call x1, Pallas kernels, tiled_body(): pl.pallas_call(early_kernel, out_shape=(jax.ShapeDtypeStruct((count // 2,...  4.01 us
    pallas_call x1, Pallas kernels, tiled_body(): pl.pallas_call(attend_kernel, out_shape=(half, half, jax.ShapeDtypeStruct...  3.4 us
    pallas_call x1, Pallas kernels, tiled_body(): pl.pallas_call(norm_kernel, out_shape=jax.ShapeDtypeStruct((count // 2, w...  2.71 us
  transfers between devices with their start and end apart: 20, of which 12 were waited for; matrix products, arithmetic and copies ran while one was open for 1% of the time, Pallas kernels for 13%

profile of v10, /device:TPU:0, one launch (start us, length us, event | category | flops | bytes accessed | tf_op | source)
XLA Modules:
  0.0 77.0 jit_solution(16507947087658307272)
XLA Ops:
  0.0 1.4 %pad_maximum_fusion.refs_0_ = bf16[4,384,384]{2,1,0:T(8,128)(2,1)S(1)} fusion(bf16[1,384,384]{2,1,0:T(8,128)(2,1)} %bitcast.14, bf16[3,384,384]{2,1,0:T(8,128)(2,1)} %bitcast.12), kind=kLoop, calls=%fused_computation | loop fusion | flops 589824 | bytes 2359296 | tf_op jit(solution)/shard_map/concatenate | solution.py:335
  1.4 5.9 %collective-permute-start = (bf16[4,384,384]{2,1,0:T(8,128)(2,1)S(1)}, bf16[4,384,384]{2,1,0:T(8,128)(2,1)S(1)}, u32[]{:S(2)}, u32[]{:S(2)}) collective-permute-start(bf16[4,384,384]{2,1,0:T(8,128)(2,1)S(1)} %pad_maximum_fusion.refs_0_), channel_id=1, source_target_pairs={{0,8},{2,10},{4,12},{6,14},{8,0},{10,2},{12,4},{14,6},{17,25},{19,... | collective-permute-start | bytes 3538952 | tf_op jit(solution)/shard_map/ppermute | solution.py:321
  7.4 1.6 %collective-permute-start.3 = (bf16[128,1536]{1,0:T(8,128)(2,1)}, bf16[128,1536]{1,0:T(8,128)(2,1)}, u32[]{:S(2)}, u32[]{:S(2)}) collective-permute-start(bf16[128,1536]{1,0:T(8,128)(2,1)} %bitcast.7.refs_1_.refs_6_), channel_id=1, source_target_pairs={{0,2},{1,3},{2,0},{3,1},{4,6},{5,7},{6,4},{7,5},{8,10},{9,11},{10,... | collective-permute-start | bytes 1179656 | tf_op jit(solution)/shard_map/ppermute | solution.py:311
  9.0 1.9 %collective-permute-start.4 = (bf16[128,1536]{1,0:T(8,128)(2,1)}, bf16[128,1536]{1,0:T(8,128)(2,1)}, u32[]{:S(2)}, u32[]{:S(2)}) collective-permute-start(bf16[128,1536]{1,0:T(8,128)(2,1)} %bitcast.7.refs_1_.refs_6_), channel_id=1, source_target_pairs={{0,16},{16,0},{1,17},{17,1},{2,18},{18,2},{3,19},{19,3},{4,20},{20... | collective-permute-start | bytes 1179656 | tf_op jit(solution)/shard_map/ppermute | solution.py:311
  10.9 3.5 %collective-permute-start.6 = (bf16[4,384,384]{2,1,0:T(8,128)(2,1)S(1)}, bf16[4,384,384]{2,1,0:T(8,128)(2,1)S(1)}, u32[]{:S(2)}, u32[]{:S(2)}) collective-permute-start(bf16[4,384,384]{2,1,0:T(8,128)(2,1)S(1)} %pad_maximum_fusion.refs_0_), channel_id=1, source_target_pairs={{0,4},{2,6},{4,0},{6,2},{8,12},{10,14},{12,8},{14,10},{17,21},{19,... | collective-permute-start | bytes 3538952 | tf_op jit(solution)/shard_map/ppermute | solution.py:321
  14.5 6.2 %collective-permute-done.2.refs_0_ = bf16[128,1536]{1,0:T(8,128)(2,1)} collective-permute-done((bf16[128,1536]{1,0:T(8,128)(2,1)}, bf16[128,1536]{1,0:T(8,128)(2,1)}, u32[]{:S(2)}, u32[]{:S(2)}) %collective-permute-start.2) | collective-permute-done | bytes 393248 | tf_op jit(solution)/shard_map/ppermute | solution.py:341
  20.7 6.6 %collective-permute-done.3.refs_2_ = bf16[128,1536]{1,0:T(8,128)(2,1)} collective-permute-done((bf16[128,1536]{1,0:T(8,128)(2,1)}, bf16[128,1536]{1,0:T(8,128)(2,1)}, u32[]{:S(2)}, u32[]{:S(2)}) %collective-permute-start.3) | collective-permute-done | bytes 393248 | tf_op jit(solution)/shard_map/ppermute | solution.py:311
  28.1 2.7 %norm.1.own_rows_ref.refs_2_ = bf16[512,1536]{1,0:T(8,128)(2,1)S(1)} custom-call(s32[4]{0:T(128)S(1)} %pad_add_fusion.spot_ref, f32[3,1,1536]{2,1,0:T(1,128)S(1)} %bitcast.10, bf16[128,1536]{1,0:T(8,128)(2,1)} %collective-permute-done.2.refs_0_, bf16[128,1536]{1,0:T(8,128)(2,1)} %bitcast.7.refs_1_.refs_6_, bf16[128,1536]{1,0:T(8,128)(2,1)} %collective-permute-done.3.refs_2_, ...), custom_call_target="tpu_custom_call" | custom-call | tf_op jit(solution)/shard_map/norm/pallas_call | solution.py:343
  31.4 2.9 %collective-permute-done.refs_2_ = bf16[4,384,384]{2,1,0:T(8,128)(2,1)S(1)} collective-permute-done((bf16[4,384,384]{2,1,0:T(8,128)(2,1)S(1)}, bf16[4,384,384]{2,1,0:T(8,128)(2,1)S(1)}, u32[]{:S(2)}, u32[]{:S(2)}) %collective-permute-start) | collective-permute-done | bytes 1179680 | tf_op jit(solution)/shard_map/ppermute | solution.py:321
  34.4 2.8 %collective-permute-start.1 = (bf16[4,384,384]{2,1,0:T(8,128)(2,1)S(1)}, bf16[4,384,384]{2,1,0:T(8,128)(2,1)S(1)}, u32[]{:S(2)}, u32[]{:S(2)}) collective-permute-start(bf16[4,384,384]{2,1,0:T(8,128)(2,1)S(1)} %collective-permute-done.refs_2_), channel_id=1, source_target_pairs={{0,4},{2,6},{4,0},{6,2},{8,12},{10,14},{12,8},{14,10},{17,21},{19,... | collective-permute-start | bytes 3538952 | tf_op jit(solution)/shard_map/ppermute | solution.py:321
  37.3 2.9 %collective-permute-done.6.refs_1_ = bf16[4,384,384]{2,1,0:T(8,128)(2,1)S(1)} collective-permute-done((bf16[4,384,384]{2,1,0:T(8,128)(2,1)S(1)}, bf16[4,384,384]{2,1,0:T(8,128)(2,1)S(1)}, u32[]{:S(2)}, u32[]{:S(2)}) %collective-permute-start.6) | collective-permute-done | bytes 1179680 | tf_op jit(solution)/shard_map/ppermute | solution.py:321
  41.5 1.2 %collective-permute-done.8.refs_4_ = bf16[3,384,384]{2,1,0:T(8,128)(2,1)S(1)} collective-permute-done((bf16[3,384,384]{2,1,0:T(8,128)(2,1)S(1)}, bf16[3,384,384]{2,1,0:T(8,128)(2,1)S(1)}, u32[]{:S(2)}, u32[]{:S(2)}) %collective-permute-start.8) | collective-permute-done | bytes 884768 | tf_op jit(solution)/shard_map/ppermute | solution.py:311
  42.8 4.0 %early.1 = (f32[512,1152]{1,0:T(8,128)S(1)}, f32[512,768]{1,0:T(8,128)S(1)}, bf16[3,384,384]{2,1,0:T(8,128)(2,1)S(1)}, bf16[128,1536]{1,0:T(8,128)(2,1)S(1)}) custom-call(s32[4]{0:T(128)S(1)} %pad_add_fusion.spot_ref, bf16[512,1536]{1,0:T(8,128)(2,1)S(1)} %norm.1.own_rows_ref.refs_2_, bf16[512,1536]{1,0:T(8,128)(2,1)S(1)} %collective-permute-done.5.other_rows_ref.refs_3_, ...), custom_call_target="tpu_custom_call" | custom-call | tf_op jit(solution)/shard_map/early/pallas_call | solution.py:356
  46.8 6.0 %collective-permute-done.1.refs_8_ = bf16[4,384,384]{2,1,0:T(8,128)(2,1)S(1)} collective-permute-done((bf16[4,384,384]{2,1,0:T(8,128)(2,1)S(1)}, bf16[4,384,384]{2,1,0:T(8,128)(2,1)S(1)}, u32[]{:S(2)}, u32[]{:S(2)}) %collective-permute-start.1) | collective-permute-done | bytes 1179680 | tf_op jit(solution)/shard_map/ppermute | solution.py:321
  53.5 2.2 %collective-permute-done.13.refs_9_ = bf16[4,384,384]{2,1,0:T(8,128)(2,1)S(1)} collective-permute-done((bf16[4,384,384]{2,1,0:T(8,128)(2,1)S(1)}, bf16[4,384,384]{2,1,0:T(8,128)(2,1)S(1)}, u32[]{:S(2)}, u32[]{:S(2)}) %collective-permute-start.13) | collective-permute-done | bytes 1179680 | tf_op jit(solution)/shard_map/ppermute | solution.py:311
  55.7 3.4 %attend.1 = (bf16[64,1536]{1,0:T(8,128)(2,1)S(1)}, bf16[64,1536]{1,0:T(8,128)(2,1)S(1)}, f32[1,1024]{1,0:T(1,128)S(1)}, bf16[512,384]{1,0:T(8,128)(2,1)S(1)}, bf...) custom-call(s32[4]{0:T(128)S(1)} %pad_add_fusion.spot_ref, ...), custom_call_target="tpu_custom_call" | custom-call | tf_op jit(solution)/shard_map/attend/pallas_call | solution.py:380
  59.1 1.9 %collective-permute-start.18 = (bf16[64,1536]{1,0:T(8,128)(2,1)S(1)}, bf16[64,1536]{1,0:T(8,128)(2,1)S(1)}, u32[]{:S(2)}, u32[]{:S(2)}) collective-permute-start(bf16[64,1536]{1,0:T(8,128)(2,1)S(1)} %get-tuple-element.43), channel_id=1, source_target_pairs={{0,2},{1,3},{2,0},{3,1},{4,6},{5,7},{6,4},{7,5},{8,10},{9,11},{10,... | collective-permute-start | bytes 589832 | tf_op jit(solution)/shard_map/ppermute | solution.py:311
  61.0 2.0 %attend_rest.1 = (f32[64,1536]{1,0:T(8,128)S(1)}, bf16[64,1536]{1,0:T(8,128)(2,1)S(1)}, bf16[64,1536]{1,0:T(8,128)(2,1)S(1)}, f32[64,1536]{1,0:T(8,128)S(1)}) custom-call(f32[1,1024]{1,0:T(1,128)S(1)} %get-tuple-element.33.bias_ref, bf16[512,384]{1,0:T(8,128)(2,1)S(1)} %get-tuple-element.34.query_ref, bf16[1024,384]{1,0:T(8,128)(2,1)S(1)} %get-tuple-element.35.key_ref, ...), custom_call_target="tpu_custom_call" | custom-call | tf_op jit(solution)/shard_map/attend_rest/pallas_call | solution.py:398
  63.2 2.0 %collective-permute-start.17 = (bf16[64,1536]{1,0:T(8,128)(2,1)S(1)}, bf16[64,1536]{1,0:T(8,128)(2,1)S(1)}, u32[]{:S(2)}, u32[]{:S(2)}) collective-permute-start(bf16[64,1536]{1,0:T(8,128)(2,1)S(1)} %get-tuple-element.41), channel_id=1, source_target_pairs={{0,16},{16,0},{1,17},{17,1},{2,18},{18,2},{3,19},{19,3},{4,20},{20... | collective-permute-start | bytes 589832 | tf_op jit(solution)/shard_map/ppermute | solution.py:311
  65.3 1.6 %collective-permute-done.18 = bf16[64,1536]{1,0:T(8,128)(2,1)S(1)} collective-permute-done((bf16[64,1536]{1,0:T(8,128)(2,1)S(1)}, bf16[64,1536]{1,0:T(8,128)(2,1)S(1)}, u32[]{:S(2)}, u32[]{:S(2)}) %collective-permute-start.18) | collective-permute-done | bytes 196640 | tf_op jit(solution)/shard_map/ppermute | solution.py:311
  67.0 1.8 %collective-permute-done.14 = bf16[64,1536]{1,0:T(8,128)(2,1)S(1)} collective-permute-done((bf16[64,1536]{1,0:T(8,128)(2,1)S(1)}, bf16[64,1536]{1,0:T(8,128)(2,1)S(1)}, u32[]{:S(2)}, u32[]{:S(2)}) %collective-permute-start.14) | collective-permute-done | bytes 196640 | tf_op jit(solution)/shard_map/ppermute | solution.py:311
  69.0 1.3 %attend_own.1 = f32[128,1536]{1,0:T(8,128)S(1)} custom-call(bf16[384,1536]{1,0:T(8,128)(2,1)S(1)} %get-tuple-element.37.out_weight_ref, bf16[3,1024,256]{2,1,0:T(8,128)(2,1)S(1)} %get-tuple-element.36.value_ref, bf16[1024,384]{1,0:T(8,128)(2,1)S(1)} %get-tuple-element.35.key_ref, bf16[512,384]{1,0:T(8,128)(2,1)S(1)} %get-tuple-element.34.query_ref, ...), custom_call_target="tpu_custom_call" | custom-call | tf_op jit(solution)/shard_map/attend_own/pallas_call | solution.py:406
  71.1 1.9 %collective-permute-done.17 = bf16[64,1536]{1,0:T(8,128)(2,1)S(1)} collective-permute-done((bf16[64,1536]{1,0:T(8,128)(2,1)S(1)}, bf16[64,1536]{1,0:T(8,128)(2,1)S(1)}, u32[]{:S(2)}, u32[]{:S(2)}) %collective-permute-start.17) | collective-permute-done | bytes 196640 | tf_op jit(solution)/shard_map/ppermute | solution.py:311
  73.0 3.1 %collective-permute-done.19 = bf16[64,1536]{1,0:T(8,128)(2,1)S(1)} collective-permute-done((bf16[64,1536]{1,0:T(8,128)(2,1)S(1)}, bf16[64,1536]{1,0:T(8,128)(2,1)S(1)}, u32[]{:S(2)}, u32[]{:S(2)}) %collective-permute-start.19) | collective-permute-done | bytes 196640 | tf_op jit(solution)/shard_map/ppermute | solution.py:311
  (39 shorter events, 5.2 us)
Async XLA Ops:
  1.4 32.9 %collective-permute-start = (bf16[4,384,384]{2,1,0:T(8,128)(2,1)S(1)}, bf16[4,384,384]{2,1,0:T(8,128)(2,1)S(1)}, u32[]{:S(2)}, u32[]{:S(2)}) collective-permute-start(bf16[4,384,384]{2,1,0:T(8,128)(2,1)S(1)} %pad_maximum_fusion.refs_0_), channel_id=1, source_target_pairs={{0,8},{2,10},{4,12},{6,14},{8,0},{10,2},{12,4},{14,6},{17,25},{19,... | collective-permute-start | bytes 3538952 | tf_op jit(solution)/shard_map/ppermute | solution.py:321
  7.4 13.4 %collective-permute-start.2 = (bf16[128,1536]{1,0:T(8,128)(2,1)}, bf16[128,1536]{1,0:T(8,128)(2,1)}, u32[]{:S(2)}, u32[]{:S(2)}) collective-permute-start(bf16[128,1536]{1,0:T(8,128)(2,1)} %bitcast.7.refs_1_.refs_6_), channel_id=1, source_target_pairs={{0,18},{1,19},{2,16},{3,17},{16,2},{17,3},{18,0},{19,1},{4,22},{5,... | collective-permute-start | bytes 1179656 | tf_op jit(solution)/shard_map/ppermute | solution.py:341
  7.4 19.9 %collective-permute-start.3 = (bf16[128,1536]{1,0:T(8,128)(2,1)}, bf16[128,1536]{1,0:T(8,128)(2,1)}, u32[]{:S(2)}, u32[]{:S(2)}) collective-permute-start(bf16[128,1536]{1,0:T(8,128)(2,1)} %bitcast.7.refs_1_.refs_6_), channel_id=1, source_target_pairs={{0,2},{1,3},{2,0},{3,1},{4,6},{5,7},{6,4},{7,5},{8,10},{9,11},{10,... | collective-permute-start | bytes 1179656 | tf_op jit(solution)/shard_map/ppermute | solution.py:311
  9.0 18.4 %collective-permute-start.4 = (bf16[128,1536]{1,0:T(8,128)(2,1)}, bf16[128,1536]{1,0:T(8,128)(2,1)}, u32[]{:S(2)}, u32[]{:S(2)}) collective-permute-start(bf16[128,1536]{1,0:T(8,128)(2,1)} %bitcast.7.refs_1_.refs_6_), channel_id=1, source_target_pairs={{0,16},{16,0},{1,17},{17,1},{2,18},{18,2},{3,19},{19,3},{4,20},{20... | collective-permute-start | bytes 1179656 | tf_op jit(solution)/shard_map/ppermute | solution.py:311
  10.9 29.3 %collective-permute-start.6 = (bf16[4,384,384]{2,1,0:T(8,128)(2,1)S(1)}, bf16[4,384,384]{2,1,0:T(8,128)(2,1)S(1)}, u32[]{:S(2)}, u32[]{:S(2)}) collective-permute-start(bf16[4,384,384]{2,1,0:T(8,128)(2,1)S(1)} %pad_maximum_fusion.refs_0_), channel_id=1, source_target_pairs={{0,4},{2,6},{4,0},{6,2},{8,12},{10,14},{12,8},{14,10},{17,21},{19,... | collective-permute-start | bytes 3538952 | tf_op jit(solution)/shard_map/ppermute | solution.py:321
  27.4 0.7 copy-start
  28.1 2.9 %copy-start.2 = (bf16[384,3,384]{2,0,1:T(8,128)(2,1)S(1)}, bf16[384,3,384]{2,0,1:T(8,128)(2,1)}, u32[]{:S(2)}) copy-start(bf16[384,3,384]{2,0,1:T(8,128)(2,1)} %param.7) | copy-start | bytes 2654212
  30.8 10.2 %collective-permute-start.5 = (bf16[512,1536]{1,0:T(8,128)(2,1)S(1)}, bf16[512,1536]{1,0:T(8,128)(2,1)S(1)}, u32[]{:S(2)}, u32[]{:S(2)}) collective-permute-start(bf16[512,1536]{1,0:T(8,128)(2,1)S(1)} %norm.1.own_rows_ref.refs_2_), channel_id=1, source_target_pairs={{0,1},{1,0},{2,3},{3,2},{4,5},{5,4},{6,7},{7,6},{8,9},{9,8},{10,11... | collective-permute-start | bytes 4718600 | tf_op jit(solution)/shard_map/ppermute | solution.py:311
  31.0 9.4 %collective-permute-start.7 = (bf16[3,384,384]{2,1,0:T(8,128)(2,1)S(1)}, bf16[3,384,384]{2,1,0:T(8,128)(2,1)S(1)}, u32[]{:S(2)}, u32[]{:S(2)}) collective-permute-start(bf16[3,384,384]{2,1,0:T(8,128)(2,1)S(1)} %bitcast.13), channel_id=1, source_target_pairs={{0,1},{1,0},{2,3},{3,2},{4,5},{5,4},{6,7},{7,6},{8,9},{9,8},{10,11... | collective-permute-start | bytes 2654216 | tf_op jit(solution)/shard_map/ppermute | solution.py:311
  34.4 6.1 %copy-start.3 = (bf16[384,384]{1,0:T(8,128)(2,1)S(1)}, bf16[384,384]{1,0:T(8,128)(2,1)}, u32[]{:S(2)}) copy-start(bf16[384,384]{1,0:T(8,128)(2,1)} %param.8) | copy-start | bytes 884740
  34.4 6.7 %collective-permute-start.9 = (bf16[3,384,384]{2,1,0:T(8,128)(2,1)S(1)}, bf16[3,384,384]{2,1,0:T(8,128)(2,1)S(1)}, u32[]{:S(2)}, u32[]{:S(2)}) collective-permute-start(bf16[3,384,384]{2,1,0:T(8,128)(2,1)S(1)} %slice.22), channel_id=1, source_target_pairs={{0,1},{1,0},{2,3},{3,2},{4,5},{5,4},{6,7},{7,6},{8,9},{9,8},{10,11... | collective-permute-start | bytes 2654216 | tf_op jit(solution)/shard_map/ppermute | solution.py:311
  34.4 18.4 %collective-permute-start.1 = (bf16[4,384,384]{2,1,0:T(8,128)(2,1)S(1)}, bf16[4,384,384]{2,1,0:T(8,128)(2,1)S(1)}, u32[]{:S(2)}, u32[]{:S(2)}) collective-permute-start(bf16[4,384,384]{2,1,0:T(8,128)(2,1)S(1)} %collective-permute-done.refs_2_), channel_id=1, source_target_pairs={{0,4},{2,6},{4,0},{6,2},{8,12},{10,14},{12,8},{14,10},{17,21},{19,... | collective-permute-start | bytes 3538952 | tf_op jit(solution)/shard_map/ppermute | solution.py:321
  40.3 2.5 %collective-permute-start.8 = (bf16[3,384,384]{2,1,0:T(8,128)(2,1)S(1)}, bf16[3,384,384]{2,1,0:T(8,128)(2,1)S(1)}, u32[]{:S(2)}, u32[]{:S(2)}) collective-permute-start(bf16[3,384,384]{2,1,0:T(8,128)(2,1)S(1)} %slice.21), channel_id=1, source_target_pairs={{0,1},{1,0},{2,3},{3,2},{4,5},{5,4},{6,7},{7,6},{8,9},{9,8},{10,11... | collective-permute-start | bytes 2654216 | tf_op jit(solution)/shard_map/ppermute | solution.py:311
  40.5 6.3 %collective-permute-start.10 = (bf16[1,384,384]{2,1,0:T(8,128)(2,1)S(1)}, bf16[1,384,384]{2,1,0:T(8,128)(2,1)S(1)}, u32[]{:S(2)}, u32[]{:S(2)}) collective-permute-start(bf16[1,384,384]{2,1,0:T(8,128)(2,1)S(1)} %bitcast.15), channel_id=1, source_target_pairs={{0,1},{1,0},{2,3},{3,2},{4,5},{5,4},{6,7},{7,6},{8,9},{9,8},{10,11... | collective-permute-start | bytes 884744 | tf_op jit(solution)/shard_map/ppermute | solution.py:311
  41.0 5.8 %collective-permute-start.12 = (bf16[1,384,384]{2,1,0:T(8,128)(2,1)S(1)}, bf16[1,384,384]{2,1,0:T(8,128)(2,1)S(1)}, u32[]{:S(2)}, u32[]{:S(2)}) collective-permute-start(bf16[1,384,384]{2,1,0:T(8,128)(2,1)S(1)} %slice.24), channel_id=1, source_target_pairs={{0,1},{1,0},{2,3},{3,2},{4,5},{5,4},{6,7},{7,6},{8,9},{9,8},{10,11... | collective-permute-start | bytes 884744 | tf_op jit(solution)/shard_map/ppermute | solution.py:311
  41.1 5.7 %collective-permute-start.11 = (bf16[1,384,384]{2,1,0:T(8,128)(2,1)S(1)}, bf16[1,384,384]{2,1,0:T(8,128)(2,1)S(1)}, u32[]{:S(2)}, u32[]{:S(2)}) collective-permute-start(bf16[1,384,384]{2,1,0:T(8,128)(2,1)S(1)} %slice.23), channel_id=1, source_target_pairs={{0,1},{1,0},{2,3},{3,2},{4,5},{5,4},{6,7},{7,6},{8,9},{9,8},{10,11... | collective-permute-start | bytes 884744 | tf_op jit(solution)/shard_map/ppermute | solution.py:311
  52.8 2.8 %collective-permute-start.13 = (bf16[4,384,384]{2,1,0:T(8,128)(2,1)S(1)}, bf16[4,384,384]{2,1,0:T(8,128)(2,1)S(1)}, u32[]{:S(2)}, u32[]{:S(2)}) collective-permute-start(bf16[4,384,384]{2,1,0:T(8,128)(2,1)S(1)} %collective-permute-done.1.refs_8_), channel_id=1, source_target_pairs={{0,1},{1,0},{2,3},{3,2},{4,5},{5,4},{6,7},{7,6},{8,9},{9,8},{10,11... | collective-permute-start | bytes 3538952 | tf_op jit(solution)/shard_map/ppermute | solution.py:311
  59.1 7.8 %collective-permute-start.18 = (bf16[64,1536]{1,0:T(8,128)(2,1)S(1)}, bf16[64,1536]{1,0:T(8,128)(2,1)S(1)}, u32[]{:S(2)}, u32[]{:S(2)}) collective-permute-start(bf16[64,1536]{1,0:T(8,128)(2,1)S(1)} %get-tuple-element.43), channel_id=1, source_target_pairs={{0,2},{1,3},{2,0},{3,1},{4,6},{5,7},{6,4},{7,5},{8,10},{9,11},{10,... | collective-permute-start | bytes 589832 | tf_op jit(solution)/shard_map/ppermute | solution.py:311
  61.0 7.8 %collective-permute-start.14 = (bf16[64,1536]{1,0:T(8,128)(2,1)S(1)}, bf16[64,1536]{1,0:T(8,128)(2,1)S(1)}, u32[]{:S(2)}, u32[]{:S(2)}) collective-permute-start(bf16[64,1536]{1,0:T(8,128)(2,1)S(1)} %get-tuple-element.39), channel_id=1, source_target_pairs={{0,16},{16,0},{1,17},{17,1},{2,18},{18,2},{3,19},{19,3},{4,20},{20... | collective-permute-start | bytes 589832 | tf_op jit(solution)/shard_map/ppermute | solution.py:311
  63.0 6.0 %copy-start.1 = (f32[1,3,1536]{2,0,1:T(1,128)S(1)}, f32[1,3,1536]{2,0,1:T(1,128)}, u32[]{:S(2)}) copy-start(f32[1,3,1536]{2,0,1:T(1,128)} %param.6) | copy-start | bytes 55300
  63.0 8.1 %collective-permute-start.16 = (bf16[64,1536]{1,0:T(8,128)(2,1)S(1)}, bf16[64,1536]{1,0:T(8,128)(2,1)S(1)}, u32[]{:S(2)}, u32[]{:S(2)}) collective-permute-start(bf16[64,1536]{1,0:T(8,128)(2,1)S(1)} %get-tuple-element.40), channel_id=1, source_target_pairs={{0,2},{1,3},{2,0},{3,1},{4,6},{5,7},{6,4},{7,5},{8,10},{9,11},{10,... | collective-permute-start | bytes 589832 | tf_op jit(solution)/shard_map/ppermute | solution.py:311
  63.2 9.8 %collective-permute-start.17 = (bf16[64,1536]{1,0:T(8,128)(2,1)S(1)}, bf16[64,1536]{1,0:T(8,128)(2,1)S(1)}, u32[]{:S(2)}, u32[]{:S(2)}) collective-permute-start(bf16[64,1536]{1,0:T(8,128)(2,1)S(1)} %get-tuple-element.41), channel_id=1, source_target_pairs={{0,16},{16,0},{1,17},{17,1},{2,18},{18,2},{3,19},{19,3},{4,20},{20... | collective-permute-start | bytes 589832 | tf_op jit(solution)/shard_map/ppermute | solution.py:311
  66.9 9.2 %collective-permute-start.19 = (bf16[64,1536]{1,0:T(8,128)(2,1)S(1)}, bf16[64,1536]{1,0:T(8,128)(2,1)S(1)}, u32[]{:S(2)}, u32[]{:S(2)}) collective-permute-start(bf16[64,1536]{1,0:T(8,128)(2,1)S(1)} %add_convert_fusion.1), channel_id=1, source_target_pairs={{0,16},{16,0},{1,17},{17,1},{2,18},{18,2},{3,19},{19,3},{4,20},{20... | collective-permute-start | bytes 589832 | tf_op jit(solution)/shard_map/ppermute | solution.py:311
  68.8 7.3 %collective-permute-start.15 = (bf16[64,1536]{1,0:T(8,128)(2,1)S(1)}, bf16[64,1536]{1,0:T(8,128)(2,1)S(1)}, u32[]{:S(2)}, u32[]{:S(2)}) collective-permute-start(bf16[64,1536]{1,0:T(8,128)(2,1)S(1)} %add_convert_fusion.2), channel_id=1, source_target_pairs={{0,2},{1,3},{2,0},{3,1},{4,6},{5,7},{6,4},{7,5},{8,10},{9,11},{10,... | collective-permute-start | bytes 589832 | tf_op jit(solution)/shard_map/ppermute | solution.py:311

commit v11 on v10

--- a/solution.py
+++ b/solution.py
@@ -215,7 +215,7 @@
         peak = jnp.max(scores, axis=-1, keepdims=True)
         probs = jnp.exp2((scores - peak) * rate).astype(jnp.bfloat16)
         sums = jnp.dot(probs, value_ref[h], preferred_element_type=jnp.float32)
-        heads.append((sums[:, :HD] / sums[:, HD:]).astype(jnp.bfloat16))
+        heads.append((sums[:, :HD] * (1.0 / sums[:, HD:])).astype(jnp.bfloat16))
     part = jnp.dot(
         jnp.concatenate(heads, axis=1), out_weight_ref[...], preferred_element_type=jnp.float32
     )

time: 77.3 us -> 77.3 us (level)
  no operation moved by 1% of the time
where the time goes in v11:
time: 77.3 us; the launch traced here: 77 us
  waiting for transfers between devices  37.3 us (48%)
  starting transfers between devices  22 us (28%)
  Pallas kernels  13.3 us (17%)
  other arithmetic  2.44 us (3%)
  local copies, waits for them, and re-layouts  1 us (1%)
  between operations  0.87 us (1%)
    ppermute x16, waiting for transfers between devices, swap(): return lax.ppermute(array, axis, [(i, i ^ d) for i in range(n)])  19.3 us
    ppermute x3, starting transfers between devices, owners_swap(): return lax.ppermute(array, everywhere, pairs)  12.3 us
    ppermute x3, waiting for transfers between devices, owners_swap(): return lax.ppermute(array, everywhere, pairs)  11.8 us
    ppermute x16, starting transfers between devices, swap(): return lax.ppermute(array, axis, [(i, i ^ d) for i in range(n)])  9.67 us
    ppermute x1, waiting for transfers between devices, tiled_body(): along_xy = lax.ppermute(states, ('patch', 'wcol'), diagonal)  6.24 us
    pallas_call x1, Pallas kernels, tiled_body(): pl.pallas_call(early_kernel, out_shape=(jax.ShapeDtypeStruct((count // 2,...  4.01 us
    pallas_call x1, Pallas kernels, tiled_body(): pl.pallas_call(attend_kernel, out_shape=(half, half, jax.ShapeDtypeStruct...  3.4 us
    pallas_call x1, Pallas kernels, tiled_body(): pl.pallas_call(norm_kernel, out_shape=jax.ShapeDtypeStruct((count // 2, w...  2.71 us
  transfers between devices with their start and end apart: 20, of which 12 were waited for; matrix products, arithmetic and copies ran while one was open for 1% of the time, Pallas kernels for 13%

profile of v11, /device:TPU:0, one launch (start us, length us, event | category | flops | bytes accessed | tf_op | source)
XLA Modules:
  0.0 77.0 jit_solution(16507947087658307272)
XLA Ops:
  0.0 1.4 %pad_maximum_fusion.refs_0_ = bf16[4,384,384]{2,1,0:T(8,128)(2,1)S(1)} fusion(bf16[1,384,384]{2,1,0:T(8,128)(2,1)} %bitcast.14, bf16[3,384,384]{2,1,0:T(8,128)(2,1)} %bitcast.12), kind=kLoop, calls=%fused_computation | loop fusion | flops 589824 | bytes 2359296 | tf_op jit(solution)/shard_map/concatenate | solution.py:335
  1.4 5.9 %collective-permute-start = (bf16[4,384,384]{2,1,0:T(8,128)(2,1)S(1)}, bf16[4,384,384]{2,1,0:T(8,128)(2,1)S(1)}, u32[]{:S(2)}, u32[]{:S(2)}) collective-permute-start(bf16[4,384,384]{2,1,0:T(8,128)(2,1)S(1)} %pad_maximum_fusion.refs_0_), channel_id=1, source_target_pairs={{0,8},{2,10},{4,12},{6,14},{8,0},{10,2},{12,4},{14,6},{17,25},{19,... | collective-permute-start | bytes 3538952 | tf_op jit(solution)/shard_map/ppermute | solution.py:321
  7.4 1.6 %collective-permute-start.3 = (bf16[128,1536]{1,0:T(8,128)(2,1)}, bf16[128,1536]{1,0:T(8,128)(2,1)}, u32[]{:S(2)}, u32[]{:S(2)}) collective-permute-start(bf16[128,1536]{1,0:T(8,128)(2,1)} %bitcast.7.refs_1_.refs_6_), channel_id=1, source_target_pairs={{0,2},{1,3},{2,0},{3,1},{4,6},{5,7},{6,4},{7,5},{8,10},{9,11},{10,... | collective-permute-start | bytes 1179656 | tf_op jit(solution)/shard_map/ppermute | solution.py:311
  9.0 1.9 %collective-permute-start.4 = (bf16[128,1536]{1,0:T(8,128)(2,1)}, bf16[128,1536]{1,0:T(8,128)(2,1)}, u32[]{:S(2)}, u32[]{:S(2)}) collective-permute-start(bf16[128,1536]{1,0:T(8,128)(2,1)} %bitcast.7.refs_1_.refs_6_), channel_id=1, source_target_pairs={{0,16},{16,0},{1,17},{17,1},{2,18},{18,2},{3,19},{19,3},{4,20},{20... | collective-permute-start | bytes 1179656 | tf_op jit(solution)/shard_map/ppermute | solution.py:311
  10.9 3.5 %collective-permute-start.6 = (bf16[4,384,384]{2,1,0:T(8,128)(2,1)S(1)}, bf16[4,384,384]{2,1,0:T(8,128)(2,1)S(1)}, u32[]{:S(2)}, u32[]{:S(2)}) collective-permute-start(bf16[4,384,384]{2,1,0:T(8,128)(2,1)S(1)} %pad_maximum_fusion.refs_0_), channel_id=1, source_target_pairs={{0,4},{2,6},{4,0},{6,2},{8,12},{10,14},{12,8},{14,10},{17,21},{19,... | collective-permute-start | bytes 3538952 | tf_op jit(solution)/shard_map/ppermute | solution.py:321
  14.5 6.2 %collective-permute-done.2.refs_0_ = bf16[128,1536]{1,0:T(8,128)(2,1)} collective-permute-done((bf16[128,1536]{1,0:T(8,128)(2,1)}, bf16[128,1536]{1,0:T(8,128)(2,1)}, u32[]{:S(2)}, u32[]{:S(2)}) %collective-permute-start.2) | collective-permute-done | bytes 393248 | tf_op jit(solution)/shard_map/ppermute | solution.py:341
  20.7 6.6 %collective-permute-done.3.refs_2_ = bf16[128,1536]{1,0:T(8,128)(2,1)} collective-permute-done((bf16[128,1536]{1,0:T(8,128)(2,1)}, bf16[128,1536]{1,0:T(8,128)(2,1)}, u32[]{:S(2)}, u32[]{:S(2)}) %collective-permute-start.3) | collective-permute-done | bytes 393248 | tf_op jit(solution)/shard_map/ppermute | solution.py:311
  28.1 2.7 %norm.1.own_rows_ref.refs_2_ = bf16[512,1536]{1,0:T(8,128)(2,1)S(1)} custom-call(s32[4]{0:T(128)S(1)} %pad_add_fusion.spot_ref, f32[3,1,1536]{2,1,0:T(1,128)S(1)} %bitcast.10, bf16[128,1536]{1,0:T(8,128)(2,1)} %collective-permute-done.2.refs_0_, bf16[128,1536]{1,0:T(8,128)(2,1)} %bitcast.7.refs_1_.refs_6_, bf16[128,1536]{1,0:T(8,128)(2,1)} %collective-permute-done.3.refs_2_, ...), custom_call_target="tpu_custom_call" | custom-call | tf_op jit(solution)/shard_map/norm/pallas_call | solution.py:343
  31.4 2.9 %collective-permute-done.refs_2_ = bf16[4,384,384]{2,1,0:T(8,128)(2,1)S(1)} collective-permute-done((bf16[4,384,384]{2,1,0:T(8,128)(2,1)S(1)}, bf16[4,384,384]{2,1,0:T(8,128)(2,1)S(1)}, u32[]{:S(2)}, u32[]{:S(2)}) %collective-permute-start) | collective-permute-done | bytes 1179680 | tf_op jit(solution)/shard_map/ppermute | solution.py:321
  34.4 2.8 %collective-permute-start.1 = (bf16[4,384,384]{2,1,0:T(8,128)(2,1)S(1)}, bf16[4,384,384]{2,1,0:T(8,128)(2,1)S(1)}, u32[]{:S(2)}, u32[]{:S(2)}) collective-permute-start(bf16[4,384,384]{2,1,0:T(8,128)(2,1)S(1)} %collective-permute-done.refs_2_), channel_id=1, source_target_pairs={{0,4},{2,6},{4,0},{6,2},{8,12},{10,14},{12,8},{14,10},{17,21},{19,... | collective-permute-start | bytes 3538952 | tf_op jit(solution)/shard_map/ppermute | solution.py:321
  37.3 2.9 %collective-permute-done.6.refs_1_ = bf16[4,384,384]{2,1,0:T(8,128)(2,1)S(1)} collective-permute-done((bf16[4,384,384]{2,1,0:T(8,128)(2,1)S(1)}, bf16[4,384,384]{2,1,0:T(8,128)(2,1)S(1)}, u32[]{:S(2)}, u32[]{:S(2)}) %collective-permute-start.6) | collective-permute-done | bytes 1179680 | tf_op jit(solution)/shard_map/ppermute | solution.py:321
  41.5 1.2 %collective-permute-done.8.refs_4_ = bf16[3,384,384]{2,1,0:T(8,128)(2,1)S(1)} collective-permute-done((bf16[3,384,384]{2,1,0:T(8,128)(2,1)S(1)}, bf16[3,384,384]{2,1,0:T(8,128)(2,1)S(1)}, u32[]{:S(2)}, u32[]{:S(2)}) %collective-permute-start.8) | collective-permute-done | bytes 884768 | tf_op jit(solution)/shard_map/ppermute | solution.py:311
  42.8 4.0 %early.1 = (f32[512,1152]{1,0:T(8,128)S(1)}, f32[512,768]{1,0:T(8,128)S(1)}, bf16[3,384,384]{2,1,0:T(8,128)(2,1)S(1)}, bf16[128,1536]{1,0:T(8,128)(2,1)S(1)}) custom-call(s32[4]{0:T(128)S(1)} %pad_add_fusion.spot_ref, bf16[512,1536]{1,0:T(8,128)(2,1)S(1)} %norm.1.own_rows_ref.refs_2_, bf16[512,1536]{1,0:T(8,128)(2,1)S(1)} %collective-permute-done.5.other_rows_ref.refs_3_, ...), custom_call_target="tpu_custom_call" | custom-call | tf_op jit(solution)/shard_map/early/pallas_call | solution.py:356
  46.8 6.0 %collective-permute-done.1.refs_8_ = bf16[4,384,384]{2,1,0:T(8,128)(2,1)S(1)} collective-permute-done((bf16[4,384,384]{2,1,0:T(8,128)(2,1)S(1)}, bf16[4,384,384]{2,1,0:T(8,128)(2,1)S(1)}, u32[]{:S(2)}, u32[]{:S(2)}) %collective-permute-start.1) | collective-permute-done | bytes 1179680 | tf_op jit(solution)/shard_map/ppermute | solution.py:321
  53.5 2.2 %collective-permute-done.13.refs_9_ = bf16[4,384,384]{2,1,0:T(8,128)(2,1)S(1)} collective-permute-done((bf16[4,384,384]{2,1,0:T(8,128)(2,1)S(1)}, bf16[4,384,384]{2,1,0:T(8,128)(2,1)S(1)}, u32[]{:S(2)}, u32[]{:S(2)}) %collective-permute-start.13) | collective-permute-done | bytes 1179680 | tf_op jit(solution)/shard_map/ppermute | solution.py:311
  55.7 3.4 %attend.1 = (bf16[64,1536]{1,0:T(8,128)(2,1)S(1)}, bf16[64,1536]{1,0:T(8,128)(2,1)S(1)}, f32[1,1024]{1,0:T(1,128)S(1)}, bf16[512,384]{1,0:T(8,128)(2,1)S(1)}, bf...) custom-call(s32[4]{0:T(128)S(1)} %pad_add_fusion.spot_ref, ...), custom_call_target="tpu_custom_call" | custom-call | tf_op jit(solution)/shard_map/attend/pallas_call | solution.py:380
  59.1 1.9 %collective-permute-start.18 = (bf16[64,1536]{1,0:T(8,128)(2,1)S(1)}, bf16[64,1536]{1,0:T(8,128)(2,1)S(1)}, u32[]{:S(2)}, u32[]{:S(2)}) collective-permute-start(bf16[64,1536]{1,0:T(8,128)(2,1)S(1)} %get-tuple-element.43), channel_id=1, source_target_pairs={{0,2},{1,3},{2,0},{3,1},{4,6},{5,7},{6,4},{7,5},{8,10},{9,11},{10,... | collective-permute-start | bytes 589832 | tf_op jit(solution)/shard_map/ppermute | solution.py:311
  61.0 2.0 %attend_rest.1 = (f32[64,1536]{1,0:T(8,128)S(1)}, bf16[64,1536]{1,0:T(8,128)(2,1)S(1)}, bf16[64,1536]{1,0:T(8,128)(2,1)S(1)}, f32[64,1536]{1,0:T(8,128)S(1)}) custom-call(f32[1,1024]{1,0:T(1,128)S(1)} %get-tuple-element.33.bias_ref, bf16[512,384]{1,0:T(8,128)(2,1)S(1)} %get-tuple-element.34.query_ref, bf16[1024,384]{1,0:T(8,128)(2,1)S(1)} %get-tuple-element.35.key_ref, ...), custom_call_target="tpu_custom_call" | custom-call | tf_op jit(solution)/shard_map/attend_rest/pallas_call | solution.py:398
  63.2 2.0 %collective-permute-start.17 = (bf16[64,1536]{1,0:T(8,128)(2,1)S(1)}, bf16[64,1536]{1,0:T(8,128)(2,1)S(1)}, u32[]{:S(2)}, u32[]{:S(2)}) collective-permute-start(bf16[64,1536]{1,0:T(8,128)(2,1)S(1)} %get-tuple-element.41), channel_id=1, source_target_pairs={{0,16},{16,0},{1,17},{17,1},{2,18},{18,2},{3,19},{19,3},{4,20},{20... | collective-permute-start | bytes 589832 | tf_op jit(solution)/shard_map/ppermute | solution.py:311
  65.3 1.6 %collective-permute-done.18 = bf16[64,1536]{1,0:T(8,128)(2,1)S(1)} collective-permute-done((bf16[64,1536]{1,0:T(8,128)(2,1)S(1)}, bf16[64,1536]{1,0:T(8,128)(2,1)S(1)}, u32[]{:S(2)}, u32[]{:S(2)}) %collective-permute-start.18) | collective-permute-done | bytes 196640 | tf_op jit(solution)/shard_map/ppermute | solution.py:311
  67.0 1.8 %collective-permute-done.14 = bf16[64,1536]{1,0:T(8,128)(2,1)S(1)} collective-permute-done((bf16[64,1536]{1,0:T(8,128)(2,1)S(1)}, bf16[64,1536]{1,0:T(8,128)(2,1)S(1)}, u32[]{:S(2)}, u32[]{:S(2)}) %collective-permute-start.14) | collective-permute-done | bytes 196640 | tf_op jit(solution)/shard_map/ppermute | solution.py:311
  69.0 1.3 %attend_own.1 = f32[128,1536]{1,0:T(8,128)S(1)} custom-call(bf16[384,1536]{1,0:T(8,128)(2,1)S(1)} %get-tuple-element.37.out_weight_ref, bf16[3,1024,256]{2,1,0:T(8,128)(2,1)S(1)} %get-tuple-element.36.value_ref, bf16[1024,384]{1,0:T(8,128)(2,1)S(1)} %get-tuple-element.35.key_ref, bf16[512,384]{1,0:T(8,128)(2,1)S(1)} %get-tuple-element.34.query_ref, ...), custom_call_target="tpu_custom_call" | custom-call | tf_op jit(solution)/shard_map/attend_own/pallas_call | solution.py:406
  71.1 1.9 %collective-permute-done.17 = bf16[64,1536]{1,0:T(8,128)(2,1)S(1)} collective-permute-done((bf16[64,1536]{1,0:T(8,128)(2,1)S(1)}, bf16[64,1536]{1,0:T(8,128)(2,1)S(1)}, u32[]{:S(2)}, u32[]{:S(2)}) %collective-permute-start.17) | collective-permute-done | bytes 196640 | tf_op jit(solution)/shard_map/ppermute | solution.py:311
  73.0 3.1 %collective-permute-done.19 = bf16[64,1536]{1,0:T(8,128)(2,1)S(1)} collective-permute-done((bf16[64,1536]{1,0:T(8,128)(2,1)S(1)}, bf16[64,1536]{1,0:T(8,128)(2,1)S(1)}, u32[]{:S(2)}, u32[]{:S(2)}) %collective-permute-start.19) | collective-permute-done | bytes 196640 | tf_op jit(solution)/shard_map/ppermute | solution.py:311
  (39 shorter events, 5.2 us)
Async XLA Ops:
  1.4 32.9 %collective-permute-start = (bf16[4,384,384]{2,1,0:T(8,128)(2,1)S(1)}, bf16[4,384,384]{2,1,0:T(8,128)(2,1)S(1)}, u32[]{:S(2)}, u32[]{:S(2)}) collective-permute-start(bf16[4,384,384]{2,1,0:T(8,128)(2,1)S(1)} %pad_maximum_fusion.refs_0_), channel_id=1, source_target_pairs={{0,8},{2,10},{4,12},{6,14},{8,0},{10,2},{12,4},{14,6},{17,25},{19,... | collective-permute-start | bytes 3538952 | tf_op jit(solution)/shard_map/ppermute | solution.py:321
  7.4 13.4 %collective-permute-start.2 = (bf16[128,1536]{1,0:T(8,128)(2,1)}, bf16[128,1536]{1,0:T(8,128)(2,1)}, u32[]{:S(2)}, u32[]{:S(2)}) collective-permute-start(bf16[128,1536]{1,0:T(8,128)(2,1)} %bitcast.7.refs_1_.refs_6_), channel_id=1, source_target_pairs={{0,18},{1,19},{2,16},{3,17},{16,2},{17,3},{18,0},{19,1},{4,22},{5,... | collective-permute-start | bytes 1179656 | tf_op jit(solution)/shard_map/ppermute | solution.py:341
  7.4 19.9 %collective-permute-start.3 = (bf16[128,1536]{1,0:T(8,128)(2,1)}, bf16[128,1536]{1,0:T(8,128)(2,1)}, u32[]{:S(2)}, u32[]{:S(2)}) collective-permute-start(bf16[128,1536]{1,0:T(8,128)(2,1)} %bitcast.7.refs_1_.refs_6_), channel_id=1, source_target_pairs={{0,2},{1,3},{2,0},{3,1},{4,6},{5,7},{6,4},{7,5},{8,10},{9,11},{10,... | collective-permute-start | bytes 1179656 | tf_op jit(solution)/shard_map/ppermute | solution.py:311
  9.0 18.4 %collective-permute-start.4 = (bf16[128,1536]{1,0:T(8,128)(2,1)}, bf16[128,1536]{1,0:T(8,128)(2,1)}, u32[]{:S(2)}, u32[]{:S(2)}) collective-permute-start(bf16[128,1536]{1,0:T(8,128)(2,1)} %bitcast.7.refs_1_.refs_6_), channel_id=1, source_target_pairs={{0,16},{16,0},{1,17},{17,1},{2,18},{18,2},{3,19},{19,3},{4,20},{20... | collective-permute-start | bytes 1179656 | tf_op jit(solution)/shard_map/ppermute | solution.py:311
  10.9 29.3 %collective-permute-start.6 = (bf16[4,384,384]{2,1,0:T(8,128)(2,1)S(1)}, bf16[4,384,384]{2,1,0:T(8,128)(2,1)S(1)}, u32[]{:S(2)}, u32[]{:S(2)}) collective-permute-start(bf16[4,384,384]{2,1,0:T(8,128)(2,1)S(1)} %pad_maximum_fusion.refs_0_), channel_id=1, source_target_pairs={{0,4},{2,6},{4,0},{6,2},{8,12},{10,14},{12,8},{14,10},{17,21},{19,... | collective-permute-start | bytes 3538952 | tf_op jit(solution)/shard_map/ppermute | solution.py:321
  27.4 0.7 copy-start
  28.1 2.9 %copy-start.2 = (bf16[384,3,384]{2,0,1:T(8,128)(2,1)S(1)}, bf16[384,3,384]{2,0,1:T(8,128)(2,1)}, u32[]{:S(2)}) copy-start(bf16[384,3,384]{2,0,1:T(8,128)(2,1)} %param.7) | copy-start | bytes 2654212
  30.8 10.2 %collective-permute-start.5 = (bf16[512,1536]{1,0:T(8,128)(2,1)S(1)}, bf16[512,1536]{1,0:T(8,128)(2,1)S(1)}, u32[]{:S(2)}, u32[]{:S(2)}) collective-permute-start(bf16[512,1536]{1,0:T(8,128)(2,1)S(1)} %norm.1.own_rows_ref.refs_2_), channel_id=1, source_target_pairs={{0,1},{1,0},{2,3},{3,2},{4,5},{5,4},{6,7},{7,6},{8,9},{9,8},{10,11... | collective-permute-start | bytes 4718600 | tf_op jit(solution)/shard_map/ppermute | solution.py:311
  31.0 9.4 %collective-permute-start.7 = (bf16[3,384,384]{2,1,0:T(8,128)(2,1)S(1)}, bf16[3,384,384]{2,1,0:T(8,128)(2,1)S(1)}, u32[]{:S(2)}, u32[]{:S(2)}) collective-permute-start(bf16[3,384,384]{2,1,0:T(8,128)(2,1)S(1)} %bitcast.13), channel_id=1, source_target_pairs={{0,1},{1,0},{2,3},{3,2},{4,5},{5,4},{6,7},{7,6},{8,9},{9,8},{10,11... | collective-permute-start | bytes 2654216 | tf_op jit(solution)/shard_map/ppermute | solution.py:311
  34.4 6.1 %copy-start.3 = (bf16[384,384]{1,0:T(8,128)(2,1)S(1)}, bf16[384,384]{1,0:T(8,128)(2,1)}, u32[]{:S(2)}) copy-start(bf16[384,384]{1,0:T(8,128)(2,1)} %param.8) | copy-start | bytes 884740
  34.4 6.7 %collective-permute-start.9 = (bf16[3,384,384]{2,1,0:T(8,128)(2,1)S(1)}, bf16[3,384,384]{2,1,0:T(8,128)(2,1)S(1)}, u32[]{:S(2)}, u32[]{:S(2)}) collective-permute-start(bf16[3,384,384]{2,1,0:T(8,128)(2,1)S(1)} %slice.22), channel_id=1, source_target_pairs={{0,1},{1,0},{2,3},{3,2},{4,5},{5,4},{6,7},{7,6},{8,9},{9,8},{10,11... | collective-permute-start | bytes 2654216 | tf_op jit(solution)/shard_map/ppermute | solution.py:311
  34.4 18.4 %collective-permute-start.1 = (bf16[4,384,384]{2,1,0:T(8,128)(2,1)S(1)}, bf16[4,384,384]{2,1,0:T(8,128)(2,1)S(1)}, u32[]{:S(2)}, u32[]{:S(2)}) collective-permute-start(bf16[4,384,384]{2,1,0:T(8,128)(2,1)S(1)} %collective-permute-done.refs_2_), channel_id=1, source_target_pairs={{0,4},{2,6},{4,0},{6,2},{8,12},{10,14},{12,8},{14,10},{17,21},{19,... | collective-permute-start | bytes 3538952 | tf_op jit(solution)/shard_map/ppermute | solution.py:321
  40.3 2.5 %collective-permute-start.8 = (bf16[3,384,384]{2,1,0:T(8,128)(2,1)S(1)}, bf16[3,384,384]{2,1,0:T(8,128)(2,1)S(1)}, u32[]{:S(2)}, u32[]{:S(2)}) collective-permute-start(bf16[3,384,384]{2,1,0:T(8,128)(2,1)S(1)} %slice.21), channel_id=1, source_target_pairs={{0,1},{1,0},{2,3},{3,2},{4,5},{5,4},{6,7},{7,6},{8,9},{9,8},{10,11... | collective-permute-start | bytes 2654216 | tf_op jit(solution)/shard_map/ppermute | solution.py:311
  40.5 6.3 %collective-permute-start.10 = (bf16[1,384,384]{2,1,0:T(8,128)(2,1)S(1)}, bf16[1,384,384]{2,1,0:T(8,128)(2,1)S(1)}, u32[]{:S(2)}, u32[]{:S(2)}) collective-permute-start(bf16[1,384,384]{2,1,0:T(8,128)(2,1)S(1)} %bitcast.15), channel_id=1, source_target_pairs={{0,1},{1,0},{2,3},{3,2},{4,5},{5,4},{6,7},{7,6},{8,9},{9,8},{10,11... | collective-permute-start | bytes 884744 | tf_op jit(solution)/shard_map/ppermute | solution.py:311
  41.0 5.8 %collective-permute-start.12 = (bf16[1,384,384]{2,1,0:T(8,128)(2,1)S(1)}, bf16[1,384,384]{2,1,0:T(8,128)(2,1)S(1)}, u32[]{:S(2)}, u32[]{:S(2)}) collective-permute-start(bf16[1,384,384]{2,1,0:T(8,128)(2,1)S(1)} %slice.24), channel_id=1, source_target_pairs={{0,1},{1,0},{2,3},{3,2},{4,5},{5,4},{6,7},{7,6},{8,9},{9,8},{10,11... | collective-permute-start | bytes 884744 | tf_op jit(solution)/shard_map/ppermute | solution.py:311
  41.1 5.7 %collective-permute-start.11 = (bf16[1,384,384]{2,1,0:T(8,128)(2,1)S(1)}, bf16[1,384,384]{2,1,0:T(8,128)(2,1)S(1)}, u32[]{:S(2)}, u32[]{:S(2)}) collective-permute-start(bf16[1,384,384]{2,1,0:T(8,128)(2,1)S(1)} %slice.23), channel_id=1, source_target_pairs={{0,1},{1,0},{2,3},{3,2},{4,5},{5,4},{6,7},{7,6},{8,9},{9,8},{10,11... | collective-permute-start | bytes 884744 | tf_op jit(solution)/shard_map/ppermute | solution.py:311
  52.8 2.8 %collective-permute-start.13 = (bf16[4,384,384]{2,1,0:T(8,128)(2,1)S(1)}, bf16[4,384,384]{2,1,0:T(8,128)(2,1)S(1)}, u32[]{:S(2)}, u32[]{:S(2)}) collective-permute-start(bf16[4,384,384]{2,1,0:T(8,128)(2,1)S(1)} %collective-permute-done.1.refs_8_), channel_id=1, source_target_pairs={{0,1},{1,0},{2,3},{3,2},{4,5},{5,4},{6,7},{7,6},{8,9},{9,8},{10,11... | collective-permute-start | bytes 3538952 | tf_op jit(solution)/shard_map/ppermute | solution.py:311
  59.1 7.8 %collective-permute-start.18 = (bf16[64,1536]{1,0:T(8,128)(2,1)S(1)}, bf16[64,1536]{1,0:T(8,128)(2,1)S(1)}, u32[]{:S(2)}, u32[]{:S(2)}) collective-permute-start(bf16[64,1536]{1,0:T(8,128)(2,1)S(1)} %get-tuple-element.43), channel_id=1, source_target_pairs={{0,2},{1,3},{2,0},{3,1},{4,6},{5,7},{6,4},{7,5},{8,10},{9,11},{10,... | collective-permute-start | bytes 589832 | tf_op jit(solution)/shard_map/ppermute | solution.py:311
  61.0 7.8 %collective-permute-start.14 = (bf16[64,1536]{1,0:T(8,128)(2,1)S(1)}, bf16[64,1536]{1,0:T(8,128)(2,1)S(1)}, u32[]{:S(2)}, u32[]{:S(2)}) collective-permute-start(bf16[64,1536]{1,0:T(8,128)(2,1)S(1)} %get-tuple-element.39), channel_id=1, source_target_pairs={{0,16},{16,0},{1,17},{17,1},{2,18},{18,2},{3,19},{19,3},{4,20},{20... | collective-permute-start | bytes 589832 | tf_op jit(solution)/shard_map/ppermute | solution.py:311
  63.0 6.0 %copy-start.1 = (f32[1,3,1536]{2,0,1:T(1,128)S(1)}, f32[1,3,1536]{2,0,1:T(1,128)}, u32[]{:S(2)}) copy-start(f32[1,3,1536]{2,0,1:T(1,128)} %param.6) | copy-start | bytes 55300
  63.0 8.1 %collective-permute-start.16 = (bf16[64,1536]{1,0:T(8,128)(2,1)S(1)}, bf16[64,1536]{1,0:T(8,128)(2,1)S(1)}, u32[]{:S(2)}, u32[]{:S(2)}) collective-permute-start(bf16[64,1536]{1,0:T(8,128)(2,1)S(1)} %get-tuple-element.40), channel_id=1, source_target_pairs={{0,2},{1,3},{2,0},{3,1},{4,6},{5,7},{6,4},{7,5},{8,10},{9,11},{10,... | collective-permute-start | bytes 589832 | tf_op jit(solution)/shard_map/ppermute | solution.py:311
  63.2 9.8 %collective-permute-start.17 = (bf16[64,1536]{1,0:T(8,128)(2,1)S(1)}, bf16[64,1536]{1,0:T(8,128)(2,1)S(1)}, u32[]{:S(2)}, u32[]{:S(2)}) collective-permute-start(bf16[64,1536]{1,0:T(8,128)(2,1)S(1)} %get-tuple-element.41), channel_id=1, source_target_pairs={{0,16},{16,0},{1,17},{17,1},{2,18},{18,2},{3,19},{19,3},{4,20},{20... | collective-permute-start | bytes 589832 | tf_op jit(solution)/shard_map/ppermute | solution.py:311
  66.9 9.2 %collective-permute-start.19 = (bf16[64,1536]{1,0:T(8,128)(2,1)S(1)}, bf16[64,1536]{1,0:T(8,128)(2,1)S(1)}, u32[]{:S(2)}, u32[]{:S(2)}) collective-permute-start(bf16[64,1536]{1,0:T(8,128)(2,1)S(1)} %add_convert_fusion.1), channel_id=1, source_target_pairs={{0,16},{16,0},{1,17},{17,1},{2,18},{18,2},{3,19},{19,3},{4,20},{20... | collective-permute-start | bytes 589832 | tf_op jit(solution)/shard_map/ppermute | solution.py:311
  68.8 7.3 %collective-permute-start.15 = (bf16[64,1536]{1,0:T(8,128)(2,1)S(1)}, bf16[64,1536]{1,0:T(8,128)(2,1)S(1)}, u32[]{:S(2)}, u32[]{:S(2)}) collective-permute-start(bf16[64,1536]{1,0:T(8,128)(2,1)S(1)} %add_convert_fusion.2), channel_id=1, source_target_pairs={{0,2},{1,3},{2,0},{3,1},{4,6},{5,7},{6,4},{7,5},{8,10},{9,11},{10,... | collective-permute-start | bytes 589832 | tf_op jit(solution)/shard_map/ppermute | solution.py:311
